TPU v7x, 32 devices: a whole 2x2x4 slice. The times are simulated.
32 devices in a mesh: gx: 4 (over z), gy: 4 (over x, core), gz: 2 (over y).
Axes of the slice: x: 2, y: 2, z: 4, core: 2. Of those that a mesh axis runs over, the one named last changes fastest.
Arguments:
- terminal_adjoint: float32 [5, 32, 32, 256], P(None, 'gx', 'gy', 'gz'), may hold values from -6 to 6
- density: float32 [32, 32, 256], P('gx', 'gy', 'gz'), may hold values from 0.7 to 1.5
- velocity: float32 [3, 32, 32, 256], P(None, 'gx', 'gy', 'gz'), may hold values from -0.5 to 0.5
- stiffness: float32 [32, 32, 256], P('gx', 'gy', 'gz'), may hold values from 0.6 to 1.6
- sponge: float32 [32, 32, 256], P('gx', 'gy', 'gz'), may hold values from 0.1 to 3
- source_shape: float32 [32, 32, 256], P('gx', 'gy', 'gz'), may hold values from -0.1875 to 0.1875
- brick_level: int32 [4, 4, 2], replicated, may hold values from 0 to 1
- brick_patch: int32 [4, 4, 2], replicated, may hold values from 0 to 31, as said below
- patch_owner: int32 [32], replicated, may hold values from 0 to 31, as said below
Outputs:
- adjoint: float32 [5, 32, 32, 256], P(None, 'gx', 'gy', 'gz')
- patch_gradient: float32 [32, 40], P(('gx', 'gy', 'gz'))
Inputs may be any that keep to these rules, and one draw needn't show every extreme that they name: `brick_patch`: each brick names one patch; a patch may be named by several bricks or by none. `patch_owner`: every device owns exactly one patch.
All inputs are finite; a program needn't handle non-finite values.
Results may differ from a plain program's by a relative error of at most 0.00013.
Values sent between devices are 32-bit elements; how exact they have to be, the bound alone decides.
No kernel may reach another device: no remote copies, remote signals or barrier semaphores. Data moves between devices by JAX's collectives and lax.ppermute only.
A program may use at most 64 MiB of HBM per device.

v0:
```python
import jax
import jax.numpy as jnp
from jax import lax
from jax.sharding import PartitionSpec as P

BX = 8
BY = 8
BZ = 16


step_length = 0.14
third = 1.0 / 3.0
two_thirds = 2.0 / 3.0


def with_halo(block, sides, width):
    for axis, dim in sides:
        count = lax.axis_size(axis)
        forward = [(i, i + 1) for i in range(count - 1)]
        backward = [(target, source) for source, target in forward]
        low = lax.ppermute(
            lax.slice_in_dim(block, block.shape[dim] - width, None, axis=dim), axis, forward
        )
        high = lax.ppermute(lax.slice_in_dim(block, 0, width, axis=dim), axis, backward)
        block = jnp.concatenate([low, block, high], axis=dim)
    return block


def transposed_flux(adjoint, density, velocity, stiffness, direction):
    along_speed = velocity[direction]
    components = [along_speed * adjoint[component] for component in range(5)]
    velocity_row = 1 + direction
    components[velocity_row] = (
        components[velocity_row] + density * adjoint[0] + stiffness * adjoint[4]
    )
    components[4] = components[4] + adjoint[velocity_row] / density
    return jnp.stack(components)


def apply_faces(adjoint, density, velocity, stiffness, half_inverse, sponge):
    partials = half_inverse * transposed_flux(adjoint, density, velocity, stiffness, 0)
    padded = with_halo(partials, (("gx", 1),), 1)
    summed = padded[:, 2:] - padded[:, :-2]
    partials = half_inverse * transposed_flux(adjoint, density, velocity, stiffness, 1)
    padded = with_halo(partials, (("gy", 2),), 1)
    summed = summed + (padded[:, :, 2:] - padded[:, :, :-2])
    partials = half_inverse * transposed_flux(adjoint, density, velocity, stiffness, 2)
    padded = with_halo(partials, (("gz", 3),), 1)
    summed = summed + (padded[:, :, :, 2:] - padded[:, :, :, :-2])
    return summed - sponge * adjoint


def body(
    terminal_adjoint,
    density,
    velocity,
    stiffness,
    sponge,
    source_shape,
    brick_level,
    brick_patch,
    patch_owner,
):
    index_x = lax.axis_index("gx")
    index_y = lax.axis_index("gy")
    index_z = lax.axis_index("gz")
    count_y = lax.axis_size("gy")
    count_z = lax.axis_size("gz")
    cells_x, cells_y, cells_z = density.shape
    own_brick = (index_x * count_y + index_y) * count_z + index_z
    patch_index = jnp.arange(patch_owner.shape[0], dtype=jnp.int32)
    own_patch = jnp.sum(jnp.where(patch_owner == own_brick, patch_index, 0))
    selector = (brick_patch.reshape(1, -1) == own_patch).astype(jnp.float32)
    own_level = brick_level[index_x, index_y, index_z]
    half_inverse = 0.5 * jnp.exp2(own_level.astype(jnp.float32))

    def apply_op(field_now):
        return apply_faces(field_now, density, velocity, stiffness, half_inverse, sponge)

    adjoint = terminal_adjoint
    section_one = adjoint + step_length * apply_op(adjoint)
    section_two = 0.75 * adjoint + 0.25 * (section_one + step_length * apply_op(section_one))
    adjoint = third * adjoint + two_thirds * (section_two + step_length * apply_op(section_two))
    weighted = adjoint * source_shape
    boxed = weighted.reshape(5, cells_x // BX, BX, cells_y // BY, BY, cells_z // BZ, BZ)
    block_now = step_length * jnp.sum(boxed, axis=(2, 4, 6)).reshape(1, -1)
    gradient = jnp.dot(
        selector,
        lax.all_gather(block_now, ("gx", "gy", "gz"), axis=0, tiled=True),
        preferred_element_type=jnp.float32,
        precision=lax.Precision.HIGHEST,
    )
    return (adjoint, gradient)


def solution(mesh):
    in_specs = (
        P(None, "gx", "gy", "gz"),
        P("gx", "gy", "gz"),
        P(None, "gx", "gy", "gz"),
        P("gx", "gy", "gz"),
        P("gx", "gy", "gz"),
        P("gx", "gy", "gz"),
        P(),
        P(),
        P(),
    )
    out_specs = (P(None, "gx", "gy", "gz"), P(("gx", "gy", "gz"), None))
    return jax.shard_map(body, mesh=mesh, in_specs=in_specs, out_specs=out_specs, check_vma=False)
```

profile of v0, /device:TPU:0, one launch (start us, length us, event | category | flops | bytes accessed | tf_op | source)
XLA Modules:
  0.0 132.8 jit_solution(1076123096065867272)
XLA Ops:
  0.6 1.3 dynamic_slice.3
  2.7 0.8 constant_dynamic-update-slice_fusion.9
  5.2 1.3 collective-permute-start
  6.5 5.6 %collective-permute-start.1 = (f32[5,1,8,128]{3,2,1,0:T(8,128)S(1)}, f32[5,1,8,128]{3,2,1,0:T(8,128)S(1)}, u32[]{:S(2)}, u32[]{:S(2)}) collective-permute-start(f32[5,1,8,128]{3,2,1,0:T(8,128)S(1)} %get-tuple-element.50), channel_id=1, source_target_pairs={{0,8},{8,16},{16,24},{1,9},{9,17},{17,25},{2,10},{10,18},{18,26},{... | collective-permute-start | bytes 61448 | tf_op jit(solution)/shard_map/ppermute | solution.py:21
  12.1 1.3 collective-permute-start.2
  13.4 3.0 %collective-permute-start.3 = (f32[5,8,1,128]{3,2,1,0:T(1,128)S(1)}, f32[5,8,1,128]{3,2,1,0:T(1,128)S(1)}, u32[]{:S(2)}, u32[]{:S(2)}) collective-permute-start(f32[5,8,1,128]{3,2,1,0:T(1,128)S(1)} %get-tuple-element.52), channel_id=1, source_target_pairs={{0,2},{2,4},{4,6},{1,3},{3,5},{5,7},{8,10},{10,12},{12,14},{9,11},... | collective-permute-start | bytes 61448 | tf_op jit(solution)/shard_map/ppermute | solution.py:21
  16.6 1.3 collective-permute-start.4
  17.9 7.1 %collective-permute-done.4 = f32[5,8,8,1]{3,2,1,0:T(8,128)S(1)} collective-permute-done((f32[5,8,8,1]{3,2,1,0:T(8,128)S(1)}, f32[5,8,8,1]{3,2,1,0:T(8,128)S(1)}, u32[]{:S(2)}, u32[]{:S(2)}) %collective-permute-start.4) | collective-permute-done | bytes 1312 | tf_op jit(solution)/shard_map/ppermute | solution.py:24
  25.1 1.4 %collective-permute-start.5 = (f32[5,8,8,1]{3,2,1,0:T(8,128)S(1)}, f32[5,8,8,1]{3,2,1,0:T(8,128)S(1)}, u32[]{:S(2)}, u32[]{:S(2)}) collective-permute-start(f32[5,8,8,1]{3,2,1,0:T(8,128)S(1)} %get-tuple-element.54), channel_id=1, source_target_pairs={{0,1},{2,3},{4,5},{6,7},{8,9},{10,11},{12,13},{14,15},{16,17},{18,... | collective-permute-start | bytes 3848 | tf_op jit(solution)/shard_map/ppermute | solution.py:21
  26.5 4.2 %collective-permute-done.5 = f32[5,8,8,1]{3,2,1,0:T(8,128)S(1)} collective-permute-done((f32[5,8,8,1]{3,2,1,0:T(8,128)S(1)}, f32[5,8,8,1]{3,2,1,0:T(8,128)S(1)}, u32[]{:S(2)}, u32[]{:S(2)}) %collective-permute-start.5) | collective-permute-done | bytes 1312 | tf_op jit(solution)/shard_map/ppermute | solution.py:21
  31.3 1.3 collective-permute-start.10
  32.6 4.6 %collective-permute-start.11 = (f32[5,8,8,1]{3,2,1,0:T(8,128)S(1)}, f32[5,8,8,1]{3,2,1,0:T(8,128)S(1)}, u32[]{:S(2)}, u32[]{:S(2)}) collective-permute-start(f32[5,8,8,1]{3,2,1,0:T(8,128)S(1)} %get-tuple-element.48), channel_id=1, source_target_pairs={{0,1},{2,3},{4,5},{6,7},{8,9},{10,11},{12,13},{14,15},{16,17},{18,... | collective-permute-start | bytes 3848 | tf_op jit(solution)/shard_map/ppermute | solution.py:21
  37.2 1.3 collective-permute-start.6
  38.5 4.6 %collective-permute-start.7 = (f32[5,1,8,128]{3,2,1,0:T(8,128)S(1)}, f32[5,1,8,128]{3,2,1,0:T(8,128)S(1)}, u32[]{:S(2)}, u32[]{:S(2)}) collective-permute-start(f32[5,1,8,128]{3,2,1,0:T(8,128)S(1)} %get-tuple-element.44), channel_id=1, source_target_pairs={{0,8},{8,16},{16,24},{1,9},{9,17},{17,25},{2,10},{10,18},{18,26},{... | collective-permute-start | bytes 61448 | tf_op jit(solution)/shard_map/ppermute | solution.py:21
  43.2 1.3 collective-permute-start.8
  44.5 3.0 %collective-permute-start.9 = (f32[5,8,1,128]{3,2,1,0:T(1,128)S(1)}, f32[5,8,1,128]{3,2,1,0:T(1,128)S(1)}, u32[]{:S(2)}, u32[]{:S(2)}) collective-permute-start(f32[5,8,1,128]{3,2,1,0:T(1,128)S(1)} %get-tuple-element.46), channel_id=1, source_target_pairs={{0,2},{2,4},{4,6},{1,3},{3,5},{5,7},{8,10},{10,12},{12,14},{9,11},... | collective-permute-start | bytes 61448 | tf_op jit(solution)/shard_map/ppermute | solution.py:21
  48.8 1.3 collective-permute-start.16
  50.1 4.6 %collective-permute-start.17 = (f32[5,8,8,1]{3,2,1,0:T(8,128)S(1)}, f32[5,8,8,1]{3,2,1,0:T(8,128)S(1)}, u32[]{:S(2)}, u32[]{:S(2)}) collective-permute-start(f32[5,8,8,1]{3,2,1,0:T(8,128)S(1)} %get-tuple-element.42), channel_id=1, source_target_pairs={{0,1},{2,3},{4,5},{6,7},{8,9},{10,11},{12,13},{14,15},{16,17},{18,... | collective-permute-start | bytes 3848 | tf_op jit(solution)/shard_map/ppermute | solution.py:21
  54.7 1.3 collective-permute-start.12
  56.0 4.6 %collective-permute-start.13 = (f32[5,1,8,128]{3,2,1,0:T(8,128)S(1)}, f32[5,1,8,128]{3,2,1,0:T(8,128)S(1)}, u32[]{:S(2)}, u32[]{:S(2)}) collective-permute-start(f32[5,1,8,128]{3,2,1,0:T(8,128)S(1)} %get-tuple-element.38), channel_id=1, source_target_pairs={{0,8},{8,16},{16,24},{1,9},{9,17},{17,25},{2,10},{10,18},{18,26},{... | collective-permute-start | bytes 61448 | tf_op jit(solution)/shard_map/ppermute | solution.py:21
  60.7 1.3 collective-permute-start.14
  62.0 3.0 %collective-permute-start.15 = (f32[5,8,1,128]{3,2,1,0:T(1,128)S(1)}, f32[5,8,1,128]{3,2,1,0:T(1,128)S(1)}, u32[]{:S(2)}, u32[]{:S(2)}) collective-permute-start(f32[5,8,1,128]{3,2,1,0:T(1,128)S(1)} %get-tuple-element.40), channel_id=1, source_target_pairs={{0,2},{2,4},{4,6},{1,3},{3,5},{5,7},{8,10},{10,12},{12,14},{9,11},... | collective-permute-start | bytes 61448 | tf_op jit(solution)/shard_map/ppermute | solution.py:21
  66.0 0.9 multiply_reduce_fusion
  67.1 65.1 %all-gather = f32[32,1,40]{2,1,0:T(1,128)S(1)} all-gather(f32[1,1,40]{2,1,0:T(1,128)S(1)} %reshape.40), channel_id=1, replica_groups=mesh['gx'=4,'gy'=4,'gz'=2] {'gx','gy','gz'}, dimensions={0}, use_global_device_ids=true | all-gather | bytes 5280 | tf_op jit(solution)/shard_map/all_gather | solution.py:89
  (84 shorter events, 5.4 us)
Async XLA Ops:
  0.6 2.9 %copy-start = (f32[3,8,8,128]{3,2,1,0:T(8,128)S(1)}, f32[3,8,8,128]{3,2,1,0:T(8,128)}, u32[]{:S(2)}) copy-start(f32[3,8,8,128]{3,2,1,0:T(8,128)} %param.11) | copy-start | bytes 294916
  2.6 1.6 %copy-start.1 = (f32[5,8,8,128]{3,2,1,0:T(8,128)S(1)}, f32[5,8,8,128]{3,2,1,0:T(8,128)}, u32[]{:S(2)}) copy-start(f32[5,8,8,128]{3,2,1,0:T(8,128)} %param.9) | copy-start | bytes 491524
  5.2 25.5 %collective-permute-start = (f32[5,1,8,128]{3,2,1,0:T(8,128)S(1)}, f32[5,1,8,128]{3,2,1,0:T(8,128)S(1)}, u32[]{:S(2)}, u32[]{:S(2)}) collective-permute-start(f32[5,1,8,128]{3,2,1,0:T(8,128)S(1)} %get-tuple-element.49), channel_id=1, source_target_pairs={{8,0},{16,8},{24,16},{9,1},{17,9},{25,17},{10,2},{18,10},{26,18},{... | collective-permute-start | bytes 61448 | tf_op jit(solution)/shard_map/ppermute | solution.py:24
  6.5 24.2 %collective-permute-start.1 = (f32[5,1,8,128]{3,2,1,0:T(8,128)S(1)}, f32[5,1,8,128]{3,2,1,0:T(8,128)S(1)}, u32[]{:S(2)}, u32[]{:S(2)}) collective-permute-start(f32[5,1,8,128]{3,2,1,0:T(8,128)S(1)} %get-tuple-element.50), channel_id=1, source_target_pairs={{0,8},{8,16},{16,24},{1,9},{9,17},{17,25},{2,10},{10,18},{18,26},{... | collective-permute-start | bytes 61448 | tf_op jit(solution)/shard_map/ppermute | solution.py:21
  12.1 18.6 %collective-permute-start.2 = (f32[5,8,1,128]{3,2,1,0:T(1,128)S(1)}, f32[5,8,1,128]{3,2,1,0:T(1,128)S(1)}, u32[]{:S(2)}, u32[]{:S(2)}) collective-permute-start(f32[5,8,1,128]{3,2,1,0:T(1,128)S(1)} %get-tuple-element.51), channel_id=1, source_target_pairs={{2,0},{4,2},{6,4},{3,1},{5,3},{7,5},{10,8},{12,10},{14,12},{11,9},... | collective-permute-start | bytes 61448 | tf_op jit(solution)/shard_map/ppermute | solution.py:24
  13.4 17.3 %collective-permute-start.3 = (f32[5,8,1,128]{3,2,1,0:T(1,128)S(1)}, f32[5,8,1,128]{3,2,1,0:T(1,128)S(1)}, u32[]{:S(2)}, u32[]{:S(2)}) collective-permute-start(f32[5,8,1,128]{3,2,1,0:T(1,128)S(1)} %get-tuple-element.52), channel_id=1, source_target_pairs={{0,2},{2,4},{4,6},{1,3},{3,5},{5,7},{8,10},{10,12},{12,14},{9,11},... | collective-permute-start | bytes 61448 | tf_op jit(solution)/shard_map/ppermute | solution.py:21
  16.5 14.3 %copy-start.3 = (f32[8,8,128]{2,1,0:T(8,128)S(1)}, f32[8,8,128]{2,1,0:T(8,128)}, u32[]{:S(2)}) copy-start(f32[8,8,128]{2,1,0:T(8,128)} %param.13) | copy-start | bytes 98308
  16.6 8.4 %collective-permute-start.4 = (f32[5,8,8,1]{3,2,1,0:T(8,128)S(1)}, f32[5,8,8,1]{3,2,1,0:T(8,128)S(1)}, u32[]{:S(2)}, u32[]{:S(2)}) collective-permute-start(f32[5,8,8,1]{3,2,1,0:T(8,128)S(1)} %get-tuple-element.53), channel_id=1, source_target_pairs={{1,0},{3,2},{5,4},{7,6},{9,8},{11,10},{13,12},{15,14},{17,16},{19,... | collective-permute-start | bytes 3848 | tf_op jit(solution)/shard_map/ppermute | solution.py:24
  25.1 5.7 %collective-permute-start.5 = (f32[5,8,8,1]{3,2,1,0:T(8,128)S(1)}, f32[5,8,8,1]{3,2,1,0:T(8,128)S(1)}, u32[]{:S(2)}, u32[]{:S(2)}) collective-permute-start(f32[5,8,8,1]{3,2,1,0:T(8,128)S(1)} %get-tuple-element.54), channel_id=1, source_target_pairs={{0,1},{2,3},{4,5},{6,7},{8,9},{10,11},{12,13},{14,15},{16,17},{18,... | collective-permute-start | bytes 3848 | tf_op jit(solution)/shard_map/ppermute | solution.py:21
  31.3 13.2 %collective-permute-start.10 = (f32[5,8,8,1]{3,2,1,0:T(8,128)S(1)}, f32[5,8,8,1]{3,2,1,0:T(8,128)S(1)}, u32[]{:S(2)}, u32[]{:S(2)}) collective-permute-start(f32[5,8,8,1]{3,2,1,0:T(8,128)S(1)} %get-tuple-element.47), channel_id=1, source_target_pairs={{1,0},{3,2},{5,4},{7,6},{9,8},{11,10},{13,12},{15,14},{17,16},{19,... | collective-permute-start | bytes 3848 | tf_op jit(solution)/shard_map/ppermute | solution.py:24
  32.6 15.6 %collective-permute-start.11 = (f32[5,8,8,1]{3,2,1,0:T(8,128)S(1)}, f32[5,8,8,1]{3,2,1,0:T(8,128)S(1)}, u32[]{:S(2)}, u32[]{:S(2)}) collective-permute-start(f32[5,8,8,1]{3,2,1,0:T(8,128)S(1)} %get-tuple-element.48), channel_id=1, source_target_pairs={{0,1},{2,3},{4,5},{6,7},{8,9},{10,11},{12,13},{14,15},{16,17},{18,... | collective-permute-start | bytes 3848 | tf_op jit(solution)/shard_map/ppermute | solution.py:21
  37.2 11.0 %collective-permute-start.6 = (f32[5,1,8,128]{3,2,1,0:T(8,128)S(1)}, f32[5,1,8,128]{3,2,1,0:T(8,128)S(1)}, u32[]{:S(2)}, u32[]{:S(2)}) collective-permute-start(f32[5,1,8,128]{3,2,1,0:T(8,128)S(1)} %get-tuple-element.43), channel_id=1, source_target_pairs={{8,0},{16,8},{24,16},{9,1},{17,9},{25,17},{10,2},{18,10},{26,18},{... | collective-permute-start | bytes 61448 | tf_op jit(solution)/shard_map/ppermute | solution.py:24
  38.5 9.7 %collective-permute-start.7 = (f32[5,1,8,128]{3,2,1,0:T(8,128)S(1)}, f32[5,1,8,128]{3,2,1,0:T(8,128)S(1)}, u32[]{:S(2)}, u32[]{:S(2)}) collective-permute-start(f32[5,1,8,128]{3,2,1,0:T(8,128)S(1)} %get-tuple-element.44), channel_id=1, source_target_pairs={{0,8},{8,16},{16,24},{1,9},{9,17},{17,25},{2,10},{10,18},{18,26},{... | collective-permute-start | bytes 61448 | tf_op jit(solution)/shard_map/ppermute | solution.py:21
  43.1 4.4 %copy-start.7 = (s32[32]{0:T(128)S(1)}, s32[32]{0:T(128)}, u32[]{:S(2)}) copy-start(s32[32]{0:T(128)} %param.17) | copy-start | bytes 388
  43.2 5.0 %collective-permute-start.8 = (f32[5,8,1,128]{3,2,1,0:T(1,128)S(1)}, f32[5,8,1,128]{3,2,1,0:T(1,128)S(1)}, u32[]{:S(2)}, u32[]{:S(2)}) collective-permute-start(f32[5,8,1,128]{3,2,1,0:T(1,128)S(1)} %get-tuple-element.45), channel_id=1, source_target_pairs={{2,0},{4,2},{6,4},{3,1},{5,3},{7,5},{10,8},{12,10},{14,12},{11,9},... | collective-permute-start | bytes 61448 | tf_op jit(solution)/shard_map/ppermute | solution.py:24
  44.5 3.9 %collective-permute-start.9 = (f32[5,8,1,128]{3,2,1,0:T(1,128)S(1)}, f32[5,8,1,128]{3,2,1,0:T(1,128)S(1)}, u32[]{:S(2)}, u32[]{:S(2)}) collective-permute-start(f32[5,8,1,128]{3,2,1,0:T(1,128)S(1)} %get-tuple-element.46), channel_id=1, source_target_pairs={{0,2},{2,4},{4,6},{1,3},{3,5},{5,7},{8,10},{10,12},{12,14},{9,11},... | collective-permute-start | bytes 61448 | tf_op jit(solution)/shard_map/ppermute | solution.py:21
  48.8 13.1 %collective-permute-start.16 = (f32[5,8,8,1]{3,2,1,0:T(8,128)S(1)}, f32[5,8,8,1]{3,2,1,0:T(8,128)S(1)}, u32[]{:S(2)}, u32[]{:S(2)}) collective-permute-start(f32[5,8,8,1]{3,2,1,0:T(8,128)S(1)} %get-tuple-element.41), channel_id=1, source_target_pairs={{1,0},{3,2},{5,4},{7,6},{9,8},{11,10},{13,12},{15,14},{17,16},{19,... | collective-permute-start | bytes 3848 | tf_op jit(solution)/shard_map/ppermute | solution.py:24
  50.1 15.8 %collective-permute-start.17 = (f32[5,8,8,1]{3,2,1,0:T(8,128)S(1)}, f32[5,8,8,1]{3,2,1,0:T(8,128)S(1)}, u32[]{:S(2)}, u32[]{:S(2)}) collective-permute-start(f32[5,8,8,1]{3,2,1,0:T(8,128)S(1)} %get-tuple-element.42), channel_id=1, source_target_pairs={{0,1},{2,3},{4,5},{6,7},{8,9},{10,11},{12,13},{14,15},{16,17},{18,... | collective-permute-start | bytes 3848 | tf_op jit(solution)/shard_map/ppermute | solution.py:21
  54.7 11.2 %collective-permute-start.12 = (f32[5,1,8,128]{3,2,1,0:T(8,128)S(1)}, f32[5,1,8,128]{3,2,1,0:T(8,128)S(1)}, u32[]{:S(2)}, u32[]{:S(2)}) collective-permute-start(f32[5,1,8,128]{3,2,1,0:T(8,128)S(1)} %get-tuple-element.37), channel_id=1, source_target_pairs={{8,0},{16,8},{24,16},{9,1},{17,9},{25,17},{10,2},{18,10},{26,18},{... | collective-permute-start | bytes 61448 | tf_op jit(solution)/shard_map/ppermute | solution.py:24
  56.0 9.9 %collective-permute-start.13 = (f32[5,1,8,128]{3,2,1,0:T(8,128)S(1)}, f32[5,1,8,128]{3,2,1,0:T(8,128)S(1)}, u32[]{:S(2)}, u32[]{:S(2)}) collective-permute-start(f32[5,1,8,128]{3,2,1,0:T(8,128)S(1)} %get-tuple-element.38), channel_id=1, source_target_pairs={{0,8},{8,16},{16,24},{1,9},{9,17},{17,25},{2,10},{10,18},{18,26},{... | collective-permute-start | bytes 61448 | tf_op jit(solution)/shard_map/ppermute | solution.py:21
  60.6 4.4 %copy-start.6 = (s32[4,4,2]{1,2,0:T(2,128)S(1)}, s32[4,4,2]{1,2,0:T(2,128)}, u32[]{:S(2)}) copy-start(s32[4,4,2]{1,2,0:T(2,128)} %param.16) | copy-start | bytes 388
  60.6 5.3 %copy-start.5 = (f32[8,8,128]{2,1,0:T(8,128)S(1)}, f32[8,8,128]{2,1,0:T(8,128)}, u32[]{:S(2)}) copy-start(f32[8,8,128]{2,1,0:T(8,128)} %param.14) | copy-start | bytes 98308
  60.7 5.3 %collective-permute-start.14 = (f32[5,8,1,128]{3,2,1,0:T(1,128)S(1)}, f32[5,8,1,128]{3,2,1,0:T(1,128)S(1)}, u32[]{:S(2)}, u32[]{:S(2)}) collective-permute-start(f32[5,8,1,128]{3,2,1,0:T(1,128)S(1)} %get-tuple-element.39), channel_id=1, source_target_pairs={{2,0},{4,2},{6,4},{3,1},{5,3},{7,5},{10,8},{12,10},{14,12},{11,9},... | collective-permute-start | bytes 61448 | tf_op jit(solution)/shard_map/ppermute | solution.py:24
  62.0 4.0 %collective-permute-start.15 = (f32[5,8,1,128]{3,2,1,0:T(1,128)S(1)}, f32[5,8,1,128]{3,2,1,0:T(1,128)S(1)}, u32[]{:S(2)}, u32[]{:S(2)}) collective-permute-start(f32[5,8,1,128]{3,2,1,0:T(1,128)S(1)} %get-tuple-element.40), channel_id=1, source_target_pairs={{0,2},{2,4},{4,6},{1,3},{3,5},{5,7},{8,10},{10,12},{12,14},{9,11},... | collective-permute-start | bytes 61448 | tf_op jit(solution)/shard_map/ppermute | solution.py:21
  (2 other events, 1.5 us)
where the time goes:
time: 134 us; the launch traced here: 133 us
  blocking collectives  65.1 us (49%)
  starting transfers between devices  46 us (34%)
  waiting for transfers between devices  11.6 us (9%)
  other arithmetic  4.71 us (4%)
  local copies, waits for them, and re-layouts  2.86 us (2%)
  between operations  2 us (1%)
    all_gather x1, blocking collectives, body(): lax.all_gather(block_now, ('gx', 'gy', 'gz'), axis=0, tiled=True)  65.1 us
    ppermute x9, starting transfers between devices, with_halo(): lax.ppermute(lax.slice_in_dim(block, block.shape[dim] - width, None, axis...  34.4 us
    ppermute x9, starting transfers between devices, with_halo(): lax.ppermute(lax.slice_in_dim(block, 0, width, axis=dim), axis, backward)  11.6 us
    ppermute x9, waiting for transfers between devices, with_halo(): lax.ppermute(lax.slice_in_dim(block, 0, width, axis=dim), axis, backward)  7.17 us
    ppermute x9, waiting for transfers between devices, with_halo(): lax.ppermute(lax.slice_in_dim(block, block.shape[dim] - width, None, axis...  4.4 us
  transfers between devices with their start and end apart: 18, of which 3 were waited for; matrix products, arithmetic and copies ran while one was open for 1% of the time, Pallas kernels for 0%

commit v1 on v0

--- a/solution.py
+++ b/solution.py
@@ -68,9 +68,9 @@
     count_z = lax.axis_size("gz")
     cells_x, cells_y, cells_z = density.shape
     own_brick = (index_x * count_y + index_y) * count_z + index_z
-    patch_index = jnp.arange(patch_owner.shape[0], dtype=jnp.int32)
-    own_patch = jnp.sum(jnp.where(patch_owner == own_brick, patch_index, 0))
-    selector = (brick_patch.reshape(1, -1) == own_patch).astype(jnp.float32)
+    own_patch = brick_patch[index_x, index_y, index_z]
+    target = patch_owner[own_patch]
+    devices = patch_owner.shape[0]
     own_level = brick_level[index_x, index_y, index_z]
     half_inverse = 0.5 * jnp.exp2(own_level.astype(jnp.float32))
 
@@ -84,12 +84,10 @@
     weighted = adjoint * source_shape
     boxed = weighted.reshape(5, cells_x // BX, BX, cells_y // BY, BY, cells_z // BZ, BZ)
     block_now = step_length * jnp.sum(boxed, axis=(2, 4, 6)).reshape(1, -1)
-    gradient = jnp.dot(
-        selector,
-        lax.all_gather(block_now, ("gx", "gy", "gz"), axis=0, tiled=True),
-        preferred_element_type=jnp.float32,
-        precision=lax.Precision.HIGHEST,
-    )
+    rows = jnp.arange(devices, dtype=jnp.int32)[:, None]
+    outgoing = jnp.where(rows == target, block_now, 0.0)
+    incoming = lax.all_to_all(outgoing, ("gx", "gy", "gz"), 0, 0, tiled=True)
+    gradient = jnp.sum(incoming, axis=0, keepdims=True)
     return (adjoint, gradient)
 
 

time: 134 us -> 87.5 us (0.65)
  blocking collectives: 65.1 us -> 11.8 us
  waiting for transfers between devices: 11.6 us -> 18.8 us
  starting transfers between devices: 46 us -> 42.9 us
  between operations: 2 us -> 3.92 us
  local copies, waits for them, and re-layouts: 2.86 us -> 4.49 us
    all_gather x1 -> x0, blocking collectives: 65.1 us -> none  [body(): lax.all_gather(block_now, ('gx', 'gy', 'gz'), axis=0, tiled=True)]
    all_to_all x0 -> x1, blocking collectives: none -> 11.8 us  [body(): incoming = lax.all_to_all(outgoing, ('gx', 'gy', 'gz'), 0, 0, tiled=True)]
    ppermute x9, waiting for transfers between devices: 7.17 us -> 14.4 us  [with_halo(): lax.ppermute(lax.slice_in_dim(block, 0, width, axis=dim), axis, backward)]
    ppermute x9, starting transfers between devices: 34.4 us -> 31.2 us  [with_halo(): lax.ppermute(lax.slice_in_dim(block, block.shape[dim] - width, None, axis...]
    dynamic_slice x0 -> x2, local copies, waits for them, and re-layouts: none -> 1.86 us  [the longest x1 1.27 us: body(): own_patch = brick_patch[index_x, index_y, index_z]]
  transfers between devices with their start and end apart: 18 -> 18, of which waited for: 3 -> 4; matrix products, arithmetic and copies ran while one was open for 1% -> 3% of each run, Pallas kernels for 0% -> 0%
where the time goes in v1:
time: 87.5 us; the launch traced here: 86.6 us
  starting transfers between devices  42.9 us (49%)
  waiting for transfers between devices  18.8 us (21%)
  blocking collectives  11.8 us (13%)
  other arithmetic  4.73 us (5%)
  local copies, waits for them, and re-layouts  4.49 us (5%)
  between operations  3.92 us (4%)
    ppermute x9, starting transfers between devices, with_halo(): lax.ppermute(lax.slice_in_dim(block, block.shape[dim] - width, None, axis...  31.2 us
    ppermute x9, waiting for transfers between devices, with_halo(): lax.ppermute(lax.slice_in_dim(block, 0, width, axis=dim), axis, backward)  14.4 us
    all_to_all x1, blocking collectives, body(): incoming = lax.all_to_all(outgoing, ('gx', 'gy', 'gz'), 0, 0, tiled=True)  11.8 us
    ppermute x9, starting transfers between devices, with_halo(): lax.ppermute(lax.slice_in_dim(block, 0, width, axis=dim), axis, backward)  11.6 us
    ppermute x9, waiting for transfers between devices, with_halo(): lax.ppermute(lax.slice_in_dim(block, block.shape[dim] - width, None, axis...  4.38 us
    unnamed x21, other arithmetic  1.81 us
  transfers between devices with their start and end apart: 18, of which 4 were waited for; matrix products, arithmetic and copies ran while one was open for 3% of the time, Pallas kernels for 0%

profile of v1, /device:TPU:0, one launch (start us, length us, event | category | flops | bytes accessed | tf_op | source)
XLA Modules:
  0.0 86.6 jit_solution(4547153229771091742)
XLA Ops:
  0.6 1.3 %dynamic_slice.9 = s32[1,1,1]{1,2,0:T(1,128)} dynamic-slice(s32[4,4,2]{1,2,0:T(2,128)} %param.15, s32[]{:T(128)S(6)} %select_n.26, s32[]{:T(128)S(6)} %select_n.27, s32[]{:T(128)S(6)} %select_n.28), dynamic_slice_sizes={1,1,1} | dynamic-slice | bytes 12 | tf_op jit(solution)/shard_map/dynamic_slice | solution.py:74
  5.2 1.3 %collective-permute-start = (f32[5,1,8,128]{3,2,1,0:T(8,128)S(1)}, f32[5,1,8,128]{3,2,1,0:T(8,128)S(1)}, u32[]{:S(2)}, u32[]{:S(2)}) collective-permute-start(f32[5,1,8,128]{3,2,1,0:T(8,128)S(1)} %get-tuple-element.49), channel_id=1, source_target_pairs={{8,0},{16,8},{24,16},{9,1},{17,9},{25,17},{10,2},{18,10},{26,18},{... | collective-permute-start | bytes 61448 | tf_op jit(solution)/shard_map/ppermute | solution.py:24
  6.5 5.6 %collective-permute-start.1 = (f32[5,1,8,128]{3,2,1,0:T(8,128)S(1)}, f32[5,1,8,128]{3,2,1,0:T(8,128)S(1)}, u32[]{:S(2)}, u32[]{:S(2)}) collective-permute-start(f32[5,1,8,128]{3,2,1,0:T(8,128)S(1)} %get-tuple-element.50), channel_id=1, source_target_pairs={{0,8},{8,16},{16,24},{1,9},{9,17},{17,25},{2,10},{10,18},{18,26},{... | collective-permute-start | bytes 61448 | tf_op jit(solution)/shard_map/ppermute | solution.py:21
  12.1 1.3 %collective-permute-start.2 = (f32[5,8,1,128]{3,2,1,0:T(1,128)S(1)}, f32[5,8,1,128]{3,2,1,0:T(1,128)S(1)}, u32[]{:S(2)}, u32[]{:S(2)}) collective-permute-start(f32[5,8,1,128]{3,2,1,0:T(1,128)S(1)} %get-tuple-element.51), channel_id=1, source_target_pairs={{2,0},{4,2},{6,4},{3,1},{5,3},{7,5},{10,8},{12,10},{14,12},{11,9},... | collective-permute-start | bytes 61448 | tf_op jit(solution)/shard_map/ppermute | solution.py:24
  13.4 3.0 %collective-permute-start.3 = (f32[5,8,1,128]{3,2,1,0:T(1,128)S(1)}, f32[5,8,1,128]{3,2,1,0:T(1,128)S(1)}, u32[]{:S(2)}, u32[]{:S(2)}) collective-permute-start(f32[5,8,1,128]{3,2,1,0:T(1,128)S(1)} %get-tuple-element.52), channel_id=1, source_target_pairs={{0,2},{2,4},{4,6},{1,3},{3,5},{5,7},{8,10},{10,12},{12,14},{9,11},... | collective-permute-start | bytes 61448 | tf_op jit(solution)/shard_map/ppermute | solution.py:21
  16.6 1.3 %collective-permute-start.4 = (f32[5,8,8,1]{3,2,1,0:T(8,128)S(1)}, f32[5,8,8,1]{3,2,1,0:T(8,128)S(1)}, u32[]{:S(2)}, u32[]{:S(2)}) collective-permute-start(f32[5,8,8,1]{3,2,1,0:T(8,128)S(1)} %get-tuple-element.53), channel_id=1, source_target_pairs={{1,0},{3,2},{5,4},{7,6},{9,8},{11,10},{13,12},{15,14},{17,16},{19,... | collective-permute-start | bytes 3848 | tf_op jit(solution)/shard_map/ppermute | solution.py:24
  17.9 7.1 %collective-permute-done.4 = f32[5,8,8,1]{3,2,1,0:T(8,128)S(1)} collective-permute-done((f32[5,8,8,1]{3,2,1,0:T(8,128)S(1)}, f32[5,8,8,1]{3,2,1,0:T(8,128)S(1)}, u32[]{:S(2)}, u32[]{:S(2)}) %collective-permute-start.4) | collective-permute-done | bytes 1312 | tf_op jit(solution)/shard_map/ppermute | solution.py:24
  25.1 1.4 %collective-permute-start.5 = (f32[5,8,8,1]{3,2,1,0:T(8,128)S(1)}, f32[5,8,8,1]{3,2,1,0:T(8,128)S(1)}, u32[]{:S(2)}, u32[]{:S(2)}) collective-permute-start(f32[5,8,8,1]{3,2,1,0:T(8,128)S(1)} %get-tuple-element.54), channel_id=1, source_target_pairs={{0,1},{2,3},{4,5},{6,7},{8,9},{10,11},{12,13},{14,15},{16,17},{18,... | collective-permute-start | bytes 3848 | tf_op jit(solution)/shard_map/ppermute | solution.py:21
  26.5 4.2 %collective-permute-done.5 = f32[5,8,8,1]{3,2,1,0:T(8,128)S(1)} collective-permute-done((f32[5,8,8,1]{3,2,1,0:T(8,128)S(1)}, f32[5,8,8,1]{3,2,1,0:T(8,128)S(1)}, u32[]{:S(2)}, u32[]{:S(2)}) %collective-permute-start.5) | collective-permute-done | bytes 1312 | tf_op jit(solution)/shard_map/ppermute | solution.py:21
  31.2 1.3 %collective-permute-start.6 = (f32[5,1,8,128]{3,2,1,0:T(8,128)S(1)}, f32[5,1,8,128]{3,2,1,0:T(8,128)S(1)}, u32[]{:S(2)}, u32[]{:S(2)}) collective-permute-start(f32[5,1,8,128]{3,2,1,0:T(8,128)S(1)} %get-tuple-element.43), channel_id=1, source_target_pairs={{8,0},{16,8},{24,16},{9,1},{17,9},{25,17},{10,2},{18,10},{26,18},{... | collective-permute-start | bytes 61448 | tf_op jit(solution)/shard_map/ppermute | solution.py:24
  32.5 4.6 %collective-permute-start.7 = (f32[5,1,8,128]{3,2,1,0:T(8,128)S(1)}, f32[5,1,8,128]{3,2,1,0:T(8,128)S(1)}, u32[]{:S(2)}, u32[]{:S(2)}) collective-permute-start(f32[5,1,8,128]{3,2,1,0:T(8,128)S(1)} %get-tuple-element.44), channel_id=1, source_target_pairs={{0,8},{8,16},{16,24},{1,9},{9,17},{17,25},{2,10},{10,18},{18,26},{... | collective-permute-start | bytes 61448 | tf_op jit(solution)/shard_map/ppermute | solution.py:21
  37.2 1.3 %collective-permute-start.8 = (f32[5,8,1,128]{3,2,1,0:T(1,128)S(1)}, f32[5,8,1,128]{3,2,1,0:T(1,128)S(1)}, u32[]{:S(2)}, u32[]{:S(2)}) collective-permute-start(f32[5,8,1,128]{3,2,1,0:T(1,128)S(1)} %get-tuple-element.45), channel_id=1, source_target_pairs={{2,0},{4,2},{6,4},{3,1},{5,3},{7,5},{10,8},{12,10},{14,12},{11,9},... | collective-permute-start | bytes 61448 | tf_op jit(solution)/shard_map/ppermute | solution.py:24
  38.5 3.0 %collective-permute-start.9 = (f32[5,8,1,128]{3,2,1,0:T(1,128)S(1)}, f32[5,8,1,128]{3,2,1,0:T(1,128)S(1)}, u32[]{:S(2)}, u32[]{:S(2)}) collective-permute-start(f32[5,8,1,128]{3,2,1,0:T(1,128)S(1)} %get-tuple-element.46), channel_id=1, source_target_pairs={{0,2},{2,4},{4,6},{1,3},{3,5},{5,7},{8,10},{10,12},{12,14},{9,11},... | collective-permute-start | bytes 61448 | tf_op jit(solution)/shard_map/ppermute | solution.py:21
  41.6 1.3 %collective-permute-start.10 = (f32[5,8,8,1]{3,2,1,0:T(8,128)S(1)}, f32[5,8,8,1]{3,2,1,0:T(8,128)S(1)}, u32[]{:S(2)}, u32[]{:S(2)}) collective-permute-start(f32[5,8,8,1]{3,2,1,0:T(8,128)S(1)} %get-tuple-element.47), channel_id=1, source_target_pairs={{1,0},{3,2},{5,4},{7,6},{9,8},{11,10},{13,12},{15,14},{17,16},{19,... | collective-permute-start | bytes 3848 | tf_op jit(solution)/shard_map/ppermute | solution.py:24
  42.9 7.3 %collective-permute-done.10 = f32[5,8,8,1]{3,2,1,0:T(8,128)S(1)} collective-permute-done((f32[5,8,8,1]{3,2,1,0:T(8,128)S(1)}, f32[5,8,8,1]{3,2,1,0:T(8,128)S(1)}, u32[]{:S(2)}, u32[]{:S(2)}) %collective-permute-start.10) | collective-permute-done | bytes 1312 | tf_op jit(solution)/shard_map/ppermute | solution.py:24
  50.2 1.4 %collective-permute-start.11 = (f32[5,8,8,1]{3,2,1,0:T(8,128)S(1)}, f32[5,8,8,1]{3,2,1,0:T(8,128)S(1)}, u32[]{:S(2)}, u32[]{:S(2)}) collective-permute-start(f32[5,8,8,1]{3,2,1,0:T(8,128)S(1)} %get-tuple-element.48), channel_id=1, source_target_pairs={{0,1},{2,3},{4,5},{6,7},{8,9},{10,11},{12,13},{14,15},{16,17},{18,... | collective-permute-start | bytes 3848 | tf_op jit(solution)/shard_map/ppermute | solution.py:21
  51.6 1.3 %dynamic_slice.10 = s32[1,1,1]{1,2,0:T(1,128)} dynamic-slice(s32[4,4,2]{1,2,0:T(2,128)} %param.16, s32[]{:T(128)S(6)} %select_n.26, s32[]{:T(128)S(6)} %select_n.27, s32[]{:T(128)S(6)} %select_n.28), dynamic_slice_sizes={1,1,1} | dynamic-slice | bytes 12 | tf_op jit(solution)/shard_map/dynamic_slice | solution.py:71
  56.0 1.3 %collective-permute-start.16 = (f32[5,8,8,1]{3,2,1,0:T(8,128)S(1)}, f32[5,8,8,1]{3,2,1,0:T(8,128)S(1)}, u32[]{:S(2)}, u32[]{:S(2)}) collective-permute-start(f32[5,8,8,1]{3,2,1,0:T(8,128)S(1)} %get-tuple-element.41), channel_id=1, source_target_pairs={{1,0},{3,2},{5,4},{7,6},{9,8},{11,10},{13,12},{15,14},{17,16},{19,... | collective-permute-start | bytes 3848 | tf_op jit(solution)/shard_map/ppermute | solution.py:24
  57.3 4.6 %collective-permute-start.17 = (f32[5,8,8,1]{3,2,1,0:T(8,128)S(1)}, f32[5,8,8,1]{3,2,1,0:T(8,128)S(1)}, u32[]{:S(2)}, u32[]{:S(2)}) collective-permute-start(f32[5,8,8,1]{3,2,1,0:T(8,128)S(1)} %get-tuple-element.42), channel_id=1, source_target_pairs={{0,1},{2,3},{4,5},{6,7},{8,9},{10,11},{12,13},{14,15},{16,17},{18,... | collective-permute-start | bytes 3848 | tf_op jit(solution)/shard_map/ppermute | solution.py:21
  61.9 1.3 %collective-permute-start.12 = (f32[5,1,8,128]{3,2,1,0:T(8,128)S(1)}, f32[5,1,8,128]{3,2,1,0:T(8,128)S(1)}, u32[]{:S(2)}, u32[]{:S(2)}) collective-permute-start(f32[5,1,8,128]{3,2,1,0:T(8,128)S(1)} %get-tuple-element.37), channel_id=1, source_target_pairs={{8,0},{16,8},{24,16},{9,1},{17,9},{25,17},{10,2},{18,10},{26,18},{... | collective-permute-start | bytes 61448 | tf_op jit(solution)/shard_map/ppermute | solution.py:24
  63.2 4.5 %collective-permute-start.13 = (f32[5,1,8,128]{3,2,1,0:T(8,128)S(1)}, f32[5,1,8,128]{3,2,1,0:T(8,128)S(1)}, u32[]{:S(2)}, u32[]{:S(2)}) collective-permute-start(f32[5,1,8,128]{3,2,1,0:T(8,128)S(1)} %get-tuple-element.38), channel_id=1, source_target_pairs={{0,8},{8,16},{16,24},{1,9},{9,17},{17,25},{2,10},{10,18},{18,26},{... | collective-permute-start | bytes 61448 | tf_op jit(solution)/shard_map/ppermute | solution.py:21
  67.8 1.3 %collective-permute-start.14 = (f32[5,8,1,128]{3,2,1,0:T(1,128)S(1)}, f32[5,8,1,128]{3,2,1,0:T(1,128)S(1)}, u32[]{:S(2)}, u32[]{:S(2)}) collective-permute-start(f32[5,8,1,128]{3,2,1,0:T(1,128)S(1)} %get-tuple-element.39), channel_id=1, source_target_pairs={{2,0},{4,2},{6,4},{3,1},{5,3},{7,5},{10,8},{12,10},{14,12},{11,9},... | collective-permute-start | bytes 61448 | tf_op jit(solution)/shard_map/ppermute | solution.py:24
  69.1 3.0 %collective-permute-start.15 = (f32[5,8,1,128]{3,2,1,0:T(1,128)S(1)}, f32[5,8,1,128]{3,2,1,0:T(1,128)S(1)}, u32[]{:S(2)}, u32[]{:S(2)}) collective-permute-start(f32[5,8,1,128]{3,2,1,0:T(1,128)S(1)} %get-tuple-element.40), channel_id=1, source_target_pairs={{0,2},{2,4},{4,6},{1,3},{3,5},{5,7},{8,10},{10,12},{12,14},{9,11},... | collective-permute-start | bytes 61448 | tf_op jit(solution)/shard_map/ppermute | solution.py:21
  74.3 11.8 %all_to_all.6 = f32[32,1,40]{2,1,0:T(1,128)S(1)} all-to-all(f32[32,1,40]{2,1,0:T(1,128)S(1)} %broadcast_select_fusion), channel_id=1, replica_groups=mesh['gx'=4,'gy'=4,'gz'=2] {'gx','gy','gz'}, dimensions={0} | all-to-all | bytes 10240 | tf_op jit(solution)/shard_map/all_to_all | solution.py:89
  (82 shorter events, 6.8 us)
Async XLA Ops:
  0.6 2.9 %copy-start = (f32[3,8,8,128]{3,2,1,0:T(8,128)S(1)}, f32[3,8,8,128]{3,2,1,0:T(8,128)}, u32[]{:S(2)}) copy-start(f32[3,8,8,128]{3,2,1,0:T(8,128)} %param.11) | copy-start | bytes 294916
  2.6 1.6 %copy-start.1 = (f32[5,8,8,128]{3,2,1,0:T(8,128)S(1)}, f32[5,8,8,128]{3,2,1,0:T(8,128)}, u32[]{:S(2)}) copy-start(f32[5,8,8,128]{3,2,1,0:T(8,128)} %param.9) | copy-start | bytes 491524
  4.3 0.8 copy-start.2
  4.3 0.8 copy-start.4
  5.2 25.5 %collective-permute-start = (f32[5,1,8,128]{3,2,1,0:T(8,128)S(1)}, f32[5,1,8,128]{3,2,1,0:T(8,128)S(1)}, u32[]{:S(2)}, u32[]{:S(2)}) collective-permute-start(f32[5,1,8,128]{3,2,1,0:T(8,128)S(1)} %get-tuple-element.49), channel_id=1, source_target_pairs={{8,0},{16,8},{24,16},{9,1},{17,9},{25,17},{10,2},{18,10},{26,18},{... | collective-permute-start | bytes 61448 | tf_op jit(solution)/shard_map/ppermute | solution.py:24
  6.5 24.2 %collective-permute-start.1 = (f32[5,1,8,128]{3,2,1,0:T(8,128)S(1)}, f32[5,1,8,128]{3,2,1,0:T(8,128)S(1)}, u32[]{:S(2)}, u32[]{:S(2)}) collective-permute-start(f32[5,1,8,128]{3,2,1,0:T(8,128)S(1)} %get-tuple-element.50), channel_id=1, source_target_pairs={{0,8},{8,16},{16,24},{1,9},{9,17},{17,25},{2,10},{10,18},{18,26},{... | collective-permute-start | bytes 61448 | tf_op jit(solution)/shard_map/ppermute | solution.py:21
  12.1 18.6 %collective-permute-start.2 = (f32[5,8,1,128]{3,2,1,0:T(1,128)S(1)}, f32[5,8,1,128]{3,2,1,0:T(1,128)S(1)}, u32[]{:S(2)}, u32[]{:S(2)}) collective-permute-start(f32[5,8,1,128]{3,2,1,0:T(1,128)S(1)} %get-tuple-element.51), channel_id=1, source_target_pairs={{2,0},{4,2},{6,4},{3,1},{5,3},{7,5},{10,8},{12,10},{14,12},{11,9},... | collective-permute-start | bytes 61448 | tf_op jit(solution)/shard_map/ppermute | solution.py:24
  13.4 17.3 %collective-permute-start.3 = (f32[5,8,1,128]{3,2,1,0:T(1,128)S(1)}, f32[5,8,1,128]{3,2,1,0:T(1,128)S(1)}, u32[]{:S(2)}, u32[]{:S(2)}) collective-permute-start(f32[5,8,1,128]{3,2,1,0:T(1,128)S(1)} %get-tuple-element.52), channel_id=1, source_target_pairs={{0,2},{2,4},{4,6},{1,3},{3,5},{5,7},{8,10},{10,12},{12,14},{9,11},... | collective-permute-start | bytes 61448 | tf_op jit(solution)/shard_map/ppermute | solution.py:21
  16.5 14.3 %copy-start.3 = (f32[8,8,128]{2,1,0:T(8,128)S(1)}, f32[8,8,128]{2,1,0:T(8,128)}, u32[]{:S(2)}) copy-start(f32[8,8,128]{2,1,0:T(8,128)} %param.13) | copy-start | bytes 98308
  16.6 8.4 %collective-permute-start.4 = (f32[5,8,8,1]{3,2,1,0:T(8,128)S(1)}, f32[5,8,8,1]{3,2,1,0:T(8,128)S(1)}, u32[]{:S(2)}, u32[]{:S(2)}) collective-permute-start(f32[5,8,8,1]{3,2,1,0:T(8,128)S(1)} %get-tuple-element.53), channel_id=1, source_target_pairs={{1,0},{3,2},{5,4},{7,6},{9,8},{11,10},{13,12},{15,14},{17,16},{19,... | collective-permute-start | bytes 3848 | tf_op jit(solution)/shard_map/ppermute | solution.py:24
  25.1 5.7 %collective-permute-start.5 = (f32[5,8,8,1]{3,2,1,0:T(8,128)S(1)}, f32[5,8,8,1]{3,2,1,0:T(8,128)S(1)}, u32[]{:S(2)}, u32[]{:S(2)}) collective-permute-start(f32[5,8,8,1]{3,2,1,0:T(8,128)S(1)} %get-tuple-element.54), channel_id=1, source_target_pairs={{0,1},{2,3},{4,5},{6,7},{8,9},{10,11},{12,13},{14,15},{16,17},{18,... | collective-permute-start | bytes 3848 | tf_op jit(solution)/shard_map/ppermute | solution.py:21
  31.2 24.2 %collective-permute-start.6 = (f32[5,1,8,128]{3,2,1,0:T(8,128)S(1)}, f32[5,1,8,128]{3,2,1,0:T(8,128)S(1)}, u32[]{:S(2)}, u32[]{:S(2)}) collective-permute-start(f32[5,1,8,128]{3,2,1,0:T(8,128)S(1)} %get-tuple-element.43), channel_id=1, source_target_pairs={{8,0},{16,8},{24,16},{9,1},{17,9},{25,17},{10,2},{18,10},{26,18},{... | collective-permute-start | bytes 61448 | tf_op jit(solution)/shard_map/ppermute | solution.py:24
  32.5 23.0 %collective-permute-start.7 = (f32[5,1,8,128]{3,2,1,0:T(8,128)S(1)}, f32[5,1,8,128]{3,2,1,0:T(8,128)S(1)}, u32[]{:S(2)}, u32[]{:S(2)}) collective-permute-start(f32[5,1,8,128]{3,2,1,0:T(8,128)S(1)} %get-tuple-element.44), channel_id=1, source_target_pairs={{0,8},{8,16},{16,24},{1,9},{9,17},{17,25},{2,10},{10,18},{18,26},{... | collective-permute-start | bytes 61448 | tf_op jit(solution)/shard_map/ppermute | solution.py:21
  37.2 18.3 %collective-permute-start.8 = (f32[5,8,1,128]{3,2,1,0:T(1,128)S(1)}, f32[5,8,1,128]{3,2,1,0:T(1,128)S(1)}, u32[]{:S(2)}, u32[]{:S(2)}) collective-permute-start(f32[5,8,1,128]{3,2,1,0:T(1,128)S(1)} %get-tuple-element.45), channel_id=1, source_target_pairs={{2,0},{4,2},{6,4},{3,1},{5,3},{7,5},{10,8},{12,10},{14,12},{11,9},... | collective-permute-start | bytes 61448 | tf_op jit(solution)/shard_map/ppermute | solution.py:24
  38.5 17.0 %collective-permute-start.9 = (f32[5,8,1,128]{3,2,1,0:T(1,128)S(1)}, f32[5,8,1,128]{3,2,1,0:T(1,128)S(1)}, u32[]{:S(2)}, u32[]{:S(2)}) collective-permute-start(f32[5,8,1,128]{3,2,1,0:T(1,128)S(1)} %get-tuple-element.46), channel_id=1, source_target_pairs={{0,2},{2,4},{4,6},{1,3},{3,5},{5,7},{8,10},{10,12},{12,14},{9,11},... | collective-permute-start | bytes 61448 | tf_op jit(solution)/shard_map/ppermute | solution.py:21
  41.6 8.6 %collective-permute-start.10 = (f32[5,8,8,1]{3,2,1,0:T(8,128)S(1)}, f32[5,8,8,1]{3,2,1,0:T(8,128)S(1)}, u32[]{:S(2)}, u32[]{:S(2)}) collective-permute-start(f32[5,8,8,1]{3,2,1,0:T(8,128)S(1)} %get-tuple-element.47), channel_id=1, source_target_pairs={{1,0},{3,2},{5,4},{7,6},{9,8},{11,10},{13,12},{15,14},{17,16},{19,... | collective-permute-start | bytes 3848 | tf_op jit(solution)/shard_map/ppermute | solution.py:24
  50.2 5.3 %collective-permute-start.11 = (f32[5,8,8,1]{3,2,1,0:T(8,128)S(1)}, f32[5,8,8,1]{3,2,1,0:T(8,128)S(1)}, u32[]{:S(2)}, u32[]{:S(2)}) collective-permute-start(f32[5,8,8,1]{3,2,1,0:T(8,128)S(1)} %get-tuple-element.48), channel_id=1, source_target_pairs={{0,1},{2,3},{4,5},{6,7},{8,9},{10,11},{12,13},{14,15},{16,17},{18,... | collective-permute-start | bytes 3848 | tf_op jit(solution)/shard_map/ppermute | solution.py:21
  56.0 13.1 %collective-permute-start.16 = (f32[5,8,8,1]{3,2,1,0:T(8,128)S(1)}, f32[5,8,8,1]{3,2,1,0:T(8,128)S(1)}, u32[]{:S(2)}, u32[]{:S(2)}) collective-permute-start(f32[5,8,8,1]{3,2,1,0:T(8,128)S(1)} %get-tuple-element.41), channel_id=1, source_target_pairs={{1,0},{3,2},{5,4},{7,6},{9,8},{11,10},{13,12},{15,14},{17,16},{19,... | collective-permute-start | bytes 3848 | tf_op jit(solution)/shard_map/ppermute | solution.py:24
  57.3 15.5 %collective-permute-start.17 = (f32[5,8,8,1]{3,2,1,0:T(8,128)S(1)}, f32[5,8,8,1]{3,2,1,0:T(8,128)S(1)}, u32[]{:S(2)}, u32[]{:S(2)}) collective-permute-start(f32[5,8,8,1]{3,2,1,0:T(8,128)S(1)} %get-tuple-element.42), channel_id=1, source_target_pairs={{0,1},{2,3},{4,5},{6,7},{8,9},{10,11},{12,13},{14,15},{16,17},{18,... | collective-permute-start | bytes 3848 | tf_op jit(solution)/shard_map/ppermute | solution.py:21
  61.9 10.9 %collective-permute-start.12 = (f32[5,1,8,128]{3,2,1,0:T(8,128)S(1)}, f32[5,1,8,128]{3,2,1,0:T(8,128)S(1)}, u32[]{:S(2)}, u32[]{:S(2)}) collective-permute-start(f32[5,1,8,128]{3,2,1,0:T(8,128)S(1)} %get-tuple-element.37), channel_id=1, source_target_pairs={{8,0},{16,8},{24,16},{9,1},{17,9},{25,17},{10,2},{18,10},{26,18},{... | collective-permute-start | bytes 61448 | tf_op jit(solution)/shard_map/ppermute | solution.py:24
  63.2 9.7 %collective-permute-start.13 = (f32[5,1,8,128]{3,2,1,0:T(8,128)S(1)}, f32[5,1,8,128]{3,2,1,0:T(8,128)S(1)}, u32[]{:S(2)}, u32[]{:S(2)}) collective-permute-start(f32[5,1,8,128]{3,2,1,0:T(8,128)S(1)} %get-tuple-element.38), channel_id=1, source_target_pairs={{0,8},{8,16},{16,24},{1,9},{9,17},{17,25},{2,10},{10,18},{18,26},{... | collective-permute-start | bytes 61448 | tf_op jit(solution)/shard_map/ppermute | solution.py:21
  67.8 5.2 %copy-start.5 = (f32[8,8,128]{2,1,0:T(8,128)S(1)}, f32[8,8,128]{2,1,0:T(8,128)}, u32[]{:S(2)}) copy-start(f32[8,8,128]{2,1,0:T(8,128)} %param.14) | copy-start | bytes 98308
  67.8 5.0 %collective-permute-start.14 = (f32[5,8,1,128]{3,2,1,0:T(1,128)S(1)}, f32[5,8,1,128]{3,2,1,0:T(1,128)S(1)}, u32[]{:S(2)}, u32[]{:S(2)}) collective-permute-start(f32[5,8,1,128]{3,2,1,0:T(1,128)S(1)} %get-tuple-element.39), channel_id=1, source_target_pairs={{2,0},{4,2},{6,4},{3,1},{5,3},{7,5},{10,8},{12,10},{14,12},{11,9},... | collective-permute-start | bytes 61448 | tf_op jit(solution)/shard_map/ppermute | solution.py:24
  69.1 3.9 %collective-permute-start.15 = (f32[5,8,1,128]{3,2,1,0:T(1,128)S(1)}, f32[5,8,1,128]{3,2,1,0:T(1,128)S(1)}, u32[]{:S(2)}, u32[]{:S(2)}) collective-permute-start(f32[5,8,1,128]{3,2,1,0:T(1,128)S(1)} %get-tuple-element.40), channel_id=1, source_target_pairs={{0,2},{2,4},{4,6},{1,3},{3,5},{5,7},{8,10},{10,12},{12,14},{9,11},... | collective-permute-start | bytes 61448 | tf_op jit(solution)/shard_map/ppermute | solution.py:21
  (1 other events, 0.7 us)

commit v2 on v1

v2 whole, which is shorter than its diff:
```python
import jax
import jax.numpy as jnp
from jax import lax
from jax.sharding import PartitionSpec as P

BX = 8
BY = 8
BZ = 16

AXES = ("gx", "gy", "gz")

step_length = 0.14
third = 1.0 / 3.0
two_thirds = 2.0 / 3.0


def pairings(sizes, axis, near_axis):
    size = sizes[axis]
    first, second = [], []
    for x in range(sizes[0]):
        for y in range(sizes[1]):
            for z in range(sizes[2]):
                here = [x, y, z]
                index = (x * sizes[1] + y) * sizes[2] + z
                place = here[axis]
                other = list(here)
                other[axis] = place ^ 1
                first.append((index, (other[0] * sizes[1] + other[1]) * sizes[2] + other[2]))
                other = list(here)
                if 0 < place < size - 1:
                    other[axis] = place + 1 if place % 2 else place - 1
                else:
                    other[near_axis] = here[near_axis] ^ 1
                second.append((index, (other[0] * sizes[1] + other[1]) * sizes[2] + other[2]))
    return first, second if size > 2 else None


def send_faces(low_face, high_face, position, permutations):
    even = position % 2 == 0
    first = lax.ppermute(jnp.where(even, high_face, low_face), AXES, permutations[0])
    second = None
    if permutations[1] is not None:
        second = lax.ppermute(jnp.where(even, low_face, high_face), AXES, permutations[1])
    return first, second


def sort_faces(received, position, size):
    first, second = received
    even = position % 2 == 0
    zero = jnp.zeros_like(first)
    if second is None:
        return jnp.where(even, zero, first), jnp.where(even, first, zero)
    below = jnp.where(position == 0, zero, jnp.where(even, second, first))
    above = jnp.where(position == size - 1, zero, jnp.where(even, first, second))
    return below, above


def transposed_flux(adjoint, density, velocity, stiffness, direction):
    along_speed = velocity[direction]
    components = [along_speed * adjoint[component] for component in range(5)]
    velocity_row = 1 + direction
    components[velocity_row] = (
        components[velocity_row] + density * adjoint[0] + stiffness * adjoint[4]
    )
    components[4] = components[4] + adjoint[velocity_row] / density
    return jnp.stack(components)


def body(
    terminal_adjoint,
    density,
    velocity,
    stiffness,
    sponge,
    source_shape,
    brick_level,
    brick_patch,
    patch_owner,
):
    sizes = tuple(lax.axis_size(axis) for axis in AXES)
    position = tuple(lax.axis_index(axis) for axis in AXES)
    cells_x, cells_y, cells_z = density.shape
    here = jnp.ones(sizes, bool)
    for axis in range(3):
        here = here & (lax.broadcasted_iota(jnp.int32, sizes, axis) == position[axis])
    own_level = jnp.sum(jnp.where(here, brick_level, 0))
    own_patch = jnp.sum(jnp.where(here, brick_patch, 0))
    devices = patch_owner.shape[0]
    target = jnp.sum(jnp.where(jnp.arange(devices) == own_patch, patch_owner, 0))
    half_inverse = 0.5 * jnp.exp2(own_level.astype(jnp.float32))
    permutations = (
        pairings(sizes, 0, 1),
        pairings(sizes, 1, 2),
        pairings(sizes, 2, 1),
    )

    def apply_op(adjoint):
        partials = [
            half_inverse * transposed_flux(adjoint, density, velocity, stiffness, direction)
            for direction in range(3)
        ]
        received = []
        for direction in range(3):
            block, dim = partials[direction], direction + 1
            low_face = lax.slice_in_dim(block, 0, 1, axis=dim)
            high_face = lax.slice_in_dim(block, block.shape[dim] - 1, None, axis=dim)
            received.append(
                send_faces(low_face, high_face, position[direction], permutations[direction])
            )
        summed = None
        for direction in range(3):
            dim = direction + 1
            below, above = sort_faces(received[direction], position[direction], sizes[direction])
            padded = jnp.concatenate([below, partials[direction], above], axis=dim)
            count = padded.shape[dim]
            difference = lax.slice_in_dim(padded, 2, None, axis=dim) - lax.slice_in_dim(
                padded, 0, count - 2, axis=dim
            )
            summed = difference if summed is None else summed + difference
        return summed - sponge * adjoint

    adjoint = terminal_adjoint
    section_one = adjoint + step_length * apply_op(adjoint)
    section_two = 0.75 * adjoint + 0.25 * (section_one + step_length * apply_op(section_one))
    adjoint = third * adjoint + two_thirds * (section_two + step_length * apply_op(section_two))
    weighted = adjoint * source_shape
    boxed = weighted.reshape(5, cells_x // BX, BX, cells_y // BY, BY, cells_z // BZ, BZ)
    block_now = step_length * jnp.sum(boxed, axis=(2, 4, 6)).reshape(1, -1)
    rows = jnp.arange(devices, dtype=jnp.int32)[:, None]
    outgoing = jnp.where(rows == target, block_now, 0.0)
    incoming = lax.all_to_all(outgoing, AXES, 0, 0, tiled=True)
    gradient = jnp.sum(incoming, axis=0, keepdims=True)
    return (adjoint, gradient)


def solution(mesh):
    in_specs = (
        P(None, "gx", "gy", "gz"),
        P("gx", "gy", "gz"),
        P(None, "gx", "gy", "gz"),
        P("gx", "gy", "gz"),
        P("gx", "gy", "gz"),
        P("gx", "gy", "gz"),
        P(),
        P(),
        P(),
    )
    out_specs = (P(None, "gx", "gy", "gz"), P(("gx", "gy", "gz"), None))
    return jax.shard_map(body, mesh=mesh, in_specs=in_specs, out_specs=out_specs, check_vma=False)
```

time: 87.5 us -> 43.3 us (0.49)
  starting transfers between devices: 42.9 us -> 15.5 us
  waiting for transfers between devices: 18.8 us -> 3.78 us
  other arithmetic: 4.73 us -> 7.35 us
  between operations: 3.92 us -> 1.93 us
  local copies, waits for them, and re-layouts: 4.49 us -> 2.77 us
    ppermute x18 -> x15, starting transfers between devices: 42.9 us -> 15.5 us  [the longest x9 12.3 us: send_faces(): lax.ppermute(jnp.where(even, high_face, low_face), AXES, permutations[0])]
    ppermute x18 -> x15, waiting for transfers between devices: 18.8 us -> 3.78 us  [the longest x9 3.42 us: send_faces(): lax.ppermute(jnp.where(even, high_face, low_face), AXES, permutations[0])]
    dynamic_slice x3 -> x0, local copies, waits for them, and re-layouts: 3.16 us -> none  [the longest x1 1.3 us: body(): own_level = brick_level[index_x, index_y, index_z]]
    reduce_sum x0 -> x2, other arithmetic: none -> 1.99 us  [the longest x1 1.28 us: body(): jnp.sum(jnp.where(jnp.arange(devices) == own_patch, patch_owner, 0))]
    unnamed x14 -> x18, local copies, waits for them, and re-layouts: 0.78 us -> 2.62 us
  transfers between devices with their start and end apart: 18 -> 15, of which waited for: 4 -> 5; matrix products, arithmetic and copies ran while one was open for 3% -> 5% of each run, Pallas kernels for 0% -> 0%
where the time goes in v2:
time: 43.3 us; the launch traced here: 42.8 us
  starting transfers between devices  15.5 us (36%)
  blocking collectives  11.5 us (27%)
  other arithmetic  7.35 us (17%)
  waiting for transfers between devices  3.78 us (9%)
  local copies, waits for them, and re-layouts  2.77 us (6%)
  between operations  1.93 us (4%)
    ppermute x9, starting transfers between devices, send_faces(): lax.ppermute(jnp.where(even, high_face, low_face), AXES, permutations[0])  12.3 us
    all_to_all x1, blocking collectives, body(): incoming = lax.all_to_all(outgoing, AXES, 0, 0, tiled=True)  11.5 us
    ppermute x9, waiting for transfers between devices, send_faces(): lax.ppermute(jnp.where(even, high_face, low_face), AXES, permutations[0])  3.42 us
    ppermute x6, starting transfers between devices, send_faces(): lax.ppermute(jnp.where(even, low_face, high_face), AXES, permutations[1])  3.15 us
    unnamed x18, local copies, waits for them, and re-layouts  2.62 us
    unnamed x21, other arithmetic  1.81 us
    reduce_sum x1, other arithmetic, body(): jnp.sum(jnp.where(jnp.arange(devices) == own_patch, patch_owner, 0))  1.28 us
    reduce_sum x2, other arithmetic, body(): block_now = step_length * jnp.sum(boxed, axis=(2, 4, 6)).reshape(1, -1)  0.97 us
  transfers between devices with their start and end apart: 15, of which 5 were waited for; matrix products, arithmetic and copies ran while one was open for 5% of the time, Pallas kernels for 0%

profile of v2, /device:TPU:0, one launch (start us, length us, event | category | flops | bytes accessed | tf_op | source)
XLA Modules:
  0.0 42.8 jit_solution(12161588711530324845)
XLA Ops:
  0.7 0.8 %constant_dynamic-update-slice_fusion.9 = f32[5,8,8,128]{3,2,1,0:T(8,128)S(1)} fusion(f32[5,8,8,128]{3,2,1,0:T(8,128)} %param.9, f32[3,8,8,128]{3,2,1,0:T(8,128)} %param.11), kind=kLoop, calls=%fused_computation.59 | loop fusion | flops 8191 | bytes 98304
  1.5 0.8 %constant_dynamic-update-slice_fusion.4 = (f32[5,8,8,128]{3,2,1,0:T(8,128)S(1)}, f32[5,8,8,128]{3,2,1,0:T(8,128)S(1)}, f32[5,8,8,128]{3,2,1,0:T(8,128)S(1)}) fusion(f32[5,8,8,128]{3,2,1,0:T(8,128)} %param.9, f32[3,8,8,128]{3,2,1,0:T(8,128)S(1)} %copy-done, f32[5,8,8,128]{3,2,1,0:T(8,128)S(1)} %constant_dynamic-update-slice_fusion.9), kind=kLoop, calls=%fused_computation.54 | loop fusion | flops 24574 | bytes 262144
  2.4 0.7 %copy-done.2 = f32[8,8,128]{2,1,0:T(8,128)S(1)} copy-done((f32[8,8,128]{2,1,0:T(8,128)S(1)}, f32[8,8,128]{2,1,0:T(8,128)}, u32[]{:S(2)}) %copy-start.2) | copy-done | bytes 32792
  3.2 0.7 %copy-done.7 = s32[4,4,2]{1,2,0:T(2,128)S(1)} copy-done((s32[4,4,2]{1,2,0:T(2,128)S(1)}, s32[4,4,2]{1,2,0:T(2,128)}, u32[]{:S(2)}) %copy-start.7) | copy-done | bytes 152
  3.9 0.7 %fusion.60 = (s32[]{:T(128)}, s32[]{:T(128)}) fusion(s32[4,4,2]{1,2,0:T(2,128)S(1)} %copy-done.6, pred[2]{0:T(512)(128)(4,1)S(1)} %iota_compare_fusion.1, pred[4]{0:T(512)(128)(4,1)S(1)} %get-tuple-element.69, pred[4]{0:T(512)(128)(4,1)S(1)} %get-tuple-element.70, s32[4,4,2]{1,2,0:T(2,128)S(1)} %copy-done.7), kind=kLoop, calls=%fused_computation.207 | loop fusion | flops 190 | bytes 274 | tf_op jit(solution)/shard_map/reduce_sum | solution.py:87
  5.5 3.0 %collective-permute-start.4 = (f32[5,8,8,1]{3,2,1,0:T(8,128)S(1)}, f32[5,8,8,1]{3,2,1,0:T(8,128)S(1)}, u32[]{:S(2)}, u32[]{:S(2)}) collective-permute-start(f32[5,8,8,1]{3,2,1,0:T(8,128)S(1)} %slice_select_fusion.2), channel_id=1, source_target_pairs={{0,1},{1,0},{2,3},{3,2},{4,5},{5,4},{6,7},{7,6},{8,9},{9,8},{10,11... | collective-permute-start | bytes 3848 | tf_op jit(solution)/shard_map/ppermute | solution.py:40
  8.8 2.1 %collective-permute-start = (f32[5,1,8,128]{3,2,1,0:T(8,128)S(1)}, f32[5,1,8,128]{3,2,1,0:T(8,128)S(1)}, u32[]{:S(2)}, u32[]{:S(2)}) collective-permute-start(f32[5,1,8,128]{3,2,1,0:T(8,128)S(1)} %get-tuple-element.51), channel_id=1, source_target_pairs={{0,8},{1,9},{2,10},{3,11},{4,12},{5,13},{6,14},{7,15},{8,0},{9,1},... | collective-permute-start | bytes 61448 | tf_op jit(solution)/shard_map/ppermute | solution.py:40
  10.9 0.8 %collective-permute-start.1 = (f32[5,1,8,128]{3,2,1,0:T(8,128)S(1)}, f32[5,1,8,128]{3,2,1,0:T(8,128)S(1)}, u32[]{:S(2)}, u32[]{:S(2)}) collective-permute-start(f32[5,1,8,128]{3,2,1,0:T(8,128)S(1)} %get-tuple-element.52), channel_id=1, source_target_pairs={{0,2},{1,3},{2,0},{3,1},{4,6},{5,7},{6,4},{7,5},{8,16},{9,17},{10,... | collective-permute-start | bytes 61448 | tf_op jit(solution)/shard_map/ppermute | solution.py:43
  11.7 1.3 %fusion.61 = s32[]{:T(128)} fusion(s32[32]{0:T(128)S(1)} %copy-done.8, s32[]{:T(128)} %get-tuple-element.2), kind=kLoop, calls=%fused_computation.210 | loop fusion | flops 95 | bytes 136 | tf_op jit(solution)/shard_map/reduce_sum | solution.py:89
  13.0 0.6 %iota_compare_fusion = pred[32]{0:T(512)(128)(4,1)S(1)} fusion(s32[]{:T(128)} %fusion.61), kind=kLoop, calls=%fused_computation.211 | loop fusion | flops 32 | bytes 36 | tf_op jit(solution)/shard_map/eq | solution.py:130
  13.8 0.7 %copy-done.3 = f32[8,8,128]{2,1,0:T(8,128)S(1)} copy-done((f32[8,8,128]{2,1,0:T(8,128)S(1)}, f32[8,8,128]{2,1,0:T(8,128)}, u32[]{:S(2)}) %copy-start.3) | copy-done | bytes 32792
  15.1 1.4 %collective-permute-start.9 = (f32[5,8,8,1]{3,2,1,0:T(8,128)S(1)}, f32[5,8,8,1]{3,2,1,0:T(8,128)S(1)}, u32[]{:S(2)}, u32[]{:S(2)}) collective-permute-start(f32[5,8,8,1]{3,2,1,0:T(8,128)S(1)} %slice_select_fusion.1), channel_id=1, source_target_pairs={{0,1},{1,0},{2,3},{3,2},{4,5},{5,4},{6,7},{7,6},{8,9},{9,8},{10,11... | collective-permute-start | bytes 3848 | tf_op jit(solution)/shard_map/ppermute | solution.py:40
  16.6 1.0 %collective-permute-start.8 = (f32[5,8,1,128]{3,2,1,0:T(1,128)S(1)}, f32[5,8,1,128]{3,2,1,0:T(1,128)S(1)}, u32[]{:S(2)}, u32[]{:S(2)}) collective-permute-start(f32[5,8,1,128]{3,2,1,0:T(1,128)S(1)} %get-tuple-element.48), channel_id=1, source_target_pairs={{0,1},{1,0},{2,4},{3,5},{4,2},{5,3},{6,7},{7,6},{8,9},{9,8},{10,12... | collective-permute-start | bytes 61448 | tf_op jit(solution)/shard_map/ppermute | solution.py:43
  17.7 2.3 %collective-permute-start.5 = (f32[5,1,8,128]{3,2,1,0:T(8,128)S(1)}, f32[5,1,8,128]{3,2,1,0:T(8,128)S(1)}, u32[]{:S(2)}, u32[]{:S(2)}) collective-permute-start(f32[5,1,8,128]{3,2,1,0:T(8,128)S(1)} %get-tuple-element.45), channel_id=1, source_target_pairs={{0,8},{1,9},{2,10},{3,11},{4,12},{5,13},{6,14},{7,15},{8,0},{9,1},... | collective-permute-start | bytes 61448 | tf_op jit(solution)/shard_map/ppermute | solution.py:40
  20.0 1.9 %collective-permute-done.9 = f32[5,8,8,1]{3,2,1,0:T(8,128)S(1)} collective-permute-done((f32[5,8,8,1]{3,2,1,0:T(8,128)S(1)}, f32[5,8,8,1]{3,2,1,0:T(8,128)S(1)}, u32[]{:S(2)}, u32[]{:S(2)}) %collective-permute-start.9) | collective-permute-done | bytes 1312 | tf_op jit(solution)/shard_map/ppermute | solution.py:40
  22.7 1.0 %collective-permute-start.14 = (f32[5,8,8,1]{3,2,1,0:T(8,128)S(1)}, f32[5,8,8,1]{3,2,1,0:T(8,128)S(1)}, u32[]{:S(2)}, u32[]{:S(2)}) collective-permute-start(f32[5,8,8,1]{3,2,1,0:T(8,128)S(1)} %slice_select_fusion), channel_id=1, source_target_pairs={{0,1},{1,0},{2,3},{3,2},{4,5},{5,4},{6,7},{7,6},{8,9},{9,8},{10,11... | collective-permute-start | bytes 3848 | tf_op jit(solution)/shard_map/ppermute | solution.py:40
  23.8 1.2 %collective-permute-start.13 = (f32[5,8,1,128]{3,2,1,0:T(1,128)S(1)}, f32[5,8,1,128]{3,2,1,0:T(1,128)S(1)}, u32[]{:S(2)}, u32[]{:S(2)}) collective-permute-start(f32[5,8,1,128]{3,2,1,0:T(1,128)S(1)} %get-tuple-element.42), channel_id=1, source_target_pairs={{0,1},{1,0},{2,4},{3,5},{4,2},{5,3},{6,7},{7,6},{8,9},{9,8},{10,12... | collective-permute-start | bytes 61448 | tf_op jit(solution)/shard_map/ppermute | solution.py:43
  25.0 2.3 %collective-permute-start.10 = (f32[5,1,8,128]{3,2,1,0:T(8,128)S(1)}, f32[5,1,8,128]{3,2,1,0:T(8,128)S(1)}, u32[]{:S(2)}, u32[]{:S(2)}) collective-permute-start(f32[5,1,8,128]{3,2,1,0:T(8,128)S(1)} %get-tuple-element.39), channel_id=1, source_target_pairs={{0,8},{1,9},{2,10},{3,11},{4,12},{5,13},{6,14},{7,15},{8,0},{9,1},... | collective-permute-start | bytes 61448 | tf_op jit(solution)/shard_map/ppermute | solution.py:40
  27.3 1.2 %collective-permute-done.14 = f32[5,8,8,1]{3,2,1,0:T(8,128)S(1)} collective-permute-done((f32[5,8,8,1]{3,2,1,0:T(8,128)S(1)}, f32[5,8,8,1]{3,2,1,0:T(8,128)S(1)}, u32[]{:S(2)}, u32[]{:S(2)}) %collective-permute-start.14) | collective-permute-done | bytes 1312 | tf_op jit(solution)/shard_map/ppermute | solution.py:40
  28.8 0.3 collective-permute-done.10
  29.1 0.4 %copy-done.5 = f32[8,8,128]{2,1,0:T(8,128)S(1)} copy-done((f32[8,8,128]{2,1,0:T(8,128)S(1)}, f32[8,8,128]{2,1,0:T(8,128)}, u32[]{:S(2)}) %copy-start.5) | copy-done | bytes 32792
  29.5 0.9 %multiply_reduce_fusion = (f32[5,128]{1,0:T(8,128)S(1)}, f32[5,8,8,128]{3,2,1,0:T(8,128)}) fusion(f32[8,8,128]{2,1,0:T(8,128)S(1)} %copy-done.5, f32[5,8,8,128]{3,2,1,0:T(8,128)S(1)} %fusion.16, f32[8,8,128]{2,1,0:T(8,128)S(1)} %copy-done.3, f32[5,8,8,128]{3,2,1,0:T(8,128)S(1)} %broadcast_multiply_fusion, f32[5,8,8,1]{3,2,1,0:T(8,128)S(1)} %get-tuple-element.44, ...), kind=kLoop, calls=%fused_computation.49 | loop fusion | flops 818560 | bytes 1135616 | tf_op jit(solution)/shard_map/reduce_sum | solution.py:128
  30.8 11.5 %all_to_all.6 = f32[32,1,40]{2,1,0:T(1,128)S(1)} all-to-all(f32[32,1,40]{2,1,0:T(1,128)S(1)} %broadcast_select_fusion.24), channel_id=1, replica_groups=mesh['gx'=4,'gy'=4,'gz'=2] {'gx','gy','gz'}, dimensions={0} | all-to-all | bytes 10240 | tf_op jit(solution)/shard_map/all_to_all | solution.py:131
  42.3 0.5 %reduce_sum.58 = f32[40]{0:T(128)} reduce(f32[32,1,40]{2,0,1:T(8,128)S(1)} %bitcast.261, f32[]{:T(128)} %constant.79.clone.1), dimensions={0,1}, to_apply=%region_5.6 | reduce | flops 1240 | bytes 5284 | tf_op jit(solution)/shard_map/reduce_sum | solution.py:132
  (90 shorter events, 2.6 us)
Async XLA Ops:
  0.6 0.9 %copy-start = (f32[3,8,8,128]{3,2,1,0:T(8,128)S(1)}, f32[3,8,8,128]{3,2,1,0:T(8,128)}, u32[]{:S(2)}) copy-start(f32[3,8,8,128]{3,2,1,0:T(8,128)} %param.11) | copy-start | bytes 294916
  0.7 1.7 %copy-start.1 = (f32[5,8,8,128]{3,2,1,0:T(8,128)S(1)}, f32[5,8,8,128]{3,2,1,0:T(8,128)}, u32[]{:S(2)}) copy-start(f32[5,8,8,128]{3,2,1,0:T(8,128)} %param.9) | copy-start | bytes 491524
  2.3 0.8 %copy-start.2 = (f32[8,8,128]{2,1,0:T(8,128)S(1)}, f32[8,8,128]{2,1,0:T(8,128)}, u32[]{:S(2)}) copy-start(f32[8,8,128]{2,1,0:T(8,128)} %param.10) | copy-start | bytes 98308
  2.3 0.8 %copy-start.4 = (f32[8,8,128]{2,1,0:T(8,128)S(1)}, f32[8,8,128]{2,1,0:T(8,128)}, u32[]{:S(2)}) copy-start(f32[8,8,128]{2,1,0:T(8,128)} %param.12) | copy-start | bytes 98308
  3.2 0.7 %copy-start.7 = (s32[4,4,2]{1,2,0:T(2,128)S(1)}, s32[4,4,2]{1,2,0:T(2,128)}, u32[]{:S(2)}) copy-start(s32[4,4,2]{1,2,0:T(2,128)} %param.15) | copy-start | bytes 388
  3.2 0.7 %copy-start.6 = (s32[4,4,2]{1,2,0:T(2,128)S(1)}, s32[4,4,2]{1,2,0:T(2,128)}, u32[]{:S(2)}) copy-start(s32[4,4,2]{1,2,0:T(2,128)} %param.16) | copy-start | bytes 388
  5.5 8.2 %collective-permute-start.4 = (f32[5,8,8,1]{3,2,1,0:T(8,128)S(1)}, f32[5,8,8,1]{3,2,1,0:T(8,128)S(1)}, u32[]{:S(2)}, u32[]{:S(2)}) collective-permute-start(f32[5,8,8,1]{3,2,1,0:T(8,128)S(1)} %slice_select_fusion.2), channel_id=1, source_target_pairs={{0,1},{1,0},{2,3},{3,2},{4,5},{5,4},{6,7},{7,6},{8,9},{9,8},{10,11... | collective-permute-start | bytes 3848 | tf_op jit(solution)/shard_map/ppermute | solution.py:40
  8.6 5.2 %collective-permute-start.2 = (f32[5,8,1,128]{3,2,1,0:T(1,128)S(1)}, f32[5,8,1,128]{3,2,1,0:T(1,128)S(1)}, u32[]{:S(2)}, u32[]{:S(2)}) collective-permute-start(f32[5,8,1,128]{3,2,1,0:T(1,128)S(1)} %get-tuple-element.53), channel_id=1, source_target_pairs={{0,2},{1,3},{2,0},{3,1},{4,6},{5,7},{6,4},{7,5},{8,10},{9,11},{10,... | collective-permute-start | bytes 61448 | tf_op jit(solution)/shard_map/ppermute | solution.py:40
  8.6 5.1 %collective-permute-start.3 = (f32[5,8,1,128]{3,2,1,0:T(1,128)S(1)}, f32[5,8,1,128]{3,2,1,0:T(1,128)S(1)}, u32[]{:S(2)}, u32[]{:S(2)}) collective-permute-start(f32[5,8,1,128]{3,2,1,0:T(1,128)S(1)} %get-tuple-element.54), channel_id=1, source_target_pairs={{0,1},{1,0},{2,4},{3,5},{4,2},{5,3},{6,7},{7,6},{8,9},{9,8},{10,12... | collective-permute-start | bytes 61448 | tf_op jit(solution)/shard_map/ppermute | solution.py:43
  8.8 5.0 %collective-permute-start = (f32[5,1,8,128]{3,2,1,0:T(8,128)S(1)}, f32[5,1,8,128]{3,2,1,0:T(8,128)S(1)}, u32[]{:S(2)}, u32[]{:S(2)}) collective-permute-start(f32[5,1,8,128]{3,2,1,0:T(8,128)S(1)} %get-tuple-element.51), channel_id=1, source_target_pairs={{0,8},{1,9},{2,10},{3,11},{4,12},{5,13},{6,14},{7,15},{8,0},{9,1},... | collective-permute-start | bytes 61448 | tf_op jit(solution)/shard_map/ppermute | solution.py:40
  10.9 0.8 %copy-start.8 = (s32[32]{0:T(128)S(1)}, s32[32]{0:T(128)}, u32[]{:S(2)}) copy-start(s32[32]{0:T(128)} %param.17) | copy-start | bytes 388
  10.9 2.9 %collective-permute-start.1 = (f32[5,1,8,128]{3,2,1,0:T(8,128)S(1)}, f32[5,1,8,128]{3,2,1,0:T(8,128)S(1)}, u32[]{:S(2)}, u32[]{:S(2)}) collective-permute-start(f32[5,1,8,128]{3,2,1,0:T(8,128)S(1)} %get-tuple-element.52), channel_id=1, source_target_pairs={{0,2},{1,3},{2,0},{3,1},{4,6},{5,7},{6,4},{7,5},{8,16},{9,17},{10,... | collective-permute-start | bytes 61448 | tf_op jit(solution)/shard_map/ppermute | solution.py:43
  13.8 0.8 %copy-start.3 = (f32[8,8,128]{2,1,0:T(8,128)S(1)}, f32[8,8,128]{2,1,0:T(8,128)}, u32[]{:S(2)}) copy-start(f32[8,8,128]{2,1,0:T(8,128)} %param.13) | copy-start | bytes 98308
  15.1 6.8 %collective-permute-start.9 = (f32[5,8,8,1]{3,2,1,0:T(8,128)S(1)}, f32[5,8,8,1]{3,2,1,0:T(8,128)S(1)}, u32[]{:S(2)}, u32[]{:S(2)}) collective-permute-start(f32[5,8,8,1]{3,2,1,0:T(8,128)S(1)} %slice_select_fusion.1), channel_id=1, source_target_pairs={{0,1},{1,0},{2,3},{3,2},{4,5},{5,4},{6,7},{7,6},{8,9},{9,8},{10,11... | collective-permute-start | bytes 3848 | tf_op jit(solution)/shard_map/ppermute | solution.py:40
  16.5 5.4 %collective-permute-start.7 = (f32[5,8,1,128]{3,2,1,0:T(1,128)S(1)}, f32[5,8,1,128]{3,2,1,0:T(1,128)S(1)}, u32[]{:S(2)}, u32[]{:S(2)}) collective-permute-start(f32[5,8,1,128]{3,2,1,0:T(1,128)S(1)} %get-tuple-element.47), channel_id=1, source_target_pairs={{0,2},{1,3},{2,0},{3,1},{4,6},{5,7},{6,4},{7,5},{8,10},{9,11},{10,... | collective-permute-start | bytes 61448 | tf_op jit(solution)/shard_map/ppermute | solution.py:40
  16.6 5.5 %collective-permute-start.8 = (f32[5,8,1,128]{3,2,1,0:T(1,128)S(1)}, f32[5,8,1,128]{3,2,1,0:T(1,128)S(1)}, u32[]{:S(2)}, u32[]{:S(2)}) collective-permute-start(f32[5,8,1,128]{3,2,1,0:T(1,128)S(1)} %get-tuple-element.48), channel_id=1, source_target_pairs={{0,1},{1,0},{2,4},{3,5},{4,2},{5,3},{6,7},{7,6},{8,9},{9,8},{10,12... | collective-permute-start | bytes 61448 | tf_op jit(solution)/shard_map/ppermute | solution.py:43
  17.7 4.5 %collective-permute-start.5 = (f32[5,1,8,128]{3,2,1,0:T(8,128)S(1)}, f32[5,1,8,128]{3,2,1,0:T(8,128)S(1)}, u32[]{:S(2)}, u32[]{:S(2)}) collective-permute-start(f32[5,1,8,128]{3,2,1,0:T(8,128)S(1)} %get-tuple-element.45), channel_id=1, source_target_pairs={{0,8},{1,9},{2,10},{3,11},{4,12},{5,13},{6,14},{7,15},{8,0},{9,1},... | collective-permute-start | bytes 61448 | tf_op jit(solution)/shard_map/ppermute | solution.py:40
  20.0 2.2 %collective-permute-start.6 = (f32[5,1,8,128]{3,2,1,0:T(8,128)S(1)}, f32[5,1,8,128]{3,2,1,0:T(8,128)S(1)}, u32[]{:S(2)}, u32[]{:S(2)}) collective-permute-start(f32[5,1,8,128]{3,2,1,0:T(8,128)S(1)} %get-tuple-element.46), channel_id=1, source_target_pairs={{0,2},{1,3},{2,0},{3,1},{4,6},{5,7},{6,4},{7,5},{8,16},{9,17},{10,... | collective-permute-start | bytes 61448 | tf_op jit(solution)/shard_map/ppermute | solution.py:43
  22.7 5.8 %collective-permute-start.14 = (f32[5,8,8,1]{3,2,1,0:T(8,128)S(1)}, f32[5,8,8,1]{3,2,1,0:T(8,128)S(1)}, u32[]{:S(2)}, u32[]{:S(2)}) collective-permute-start(f32[5,8,8,1]{3,2,1,0:T(8,128)S(1)} %slice_select_fusion), channel_id=1, source_target_pairs={{0,1},{1,0},{2,3},{3,2},{4,5},{5,4},{6,7},{7,6},{8,9},{9,8},{10,11... | collective-permute-start | bytes 3848 | tf_op jit(solution)/shard_map/ppermute | solution.py:40
  23.7 4.8 %collective-permute-start.12 = (f32[5,8,1,128]{3,2,1,0:T(1,128)S(1)}, f32[5,8,1,128]{3,2,1,0:T(1,128)S(1)}, u32[]{:S(2)}, u32[]{:S(2)}) collective-permute-start(f32[5,8,1,128]{3,2,1,0:T(1,128)S(1)} %get-tuple-element.41), channel_id=1, source_target_pairs={{0,2},{1,3},{2,0},{3,1},{4,6},{5,7},{6,4},{7,5},{8,10},{9,11},{10,... | collective-permute-start | bytes 61448 | tf_op jit(solution)/shard_map/ppermute | solution.py:40
  23.8 4.9 %collective-permute-start.13 = (f32[5,8,1,128]{3,2,1,0:T(1,128)S(1)}, f32[5,8,1,128]{3,2,1,0:T(1,128)S(1)}, u32[]{:S(2)}, u32[]{:S(2)}) collective-permute-start(f32[5,8,1,128]{3,2,1,0:T(1,128)S(1)} %get-tuple-element.42), channel_id=1, source_target_pairs={{0,1},{1,0},{2,4},{3,5},{4,2},{5,3},{6,7},{7,6},{8,9},{9,8},{10,12... | collective-permute-start | bytes 61448 | tf_op jit(solution)/shard_map/ppermute | solution.py:43
  25.0 4.1 %collective-permute-start.10 = (f32[5,1,8,128]{3,2,1,0:T(8,128)S(1)}, f32[5,1,8,128]{3,2,1,0:T(8,128)S(1)}, u32[]{:S(2)}, u32[]{:S(2)}) collective-permute-start(f32[5,1,8,128]{3,2,1,0:T(8,128)S(1)} %get-tuple-element.39), channel_id=1, source_target_pairs={{0,8},{1,9},{2,10},{3,11},{4,12},{5,13},{6,14},{7,15},{8,0},{9,1},... | collective-permute-start | bytes 61448 | tf_op jit(solution)/shard_map/ppermute | solution.py:40
  27.3 1.8 %collective-permute-start.11 = (f32[5,1,8,128]{3,2,1,0:T(8,128)S(1)}, f32[5,1,8,128]{3,2,1,0:T(8,128)S(1)}, u32[]{:S(2)}, u32[]{:S(2)}) collective-permute-start(f32[5,1,8,128]{3,2,1,0:T(8,128)S(1)} %get-tuple-element.40), channel_id=1, source_target_pairs={{0,2},{1,3},{2,0},{3,1},{4,6},{5,7},{6,4},{7,5},{8,16},{9,17},{10,... | collective-permute-start | bytes 61448 | tf_op jit(solution)/shard_map/ppermute | solution.py:43
  28.8 0.8 %copy-start.5 = (f32[8,8,128]{2,1,0:T(8,128)S(1)}, f32[8,8,128]{2,1,0:T(8,128)}, u32[]{:S(2)}) copy-start(f32[8,8,128]{2,1,0:T(8,128)} %param.14) | copy-start | bytes 98308

commit v3 on v2

v3 whole, which is shorter than its diff:
```python
import functools

import jax
import jax.numpy as jnp
from jax import lax
from jax.experimental import pallas as pl
from jax.experimental.pallas import tpu as pltpu
from jax.sharding import PartitionSpec as P

CX = 8
CY = 8
CZ = 128
BZ = 16
BOXES = CZ // BZ

AXES = ("gx", "gy", "gz")

step_length = 0.14
third = 1.0 / 3.0
two_thirds = 2.0 / 3.0

FULL = (CX, CY, CZ)
TILE = (CY, CZ)


def pairings(sizes, axis, near_axis):
    size = sizes[axis]
    first, second = [], []
    for x in range(sizes[0]):
        for y in range(sizes[1]):
            for z in range(sizes[2]):
                here = [x, y, z]
                index = (x * sizes[1] + y) * sizes[2] + z
                place = here[axis]
                other = list(here)
                other[axis] = place ^ 1
                first.append((index, (other[0] * sizes[1] + other[1]) * sizes[2] + other[2]))
                other = list(here)
                if 0 < place < size - 1:
                    other[axis] = place + 1 if place % 2 else place - 1
                else:
                    other[near_axis] = here[near_axis] ^ 1
                second.append((index, (other[0] * sizes[1] + other[1]) * sizes[2] + other[2]))
    return first, second if size > 2 else None


def positions():
    return [lax.axis_index(axis) for axis in AXES]


def own_half_inverse(level_ref):
    here = positions()
    level = level_ref[here[0], here[1], here[2]]
    return 0.5 * lax.shift_left(jnp.int32(1), level).astype(jnp.float32)


def load(ref):
    return [ref[component] for component in range(5)]


def transposed_partials(adjoint, density, velocity_ref, stiffness, half_inverse, direction):
    along_speed = half_inverse * velocity_ref[direction]
    components = [along_speed * component for component in adjoint]
    row = 1 + direction
    components[row] = components[row] + half_inverse * (
        density * adjoint[0] + stiffness * adjoint[4]
    )
    components[4] = components[4] + (half_inverse * adjoint[row]) / density
    return components


def all_partials(adjoint, density_ref, velocity_ref, stiffness_ref, half_inverse):
    density, stiffness = density_ref[...], stiffness_ref[...]
    return [
        transposed_partials(adjoint, density, velocity_ref, stiffness, half_inverse, direction)
        for direction in range(3)
    ]


def rows_of(block, row):
    return jnp.concatenate([block[x, row : row + 1, :] for x in range(CX)], axis=0)


def pack_x(fields, position, out_first, out_second):
    even = position % 2 == 0
    for index, field in enumerate(fields):
        low, high = field[0], field[CX - 1]
        out_first[index] = jnp.where(even, high, low)
        if out_second is not None:
            out_second[index] = jnp.where(even, low, high)


def pack_y(fields, position, out_first, out_second):
    even = position % 2 == 0
    faces = []
    for index, field in enumerate(fields):
        low, high = rows_of(field, 0), rows_of(field, CY - 1)
        out_first[index] = jnp.where(even, high, low)
        if out_second is not None:
            out_second[index] = jnp.where(even, low, high)
        faces.append((low, high))
    return faces


def pack_z(fields):
    lanes = lax.broadcasted_iota(jnp.int32, TILE, 1) // 2
    packed = jnp.zeros(TILE, jnp.float32)
    for index, field in enumerate(fields):
        for x in range(CX):
            k = index * CX + x
            packed = jnp.where(lanes == k, pltpu.roll(field[x], (2 * k + 1) % CZ, 1), packed)
    return packed


def sort_pair(first, second, position, size):
    even = position % 2 == 0
    zero = jnp.zeros_like(first)
    if second is None:
        return jnp.where(even, zero, first), jnp.where(even, first, zero)
    below = jnp.where(position == 0, zero, jnp.where(even, second, first))
    above = jnp.where(position == size - 1, zero, jnp.where(even, first, second))
    return below, above


def pair_of(refs, index):
    first, second = refs
    return first[index], None if second is None else second[index]


def lane_halo(z_refs, position, size):
    below, above = sort_pair(
        z_refs[0][...], None if z_refs[1] is None else z_refs[1][...], position, size
    )
    lanes = lax.broadcasted_iota(jnp.int32, TILE, 1)
    return jnp.where(lanes % 2 == 0, pltpu.roll(above, CZ - 1, 1), pltpu.roll(below, 1, 1))


def halo_of(x_refs, y_refs, z_halo, component, sizes):
    here = positions()
    x_below, x_above = sort_pair(*pair_of(x_refs, component), here[0], sizes[0])
    y_below, y_above = sort_pair(*pair_of(y_refs, component), here[1], sizes[1])
    spread = lambda rows: jnp.stack(
        [jnp.broadcast_to(rows[x : x + 1], TILE) for x in range(CX)]
    )
    z_both = jnp.stack(
        [pltpu.roll(z_halo, (CZ - 1 - 2 * (component * CX + x)) % CZ, 1) for x in range(CX)]
    )
    return x_below, x_above, spread(y_below), spread(y_above), z_both


def differences(partials, component, halo):
    part_x, part_y, part_z = (partials[direction][component] for direction in range(3))
    rows = lax.broadcasted_iota(jnp.int32, FULL, 1)
    lanes = lax.broadcasted_iota(jnp.int32, FULL, 2)
    if halo is None:
        zero = jnp.zeros(TILE, jnp.float32)
        x_below, x_above, y_below, y_above, z_both = zero, zero, 0.0, 0.0, 0.0
    else:
        x_below, x_above, y_below, y_above, z_both = halo
    after = jnp.concatenate([part_x[1:], x_above[None]], axis=0)
    before = jnp.concatenate([x_below[None], part_x[:-1]], axis=0)
    total = after - before
    after = jnp.where(rows == CY - 1, y_above, pltpu.roll(part_y, CY - 1, 1))
    before = jnp.where(rows == 0, y_below, pltpu.roll(part_y, 1, 1))
    total = total + (after - before)
    after = jnp.where(lanes == CZ - 1, z_both, pltpu.roll(part_z, CZ - 1, 2))
    before = jnp.where(lanes == 0, z_both, pltpu.roll(part_z, 1, 2))
    return total + (after - before)


def split(refs, sizes, count):
    refs, out = list(refs), []
    for axis in range(3):
        first = refs.pop(0)
        out.append((first, refs.pop(0) if sizes[axis] > 2 else None))
    assert len(refs) == count
    return out, refs


def send_all(partials, extra, out_x, out_y, out_z):
    here = positions()
    pack_x(partials[0] + extra, here[0], *out_x)
    faces = pack_y(partials[1] + extra, here[1], *out_y)
    packed = pack_z(partials[2] + extra)
    for ref in out_z[:1]:
        ref[...] = packed
    return faces, packed


def first_kernel(sizes, level, adjoint, density, velocity, stiffness, source, *outs):
    half_inverse = own_half_inverse(level)
    partials = all_partials(load(adjoint), density, velocity, stiffness, half_inverse)
    out_x, out_y, out_z = message_outs(outs, sizes)[0]
    send_all(partials, [source[...]], out_x, out_y, out_z)


def message_outs(refs, sizes):
    refs, out = list(refs), []
    for axis in range(2):
        first = refs.pop(0)
        out.append((first, refs.pop(0) if sizes[axis] > 2 else None))
    out.append((refs.pop(0),))
    return out, refs


def second_kernel(sizes, level, adjoint, density, velocity, stiffness, sponge, *refs):
    received, outs = split(refs, sizes, len(refs) - sum(2 if s > 2 else 1 for s in sizes))
    half_inverse = own_half_inverse(level)
    here = positions()
    old = load(adjoint)
    partials = all_partials(old, density, velocity, stiffness, half_inverse)
    z_halo = lane_halo(received[2], here[2], sizes[2])
    section, outs = outs[0], outs[1:]
    new = []
    for component in range(5):
        halo = halo_of(received[0], received[1], z_halo, component, sizes)
        change = differences(partials, component, halo) - sponge[...] * old[component]
        value = old[component] + step_length * change
        section[component] = value
        new.append(value)
    partials = all_partials(new, density, velocity, stiffness, half_inverse)
    send_all(partials, [], *message_outs(outs, sizes)[0])


def sublane_total(tile):
    for shift in (4, 2, 1):
        tile = tile + pltpu.roll(tile, shift, 0)
    return tile


def box_row(tiles):
    sublanes = lax.broadcasted_iota(jnp.int32, TILE, 0)
    lanes = lax.broadcasted_iota(jnp.int32, TILE, 1)
    rows = jnp.zeros(TILE, jnp.float32)
    for component, tile in enumerate(tiles):
        rows = jnp.where(sublanes == component, sublane_total(tile), rows)
    for shift in (1, 2, 4, 8):
        rows = rows + pltpu.roll(rows, CZ - shift, 1)
    placed = jnp.zeros(TILE, jnp.float32)
    for component in range(5):
        placed = jnp.where(
            (sublanes == component) & (lanes % BZ == component),
            pltpu.roll(rows, component, 1),
            placed,
        )
    return sublane_total(placed)


def lane_row(product, box):
    lanes = lax.broadcasted_iota(jnp.int32, TILE, 1)
    rows = sublane_total(product)
    for shift in (1, 2, 4, 8):
        rows = rows + pltpu.roll(rows, CZ - shift, 1)
    placed = jnp.zeros(TILE, jnp.float32)
    for component in range(5):
        want = box * BZ + component
        placed = jnp.where(
            lanes == want, pltpu.roll(rows, (want - 2 * CX * component) % CZ, 1), placed
        )
    return placed


def third_kernel(
    sizes, level, patches, owners, adjoint, density, velocity, stiffness, sponge, source, section, *refs
):
    received, rest = split(refs, sizes, len(refs) - sum(2 if s > 2 else 1 for s in sizes))
    (sources_x, sources_y, sources_z), outs = split(
        rest, sizes, len(rest) - sum(2 if s > 2 else 1 for s in sizes)
    )
    half_inverse = own_half_inverse(level)
    here = positions()
    base, old = load(adjoint), load(section)
    partials = all_partials(old, density, velocity, stiffness, half_inverse)
    z_halo = lane_halo(received[2], here[2], sizes[2])
    partial_out, table_out, outs = outs[0], outs[1], outs[2:]
    new = []
    for component in range(5):
        halo = halo_of(received[0], received[1], z_halo, component, sizes)
        change = differences(partials, component, halo) - sponge[...] * old[component]
        new.append(0.75 * base[component] + 0.25 * (old[component] + step_length * change))
    partials = all_partials(new, density, velocity, stiffness, half_inverse)
    faces_y, packed_z = send_all(partials, [], *message_outs(outs, sizes)[0])
    shape = source[...]
    own = []
    for component in range(5):
        change = differences(partials, component, None) - sponge[...] * new[component]
        value = third * base[component] + two_thirds * (new[component] + step_length * change)
        partial_out[component] = value
        own.append(jnp.sum(value * shape, axis=0))
    weight = two_thirds * step_length
    x_below, x_above = sort_pair(*pair_of(sources_x, 5), here[0], sizes[0])
    y_below, y_above = sort_pair(*pair_of(sources_y, 5), here[1], sizes[1])
    first, second = sources_z
    z_below, z_above = sort_pair(
        first[...], None if second is None else second[...], here[2], sizes[2]
    )
    lanes = lax.broadcasted_iota(jnp.int32, TILE, 1)
    aligned_above = jnp.zeros(TILE, jnp.float32)
    aligned_below = jnp.zeros(TILE, jnp.float32)
    for component in range(5):
        group = lanes // (2 * CX) == component
        shift = 2 * CX * (component - 5)
        aligned_above = jnp.where(
            group & (lanes % 2 == 0), pltpu.roll(z_above, (shift - 1) % CZ, 1), aligned_above
        )
        aligned_below = jnp.where(
            group & (lanes % 2 == 1), pltpu.roll(z_below, (shift + 1) % CZ, 1), aligned_below
        )
    contributions = [
        ((0, 0, 0), box_row(own)),
        ((1, 0, 0), -weight * box_row([x_above * partials[0][f][CX - 1] for f in range(5)])),
        ((-1, 0, 0), weight * box_row([x_below * partials[0][f][0] for f in range(5)])),
        ((0, 1, 0), -weight * box_row([y_above * faces_y[f][1] for f in range(5)])),
        ((0, -1, 0), weight * box_row([y_below * faces_y[f][0] for f in range(5)])),
        ((0, 0, 1), -weight * lane_row(aligned_above * packed_z, 0)),
        ((0, 0, -1), weight * lane_row(aligned_below * packed_z, BOXES - 1)),
    ]
    targets = []
    for offset, row in contributions:
        place = [
            jnp.clip(here[axis] + offset[axis], 0, sizes[axis] - 1) for axis in range(3)
        ]
        targets.append(owners[patches[place[0], place[1], place[2]]])
    sublanes = lax.broadcasted_iota(jnp.int32, TILE, 0)
    rows_total = table_out.shape[0]
    for start in range(0, rows_total, CY):
        table = jnp.zeros(TILE, jnp.float32)
        for (offset, row), target in zip(contributions, targets):
            table = table + jnp.where(sublanes + start == target, step_length * row, 0.0)
        table_out[start : start + CY, :] = table


def last_kernel(sizes, partial, table, *refs):
    received, (out, gradient) = split(refs, sizes, 2)
    here = positions()
    weight = two_thirds * step_length
    z_halo = lane_halo(received[2], here[2], sizes[2])
    rows = lax.broadcasted_iota(jnp.int32, FULL, 1)
    lanes = lax.broadcasted_iota(jnp.int32, FULL, 2)
    for component in range(5):
        x_below, x_above, y_below, y_above, z_both = halo_of(
            received[0], received[1], z_halo, component, sizes
        )
        change = jnp.where(rows == CY - 1, y_above, 0.0) - jnp.where(rows == 0, y_below, 0.0)
        change = change + jnp.where(lanes == CZ - 1, z_both, 0.0)
        change = change - jnp.where(lanes == 0, z_both, 0.0)
        value = partial[component] + weight * change
        out[component] = value
        out[component, CX - 1] = value[CX - 1] + weight * x_above
        out[component, 0] = value[0] - weight * x_below
    total = jnp.zeros(TILE, jnp.float32)
    for start in range(0, table.shape[0], CY):
        total = total + table[start : start + CY, :]
    total = sublane_total(total)
    tile_lanes = lax.broadcasted_iota(jnp.int32, TILE, 1)
    result = jnp.zeros(TILE, jnp.float32)
    for component in range(5):
        for box in range(BOXES):
            want = component * BOXES + box
            have = box * BZ + component
            result = jnp.where(tile_lanes == want, pltpu.roll(total, (want - have) % CZ, 1), result)
    gradient[...] = result[0:1, : 5 * BOXES]


def call(kernel, sizes, tables, arrays, out_shapes):
    vmem = pl.BlockSpec(memory_space=pltpu.VMEM)
    smem = pl.BlockSpec(memory_space=pltpu.SMEM)
    return pl.pallas_call(
        functools.partial(kernel, sizes),
        out_shape=[jax.ShapeDtypeStruct(shape, jnp.float32) for shape in out_shapes],
        in_specs=[smem] * len(tables) + [vmem] * len(arrays),
        out_specs=[vmem] * len(out_shapes),
        compiler_params=pltpu.CompilerParams(vmem_limit_bytes=32 * 1024 * 1024),
    )(*tables, *arrays)


def body(
    terminal_adjoint,
    density,
    velocity,
    stiffness,
    sponge,
    source_shape,
    brick_level,
    brick_patch,
    patch_owner,
):
    sizes = tuple(lax.axis_size(axis) for axis in AXES)
    permutations = (
        pairings(sizes, 0, 1),
        pairings(sizes, 1, 2),
        pairings(sizes, 2, 1),
    )
    devices = patch_owner.shape[0]
    state = (5,) + FULL

    def message_shapes(fields):
        shapes = []
        for axis in range(2):
            shapes += [(fields,) + TILE] * (2 if sizes[axis] > 2 else 1)
        return shapes + [TILE]

    def exchange(messages):
        messages = list(messages)
        sends = []
        for axis in range(2):
            for permutation in permutations[axis]:
                if permutation is not None:
                    sends.append((messages.pop(0), permutation))
        packed = messages.pop(0)
        for permutation in permutations[2]:
            if permutation is not None:
                sends.append((packed, permutation))
        return [lax.ppermute(message, AXES, permutation) for message, permutation in sends]

    mean = (density, velocity, stiffness)
    sent = call(
        first_kernel,
        sizes,
        (brick_level,),
        (terminal_adjoint, *mean, source_shape),
        message_shapes(6),
    )
    received_one = exchange(sent)
    section, *sent = call(
        second_kernel,
        sizes,
        (brick_level,),
        (terminal_adjoint, *mean, sponge, *received_one),
        [state] + message_shapes(5),
    )
    received = exchange(sent)
    partial, table, *sent = call(
        third_kernel,
        sizes,
        (brick_level, brick_patch, patch_owner),
        (terminal_adjoint, *mean, sponge, source_shape, section, *received, *received_one),
        [state, (devices, CZ)] + message_shapes(5),
    )
    received = exchange(sent)
    table = lax.all_to_all(table.reshape(devices, 1, CZ), AXES, 0, 0, tiled=True)
    adjoint, gradient = call(
        last_kernel,
        sizes,
        (),
        (partial, table.reshape(devices, CZ), *received),
        [state, (1, 5 * BOXES)],
    )
    return adjoint, gradient


def solution(mesh):
    in_specs = (
        P(None, "gx", "gy", "gz"),
        P("gx", "gy", "gz"),
        P(None, "gx", "gy", "gz"),
        P("gx", "gy", "gz"),
        P("gx", "gy", "gz"),
        P("gx", "gy", "gz"),
        P(),
        P(),
        P(),
    )
    out_specs = (P(None, "gx", "gy", "gz"), P(("gx", "gy", "gz"), None))
    return jax.shard_map(body, mesh=mesh, in_specs=in_specs, out_specs=out_specs, check_vma=False)
```

time: 43.3 us -> 37.1 us (0.86)
  blocking collectives: 11.5 us -> 0 us
  other arithmetic: 7.35 us -> 0 us
  Pallas kernels: 0 us -> 4.92 us
  waiting for transfers between devices: 3.78 us -> 8.18 us
  local copies, waits for them, and re-layouts: 2.77 us -> 5.02 us
  starting transfers between devices: 15.5 us -> 17.7 us
  between operations: 1.93 us -> 0.8 us
    all_to_all x1 -> x0, blocking collectives: 11.5 us -> none  [body(): incoming = lax.all_to_all(outgoing, AXES, 0, 0, tiled=True)]
    pallas_call x0 -> x4, Pallas kernels: none -> 4.92 us  [call(): pl.pallas_call(functools.partial(kernel, sizes), out_shape=[jax.ShapeDtyp...]
    ppermute x15, waiting for transfers between devices: 3.78 us -> 8.18 us  [exchange(): lax.ppermute(message, AXES, permutation)]
    reduce_sum x5 -> x0, other arithmetic: 3.49 us -> none  [the longest x1 1.28 us: body(): jnp.sum(jnp.where(jnp.arange(devices) == own_patch, patch_owner, 0))]
    all_to_all x0 -> x1, starting transfers between devices: none -> 2.54 us  [body(): lax.all_to_all(table.reshape(devices, 1, CZ), AXES, 0, 0, tiled=True)]
    unnamed x18 -> x28, local copies, waits for them, and re-layouts: 2.62 us -> 5.02 us
    unnamed x21 -> x0, other arithmetic: 1.81 us -> none
    select_n x19 -> x0, other arithmetic: 0.76 us -> none  [the longest x9 0.42 us: send_faces(): jnp.where(even, high_face, low_face)]
  transfers between devices with their start and end apart: 15 -> 16, of which waited for: 5 -> 3; matrix products, arithmetic and copies ran while one was open for 5% -> 0% of each run, Pallas kernels for 0% -> 0%
where the time goes in v3:
time: 37.1 us; the launch traced here: 36.6 us
  starting transfers between devices  17.7 us (48%)
  waiting for transfers between devices  8.18 us (22%)
  local copies, waits for them, and re-layouts  5.02 us (14%)
  Pallas kernels  4.92 us (13%)
  between operations  0.8 us (2%)
    ppermute x15, starting transfers between devices, exchange(): lax.ppermute(message, AXES, permutation)  15.2 us
    ppermute x15, waiting for transfers between devices, exchange(): lax.ppermute(message, AXES, permutation)  8.18 us
    unnamed x28, local copies, waits for them, and re-layouts  5.02 us
    pallas_call x4, Pallas kernels, call(): pl.pallas_call(functools.partial(kernel, sizes), out_shape=[jax.ShapeDtyp...  4.92 us
    all_to_all x1, starting transfers between devices, body(): lax.all_to_all(table.reshape(devices, 1, CZ), AXES, 0, 0, tiled=True)  2.54 us
  transfers between devices with their start and end apart: 16, of which 3 were waited for; matrix products, arithmetic and copies ran while one was open for 0% of the time, Pallas kernels for 0%

profile of v3, /device:TPU:0, one launch (start us, length us, event | category | flops | bytes accessed | tf_op | source)
XLA Modules:
  0.0 36.6 jit_solution(11469890336201593988)
XLA Ops:
  0.6 0.8 %copy.17.level = s32[4,4,2]{2,1,0:T(4,128)S(1)} copy(s32[4,4,2]{1,2,0:T(2,128)} %param.15) | data formatting | bytes 256 | tf_op args[6]
  1.4 0.9 %copy-done = f32[5,8,8,128]{3,2,1,0:T(8,128)S(1)} copy-done((f32[5,8,8,128]{3,2,1,0:T(8,128)S(1)}, f32[5,8,8,128]{3,2,1,0:T(8,128)}, u32[]{:S(2)}) %copy-start) | copy-done | bytes 163864
  2.3 0.9 %copy-done.2 = f32[3,8,8,128]{3,2,1,0:T(8,128)S(1)} copy-done((f32[3,8,8,128]{3,2,1,0:T(8,128)S(1)}, f32[3,8,8,128]{3,2,1,0:T(8,128)}, u32[]{:S(2)}) %copy-start.2) | copy-done | bytes 98328
  3.2 0.8 %copy-done.4 = f32[8,8,128]{2,1,0:T(8,128)S(1)} copy-done((f32[8,8,128]{2,1,0:T(8,128)S(1)}, f32[8,8,128]{2,1,0:T(8,128)}, u32[]{:S(2)}) %copy-start.4) | copy-done | bytes 32792
  4.0 0.8 %copy-done.6 = f32[8,8,128]{2,1,0:T(8,128)S(1)} copy-done((f32[8,8,128]{2,1,0:T(8,128)S(1)}, f32[8,8,128]{2,1,0:T(8,128)}, u32[]{:S(2)}) %copy-start.6) | copy-done | bytes 32792
  4.7 0.8 %copy-done.9 = f32[8,8,128]{2,1,0:T(8,128)S(1)} copy-done((f32[8,8,128]{2,1,0:T(8,128)S(1)}, f32[8,8,128]{2,1,0:T(8,128)}, u32[]{:S(2)}) %copy-start.9) | copy-done | bytes 32792
  5.5 0.8 %shard_map.104 = (f32[6,8,128]{2,1,0:T(8,128)S(1)}, f32[6,8,128]{2,1,0:T(8,128)S(1)}, f32[6,8,128]{2,1,0:T(8,128)S(1)}, f32[6,8,128]{2,1,0:T(8,128)S(1)}, f32[8,128]{1,0:T(8,128)S(1)}) custom-call(s32[4,4,2]{2,1,0:T(4,128)S(1)} %copy.17.level, f32[5,8,8,128]{3,2,1,0:T(8,128)S(1)} %copy-done, f32[8,8,128]{2,1,0:T(8,128)S(1)} %copy-done.4, ...), custom_call_target="tpu_custom_call" | custom-call | tf_op jit(solution)/shard_map/pallas_call | solution.py:368
  6.3 3.1 %collective-permute-start = (f32[6,8,128]{2,1,0:T(8,128)S(1)}, f32[6,8,128]{2,1,0:T(8,128)S(1)}, u32[]{:S(2)}, u32[]{:S(2)}) collective-permute-start(f32[6,8,128]{2,1,0:T(8,128)S(1)} %get-tuple-element.20), channel_id=1, source_target_pairs={{0,8},{1,9},{2,10},{3,11},{4,12},{5,13},{6,14},{7,15},{8,0},{9,1},... | collective-permute-start | bytes 73736 | tf_op jit(solution)/shard_map/ppermute | solution.py:414
  9.4 0.5 %collective-permute-start.2 = (f32[6,8,128]{2,1,0:T(8,128)S(1)}, f32[6,8,128]{2,1,0:T(8,128)S(1)}, u32[]{:S(2)}, u32[]{:S(2)}) collective-permute-start(f32[6,8,128]{2,1,0:T(8,128)S(1)} %get-tuple-element.22), channel_id=1, source_target_pairs={{0,2},{1,3},{2,0},{3,1},{4,6},{5,7},{6,4},{7,5},{8,10},{9,11},{10,... | collective-permute-start | bytes 73736 | tf_op jit(solution)/shard_map/ppermute | solution.py:414
  9.9 1.5 %collective-permute-start.3 = (f32[6,8,128]{2,1,0:T(8,128)S(1)}, f32[6,8,128]{2,1,0:T(8,128)S(1)}, u32[]{:S(2)}, u32[]{:S(2)}) collective-permute-start(f32[6,8,128]{2,1,0:T(8,128)S(1)} %get-tuple-element.23), channel_id=1, source_target_pairs={{0,1},{1,0},{2,4},{3,5},{4,2},{5,3},{6,7},{7,6},{8,9},{9,8},{10,12... | collective-permute-start | bytes 73736 | tf_op jit(solution)/shard_map/ppermute | solution.py:414
  12.0 3.1 %collective-permute-done.4.refs_4_.refs_9_ = f32[8,128]{1,0:T(8,128)S(1)} collective-permute-done((f32[8,128]{1,0:T(8,128)S(1)}, f32[8,128]{1,0:T(8,128)S(1)}, u32[]{:S(2)}, u32[]{:S(2)}) %collective-permute-start.4) | collective-permute-done | bytes 4128 | tf_op jit(solution)/shard_map/ppermute | solution.py:414
  15.1 1.0 %shard_map.105 = (f32[5,8,8,128]{3,2,1,0:T(8,128)S(1)}, f32[5,8,128]{2,1,0:T(8,128)S(1)}, f32[5,8,128]{2,1,0:T(8,128)S(1)}, f32[5,8,128]{2,1,0:T(8,128)S(1)}, f3...) custom-call(s32[4,4,2]{2,1,0:T(4,128)S(1)} %copy.17.level, f32[5,8,8,128]{3,2,1,0:T(8,128)S(1)} %copy-done, ...), custom_call_target="tpu_custom_call" | custom-call | tf_op jit(solution)/shard_map/pallas_call | solution.py:368
  16.2 2.7 %collective-permute-start.5 = (f32[5,8,128]{2,1,0:T(8,128)S(1)}, f32[5,8,128]{2,1,0:T(8,128)S(1)}, u32[]{:S(2)}, u32[]{:S(2)}) collective-permute-start(f32[5,8,128]{2,1,0:T(8,128)S(1)} %get-tuple-element.26), channel_id=1, source_target_pairs={{0,8},{1,9},{2,10},{3,11},{4,12},{5,13},{6,14},{7,15},{8,0},{9,1},... | collective-permute-start | bytes 61448 | tf_op jit(solution)/shard_map/ppermute | solution.py:414
  18.9 0.5 %collective-permute-start.7 = (f32[5,8,128]{2,1,0:T(8,128)S(1)}, f32[5,8,128]{2,1,0:T(8,128)S(1)}, u32[]{:S(2)}, u32[]{:S(2)}) collective-permute-start(f32[5,8,128]{2,1,0:T(8,128)S(1)} %get-tuple-element.28), channel_id=1, source_target_pairs={{0,2},{1,3},{2,0},{3,1},{4,6},{5,7},{6,4},{7,5},{8,10},{9,11},{10,... | collective-permute-start | bytes 61448 | tf_op jit(solution)/shard_map/ppermute | solution.py:414
  19.9 1.5 %collective-permute-start.9 = (f32[8,128]{1,0:T(8,128)S(1)}, f32[8,128]{1,0:T(8,128)S(1)}, u32[]{:S(2)}, u32[]{:S(2)}) collective-permute-start(f32[8,128]{1,0:T(8,128)S(1)} %get-tuple-element.30), channel_id=1, source_target_pairs={{0,1},{1,0},{2,3},{3,2},{4,5},{5,4},{6,7},{7,6},{8,9},{9,8},{10,11... | collective-permute-start | bytes 12296 | tf_op jit(solution)/shard_map/ppermute | solution.py:414
  21.5 2.0 %collective-permute-done.9.refs_4_ = f32[8,128]{1,0:T(8,128)S(1)} collective-permute-done((f32[8,128]{1,0:T(8,128)S(1)}, f32[8,128]{1,0:T(8,128)S(1)}, u32[]{:S(2)}, u32[]{:S(2)}) %collective-permute-start.9) | collective-permute-done | bytes 4128 | tf_op jit(solution)/shard_map/ppermute | solution.py:414
  23.6 2.2 %shard_map.106 = (f32[5,8,8,128]{3,2,1,0:T(8,128)S(1)}, f32[32,128]{1,0:T(8,128)}, f32[5,8,128]{2,1,0:T(8,128)S(1)}, f32[5,8,128]{2,1,0:T(8,128)S(1)}, f32[5,8,1...) custom-call(s32[4,4,2]{2,1,0:T(4,128)S(1)} %copy.17.level, s32[4,4,2]{2,1,0:T(4,128)S(1)} %copy.18.patches, ...), custom_call_target="tpu_custom_call" | custom-call | tf_op jit(solution)/shard_map/pallas_call | solution.py:368
  25.8 2.5 %all-to-all-start = ((f32[32,1,128]{2,1,0:T(1,128)}), f32[32,1,128]{2,1,0:T(1,128)S(1)}, u32[]{:S(2)}, u32[]{:S(2)}) async-start(f32[32,1,128]{2,1,0:T(1,128)} %bitcast.1), calls=%async_computation | async-start | bytes 32768 | tf_op jit(solution)/shard_map/all_to_all | solution.py:441
  28.3 1.8 %collective-permute-start.10 = (f32[5,8,128]{2,1,0:T(8,128)S(1)}, f32[5,8,128]{2,1,0:T(8,128)S(1)}, u32[]{:S(2)}, u32[]{:S(2)}) collective-permute-start(f32[5,8,128]{2,1,0:T(8,128)S(1)} %get-tuple-element.33), channel_id=1, source_target_pairs={{0,8},{1,9},{2,10},{3,11},{4,12},{5,13},{6,14},{7,15},{8,0},{9,1},... | collective-permute-start | bytes 61448 | tf_op jit(solution)/shard_map/ppermute | solution.py:414
  30.1 0.5 %collective-permute-start.12 = (f32[5,8,128]{2,1,0:T(8,128)S(1)}, f32[5,8,128]{2,1,0:T(8,128)S(1)}, u32[]{:S(2)}, u32[]{:S(2)}) collective-permute-start(f32[5,8,128]{2,1,0:T(8,128)S(1)} %get-tuple-element.35), channel_id=1, source_target_pairs={{0,2},{1,3},{2,0},{3,1},{4,6},{5,7},{6,4},{7,5},{8,10},{9,11},{10,... | collective-permute-start | bytes 61448 | tf_op jit(solution)/shard_map/ppermute | solution.py:414
  30.6 1.5 %collective-permute-start.13 = (f32[5,8,128]{2,1,0:T(8,128)S(1)}, f32[5,8,128]{2,1,0:T(8,128)S(1)}, u32[]{:S(2)}, u32[]{:S(2)}) collective-permute-start(f32[5,8,128]{2,1,0:T(8,128)S(1)} %get-tuple-element.36), channel_id=1, source_target_pairs={{0,1},{1,0},{2,4},{3,5},{4,2},{5,3},{6,7},{7,6},{8,9},{9,8},{10,12... | collective-permute-start | bytes 61448 | tf_op jit(solution)/shard_map/ppermute | solution.py:414
  32.1 0.5 %collective-permute-start.14 = (f32[8,128]{1,0:T(8,128)S(1)}, f32[8,128]{1,0:T(8,128)S(1)}, u32[]{:S(2)}, u32[]{:S(2)}) collective-permute-start(f32[8,128]{1,0:T(8,128)S(1)} %get-tuple-element.37), channel_id=1, source_target_pairs={{0,1},{1,0},{2,3},{3,2},{4,5},{5,4},{6,7},{7,6},{8,9},{9,8},{10,11... | collective-permute-start | bytes 12296 | tf_op jit(solution)/shard_map/ppermute | solution.py:414
  32.6 3.1 %collective-permute-done.14.refs_4_ = f32[8,128]{1,0:T(8,128)S(1)} collective-permute-done((f32[8,128]{1,0:T(8,128)S(1)}, f32[8,128]{1,0:T(8,128)S(1)}, u32[]{:S(2)}, u32[]{:S(2)}) %collective-permute-start.14) | collective-permute-done | bytes 4128 | tf_op jit(solution)/shard_map/ppermute | solution.py:414
  35.7 0.9 %shard_map.107 = (f32[5,8,8,128]{3,2,1,0:T(8,128)}, f32[1,40]{1,0:T(1,128)}) custom-call(f32[5,8,8,128]{3,2,1,0:T(8,128)S(1)} %get-tuple-element.31.partial, f32[32,128]{1,0:T(8,128)S(1)} %bitcast.4, f32[5,8,128]{2,1,0:T(8,128)S(1)} %collective-permute-done.10.refs_0_, f32[5,8,128]{2,1,0:T(8,128)S(1)} %collective-permute-done.11.refs_1_, ...), custom_call_target="tpu_custom_call" | custom-call | tf_op jit(solution)/shard_map/pallas_call | solution.py:368
  (40 shorter events, 1.2 us)
Async XLA Ops:
  5.5 9.6 %copy-start.8 = (f32[8,8,128]{2,1,0:T(8,128)S(1)}, f32[8,8,128]{2,1,0:T(8,128)}, u32[]{:S(2)}) copy-start(f32[8,8,128]{2,1,0:T(8,128)} %sponge.3) | copy-start | bytes 98308
  6.3 8.7 %collective-permute-start = (f32[6,8,128]{2,1,0:T(8,128)S(1)}, f32[6,8,128]{2,1,0:T(8,128)S(1)}, u32[]{:S(2)}, u32[]{:S(2)}) collective-permute-start(f32[6,8,128]{2,1,0:T(8,128)S(1)} %get-tuple-element.20), channel_id=1, source_target_pairs={{0,8},{1,9},{2,10},{3,11},{4,12},{5,13},{6,14},{7,15},{8,0},{9,1},... | collective-permute-start | bytes 73736 | tf_op jit(solution)/shard_map/ppermute | solution.py:414
  9.4 5.6 %collective-permute-start.1 = (f32[6,8,128]{2,1,0:T(8,128)S(1)}, f32[6,8,128]{2,1,0:T(8,128)S(1)}, u32[]{:S(2)}, u32[]{:S(2)}) collective-permute-start(f32[6,8,128]{2,1,0:T(8,128)S(1)} %get-tuple-element.21), channel_id=1, source_target_pairs={{0,2},{1,3},{2,0},{3,1},{4,6},{5,7},{6,4},{7,5},{8,16},{9,17},{10,... | collective-permute-start | bytes 73736 | tf_op jit(solution)/shard_map/ppermute | solution.py:414
  9.4 5.6 %collective-permute-start.2 = (f32[6,8,128]{2,1,0:T(8,128)S(1)}, f32[6,8,128]{2,1,0:T(8,128)S(1)}, u32[]{:S(2)}, u32[]{:S(2)}) collective-permute-start(f32[6,8,128]{2,1,0:T(8,128)S(1)} %get-tuple-element.22), channel_id=1, source_target_pairs={{0,2},{1,3},{2,0},{3,1},{4,6},{5,7},{6,4},{7,5},{8,10},{9,11},{10,... | collective-permute-start | bytes 73736 | tf_op jit(solution)/shard_map/ppermute | solution.py:414
  9.9 5.1 %collective-permute-start.3 = (f32[6,8,128]{2,1,0:T(8,128)S(1)}, f32[6,8,128]{2,1,0:T(8,128)S(1)}, u32[]{:S(2)}, u32[]{:S(2)}) collective-permute-start(f32[6,8,128]{2,1,0:T(8,128)S(1)} %get-tuple-element.23), channel_id=1, source_target_pairs={{0,1},{1,0},{2,4},{3,5},{4,2},{5,3},{6,7},{7,6},{8,9},{9,8},{10,12... | collective-permute-start | bytes 73736 | tf_op jit(solution)/shard_map/ppermute | solution.py:414
  11.4 12.1 %copy-start.1 = (f32[5,8,8,128]{3,2,1,0:T(8,128)S(1)}, f32[5,8,8,128]{3,2,1,0:T(8,128)}, u32[]{:S(2)}) copy-start(f32[5,8,8,128]{3,2,1,0:T(8,128)} %adjoint.5) | copy-start | bytes 491524
  11.4 12.1 %copy-start.3 = (f32[3,8,8,128]{3,2,1,0:T(8,128)S(1)}, f32[3,8,8,128]{3,2,1,0:T(8,128)}, u32[]{:S(2)}) copy-start(f32[3,8,8,128]{3,2,1,0:T(8,128)} %velocity.5) | copy-start | bytes 294916
  11.4 3.6 %collective-permute-start.4 = (f32[8,128]{1,0:T(8,128)S(1)}, f32[8,128]{1,0:T(8,128)S(1)}, u32[]{:S(2)}, u32[]{:S(2)}) collective-permute-start(f32[8,128]{1,0:T(8,128)S(1)} %get-tuple-element.24), channel_id=1, source_target_pairs={{0,1},{1,0},{2,3},{3,2},{4,5},{5,4},{6,7},{7,6},{8,9},{9,8},{10,11... | collective-permute-start | bytes 12296 | tf_op jit(solution)/shard_map/ppermute | solution.py:414
  15.1 8.4 %copy-start.5 = (f32[8,8,128]{2,1,0:T(8,128)S(1)}, f32[8,8,128]{2,1,0:T(8,128)}, u32[]{:S(2)}) copy-start(f32[8,8,128]{2,1,0:T(8,128)} %density.5) | copy-start | bytes 98308
  15.1 8.4 %copy-start.7 = (f32[8,8,128]{2,1,0:T(8,128)S(1)}, f32[8,8,128]{2,1,0:T(8,128)}, u32[]{:S(2)}) copy-start(f32[8,8,128]{2,1,0:T(8,128)} %stiffness.5) | copy-start | bytes 98308
  15.1 8.4 %copy-start.10 = (f32[8,8,128]{2,1,0:T(8,128)S(1)}, f32[8,8,128]{2,1,0:T(8,128)}, u32[]{:S(2)}) copy-start(f32[8,8,128]{2,1,0:T(8,128)} %source.3) | copy-start | bytes 98308
  16.1 5.3 %copy-start.12 = (s32[4,4,2]{1,2,0:T(2,128)S(1)}, s32[4,4,2]{1,2,0:T(2,128)}, u32[]{:S(2)}) copy-start(s32[4,4,2]{1,2,0:T(2,128)} %param.16) | copy-start | bytes 388
  16.2 7.3 %collective-permute-start.5 = (f32[5,8,128]{2,1,0:T(8,128)S(1)}, f32[5,8,128]{2,1,0:T(8,128)S(1)}, u32[]{:S(2)}, u32[]{:S(2)}) collective-permute-start(f32[5,8,128]{2,1,0:T(8,128)S(1)} %get-tuple-element.26), channel_id=1, source_target_pairs={{0,8},{1,9},{2,10},{3,11},{4,12},{5,13},{6,14},{7,15},{8,0},{9,1},... | collective-permute-start | bytes 61448 | tf_op jit(solution)/shard_map/ppermute | solution.py:414
  18.9 4.6 %collective-permute-start.6 = (f32[5,8,128]{2,1,0:T(8,128)S(1)}, f32[5,8,128]{2,1,0:T(8,128)S(1)}, u32[]{:S(2)}, u32[]{:S(2)}) collective-permute-start(f32[5,8,128]{2,1,0:T(8,128)S(1)} %get-tuple-element.27), channel_id=1, source_target_pairs={{0,2},{1,3},{2,0},{3,1},{4,6},{5,7},{6,4},{7,5},{8,16},{9,17},{10,... | collective-permute-start | bytes 61448 | tf_op jit(solution)/shard_map/ppermute | solution.py:414
  18.9 4.6 %collective-permute-start.7 = (f32[5,8,128]{2,1,0:T(8,128)S(1)}, f32[5,8,128]{2,1,0:T(8,128)S(1)}, u32[]{:S(2)}, u32[]{:S(2)}) collective-permute-start(f32[5,8,128]{2,1,0:T(8,128)S(1)} %get-tuple-element.28), channel_id=1, source_target_pairs={{0,2},{1,3},{2,0},{3,1},{4,6},{5,7},{6,4},{7,5},{8,10},{9,11},{10,... | collective-permute-start | bytes 61448 | tf_op jit(solution)/shard_map/ppermute | solution.py:414
  19.4 4.1 %collective-permute-start.8 = (f32[5,8,128]{2,1,0:T(8,128)S(1)}, f32[5,8,128]{2,1,0:T(8,128)S(1)}, u32[]{:S(2)}, u32[]{:S(2)}) collective-permute-start(f32[5,8,128]{2,1,0:T(8,128)S(1)} %get-tuple-element.29), channel_id=1, source_target_pairs={{0,1},{1,0},{2,4},{3,5},{4,2},{5,3},{6,7},{7,6},{8,9},{9,8},{10,12... | collective-permute-start | bytes 61448 | tf_op jit(solution)/shard_map/ppermute | solution.py:414
  19.9 3.6 %collective-permute-start.9 = (f32[8,128]{1,0:T(8,128)S(1)}, f32[8,128]{1,0:T(8,128)S(1)}, u32[]{:S(2)}, u32[]{:S(2)}) collective-permute-start(f32[8,128]{1,0:T(8,128)S(1)} %get-tuple-element.30), channel_id=1, source_target_pairs={{0,1},{1,0},{2,3},{3,2},{4,5},{5,4},{6,7},{7,6},{8,9},{9,8},{10,11... | collective-permute-start | bytes 12296 | tf_op jit(solution)/shard_map/ppermute | solution.py:414
  21.5 2.0 %copy-start.11 = (s32[32]{0:T(128)S(1)}, s32[32]{0:T(128)}, u32[]{:S(2)}) copy-start(s32[32]{0:T(128)} %owners.1) | copy-start | bytes 388
  25.8 9.9 %all-to-all-start = ((f32[32,1,128]{2,1,0:T(1,128)}), f32[32,1,128]{2,1,0:T(1,128)S(1)}, u32[]{:S(2)}, u32[]{:S(2)}) async-start(f32[32,1,128]{2,1,0:T(1,128)} %bitcast.1), calls=%async_computation | async-start | bytes 32768 | tf_op jit(solution)/shard_map/all_to_all | solution.py:441
  28.3 7.4 %collective-permute-start.10 = (f32[5,8,128]{2,1,0:T(8,128)S(1)}, f32[5,8,128]{2,1,0:T(8,128)S(1)}, u32[]{:S(2)}, u32[]{:S(2)}) collective-permute-start(f32[5,8,128]{2,1,0:T(8,128)S(1)} %get-tuple-element.33), channel_id=1, source_target_pairs={{0,8},{1,9},{2,10},{3,11},{4,12},{5,13},{6,14},{7,15},{8,0},{9,1},... | collective-permute-start | bytes 61448 | tf_op jit(solution)/shard_map/ppermute | solution.py:414
  30.1 5.6 %collective-permute-start.11 = (f32[5,8,128]{2,1,0:T(8,128)S(1)}, f32[5,8,128]{2,1,0:T(8,128)S(1)}, u32[]{:S(2)}, u32[]{:S(2)}) collective-permute-start(f32[5,8,128]{2,1,0:T(8,128)S(1)} %get-tuple-element.34), channel_id=1, source_target_pairs={{0,2},{1,3},{2,0},{3,1},{4,6},{5,7},{6,4},{7,5},{8,16},{9,17},{10,... | collective-permute-start | bytes 61448 | tf_op jit(solution)/shard_map/ppermute | solution.py:414
  30.1 5.6 %collective-permute-start.12 = (f32[5,8,128]{2,1,0:T(8,128)S(1)}, f32[5,8,128]{2,1,0:T(8,128)S(1)}, u32[]{:S(2)}, u32[]{:S(2)}) collective-permute-start(f32[5,8,128]{2,1,0:T(8,128)S(1)} %get-tuple-element.35), channel_id=1, source_target_pairs={{0,2},{1,3},{2,0},{3,1},{4,6},{5,7},{6,4},{7,5},{8,10},{9,11},{10,... | collective-permute-start | bytes 61448 | tf_op jit(solution)/shard_map/ppermute | solution.py:414
  30.6 5.1 %collective-permute-start.13 = (f32[5,8,128]{2,1,0:T(8,128)S(1)}, f32[5,8,128]{2,1,0:T(8,128)S(1)}, u32[]{:S(2)}, u32[]{:S(2)}) collective-permute-start(f32[5,8,128]{2,1,0:T(8,128)S(1)} %get-tuple-element.36), channel_id=1, source_target_pairs={{0,1},{1,0},{2,4},{3,5},{4,2},{5,3},{6,7},{7,6},{8,9},{9,8},{10,12... | collective-permute-start | bytes 61448 | tf_op jit(solution)/shard_map/ppermute | solution.py:414
  32.1 3.6 %collective-permute-start.14 = (f32[8,128]{1,0:T(8,128)S(1)}, f32[8,128]{1,0:T(8,128)S(1)}, u32[]{:S(2)}, u32[]{:S(2)}) collective-permute-start(f32[8,128]{1,0:T(8,128)S(1)} %get-tuple-element.37), channel_id=1, source_target_pairs={{0,1},{1,0},{2,3},{3,2},{4,5},{5,4},{6,7},{7,6},{8,9},{9,8},{10,11... | collective-permute-start | bytes 12296 | tf_op jit(solution)/shard_map/ppermute | solution.py:414
  (5 other events, 4.1 us)

commit v4 on v2

v4 whole, which is shorter than its diff:
```python
import functools

import jax
import jax.numpy as jnp
from jax import lax
from jax.experimental import pallas as pl
from jax.experimental.pallas import tpu as pltpu
from jax.sharding import PartitionSpec as P

CX = 8
CY = 8
CZ = 128
BZ = 16
BOXES = CZ // BZ
ROWS = CX * CY

AXES = ("gx", "gy", "gz")

step_length = 0.14
third = 1.0 / 3.0
two_thirds = 2.0 / 3.0

TILE = (CY, CZ)
FLAT = (ROWS, CZ)
STATE = (5,) + FLAT


def pairings(sizes, axis, near_axis):
    size = sizes[axis]
    first, second = [], []
    for x in range(sizes[0]):
        for y in range(sizes[1]):
            for z in range(sizes[2]):
                here = [x, y, z]
                index = (x * sizes[1] + y) * sizes[2] + z
                place = here[axis]
                other = list(here)
                other[axis] = place ^ 1
                first.append((index, (other[0] * sizes[1] + other[1]) * sizes[2] + other[2]))
                other = list(here)
                if 0 < place < size - 1 or near_axis == axis:
                    other[axis] = (place + (1 if place % 2 else -1)) % size
                else:
                    other[near_axis] = here[near_axis] ^ 1
                second.append((index, (other[0] * sizes[1] + other[1]) * sizes[2] + other[2]))
    return first, second if size > 2 else None


def positions():
    return [lax.axis_index(axis) for axis in AXES]


def tile_at(x):
    return slice(x * CY, (x + 1) * CY)


def row_at(y):
    return pl.ds(y, CX, stride=CY)


def partials_of(adjoint, speed, density, stiffness, inverse, direction):
    components = [speed * component for component in adjoint]
    row = 1 + direction
    components[row] = components[row] + (density * adjoint[0] + stiffness * adjoint[4])
    components[4] = components[4] + adjoint[row] * inverse
    return components


def faces_at(state, scaled, rows, direction):
    adjoint = [state[component, rows, :] for component in range(5)]
    return partials_of(
        adjoint,
        scaled[direction, rows, :],
        scaled[3, rows, :],
        scaled[4, rows, :],
        scaled[5, rows, :],
        direction,
    )


def pack_lanes(fields):
    lanes = lax.broadcasted_iota(jnp.int32, TILE, 1) // 2
    packed = jnp.zeros(TILE, jnp.float32)
    for index, field in enumerate(fields):
        for x in range(CX):
            k = index * CX + x
            packed = jnp.where(lanes == k, pltpu.roll(field[x], (2 * k + 1) % CZ, 1), packed)
    return packed


def put_pair(low, high, position, outs):
    even = position % 2 == 0
    for index, (below, above) in enumerate(zip(low, high)):
        outs[0][index] = jnp.where(even, above, below)
        if outs[1] is not None:
            outs[1][index] = jnp.where(even, below, above)


def put_messages(state, scaled, source, outs):
    here = positions()
    x_low = faces_at(state, scaled, tile_at(0), 0)
    x_high = faces_at(state, scaled, tile_at(CX - 1), 0)
    y_low = faces_at(state, scaled, row_at(0), 1)
    y_high = faces_at(state, scaled, row_at(CY - 1), 1)
    z_tiles = [faces_at(state, scaled, tile_at(x), 2) for x in range(CX)]
    z_fields = [[z_tiles[x][component] for x in range(CX)] for component in range(5)]
    if source is None:
        extra = [[]] * 4
    else:
        rows = (tile_at(0), tile_at(CX - 1), row_at(0), row_at(CY - 1))
        extra = [[source[row, :]] for row in rows]
        z_fields.append([source[tile_at(x), :] for x in range(CX)])
    put_pair(x_low + extra[0], x_high + extra[1], here[0], outs[0])
    put_pair(y_low + extra[2], y_high + extra[3], here[1], outs[1])
    packed = pack_lanes(z_fields)
    outs[2][0][...] = packed
    return x_low, x_high, y_low, y_high, packed


def sort_pair(first, second, position, size):
    even = position % 2 == 0
    zero = jnp.zeros_like(first)
    if second is None:
        return jnp.where(even, zero, first), jnp.where(even, first, zero)
    below = jnp.where(position == 0, zero, jnp.where(even, second, first))
    above = jnp.where(position == size - 1, zero, jnp.where(even, first, second))
    return below, above


def sorted_field(refs, index, position, size):
    first, second = refs
    return sort_pair(first[index], None if second is None else second[index], position, size)


def sorted_lanes(refs, position, size):
    first, second = refs
    return sort_pair(first[...], None if second is None else second[...], position, size)


def add_halo(base, received, weight, sizes, out):
    here = positions()
    lanes = lax.broadcasted_iota(jnp.int32, TILE, 1)
    edges = (lanes == 0) | (lanes == CZ - 1)
    z_below, z_above = sorted_lanes(received[2], here[2], sizes[2])
    z_halo = weight * jnp.where(
        lanes % 2 == 0, pltpu.roll(z_above, CZ - 1, 1), -pltpu.roll(z_below, 1, 1)
    )
    for component in range(5):
        x_below, x_above = sorted_field(received[0], component, here[0], sizes[0])
        y_below, y_above = sorted_field(received[1], component, here[1], sizes[1])
        for x in range(CX):
            k = component * CX + x
            value = base[component, tile_at(x), :]
            value = value + jnp.where(edges, pltpu.roll(z_halo, (CZ - 1 - 2 * k) % CZ, 1), 0.0)
            if x == 0:
                value = value - weight * x_below
            if x == CX - 1:
                value = value + weight * x_above
            out[component, tile_at(x), :] = value
        out[component, row_at(0), :] = out[component, row_at(0), :] - weight * y_below
        out[component, row_at(CY - 1), :] = out[component, row_at(CY - 1), :] + weight * y_above


ORDER = ((1, 0), (2, 0), (0, 1), (0, 0), (1, 1), (2, 1))


def message_keys(sizes, sent):
    keys = [key for key in ORDER if key[1] == 0 or sizes[key[0]] > 2]
    return [key for key in keys if not (sent and key == (2, 1))]


def split(refs, sizes, sent=False):
    refs, out = list(refs), [[None, None] for axis in range(3)]
    for axis, which in message_keys(sizes, sent):
        out[axis][which] = refs.pop(0)
    return out, refs


def first_kernel(sizes, level, adjoint, density, velocity, stiffness, source, scaled, *refs):
    outs, scratch = split(refs, sizes, True)
    adjoint_now, density_now, velocity_now, stiffness_now, source_now, arrived = scratch
    pairs = (
        (density, density_now),
        (velocity, velocity_now),
        (stiffness, stiffness_now),
        (adjoint, adjoint_now),
        (source, source_now),
    )
    copies = [
        pltpu.make_async_copy(there, here, arrived.at[index])
        for index, (there, here) in enumerate(pairs)
    ]
    for copy in copies:
        copy.start()
    here = positions()
    own_level = level[here[0], here[2], here[1]]
    half_inverse = 0.5 * lax.shift_left(jnp.int32(1), own_level).astype(jnp.float32)
    for copy in copies:
        copy.wait()
    for direction in range(3):
        scaled[direction] = half_inverse * velocity_now[direction]
    scaled[3] = half_inverse * density_now[...]
    scaled[4] = half_inverse * stiffness_now[...]
    scaled[5] = half_inverse / density_now[...]
    put_messages(adjoint_now, scaled, source_now, outs)


def own_kernel(weights, scaled, sponge, *refs):
    keep, blend = weights
    start, state, out = refs if keep else (None,) + refs
    rows = lax.broadcasted_iota(jnp.int32, TILE, 0)
    lanes = lax.broadcasted_iota(jnp.int32, TILE, 1)
    tiles = [
        [faces_at(state, scaled, tile_at(x), direction) for direction in range(3)]
        for x in range(CX)
    ]
    for x in range(CX):
        damp = sponge[tile_at(x), :]
        for component in range(5):
            total = None
            if x < CX - 1:
                total = tiles[x + 1][0][component]
            if x > 0:
                before = tiles[x - 1][0][component]
                total = -before if total is None else total - before
            part = tiles[x][1][component]
            total = total + jnp.where(rows == CY - 1, 0.0, pltpu.roll(part, CY - 1, 0))
            total = total - jnp.where(rows == 0, 0.0, pltpu.roll(part, 1, 0))
            part = tiles[x][2][component]
            total = total + jnp.where(lanes == CZ - 1, 0.0, pltpu.roll(part, CZ - 1, 1))
            total = total - jnp.where(lanes == 0, 0.0, pltpu.roll(part, 1, 1))
            value = state[component, tile_at(x), :]
            value = blend * (value + step_length * (total - damp * value))
            if keep:
                value = value + keep * start[component, tile_at(x), :]
            out[component, tile_at(x), :] = value


def shape_kernel(source, scaled, sponge, start, shapes, sums):
    rows = lax.broadcasted_iota(jnp.int32, TILE, 0)
    lanes = lax.broadcasted_iota(jnp.int32, TILE, 1)
    outer = step_length * two_thirds
    inner = outer * step_length
    totals = [None] * 5
    for x in range(CX):
        at = tile_at(x)
        shape = source[at, :]
        along_x = jnp.zeros(TILE, jnp.float32)
        if x > 0:
            along_x = along_x + source[tile_at(x - 1), :]
        if x < CX - 1:
            along_x = along_x - source[tile_at(x + 1), :]
        along_y = jnp.where(rows == 0, 0.0, pltpu.roll(shape, 1, 0)) - jnp.where(
            rows == CY - 1, 0.0, pltpu.roll(shape, CY - 1, 0)
        )
        before = inner * jnp.where(lanes == 0, 0.0, pltpu.roll(shape, 1, 1))
        after = inner * jnp.where(lanes == CZ - 1, 0.0, pltpu.roll(shape, CZ - 1, 1))
        along_x, along_y = inner * along_x, inner * along_y
        own = outer * shape * (1.0 - step_length * sponge[at, :])
        own = own + scaled[0, at, :] * along_x + scaled[1, at, :] * along_y
        for index, value in enumerate(
            (own, scaled[2, at, :] * before, scaled[2, at, :] * after, along_x, along_y, before, after)
        ):
            shapes[index, at, :] = value
        weighted = (step_length * third) * shape
        for component in range(5):
            value = weighted * start[component, at, :]
            totals[component] = value if totals[component] is None else totals[component] + value
    for component in range(5):
        sums[component] = totals[component]


def stage_kernel(sizes, weight, base, scaled, *refs):
    received, (section, *outs) = split(refs, sizes)
    add_halo(base, received, weight, sizes, section)
    put_messages(section, scaled, None, split(outs, sizes, True)[0])


def merge_rows(tiles):
    sublanes = lax.broadcasted_iota(jnp.int32, TILE, 0)
    zero = jnp.zeros(TILE, jnp.float32)
    tiles = list(tiles) + [None] * (CY - len(tiles))
    for width in (4, 2, 1):
        upper = (sublanes & width) != 0
        merged = []
        for index in range(width):
            low, high = tiles[index], tiles[index + width]
            low = zero if low is None else low + pltpu.roll(low, CY - width, 0)
            high = zero if high is None else high + pltpu.roll(high, width, 0)
            merged.append(jnp.where(upper, high, low))
        tiles = merged
    return tiles[0]


def target_kernel(sizes, patches, owners, out):
    here = positions()
    sublanes = lax.broadcasted_iota(jnp.int32, TILE, 0)
    result = jnp.zeros(TILE, jnp.int32)
    for index, offset in enumerate(OFFSETS):
        place = [
            jnp.clip(here[axis] + offset[axis], 0, sizes[axis] - 1) for axis in range(3)
        ]
        target = owners[patches[place[0], place[2], place[1]]]
        result = jnp.where(sublanes == index, target, result)
    out[...] = result


OFFSETS = (
    (0, 0, 0),
    (1, 0, 0),
    (-1, 0, 0),
    (0, 1, 0),
    (0, -1, 0),
    (0, 0, 1),
    (0, 0, -1),
)


def gradient_kernel(sizes, weight, base, scaled, shapes, sums, targets, *refs):
    received, rest = split(refs, sizes)
    sources, (section, table, *outs) = split(rest, sizes)
    here = positions()
    add_halo(base, received, weight, sizes, section)
    x_low, x_high, y_low, y_high, packed = put_messages(
        section, scaled, None, split(outs, sizes, True)[0]
    )
    main = [sums[component] for component in range(5)]
    before = [None] * 5
    after = [None] * 5

    def accumulate(totals, component, value):
        old = totals[component]
        totals[component] = value if old is None else old + value

    for x in range(CX):
        at = tile_at(x)
        state = [section[component, at, :] for component in range(5)]
        own, lane_before, lane_after, along_x, along_y, shape_before, shape_after = (
            shapes[index, at, :] for index in range(7)
        )
        push = scaled[3, at, :] * state[0] + scaled[4, at, :] * state[4]
        drawn = [scaled[5, at, :] * state[1 + direction] for direction in range(3)]
        for component in range(5):
            accumulate(main, component, own * state[component])
            accumulate(before, component, lane_before * state[component])
            accumulate(after, component, lane_after * state[component])
        accumulate(main, 1, along_x * push)
        accumulate(main, 2, along_y * push)
        accumulate(before, 3, shape_before * push)
        accumulate(after, 3, shape_after * push)
        accumulate(main, 4, along_x * drawn[0] + along_y * drawn[1])
        accumulate(before, 4, shape_before * drawn[2])
        accumulate(after, 4, shape_after * drawn[2])
    own_tiles = [
        main[f] + pltpu.roll(before[f], CZ - 1, 1) - pltpu.roll(after[f], 1, 1) for f in range(5)
    ]
    lanes = lax.broadcasted_iota(jnp.int32, TILE, 1)
    outer = step_length * two_thirds * step_length
    x_below, x_above = sorted_field(sources[0], 5, here[0], sizes[0])
    y_below, y_above = sorted_field(sources[1], 5, here[1], sizes[1])
    z_below, z_above = sorted_lanes(sources[2], here[2], sizes[2])
    aligned_above = jnp.zeros(TILE, jnp.float32)
    aligned_below = jnp.zeros(TILE, jnp.float32)
    for component in range(5):
        group = lanes // (2 * CX) == component
        shift = 2 * CX * (component - 5)
        aligned_above = jnp.where(
            group & (lanes % 2 == 0), pltpu.roll(z_above, (shift - 1) % CZ, 1), aligned_above
        )
        aligned_below = jnp.where(
            group & (lanes % 2 == 1), pltpu.roll(z_below, (shift + 1) % CZ, 1), aligned_below
        )
    above = -outer * aligned_above * packed
    below = outer * aligned_below * packed
    last = CZ - BZ
    contributions = [
        own_tiles,
        [(-outer * x_above) * x_high[f] for f in range(5)],
        [(outer * x_below) * x_low[f] for f in range(5)],
        [(-outer * y_above) * y_high[f] for f in range(5)],
        [(outer * y_below) * y_low[f] for f in range(5)],
        [jnp.where(lanes < BZ, pltpu.roll(above, (-BZ * f) % CZ, 1), 0.0) for f in range(5)],
        [jnp.where(lanes >= last, pltpu.roll(below, (last - BZ * f) % CZ, 1), 0.0) for f in range(5)],
    ]
    merged = [merge_rows(tiles) for tiles in contributions]
    aims = [jnp.broadcast_to(targets[j : j + 1, :], TILE) for j in range(len(OFFSETS))]

    def fill(device):
        total = None
        for tile, aim in zip(merged, aims):
            part = jnp.where(aim == device, tile, 0.0)
            total = part if total is None else total + part
        table[device] = total

    devices = table.shape[0]
    if devices <= 64:
        for device in range(devices):
            fill(device)
    else:
        lax.fori_loop(0, devices, lambda device, carry: (fill(device), carry)[1], 0)


def last_kernel(sizes, base, table, *refs):
    received, (out, gradient, done, sent) = split(refs, sizes)
    add_halo(base, received, two_thirds * step_length, sizes, done)
    copy = pltpu.make_async_copy(done, out, sent)
    copy.start()
    devices = table.shape[0]
    total = table[0]
    if devices <= 64:
        for device in range(1, devices):
            total = total + table[device]
    else:
        total = lax.fori_loop(1, devices, lambda device, old: old + table[device], total)
    for shift in (1, 2, 4, 8):
        total = total + pltpu.roll(total, CZ - shift, 1)
    sublanes = lax.broadcasted_iota(jnp.int32, TILE, 0)
    lanes = lax.broadcasted_iota(jnp.int32, TILE, 1)
    result = jnp.zeros(TILE, jnp.float32)
    total = pltpu.roll(total, 0, 1, stride=BOXES, stride_axis=0)
    for box in range(BOXES):
        moved = pltpu.roll(total, (box - BZ * box) % CZ, 1)
        result = jnp.where(lanes == BOXES * sublanes + box, moved, result)
    for shift in (4, 2, 1):
        result = result + pltpu.roll(result, shift, 0)
    gradient[...] = result[0:1, : 5 * BOXES]
    copy.wait()


VMEM = pl.BlockSpec(memory_space=pltpu.VMEM)
SMEM = pl.BlockSpec(memory_space=pltpu.SMEM)
HBM = pl.BlockSpec(memory_space=pltpu.HBM)


def call(
    kernel, in_specs, operands, out_shapes, out_specs=None, scratch=(), dtype=jnp.float32, vmem=16
):
    return pl.pallas_call(
        kernel,
        out_shape=[jax.ShapeDtypeStruct(shape, dtype) for shape in out_shapes],
        in_specs=in_specs,
        out_specs=out_specs or [VMEM] * len(out_shapes),
        scratch_shapes=list(scratch),
        compiler_params=pltpu.CompilerParams(vmem_limit_bytes=vmem * 1024 * 1024),
        cost_estimate=pl.CostEstimate(flops=2000000, bytes_accessed=1000000, transcendentals=0),
    )(*operands)


def body(
    terminal_adjoint,
    density,
    velocity,
    stiffness,
    sponge,
    source_shape,
    brick_level,
    brick_patch,
    patch_owner,
):
    sizes = tuple(lax.axis_size(axis) for axis in AXES)
    permutations = (
        pairings(sizes, 0, 1),
        pairings(sizes, 1, 1),
        pairings(sizes, 2, 1),
    )
    devices = patch_owner.shape[0]
    state_shape = terminal_adjoint.shape
    start = terminal_adjoint.reshape(STATE)
    density, stiffness, sponge, source = (
        array.reshape(FLAT) for array in (density, stiffness, sponge, source_shape)
    )
    velocity = velocity.reshape((3,) + FLAT)
    level = jnp.transpose(brick_level, (0, 2, 1))
    patches = jnp.transpose(brick_patch, (0, 2, 1))

    def message_shapes(fields):
        return [
            TILE if key[0] == 2 else (fields,) + TILE for key in message_keys(sizes, True)
        ]

    def exchange(messages):
        sends = dict(zip(message_keys(sizes, True), messages))
        sends[2, 1] = sends[2, 0]
        return [
            lax.ppermute(sends[key], AXES, permutations[key[0]][key[1]])
            for key in message_keys(sizes, False)
        ]

    scaled, *sent = call(
        functools.partial(first_kernel, sizes),
        [SMEM] + [HBM] * 5,
        (level, start, density, velocity, stiffness, source),
        [(6,) + FLAT] + message_shapes(6),
        scratch=[
            pltpu.VMEM(STATE, jnp.float32),
            pltpu.VMEM(FLAT, jnp.float32),
            pltpu.VMEM((3,) + FLAT, jnp.float32),
            pltpu.VMEM(FLAT, jnp.float32),
            pltpu.VMEM(FLAT, jnp.float32),
            pltpu.SemaphoreType.DMA((5,)),
        ],
        vmem=60,
    )
    received_one = exchange(sent)
    (targets,) = call(
        functools.partial(target_kernel, sizes),
        [SMEM] * 2,
        (patches, patch_owner),
        [TILE],
        dtype=jnp.int32,
    )
    (base,) = call(
        functools.partial(own_kernel, (0.0, 1.0)), [VMEM] * 3, (scaled, sponge, start), [STATE]
    )
    operands = (base, scaled, *received_one)
    section, *sent = call(
        functools.partial(stage_kernel, sizes, step_length),
        [VMEM] * len(operands),
        operands,
        [STATE] + message_shapes(5),
    )
    received = exchange(sent)
    (base,) = call(
        functools.partial(own_kernel, (0.75, 0.25)),
        [VMEM] * 4,
        (scaled, sponge, start, section),
        [STATE],
    )
    shapes, sums = call(
        shape_kernel, [VMEM] * 4, (source, scaled, sponge, start), [(7,) + FLAT, (5,) + TILE]
    )
    operands = (base, scaled, shapes, sums, targets, *received, *received_one)
    section, table, *sent = call(
        functools.partial(gradient_kernel, sizes, 0.25 * step_length),
        [VMEM] * len(operands),
        operands,
        [STATE, (devices,) + TILE] + message_shapes(5),
    )
    table = lax.all_to_all(table, AXES, 0, 0, tiled=True)
    received = exchange(sent)
    (base,) = call(
        functools.partial(own_kernel, (third, two_thirds)),
        [VMEM] * 4,
        (scaled, sponge, start, section),
        [STATE],
    )
    operands = (base, table, *received)
    adjoint, gradient = call(
        functools.partial(last_kernel, sizes),
        [VMEM] * len(operands),
        operands,
        [STATE, (1, 5 * BOXES)],
        [HBM, VMEM],
        [pltpu.VMEM(STATE, jnp.float32), pltpu.SemaphoreType.DMA],
    )
    return adjoint.reshape(state_shape), gradient


def solution(mesh):
    in_specs = (
        P(None, "gx", "gy", "gz"),
        P("gx", "gy", "gz"),
        P(None, "gx", "gy", "gz"),
        P("gx", "gy", "gz"),
        P("gx", "gy", "gz"),
        P("gx", "gy", "gz"),
        P(),
        P(),
        P(),
    )
    out_specs = (P(None, "gx", "gy", "gz"), P(("gx", "gy", "gz"), None))
    return jax.shard_map(body, mesh=mesh, in_specs=in_specs, out_specs=out_specs, check_vma=False)
```

time: 43.3 us -> 34.1 us (0.79)
  blocking collectives: 11.5 us -> 0 us
  other arithmetic: 7.35 us -> 0 us
  Pallas kernels: 0 us -> 6.9 us
  starting transfers between devices: 15.5 us -> 20.2 us
  local copies, waits for them, and re-layouts: 2.77 us -> 1.59 us
  between operations: 1.93 us -> 0.79 us
  waiting for transfers between devices: 3.78 us -> 4.34 us
    all_to_all x1 -> x0, blocking collectives: 11.5 us -> none  [body(): incoming = lax.all_to_all(outgoing, AXES, 0, 0, tiled=True)]
    pallas_call x0 -> x9, Pallas kernels: none -> 6.9 us  [call(): pl.pallas_call(kernel, out_shape=[jax.ShapeDtypeStruct(shape, dtype) for...]
    reduce_sum x5 -> x0, other arithmetic: 3.49 us -> none  [the longest x1 1.28 us: body(): jnp.sum(jnp.where(jnp.arange(devices) == own_patch, patch_owner, 0))]
    all_to_all x0 -> x1, starting transfers between devices: none -> 3.42 us  [body(): table = lax.all_to_all(table, AXES, 0, 0, tiled=True)]
    unnamed x21 -> x0, other arithmetic: 1.81 us -> none
    ppermute x15, starting transfers between devices: 15.5 us -> 16.8 us  [exchange(): lax.ppermute(sends[key], AXES, permutations[key[0]][key[1]])]
    unnamed x18 -> x16, local copies, waits for them, and re-layouts: 2.62 us -> 1.59 us
    all_to_all x0 -> x1, waiting for transfers between devices: none -> 0.89 us  [body(): table = lax.all_to_all(table, AXES, 0, 0, tiled=True)]
  transfers between devices with their start and end apart: 15 -> 16, of which waited for: 5 -> 4; matrix products, arithmetic and copies ran while one was open for 5% -> 0% of each run, Pallas kernels for 0% -> 4%
where the time goes in v4:
time: 34.1 us; the launch traced here: 33.8 us
  starting transfers between devices  20.2 us (59%)
  Pallas kernels  6.9 us (20%)
  waiting for transfers between devices  4.34 us (13%)
  local copies, waits for them, and re-layouts  1.59 us (5%)
  between operations  0.79 us (2%)
    ppermute x15, starting transfers between devices, exchange(): lax.ppermute(sends[key], AXES, permutations[key[0]][key[1]])  16.8 us
    pallas_call x9, Pallas kernels, call(): pl.pallas_call(kernel, out_shape=[jax.ShapeDtypeStruct(shape, dtype) for...  6.9 us
    ppermute x15, waiting for transfers between devices, exchange(): lax.ppermute(sends[key], AXES, permutations[key[0]][key[1]])  3.45 us
    all_to_all x1, starting transfers between devices, body(): table = lax.all_to_all(table, AXES, 0, 0, tiled=True)  3.42 us
    unnamed x16, local copies, waits for them, and re-layouts  1.59 us
    all_to_all x1, waiting for transfers between devices, body(): table = lax.all_to_all(table, AXES, 0, 0, tiled=True)  0.89 us
  transfers between devices with their start and end apart: 16, of which 4 were waited for; matrix products, arithmetic and copies ran while one was open for 0% of the time, Pallas kernels for 4%

profile of v4, /device:TPU:0, one launch (start us, length us, event | category | flops | bytes accessed | tf_op | source)
XLA Modules:
  0.0 33.8 jit_solution(5467631822768638059)
XLA Ops:
  0.7 2.6 %shard_map.104 = (f32[6,64,128]{2,1,0:T(8,128)}, f32[6,8,128]{2,1,0:T(8,128)}, f32[8,128]{1,0:T(8,128)}, f32[6,8,128]{2,1,0:T(8,128)}, f32[6,8,128]{2,1,0:T(8,128)}, /*index=5*/f32[6,8,128]{2,1,0:T(8,128)}) custom-call(s32[4,2,4]{2,1,0:T(2,128)} %bitcast.24, f32[5,64,128]{2,1,0:T(8,128)} %bitcast.9, f32[64,128]{1,0:T(8,128)} %bitcast.22, ...), custom_call_target="tpu_custom_call" | custom-call | flops 2000000 | bytes 1000000 | tf_op jit(solution)/shard_map/pallas_call | solution.py:438
  3.3 0.5 %collective-permute-start = (f32[6,8,128]{2,1,0:T(8,128)}, f32[6,8,128]{2,1,0:T(8,128)S(1)}, u32[]{:S(2)}, u32[]{:S(2)}) collective-permute-start(f32[6,8,128]{2,1,0:T(8,128)} %get-tuple-element.26), channel_id=1, source_target_pairs={{0,2},{1,3},{2,0},{3,1},{4,6},{5,7},{6,4},{7,5},{8,10},{9,11},{10,... | collective-permute-start | bytes 73736 | tf_op jit(solution)/shard_map/ppermute | solution.py:485
  3.9 4.1 %collective-permute-start.3 = (f32[6,8,128]{2,1,0:T(8,128)}, f32[6,8,128]{2,1,0:T(8,128)S(1)}, u32[]{:S(2)}, u32[]{:S(2)}) collective-permute-start(f32[6,8,128]{2,1,0:T(8,128)} %get-tuple-element.29), channel_id=1, source_target_pairs={{0,8},{1,9},{2,10},{3,11},{4,12},{5,13},{6,14},{7,15},{8,0},{9,1},... | collective-permute-start | bytes 73736 | tf_op jit(solution)/shard_map/ppermute | solution.py:485
  8.1 1.0 %collective-permute-start.4 = (f32[6,8,128]{2,1,0:T(8,128)}, f32[6,8,128]{2,1,0:T(8,128)S(1)}, u32[]{:S(2)}, u32[]{:S(2)}) collective-permute-start(f32[6,8,128]{2,1,0:T(8,128)} %get-tuple-element.30), channel_id=1, source_target_pairs={{0,6},{1,7},{2,4},{3,5},{4,2},{5,3},{6,0},{7,1},{8,14},{9,15},{10,... | collective-permute-start | bytes 73736 | tf_op jit(solution)/shard_map/ppermute | solution.py:485
  9.0 1.5 %collective-permute-start.1 = (f32[8,128]{1,0:T(8,128)S(1)}, f32[8,128]{1,0:T(8,128)S(1)}, u32[]{:S(2)}, u32[]{:S(2)}) collective-permute-start(f32[8,128]{1,0:T(8,128)S(1)} %copy-done.7), channel_id=1, source_target_pairs={{0,1},{1,0},{2,3},{3,2},{4,5},{5,4},{6,7},{7,6},{8,9},{9,8},{10,11... | collective-permute-start | bytes 12296 | tf_op jit(solution)/shard_map/ppermute | solution.py:485
  10.6 0.9 %copy-done = f32[6,64,128]{2,1,0:T(8,128)S(1)} copy-done((f32[6,64,128]{2,1,0:T(8,128)S(1)}, f32[6,64,128]{2,1,0:T(8,128)}, u32[]{:S(2)}) %copy-start) | copy-done | bytes 196632
  11.7 1.0 %collective-permute-done.1.refs_1_.refs_6_ = f32[8,128]{1,0:T(8,128)S(1)} collective-permute-done((f32[8,128]{1,0:T(8,128)S(1)}, f32[8,128]{1,0:T(8,128)S(1)}, u32[]{:S(2)}, u32[]{:S(2)}) %collective-permute-start.1) | collective-permute-done | bytes 4128 | tf_op jit(solution)/shard_map/ppermute | solution.py:485
  12.7 0.3 shard_map.106
  13.1 0.4 %collective-permute-start.7 = (f32[5,8,128]{2,1,0:T(8,128)S(1)}, f32[5,8,128]{2,1,0:T(8,128)S(1)}, u32[]{:S(2)}, u32[]{:S(2)}) collective-permute-start(f32[5,8,128]{2,1,0:T(8,128)S(1)} %get-tuple-element.36), channel_id=1, source_target_pairs={{0,2},{1,3},{2,0},{3,1},{4,6},{5,7},{6,4},{7,5},{8,16},{9,17},{10,... | collective-permute-start | bytes 61448 | tf_op jit(solution)/shard_map/ppermute | solution.py:485
  13.6 1.6 %collective-permute-start.8 = (f32[5,8,128]{2,1,0:T(8,128)S(1)}, f32[5,8,128]{2,1,0:T(8,128)S(1)}, u32[]{:S(2)}, u32[]{:S(2)}) collective-permute-start(f32[5,8,128]{2,1,0:T(8,128)S(1)} %get-tuple-element.37), channel_id=1, source_target_pairs={{0,8},{1,9},{2,10},{3,11},{4,12},{5,13},{6,14},{7,15},{8,0},{9,1},... | collective-permute-start | bytes 61448 | tf_op jit(solution)/shard_map/ppermute | solution.py:485
  15.2 1.5 %collective-permute-start.6 = (f32[8,128]{1,0:T(8,128)S(1)}, f32[8,128]{1,0:T(8,128)S(1)}, u32[]{:S(2)}, u32[]{:S(2)}) collective-permute-start(f32[8,128]{1,0:T(8,128)S(1)} %get-tuple-element.35), channel_id=1, source_target_pairs={{0,1},{1,0},{2,3},{3,2},{4,5},{5,4},{6,7},{7,6},{8,9},{9,8},{10,11... | collective-permute-start | bytes 12296 | tf_op jit(solution)/shard_map/ppermute | solution.py:485
  16.9 0.6 %copy-done.6 = s32[32]{0:T(128)S(1)} copy-done((s32[32]{0:T(128)S(1)}, s32[32]{0:T(128)}, u32[]{:S(2)}) %copy-start.6) | copy-done | bytes 152
  17.5 0.6 %shard_map.109.targets = s32[8,128]{1,0:T(8,128)S(1)} custom-call(s32[4,2,4]{2,1,0:T(2,128)S(1)} %bitcast.20, s32[32]{0:T(128)S(1)} %copy-done.6), custom_call_target="tpu_custom_call" | custom-call | flops 2000000 | bytes 1000000 | tf_op jit(solution)/shard_map/pallas_call | solution.py:438
  18.3 0.5 %collective-permute-done.6.refs_1_ = f32[8,128]{1,0:T(8,128)S(1)} collective-permute-done((f32[8,128]{1,0:T(8,128)S(1)}, f32[8,128]{1,0:T(8,128)S(1)}, u32[]{:S(2)}, u32[]{:S(2)}) %collective-permute-start.6) | collective-permute-done | bytes 4128 | tf_op jit(solution)/shard_map/ppermute | solution.py:485
  18.8 1.1 %shard_map.110 = (f32[5,64,128]{2,1,0:T(8,128)S(1)}, f32[32,8,128]{2,1,0:T(8,128)}, f32[5,8,128]{2,1,0:T(8,128)S(1)}, f32[8,128]{1,0:T(8,128)S(1)}, f32[5,8,128]...) custom-call(f32[5,64,128]{2,1,0:T(8,128)S(1)} %shard_map.107.base, f32[6,64,128]{2,1,0:T(8,128)S(1)} %copy-done.1, ...), custom_call_target="tpu_custom_call" | custom-call | flops 2000000 | bytes 1000000 | tf_op jit(solution)/shard_map/pallas_call | solution.py:438
  19.9 3.4 %all-to-all-start = ((f32[32,8,128]{2,1,0:T(8,128)}), f32[32,8,128]{2,1,0:T(8,128)S(1)}, u32[]{:S(2)}, u32[]{:S(2)}) async-start(f32[32,8,128]{2,1,0:T(8,128)} %get-tuple-element.40), calls=%async_computation | async-start | bytes 262144 | tf_op jit(solution)/shard_map/all_to_all | solution.py:539
  23.4 0.3 collective-permute-start.10
  23.7 0.3 collective-permute-start.12
  23.9 2.9 %collective-permute-start.13 = (f32[5,8,128]{2,1,0:T(8,128)S(1)}, f32[5,8,128]{2,1,0:T(8,128)S(1)}, u32[]{:S(2)}, u32[]{:S(2)}) collective-permute-start(f32[5,8,128]{2,1,0:T(8,128)S(1)} %get-tuple-element.44), channel_id=1, source_target_pairs={{0,8},{1,9},{2,10},{3,11},{4,12},{5,13},{6,14},{7,15},{8,0},{9,1},... | collective-permute-start | bytes 61448 | tf_op jit(solution)/shard_map/ppermute | solution.py:485
  26.8 0.9 %collective-permute-start.14 = (f32[5,8,128]{2,1,0:T(8,128)S(1)}, f32[5,8,128]{2,1,0:T(8,128)S(1)}, u32[]{:S(2)}, u32[]{:S(2)}) collective-permute-start(f32[5,8,128]{2,1,0:T(8,128)S(1)} %get-tuple-element.45), channel_id=1, source_target_pairs={{0,6},{1,7},{2,4},{3,5},{4,2},{5,3},{6,0},{7,1},{8,14},{9,15},{10,... | collective-permute-start | bytes 61448 | tf_op jit(solution)/shard_map/ppermute | solution.py:485
  27.7 1.5 %collective-permute-start.11 = (f32[8,128]{1,0:T(8,128)S(1)}, f32[8,128]{1,0:T(8,128)S(1)}, u32[]{:S(2)}, u32[]{:S(2)}) collective-permute-start(f32[8,128]{1,0:T(8,128)S(1)} %get-tuple-element.42), channel_id=1, source_target_pairs={{0,1},{1,0},{2,3},{3,2},{4,5},{5,4},{6,7},{7,6},{8,9},{9,8},{10,11... | collective-permute-start | bytes 12296 | tf_op jit(solution)/shard_map/ppermute | solution.py:485
  29.4 1.9 %collective-permute-done.11.refs_1_ = f32[8,128]{1,0:T(8,128)S(1)} collective-permute-done((f32[8,128]{1,0:T(8,128)S(1)}, f32[8,128]{1,0:T(8,128)S(1)}, u32[]{:S(2)}, u32[]{:S(2)}) %collective-permute-start.11) | collective-permute-done | bytes 4128 | tf_op jit(solution)/shard_map/ppermute | solution.py:485
  31.3 0.9 %all-to-all-done.table = f32[32,8,128]{2,1,0:T(8,128)S(1)} async-done(((f32[32,8,128]{2,1,0:T(8,128)}), f32[32,8,128]{2,1,0:T(8,128)S(1)}, u32[]{:S(2)}, u32[]{:S(2)}) %all-to-all-start) | async-done | bytes 131104 | tf_op jit(solution)/shard_map/all_to_all | solution.py:539
  32.2 1.6 %shard_map.112 = (f32[5,64,128]{2,1,0:T(8,128)}, f32[1,40]{1,0:T(1,128)}) custom-call(f32[5,64,128]{2,1,0:T(8,128)S(1)} %shard_map.111.base, f32[32,8,128]{2,1,0:T(8,128)S(1)} %all-to-all-done.table, f32[5,8,128]{2,1,0:T(8,128)S(1)} %collective-permute-done.10.refs_0_, f32[8,128]{1,0:T(8,128)S(1)} %collective-permute-done.11.refs_1_, ...), custom_call_target="tpu_custom_call" | custom-call | flops 2000000 | bytes 1000000 | tf_op jit(solution)/shard_map/pallas_call | solution.py:438
  (33 shorter events, 0.9 us)
Async XLA Ops:
  0.6 9.9 %copy-start.2 = (f32[5,8,8,128]{3,2,1,0:T(8,128)S(1)}, f32[5,8,8,128]{3,2,1,0:T(8,128)}, u32[]{:S(2)}) copy-start(f32[5,8,8,128]{3,2,1,0:T(8,128)} %param.9) | copy-start | bytes 491524
  0.6 9.9 %copy-start.3 = (f32[8,8,128]{2,1,0:T(8,128)S(1)}, f32[8,8,128]{2,1,0:T(8,128)}, u32[]{:S(2)}) copy-start(f32[8,8,128]{2,1,0:T(8,128)} %param.13) | copy-start | bytes 98308
  3.3 5.7 %copy-start.7 = (f32[8,128]{1,0:T(8,128)S(1)}, f32[8,128]{1,0:T(8,128)}, u32[]{:S(2)}) copy-start(f32[8,128]{1,0:T(8,128)} %get-tuple-element.27) | copy-start | bytes 12292
  3.3 9.3 %collective-permute-start = (f32[6,8,128]{2,1,0:T(8,128)}, f32[6,8,128]{2,1,0:T(8,128)S(1)}, u32[]{:S(2)}, u32[]{:S(2)}) collective-permute-start(f32[6,8,128]{2,1,0:T(8,128)} %get-tuple-element.26), channel_id=1, source_target_pairs={{0,2},{1,3},{2,0},{3,1},{4,6},{5,7},{6,4},{7,5},{8,10},{9,11},{10,... | collective-permute-start | bytes 73736 | tf_op jit(solution)/shard_map/ppermute | solution.py:485
  3.8 8.8 %collective-permute-start.2 = (f32[6,8,128]{2,1,0:T(8,128)}, f32[6,8,128]{2,1,0:T(8,128)S(1)}, u32[]{:S(2)}, u32[]{:S(2)}) collective-permute-start(f32[6,8,128]{2,1,0:T(8,128)} %get-tuple-element.28), channel_id=1, source_target_pairs={{0,2},{1,3},{2,0},{3,1},{4,6},{5,7},{6,4},{7,5},{8,16},{9,17},{10,... | collective-permute-start | bytes 73736 | tf_op jit(solution)/shard_map/ppermute | solution.py:485
  3.9 8.8 %collective-permute-start.3 = (f32[6,8,128]{2,1,0:T(8,128)}, f32[6,8,128]{2,1,0:T(8,128)S(1)}, u32[]{:S(2)}, u32[]{:S(2)}) collective-permute-start(f32[6,8,128]{2,1,0:T(8,128)} %get-tuple-element.29), channel_id=1, source_target_pairs={{0,8},{1,9},{2,10},{3,11},{4,12},{5,13},{6,14},{7,15},{8,0},{9,1},... | collective-permute-start | bytes 73736 | tf_op jit(solution)/shard_map/ppermute | solution.py:485
  8.1 4.6 %collective-permute-start.4 = (f32[6,8,128]{2,1,0:T(8,128)}, f32[6,8,128]{2,1,0:T(8,128)S(1)}, u32[]{:S(2)}, u32[]{:S(2)}) collective-permute-start(f32[6,8,128]{2,1,0:T(8,128)} %get-tuple-element.30), channel_id=1, source_target_pairs={{0,6},{1,7},{2,4},{3,5},{4,2},{5,3},{6,0},{7,1},{8,14},{9,15},{10,... | collective-permute-start | bytes 73736 | tf_op jit(solution)/shard_map/ppermute | solution.py:485
  9.0 3.6 %collective-permute-start.1 = (f32[8,128]{1,0:T(8,128)S(1)}, f32[8,128]{1,0:T(8,128)S(1)}, u32[]{:S(2)}, u32[]{:S(2)}) collective-permute-start(f32[8,128]{1,0:T(8,128)S(1)} %copy-done.7), channel_id=1, source_target_pairs={{0,1},{1,0},{2,3},{3,2},{4,5},{5,4},{6,7},{7,6},{8,9},{9,8},{10,11... | collective-permute-start | bytes 12296 | tf_op jit(solution)/shard_map/ppermute | solution.py:485
  10.6 0.9 %copy-start = (f32[6,64,128]{2,1,0:T(8,128)S(1)}, f32[6,64,128]{2,1,0:T(8,128)}, u32[]{:S(2)}) copy-start(f32[6,64,128]{2,1,0:T(8,128)} %get-tuple-element.25.scaled) | copy-start | bytes 589828
  11.5 1.2 %copy-start.1 = (f32[6,64,128]{2,1,0:T(8,128)S(1)}, f32[6,64,128]{2,1,0:T(8,128)}, u32[]{:S(2)}) copy-start(f32[6,64,128]{2,1,0:T(8,128)} %get-tuple-element.25.scaled) | copy-start | bytes 589828
  11.7 5.1 %copy-start.4 = (f32[8,8,128]{2,1,0:T(8,128)S(1)}, f32[8,8,128]{2,1,0:T(8,128)}, u32[]{:S(2)}) copy-start(f32[8,8,128]{2,1,0:T(8,128)} %param.14) | copy-start | bytes 98308
  13.0 5.8 %collective-permute-start.5 = (f32[5,8,128]{2,1,0:T(8,128)S(1)}, f32[5,8,128]{2,1,0:T(8,128)S(1)}, u32[]{:S(2)}, u32[]{:S(2)}) collective-permute-start(f32[5,8,128]{2,1,0:T(8,128)S(1)} %get-tuple-element.34), channel_id=1, source_target_pairs={{0,2},{1,3},{2,0},{3,1},{4,6},{5,7},{6,4},{7,5},{8,10},{9,11},{10,... | collective-permute-start | bytes 61448 | tf_op jit(solution)/shard_map/ppermute | solution.py:485
  13.1 5.7 %collective-permute-start.7 = (f32[5,8,128]{2,1,0:T(8,128)S(1)}, f32[5,8,128]{2,1,0:T(8,128)S(1)}, u32[]{:S(2)}, u32[]{:S(2)}) collective-permute-start(f32[5,8,128]{2,1,0:T(8,128)S(1)} %get-tuple-element.36), channel_id=1, source_target_pairs={{0,2},{1,3},{2,0},{3,1},{4,6},{5,7},{6,4},{7,5},{8,16},{9,17},{10,... | collective-permute-start | bytes 61448 | tf_op jit(solution)/shard_map/ppermute | solution.py:485
  13.6 5.2 %collective-permute-start.8 = (f32[5,8,128]{2,1,0:T(8,128)S(1)}, f32[5,8,128]{2,1,0:T(8,128)S(1)}, u32[]{:S(2)}, u32[]{:S(2)}) collective-permute-start(f32[5,8,128]{2,1,0:T(8,128)S(1)} %get-tuple-element.37), channel_id=1, source_target_pairs={{0,8},{1,9},{2,10},{3,11},{4,12},{5,13},{6,14},{7,15},{8,0},{9,1},... | collective-permute-start | bytes 61448 | tf_op jit(solution)/shard_map/ppermute | solution.py:485
  15.2 3.7 %collective-permute-start.9 = (f32[5,8,128]{2,1,0:T(8,128)S(1)}, f32[5,8,128]{2,1,0:T(8,128)S(1)}, u32[]{:S(2)}, u32[]{:S(2)}) collective-permute-start(f32[5,8,128]{2,1,0:T(8,128)S(1)} %get-tuple-element.38), channel_id=1, source_target_pairs={{0,6},{1,7},{2,4},{3,5},{4,2},{5,3},{6,0},{7,1},{8,14},{9,15},{10,... | collective-permute-start | bytes 61448 | tf_op jit(solution)/shard_map/ppermute | solution.py:485
  15.2 1.6 %copy-start.5 = (s32[4,4,2]{1,2,0:T(2,128)S(1)}, s32[4,4,2]{1,2,0:T(2,128)}, u32[]{:S(2)}) copy-start(s32[4,4,2]{1,2,0:T(2,128)} %param.16) | copy-start | bytes 388
  15.2 3.6 %collective-permute-start.6 = (f32[8,128]{1,0:T(8,128)S(1)}, f32[8,128]{1,0:T(8,128)S(1)}, u32[]{:S(2)}, u32[]{:S(2)}) collective-permute-start(f32[8,128]{1,0:T(8,128)S(1)} %get-tuple-element.35), channel_id=1, source_target_pairs={{0,1},{1,0},{2,3},{3,2},{4,5},{5,4},{6,7},{7,6},{8,9},{9,8},{10,11... | collective-permute-start | bytes 12296 | tf_op jit(solution)/shard_map/ppermute | solution.py:485
  16.8 0.7 %copy-start.6 = (s32[32]{0:T(128)S(1)}, s32[32]{0:T(128)}, u32[]{:S(2)}) copy-start(s32[32]{0:T(128)} %owners.1) | copy-start | bytes 388
  19.9 12.3 %all-to-all-start = ((f32[32,8,128]{2,1,0:T(8,128)}), f32[32,8,128]{2,1,0:T(8,128)S(1)}, u32[]{:S(2)}, u32[]{:S(2)}) async-start(f32[32,8,128]{2,1,0:T(8,128)} %get-tuple-element.40), calls=%async_computation | async-start | bytes 262144 | tf_op jit(solution)/shard_map/all_to_all | solution.py:539
  23.4 7.9 %collective-permute-start.10 = (f32[5,8,128]{2,1,0:T(8,128)S(1)}, f32[5,8,128]{2,1,0:T(8,128)S(1)}, u32[]{:S(2)}, u32[]{:S(2)}) collective-permute-start(f32[5,8,128]{2,1,0:T(8,128)S(1)} %get-tuple-element.41), channel_id=1, source_target_pairs={{0,2},{1,3},{2,0},{3,1},{4,6},{5,7},{6,4},{7,5},{8,10},{9,11},{10,... | collective-permute-start | bytes 61448 | tf_op jit(solution)/shard_map/ppermute | solution.py:485
  23.7 7.6 %collective-permute-start.12 = (f32[5,8,128]{2,1,0:T(8,128)S(1)}, f32[5,8,128]{2,1,0:T(8,128)S(1)}, u32[]{:S(2)}, u32[]{:S(2)}) collective-permute-start(f32[5,8,128]{2,1,0:T(8,128)S(1)} %get-tuple-element.43), channel_id=1, source_target_pairs={{0,2},{1,3},{2,0},{3,1},{4,6},{5,7},{6,4},{7,5},{8,16},{9,17},{10,... | collective-permute-start | bytes 61448 | tf_op jit(solution)/shard_map/ppermute | solution.py:485
  23.9 7.4 %collective-permute-start.13 = (f32[5,8,128]{2,1,0:T(8,128)S(1)}, f32[5,8,128]{2,1,0:T(8,128)S(1)}, u32[]{:S(2)}, u32[]{:S(2)}) collective-permute-start(f32[5,8,128]{2,1,0:T(8,128)S(1)} %get-tuple-element.44), channel_id=1, source_target_pairs={{0,8},{1,9},{2,10},{3,11},{4,12},{5,13},{6,14},{7,15},{8,0},{9,1},... | collective-permute-start | bytes 61448 | tf_op jit(solution)/shard_map/ppermute | solution.py:485
  26.8 4.5 %collective-permute-start.14 = (f32[5,8,128]{2,1,0:T(8,128)S(1)}, f32[5,8,128]{2,1,0:T(8,128)S(1)}, u32[]{:S(2)}, u32[]{:S(2)}) collective-permute-start(f32[5,8,128]{2,1,0:T(8,128)S(1)} %get-tuple-element.45), channel_id=1, source_target_pairs={{0,6},{1,7},{2,4},{3,5},{4,2},{5,3},{6,0},{7,1},{8,14},{9,15},{10,... | collective-permute-start | bytes 61448 | tf_op jit(solution)/shard_map/ppermute | solution.py:485
  27.7 3.6 %collective-permute-start.11 = (f32[8,128]{1,0:T(8,128)S(1)}, f32[8,128]{1,0:T(8,128)S(1)}, u32[]{:S(2)}, u32[]{:S(2)}) collective-permute-start(f32[8,128]{1,0:T(8,128)S(1)} %get-tuple-element.42), channel_id=1, source_target_pairs={{0,1},{1,0},{2,3},{3,2},{4,5},{5,4},{6,7},{7,6},{8,9},{9,8},{10,11... | collective-permute-start | bytes 12296 | tf_op jit(solution)/shard_map/ppermute | solution.py:485

commit v5 on v4

--- a/solution.py
+++ b/solution.py
@@ -137,7 +137,7 @@
     return sort_pair(first[...], None if second is None else second[...], position, size)
 
 
-def add_halo(base, received, weight, sizes, out):
+def add_halo(base, received, weight, sizes, out, finish=None):
     here = positions()
     lanes = lax.broadcasted_iota(jnp.int32, TILE, 1)
     edges = (lanes == 0) | (lanes == CZ - 1)
@@ -159,6 +159,8 @@
             out[component, tile_at(x), :] = value
         out[component, row_at(0), :] = out[component, row_at(0), :] - weight * y_below
         out[component, row_at(CY - 1), :] = out[component, row_at(CY - 1), :] + weight * y_above
+        if finish is not None:
+            finish(component)
 
 
 ORDER = ((1, 0), (2, 0), (0, 1), (0, 0), (1, 1), (2, 1))
@@ -178,8 +180,9 @@
 
 def first_kernel(sizes, level, adjoint, density, velocity, stiffness, source, scaled, *refs):
     outs, scratch = split(refs, sizes, True)
-    adjoint_now, density_now, velocity_now, stiffness_now, source_now, arrived = scratch
+    level_now, adjoint_now, density_now, velocity_now, stiffness_now, source_now, arrived = scratch
     pairs = (
+        (level, level_now),
         (density, density_now),
         (velocity, velocity_now),
         (stiffness, stiffness_now),
@@ -192,11 +195,11 @@
     ]
     for copy in copies:
         copy.start()
-    here = positions()
-    own_level = level[here[0], here[2], here[1]]
-    half_inverse = 0.5 * lax.shift_left(jnp.int32(1), own_level).astype(jnp.float32)
     for copy in copies:
         copy.wait()
+    here = positions()
+    own_level = level_now[here[0], here[2], here[1]]
+    half_inverse = 0.5 * lax.shift_left(jnp.int32(1), own_level).astype(jnp.float32)
     for direction in range(3):
         scaled[direction] = half_inverse * velocity_now[direction]
     scaled[3] = half_inverse * density_now[...]
@@ -236,7 +239,8 @@
             out[component, tile_at(x), :] = value
 
 
-def shape_kernel(source, scaled, sponge, start, shapes, sums):
+def shape_kernel(sizes, source, scaled, sponge, start, *refs):
+    sources, (shapes, sums, faces) = split(refs, sizes)
     rows = lax.broadcasted_iota(jnp.int32, TILE, 0)
     lanes = lax.broadcasted_iota(jnp.int32, TILE, 1)
     outer = step_length * two_thirds
@@ -268,6 +272,32 @@
             totals[component] = value if totals[component] is None else totals[component] + value
     for component in range(5):
         sums[component] = totals[component]
+    here = positions()
+    x_below, x_above = sorted_field(sources[0], 5, here[0], sizes[0])
+    y_below, y_above = sorted_field(sources[1], 5, here[1], sizes[1])
+    z_below, z_above = sorted_lanes(sources[2], here[2], sizes[2])
+    aligned_above = jnp.zeros(TILE, jnp.float32)
+    aligned_below = jnp.zeros(TILE, jnp.float32)
+    for component in range(5):
+        group = lanes // (2 * CX) == component
+        shift = 2 * CX * (component - 5)
+        aligned_above = jnp.where(
+            group & (lanes % 2 == 0), pltpu.roll(z_above, (shift - 1) % CZ, 1), aligned_above
+        )
+        aligned_below = jnp.where(
+            group & (lanes % 2 == 1), pltpu.roll(z_below, (shift + 1) % CZ, 1), aligned_below
+        )
+    for index, (sign, face) in enumerate(
+        (
+            (-inner, x_above),
+            (inner, x_below),
+            (-inner, y_above),
+            (inner, y_below),
+            (-inner, aligned_above),
+            (inner, aligned_below),
+        )
+    ):
+        faces[index] = sign * face
 
 
 def stage_kernel(sizes, weight, base, scaled, *refs):
@@ -276,20 +306,16 @@
     put_messages(section, scaled, None, split(outs, sizes, True)[0])
 
 
-def merge_rows(tiles):
-    sublanes = lax.broadcasted_iota(jnp.int32, TILE, 0)
-    zero = jnp.zeros(TILE, jnp.float32)
-    tiles = list(tiles) + [None] * (CY - len(tiles))
-    for width in (4, 2, 1):
-        upper = (sublanes & width) != 0
-        merged = []
-        for index in range(width):
-            low, high = tiles[index], tiles[index + width]
-            low = zero if low is None else low + pltpu.roll(low, CY - width, 0)
-            high = zero if high is None else high + pltpu.roll(high, width, 0)
-            merged.append(jnp.where(upper, high, low))
-        tiles = merged
-    return tiles[0]
+def sublane_total(tile):
+    for shift in (4, 2, 1):
+        tile = tile + pltpu.roll(tile, shift, 0)
+    return tile
+
+
+def group_totals(tile):
+    for shift in (1, 2, 4, 8):
+        tile = tile + pltpu.roll(tile, CZ - shift, 1)
+    return tile
 
 
 def target_kernel(sizes, patches, owners, out):
@@ -316,14 +342,11 @@
 )
 
 
-def gradient_kernel(sizes, weight, base, scaled, shapes, sums, targets, *refs):
-    received, rest = split(refs, sizes)
-    sources, (section, table, *outs) = split(rest, sizes)
-    here = positions()
+def gradient_kernel(sizes, weight, base, scaled, shapes, sums, faces, targets, *refs):
+    received, (section, table, *rest) = split(refs, sizes)
+    outs, (tiles, blocks) = split(rest, sizes, True)
     add_halo(base, received, weight, sizes, section)
-    x_low, x_high, y_low, y_high, packed = put_messages(
-        section, scaled, None, split(outs, sizes, True)[0]
-    )
+    x_low, x_high, y_low, y_high, packed = put_messages(section, scaled, None, outs)
     main = [sums[component] for component in range(5)]
     before = [None] * 5
     after = [None] * 5
@@ -351,80 +374,87 @@
         accumulate(main, 4, along_x * drawn[0] + along_y * drawn[1])
         accumulate(before, 4, shape_before * drawn[2])
         accumulate(after, 4, shape_after * drawn[2])
-    own_tiles = [
-        main[f] + pltpu.roll(before[f], CZ - 1, 1) - pltpu.roll(after[f], 1, 1) for f in range(5)
-    ]
     lanes = lax.broadcasted_iota(jnp.int32, TILE, 1)
-    outer = step_length * two_thirds * step_length
-    x_below, x_above = sorted_field(sources[0], 5, here[0], sizes[0])
-    y_below, y_above = sorted_field(sources[1], 5, here[1], sizes[1])
-    z_below, z_above = sorted_lanes(sources[2], here[2], sizes[2])
-    aligned_above = jnp.zeros(TILE, jnp.float32)
-    aligned_below = jnp.zeros(TILE, jnp.float32)
-    for component in range(5):
-        group = lanes // (2 * CX) == component
-        shift = 2 * CX * (component - 5)
-        aligned_above = jnp.where(
-            group & (lanes % 2 == 0), pltpu.roll(z_above, (shift - 1) % CZ, 1), aligned_above
-        )
-        aligned_below = jnp.where(
-            group & (lanes % 2 == 1), pltpu.roll(z_below, (shift + 1) % CZ, 1), aligned_below
-        )
-    above = -outer * aligned_above * packed
-    below = outer * aligned_below * packed
-    last = CZ - BZ
-    contributions = [
-        own_tiles,
-        [(-outer * x_above) * x_high[f] for f in range(5)],
-        [(outer * x_below) * x_low[f] for f in range(5)],
-        [(-outer * y_above) * y_high[f] for f in range(5)],
-        [(outer * y_below) * y_low[f] for f in range(5)],
-        [jnp.where(lanes < BZ, pltpu.roll(above, (-BZ * f) % CZ, 1), 0.0) for f in range(5)],
-        [jnp.where(lanes >= last, pltpu.roll(below, (last - BZ * f) % CZ, 1), 0.0) for f in range(5)],
-    ]
-    merged = [merge_rows(tiles) for tiles in contributions]
+    for f in range(5):
+        own = main[f] + pltpu.roll(before[f], CZ - 1, 1) - pltpu.roll(after[f], 1, 1)
+        for index, tile in enumerate(
+            (own, faces[0] * x_high[f], faces[1] * x_low[f], faces[2] * y_high[f], faces[3] * y_low[f])
+        ):
+            tiles[index, f * CY : (f + 1) * CY, :] = tile
+    sublanes = lax.broadcasted_iota(jnp.int32, TILE, 0)
+    for index in range(5):
+        total = tiles[index, pl.ds(0, 5, stride=CY), :]
+        for row in range(1, CY):
+            total = total + tiles[index, pl.ds(row, 5, stride=CY), :]
+        total = jnp.concatenate([total, jnp.zeros((CY - 5, CZ), jnp.float32)], axis=0)
+        total = jnp.where(lanes % BZ == 0, group_totals(total), 0.0)
+        total = pltpu.roll(total, 0, 1, stride=1, stride_axis=0)
+        blocks[index] = total
+    for index, (face, first) in enumerate(((faces[4], 0), (faces[5], CZ - BZ))):
+        total = group_totals(sublane_total(face * packed))
+        placed = jnp.zeros(TILE, jnp.float32)
+        for f in range(5):
+            moved = pltpu.roll(total, (first + f - 2 * CX * f) % CZ, 1)
+            placed = jnp.where(lanes == first + f, moved, placed)
+        blocks[5 + index] = jnp.where(sublanes == 0, placed, 0.0)
+    sums_over = []
+    for index in range(7):
+        total = blocks[index, 0:1, :]
+        for row in range(1, 5 if index < 5 else 1):
+            total = total + blocks[index, row : row + 1, :]
+        sums_over.append(jnp.broadcast_to(total, TILE))
     aims = [jnp.broadcast_to(targets[j : j + 1, :], TILE) for j in range(len(OFFSETS))]
 
-    def fill(device):
+    def fill(start):
         total = None
-        for tile, aim in zip(merged, aims):
-            part = jnp.where(aim == device, tile, 0.0)
+        for block, aim in zip(sums_over, aims):
+            part = jnp.where(aim == sublanes + start, block, 0.0)
             total = part if total is None else total + part
-        table[device] = total
+        table[pl.ds(start, CY), :] = total
 
     devices = table.shape[0]
     if devices <= 64:
-        for device in range(devices):
-            fill(device)
+        for start in range(0, devices, CY):
+            fill(start)
     else:
-        lax.fori_loop(0, devices, lambda device, carry: (fill(device), carry)[1], 0)
+        lax.fori_loop(
+            0, devices // CY, lambda step, carry: (fill(pl.multiple_of(step * CY, CY)), carry)[1], 0
+        )
 
 
 def last_kernel(sizes, base, table, *refs):
-    received, (out, gradient, done, sent) = split(refs, sizes)
-    add_halo(base, received, two_thirds * step_length, sizes, done)
-    copy = pltpu.make_async_copy(done, out, sent)
-    copy.start()
+    received, (out, gradient, done, block, sent) = split(refs, sizes)
     devices = table.shape[0]
-    total = table[0]
+    total = table[0:CY, :]
     if devices <= 64:
-        for device in range(1, devices):
-            total = total + table[device]
+        for start in range(CY, devices, CY):
+            total = total + table[start : start + CY, :]
     else:
-        total = lax.fori_loop(1, devices, lambda device, old: old + table[device], total)
-    for shift in (1, 2, 4, 8):
-        total = total + pltpu.roll(total, CZ - shift, 1)
-    sublanes = lax.broadcasted_iota(jnp.int32, TILE, 0)
+        total = lax.fori_loop(
+            1,
+            devices // CY,
+            lambda step, old: old + table[pl.ds(pl.multiple_of(step * CY, CY), CY), :],
+            total,
+        )
+    total = sublane_total(total)
     lanes = lax.broadcasted_iota(jnp.int32, TILE, 1)
     result = jnp.zeros(TILE, jnp.float32)
-    total = pltpu.roll(total, 0, 1, stride=BOXES, stride_axis=0)
-    for box in range(BOXES):
-        moved = pltpu.roll(total, (box - BZ * box) % CZ, 1)
-        result = jnp.where(lanes == BOXES * sublanes + box, moved, result)
-    for shift in (4, 2, 1):
-        result = result + pltpu.roll(result, shift, 0)
-    gradient[...] = result[0:1, : 5 * BOXES]
-    copy.wait()
+    for component in range(5):
+        for box in range(BOXES):
+            want, have = component * BOXES + box, box * BZ + component
+            result = jnp.where(lanes == want, pltpu.roll(total, (want - have) % CZ, 1), result)
+    block[...] = result[0:1, : 5 * BOXES]
+    copies = [pltpu.make_async_copy(block, gradient, sent.at[5])]
+    copies[0].start()
+
+    def send(component):
+        copy = pltpu.make_async_copy(done.at[component], out.at[component], sent.at[component])
+        copy.start()
+        copies.append(copy)
+
+    add_halo(base, received, two_thirds * step_length, sizes, done, send)
+    for copy in copies:
+        copy.wait()
 
 
 VMEM = pl.BlockSpec(memory_space=pltpu.VMEM)
@@ -432,16 +462,18 @@
 HBM = pl.BlockSpec(memory_space=pltpu.HBM)
 
 
-def call(
-    kernel, in_specs, operands, out_shapes, out_specs=None, scratch=(), dtype=jnp.float32, vmem=16
-):
+def call(kernel, in_specs, operands, out_shapes, scratch=(), dtype=jnp.float32, space=pltpu.VMEM):
+    operands = [
+        pltpu.with_memory_space_constraint(operand, pltpu.HBM) if spec is HBM else operand
+        for spec, operand in zip(in_specs, operands)
+    ]
     return pl.pallas_call(
         kernel,
-        out_shape=[jax.ShapeDtypeStruct(shape, dtype) for shape in out_shapes],
+        out_shape=[space(shape, dtype) for shape in out_shapes],
         in_specs=in_specs,
-        out_specs=out_specs or [VMEM] * len(out_shapes),
+        out_specs=[pl.BlockSpec(memory_space=space)] * len(out_shapes),
         scratch_shapes=list(scratch),
-        compiler_params=pltpu.CompilerParams(vmem_limit_bytes=vmem * 1024 * 1024),
+        compiler_params=pltpu.CompilerParams(vmem_limit_bytes=16 * 1024 * 1024),
         cost_estimate=pl.CostEstimate(flops=2000000, bytes_accessed=1000000, transcendentals=0),
     )(*operands)
 
@@ -488,18 +520,18 @@
 
     scaled, *sent = call(
         functools.partial(first_kernel, sizes),
-        [SMEM] + [HBM] * 5,
+        [HBM] * 6,
         (level, start, density, velocity, stiffness, source),
         [(6,) + FLAT] + message_shapes(6),
         scratch=[
+            pltpu.SMEM(level.shape, jnp.int32),
             pltpu.VMEM(STATE, jnp.float32),
             pltpu.VMEM(FLAT, jnp.float32),
             pltpu.VMEM((3,) + FLAT, jnp.float32),
             pltpu.VMEM(FLAT, jnp.float32),
             pltpu.VMEM(FLAT, jnp.float32),
-            pltpu.SemaphoreType.DMA((5,)),
+            pltpu.SemaphoreType.DMA((6,)),
         ],
-        vmem=60,
     )
     received_one = exchange(sent)
     (targets,) = call(
@@ -526,17 +558,25 @@
         (scaled, sponge, start, section),
         [STATE],
     )
-    shapes, sums = call(
-        shape_kernel, [VMEM] * 4, (source, scaled, sponge, start), [(7,) + FLAT, (5,) + TILE]
-    )
-    operands = (base, scaled, shapes, sums, targets, *received, *received_one)
+    operands = (source, scaled, sponge, start, *received_one)
+    shapes, sums, faces = call(
+        functools.partial(shape_kernel, sizes),
+        [VMEM] * len(operands),
+        operands,
+        [(7,) + FLAT, (5,) + TILE, (6,) + TILE],
+    )
+    operands = (base, scaled, shapes, sums, faces, targets, *received)
     section, table, *sent = call(
         functools.partial(gradient_kernel, sizes, 0.25 * step_length),
         [VMEM] * len(operands),
         operands,
-        [STATE, (devices,) + TILE] + message_shapes(5),
-    )
-    table = lax.all_to_all(table, AXES, 0, 0, tiled=True)
+        [STATE, (devices, CZ)] + message_shapes(5),
+        scratch=[
+            pltpu.VMEM((5, 5 * CY, CZ), jnp.float32),
+            pltpu.VMEM((7,) + TILE, jnp.float32),
+        ],
+    )
+    table = lax.all_to_all(table.reshape(devices, 1, CZ), AXES, 0, 0, tiled=True)
     received = exchange(sent)
     (base,) = call(
         functools.partial(own_kernel, (third, two_thirds)),
@@ -544,14 +584,18 @@
         (scaled, sponge, start, section),
         [STATE],
     )
-    operands = (base, table, *received)
+    operands = (base, table.reshape(devices, CZ), *received)
     adjoint, gradient = call(
         functools.partial(last_kernel, sizes),
         [VMEM] * len(operands),
         operands,
         [STATE, (1, 5 * BOXES)],
-        [HBM, VMEM],
-        [pltpu.VMEM(STATE, jnp.float32), pltpu.SemaphoreType.DMA],
+        scratch=[
+            pltpu.VMEM(STATE, jnp.float32),
+            pltpu.VMEM((1, 5 * BOXES), jnp.float32),
+            pltpu.SemaphoreType.DMA((6,)),
+        ],
+        space=pltpu.HBM,
     )
     return adjoint.reshape(state_shape), gradient
 

time: 34.1 us -> 31.3 us (0.918)
  Pallas kernels: 6.9 us -> 5.03 us
  local copies, waits for them, and re-layouts: 1.59 us -> 0.58 us
    pallas_call x9, Pallas kernels: 6.9 us -> 5.03 us  [call(): pl.pallas_call(kernel, out_shape=[space(shape, dtype) for shape in out_sh...]
    unnamed x16 -> x10, local copies, waits for them, and re-layouts: 1.59 us -> 0.58 us
    ppermute x15, waiting for transfers between devices: 3.45 us -> 4.45 us  [exchange(): lax.ppermute(sends[key], AXES, permutations[key[0]][key[1]])]
    all_to_all x1, waiting for transfers between devices: 0.89 us -> 0.01 us  [body(): lax.all_to_all(table.reshape(devices, 1, CZ), AXES, 0, 0, tiled=True)]
  transfers between devices with their start and end apart: 16 -> 16, of which waited for: 4 -> 3; matrix products, arithmetic and copies ran while one was open for 0% -> 0% of each run, Pallas kernels for 4% -> 4%
where the time goes in v5:
time: 31.3 us; the launch traced here: 31 us
  starting transfers between devices  20.2 us (65%)
  Pallas kernels  5.03 us (16%)
  waiting for transfers between devices  4.45 us (14%)
  between operations  0.78 us (2%)
  local copies, waits for them, and re-layouts  0.58 us (2%)
    ppermute x15, starting transfers between devices, exchange(): lax.ppermute(sends[key], AXES, permutations[key[0]][key[1]])  16.7 us
    pallas_call x9, Pallas kernels, call(): pl.pallas_call(kernel, out_shape=[space(shape, dtype) for shape in out_sh...  5.03 us
    ppermute x15, waiting for transfers between devices, exchange(): lax.ppermute(sends[key], AXES, permutations[key[0]][key[1]])  4.45 us
    all_to_all x1, starting transfers between devices, body(): lax.all_to_all(table.reshape(devices, 1, CZ), AXES, 0, 0, tiled=True)  3.47 us
  transfers between devices with their start and end apart: 16, of which 3 were waited for; matrix products, arithmetic and copies ran while one was open for 0% of the time, Pallas kernels for 4%

profile of v5, /device:TPU:0, one launch (start us, length us, event | category | flops | bytes accessed | tf_op | source)
XLA Modules:
  0.0 31.0 jit_solution(14538639800698191108)
XLA Ops:
  0.7 1.2 %shard_map.104 = (f32[6,64,128]{2,1,0:T(8,128)S(1)}, f32[6,8,128]{2,1,0:T(8,128)S(1)}, f32[8,128]{1,0:T(8,128)S(1)}, f32[6,8,128]{2,1,0:T(8,128)S(1)}, f32[6,8,1...) custom-call(s32[4,2,4]{2,1,0:T(2,128)} %bitcast.29, f32[5,64,128]{2,1,0:T(8,128)} %bitcast.13, f32[64,128]{1,0:T(8,128)} %bitcast.27, ...), custom_call_target="tpu_custom_call" | custom-call | flops 2000000 | bytes 1000000 | tf_op jit(solution)/shard_map/pallas_call | solution.py:470
  1.9 0.5 %collective-permute-start = (f32[6,8,128]{2,1,0:T(8,128)S(1)}, f32[6,8,128]{2,1,0:T(8,128)S(1)}, u32[]{:S(2)}, u32[]{:S(2)}) collective-permute-start(f32[6,8,128]{2,1,0:T(8,128)S(1)} %get-tuple-element.27), channel_id=1, source_target_pairs={{0,2},{1,3},{2,0},{3,1},{4,6},{5,7},{6,4},{7,5},{8,10},{9,11},{10,... | collective-permute-start | bytes 73736 | tf_op jit(solution)/shard_map/ppermute | solution.py:517
  2.5 4.1 %collective-permute-start.3 = (f32[6,8,128]{2,1,0:T(8,128)S(1)}, f32[6,8,128]{2,1,0:T(8,128)S(1)}, u32[]{:S(2)}, u32[]{:S(2)}) collective-permute-start(f32[6,8,128]{2,1,0:T(8,128)S(1)} %get-tuple-element.30), channel_id=1, source_target_pairs={{0,8},{1,9},{2,10},{3,11},{4,12},{5,13},{6,14},{7,15},{8,0},{9,1},... | collective-permute-start | bytes 73736 | tf_op jit(solution)/shard_map/ppermute | solution.py:517
  6.6 1.0 %collective-permute-start.4 = (f32[6,8,128]{2,1,0:T(8,128)S(1)}, f32[6,8,128]{2,1,0:T(8,128)S(1)}, u32[]{:S(2)}, u32[]{:S(2)}) collective-permute-start(f32[6,8,128]{2,1,0:T(8,128)S(1)} %get-tuple-element.31), channel_id=1, source_target_pairs={{0,6},{1,7},{2,4},{3,5},{4,2},{5,3},{6,0},{7,1},{8,14},{9,15},{10,... | collective-permute-start | bytes 73736 | tf_op jit(solution)/shard_map/ppermute | solution.py:517
  7.6 1.5 %collective-permute-start.1 = (f32[8,128]{1,0:T(8,128)S(1)}, f32[8,128]{1,0:T(8,128)S(1)}, u32[]{:S(2)}, u32[]{:S(2)}) collective-permute-start(f32[8,128]{1,0:T(8,128)S(1)} %get-tuple-element.28), channel_id=1, source_target_pairs={{0,1},{1,0},{2,3},{3,2},{4,5},{5,4},{6,7},{7,6},{8,9},{9,8},{10,11... | collective-permute-start | bytes 12296 | tf_op jit(solution)/shard_map/ppermute | solution.py:517
  9.3 1.9 %collective-permute-done.1.refs_1_ = f32[8,128]{1,0:T(8,128)S(1)} collective-permute-done((f32[8,128]{1,0:T(8,128)S(1)}, f32[8,128]{1,0:T(8,128)S(1)}, u32[]{:S(2)}, u32[]{:S(2)}) %collective-permute-start.1) | collective-permute-done | bytes 4128 | tf_op jit(solution)/shard_map/ppermute | solution.py:517
  11.2 0.3 %shard_map.106 = (f32[5,64,128]{2,1,0:T(8,128)S(1)}, f32[5,8,128]{2,1,0:T(8,128)S(1)}, f32[8,128]{1,0:T(8,128)S(1)}, f32[5,8,128]{2,1,0:T(8,128)S(1)}, f32[5,8,1...) custom-call(f32[5,64,128]{2,1,0:T(8,128)S(1)} %shard_map.105.base, f32[6,64,128]{2,1,0:T(8,128)S(1)} %get-tuple-element.26.scaled, ...), custom_call_target="tpu_custom_call" | custom-call | flops 2000000 | bytes 1000000 | tf_op jit(solution)/shard_map/pallas_call | solution.py:470
  11.7 0.5 %collective-permute-start.7 = (f32[5,8,128]{2,1,0:T(8,128)S(1)}, f32[5,8,128]{2,1,0:T(8,128)S(1)}, u32[]{:S(2)}, u32[]{:S(2)}) collective-permute-start(f32[5,8,128]{2,1,0:T(8,128)S(1)} %get-tuple-element.38), channel_id=1, source_target_pairs={{0,2},{1,3},{2,0},{3,1},{4,6},{5,7},{6,4},{7,5},{8,16},{9,17},{10,... | collective-permute-start | bytes 61448 | tf_op jit(solution)/shard_map/ppermute | solution.py:517
  12.1 1.5 %collective-permute-start.8 = (f32[5,8,128]{2,1,0:T(8,128)S(1)}, f32[5,8,128]{2,1,0:T(8,128)S(1)}, u32[]{:S(2)}, u32[]{:S(2)}) collective-permute-start(f32[5,8,128]{2,1,0:T(8,128)S(1)} %get-tuple-element.39), channel_id=1, source_target_pairs={{0,8},{1,9},{2,10},{3,11},{4,12},{5,13},{6,14},{7,15},{8,0},{9,1},... | collective-permute-start | bytes 61448 | tf_op jit(solution)/shard_map/ppermute | solution.py:517
  13.7 1.5 %collective-permute-start.6 = (f32[8,128]{1,0:T(8,128)S(1)}, f32[8,128]{1,0:T(8,128)S(1)}, u32[]{:S(2)}, u32[]{:S(2)}) collective-permute-start(f32[8,128]{1,0:T(8,128)S(1)} %get-tuple-element.37), channel_id=1, source_target_pairs={{0,1},{1,0},{2,3},{3,2},{4,5},{5,4},{6,7},{7,6},{8,9},{9,8},{10,11... | collective-permute-start | bytes 12296 | tf_op jit(solution)/shard_map/ppermute | solution.py:517
  15.3 0.6 %shard_map.109.targets = s32[8,128]{1,0:T(8,128)S(1)} custom-call(s32[4,2,4]{2,1,0:T(2,128)S(1)} %bitcast.25, s32[32]{0:T(128)S(1)} %copy-done.4), custom_call_target="tpu_custom_call" | custom-call | flops 2000000 | bytes 1000000 | tf_op jit(solution)/shard_map/pallas_call | solution.py:470
  15.9 0.2 shard_map.107.base
  16.1 0.6 %copy-done.2 = f32[8,8,128]{2,1,0:T(8,128)S(1)} copy-done((f32[8,8,128]{2,1,0:T(8,128)S(1)}, f32[8,8,128]{2,1,0:T(8,128)}, u32[]{:S(2)}) %copy-start.2) | copy-done | bytes 32792
  16.8 0.6 %collective-permute-done.6.refs_1_ = f32[8,128]{1,0:T(8,128)S(1)} collective-permute-done((f32[8,128]{1,0:T(8,128)S(1)}, f32[8,128]{1,0:T(8,128)S(1)}, u32[]{:S(2)}, u32[]{:S(2)}) %collective-permute-start.6) | collective-permute-done | bytes 4128 | tf_op jit(solution)/shard_map/ppermute | solution.py:517
  17.4 1.3 %shard_map.110 = (f32[5,64,128]{2,1,0:T(8,128)S(1)}, f32[32,128]{1,0:T(8,128)}, f32[5,8,128]{2,1,0:T(8,128)S(1)}, f32[8,128]{1,0:T(8,128)S(1)}, f32[5,8,128]{2,1...) custom-call(f32[5,64,128]{2,1,0:T(8,128)S(1)} %shard_map.107.base, ...), custom_call_target="tpu_custom_call" | custom-call | flops 2000000 | bytes 1000000 | tf_op jit(solution)/shard_map/pallas_call | solution.py:470
  18.7 3.5 %all-to-all-start = ((f32[32,1,128]{2,1,0:T(1,128)}), f32[32,1,128]{2,1,0:T(1,128)S(1)}, u32[]{:S(2)}, u32[]{:S(2)}) async-start(f32[32,1,128]{2,1,0:T(1,128)} %bitcast.9), calls=%async_computation | async-start | bytes 32768 | tf_op jit(solution)/shard_map/all_to_all | solution.py:579
  22.2 0.3 %collective-permute-start.10 = (f32[5,8,128]{2,1,0:T(8,128)S(1)}, f32[5,8,128]{2,1,0:T(8,128)S(1)}, u32[]{:S(2)}, u32[]{:S(2)}) collective-permute-start(f32[5,8,128]{2,1,0:T(8,128)S(1)} %get-tuple-element.43), channel_id=1, source_target_pairs={{0,2},{1,3},{2,0},{3,1},{4,6},{5,7},{6,4},{7,5},{8,10},{9,11},{10,... | collective-permute-start | bytes 61448 | tf_op jit(solution)/shard_map/ppermute | solution.py:517
  22.5 0.3 collective-permute-start.12
  22.7 2.9 %collective-permute-start.13 = (f32[5,8,128]{2,1,0:T(8,128)S(1)}, f32[5,8,128]{2,1,0:T(8,128)S(1)}, u32[]{:S(2)}, u32[]{:S(2)}) collective-permute-start(f32[5,8,128]{2,1,0:T(8,128)S(1)} %get-tuple-element.46), channel_id=1, source_target_pairs={{0,8},{1,9},{2,10},{3,11},{4,12},{5,13},{6,14},{7,15},{8,0},{9,1},... | collective-permute-start | bytes 61448 | tf_op jit(solution)/shard_map/ppermute | solution.py:517
  25.6 0.9 %collective-permute-start.14 = (f32[5,8,128]{2,1,0:T(8,128)S(1)}, f32[5,8,128]{2,1,0:T(8,128)S(1)}, u32[]{:S(2)}, u32[]{:S(2)}) collective-permute-start(f32[5,8,128]{2,1,0:T(8,128)S(1)} %get-tuple-element.47), channel_id=1, source_target_pairs={{0,6},{1,7},{2,4},{3,5},{4,2},{5,3},{6,0},{7,1},{8,14},{9,15},{10,... | collective-permute-start | bytes 61448 | tf_op jit(solution)/shard_map/ppermute | solution.py:517
  26.5 1.5 %collective-permute-start.11 = (f32[8,128]{1,0:T(8,128)S(1)}, f32[8,128]{1,0:T(8,128)S(1)}, u32[]{:S(2)}, u32[]{:S(2)}) collective-permute-start(f32[8,128]{1,0:T(8,128)S(1)} %get-tuple-element.44), channel_id=1, source_target_pairs={{0,1},{1,0},{2,3},{3,2},{4,5},{5,4},{6,7},{7,6},{8,9},{9,8},{10,11... | collective-permute-start | bytes 12296 | tf_op jit(solution)/shard_map/ppermute | solution.py:517
  28.0 0.2 shard_map.111.base
  28.2 1.9 %collective-permute-done.11.refs_1_ = f32[8,128]{1,0:T(8,128)S(1)} collective-permute-done((f32[8,128]{1,0:T(8,128)S(1)}, f32[8,128]{1,0:T(8,128)S(1)}, u32[]{:S(2)}, u32[]{:S(2)}) %collective-permute-start.11) | collective-permute-done | bytes 4128 | tf_op jit(solution)/shard_map/ppermute | solution.py:517
  30.1 0.9 %shard_map.112 = (f32[5,64,128]{2,1,0:T(8,128)}, f32[1,40]{1,0:T(1,128)}) custom-call(f32[5,64,128]{2,1,0:T(8,128)S(1)} %shard_map.111.base, f32[32,128]{1,0:T(8,128)S(1)} %bitcast.24, f32[5,8,128]{2,1,0:T(8,128)S(1)} %collective-permute-done.10.refs_0_, f32[8,128]{1,0:T(8,128)S(1)} %collective-permute-done.11.refs_1_, ...), custom_call_target="tpu_custom_call" | custom-call | flops 2000000 | bytes 1000000 | tf_op jit(solution)/shard_map/pallas_call | solution.py:470
  (27 shorter events, 0.6 us)
Async XLA Ops:
  0.6 8.5 %copy-start = (f32[5,8,8,128]{3,2,1,0:T(8,128)S(1)}, f32[5,8,8,128]{3,2,1,0:T(8,128)}, u32[]{:S(2)}) copy-start(f32[5,8,8,128]{3,2,1,0:T(8,128)} %param.9) | copy-start | bytes 491524
  0.6 8.5 %copy-start.1 = (f32[8,8,128]{2,1,0:T(8,128)S(1)}, f32[8,8,128]{2,1,0:T(8,128)}, u32[]{:S(2)}) copy-start(f32[8,8,128]{2,1,0:T(8,128)} %param.13) | copy-start | bytes 98308
  1.9 9.3 %collective-permute-start = (f32[6,8,128]{2,1,0:T(8,128)S(1)}, f32[6,8,128]{2,1,0:T(8,128)S(1)}, u32[]{:S(2)}, u32[]{:S(2)}) collective-permute-start(f32[6,8,128]{2,1,0:T(8,128)S(1)} %get-tuple-element.27), channel_id=1, source_target_pairs={{0,2},{1,3},{2,0},{3,1},{4,6},{5,7},{6,4},{7,5},{8,10},{9,11},{10,... | collective-permute-start | bytes 73736 | tf_op jit(solution)/shard_map/ppermute | solution.py:517
  2.4 8.8 %collective-permute-start.2 = (f32[6,8,128]{2,1,0:T(8,128)S(1)}, f32[6,8,128]{2,1,0:T(8,128)S(1)}, u32[]{:S(2)}, u32[]{:S(2)}) collective-permute-start(f32[6,8,128]{2,1,0:T(8,128)S(1)} %get-tuple-element.29), channel_id=1, source_target_pairs={{0,2},{1,3},{2,0},{3,1},{4,6},{5,7},{6,4},{7,5},{8,16},{9,17},{10,... | collective-permute-start | bytes 73736 | tf_op jit(solution)/shard_map/ppermute | solution.py:517
  2.5 8.7 %collective-permute-start.3 = (f32[6,8,128]{2,1,0:T(8,128)S(1)}, f32[6,8,128]{2,1,0:T(8,128)S(1)}, u32[]{:S(2)}, u32[]{:S(2)}) collective-permute-start(f32[6,8,128]{2,1,0:T(8,128)S(1)} %get-tuple-element.30), channel_id=1, source_target_pairs={{0,8},{1,9},{2,10},{3,11},{4,12},{5,13},{6,14},{7,15},{8,0},{9,1},... | collective-permute-start | bytes 73736 | tf_op jit(solution)/shard_map/ppermute | solution.py:517
  6.6 4.6 %collective-permute-start.4 = (f32[6,8,128]{2,1,0:T(8,128)S(1)}, f32[6,8,128]{2,1,0:T(8,128)S(1)}, u32[]{:S(2)}, u32[]{:S(2)}) collective-permute-start(f32[6,8,128]{2,1,0:T(8,128)S(1)} %get-tuple-element.31), channel_id=1, source_target_pairs={{0,6},{1,7},{2,4},{3,5},{4,2},{5,3},{6,0},{7,1},{8,14},{9,15},{10,... | collective-permute-start | bytes 73736 | tf_op jit(solution)/shard_map/ppermute | solution.py:517
  7.6 3.6 %collective-permute-start.1 = (f32[8,128]{1,0:T(8,128)S(1)}, f32[8,128]{1,0:T(8,128)S(1)}, u32[]{:S(2)}, u32[]{:S(2)}) collective-permute-start(f32[8,128]{1,0:T(8,128)S(1)} %get-tuple-element.28), channel_id=1, source_target_pairs={{0,1},{1,0},{2,3},{3,2},{4,5},{5,4},{6,7},{7,6},{8,9},{9,8},{10,11... | collective-permute-start | bytes 12296 | tf_op jit(solution)/shard_map/ppermute | solution.py:517
  11.6 5.8 %collective-permute-start.5 = (f32[5,8,128]{2,1,0:T(8,128)S(1)}, f32[5,8,128]{2,1,0:T(8,128)S(1)}, u32[]{:S(2)}, u32[]{:S(2)}) collective-permute-start(f32[5,8,128]{2,1,0:T(8,128)S(1)} %get-tuple-element.36), channel_id=1, source_target_pairs={{0,2},{1,3},{2,0},{3,1},{4,6},{5,7},{6,4},{7,5},{8,10},{9,11},{10,... | collective-permute-start | bytes 61448 | tf_op jit(solution)/shard_map/ppermute | solution.py:517
  11.6 3.6 %copy-start.3 = (s32[4,4,2]{1,2,0:T(2,128)S(1)}, s32[4,4,2]{1,2,0:T(2,128)}, u32[]{:S(2)}) copy-start(s32[4,4,2]{1,2,0:T(2,128)} %param.16) | copy-start | bytes 388
  11.7 5.7 %collective-permute-start.7 = (f32[5,8,128]{2,1,0:T(8,128)S(1)}, f32[5,8,128]{2,1,0:T(8,128)S(1)}, u32[]{:S(2)}, u32[]{:S(2)}) collective-permute-start(f32[5,8,128]{2,1,0:T(8,128)S(1)} %get-tuple-element.38), channel_id=1, source_target_pairs={{0,2},{1,3},{2,0},{3,1},{4,6},{5,7},{6,4},{7,5},{8,16},{9,17},{10,... | collective-permute-start | bytes 61448 | tf_op jit(solution)/shard_map/ppermute | solution.py:517
  12.1 5.2 %collective-permute-start.8 = (f32[5,8,128]{2,1,0:T(8,128)S(1)}, f32[5,8,128]{2,1,0:T(8,128)S(1)}, u32[]{:S(2)}, u32[]{:S(2)}) collective-permute-start(f32[5,8,128]{2,1,0:T(8,128)S(1)} %get-tuple-element.39), channel_id=1, source_target_pairs={{0,8},{1,9},{2,10},{3,11},{4,12},{5,13},{6,14},{7,15},{8,0},{9,1},... | collective-permute-start | bytes 61448 | tf_op jit(solution)/shard_map/ppermute | solution.py:517
  13.6 3.7 %collective-permute-start.9 = (f32[5,8,128]{2,1,0:T(8,128)S(1)}, f32[5,8,128]{2,1,0:T(8,128)S(1)}, u32[]{:S(2)}, u32[]{:S(2)}) collective-permute-start(f32[5,8,128]{2,1,0:T(8,128)S(1)} %get-tuple-element.40), channel_id=1, source_target_pairs={{0,6},{1,7},{2,4},{3,5},{4,2},{5,3},{6,0},{7,1},{8,14},{9,15},{10,... | collective-permute-start | bytes 61448 | tf_op jit(solution)/shard_map/ppermute | solution.py:517
  13.7 1.5 %copy-start.4 = (s32[32]{0:T(128)S(1)}, s32[32]{0:T(128)}, u32[]{:S(2)}) copy-start(s32[32]{0:T(128)} %owners.1) | copy-start | bytes 388
  13.7 3.6 %collective-permute-start.6 = (f32[8,128]{1,0:T(8,128)S(1)}, f32[8,128]{1,0:T(8,128)S(1)}, u32[]{:S(2)}, u32[]{:S(2)}) collective-permute-start(f32[8,128]{1,0:T(8,128)S(1)} %get-tuple-element.37), channel_id=1, source_target_pairs={{0,1},{1,0},{2,3},{3,2},{4,5},{5,4},{6,7},{7,6},{8,9},{9,8},{10,11... | collective-permute-start | bytes 12296 | tf_op jit(solution)/shard_map/ppermute | solution.py:517
  15.9 0.8 %copy-start.2 = (f32[8,8,128]{2,1,0:T(8,128)S(1)}, f32[8,8,128]{2,1,0:T(8,128)}, u32[]{:S(2)}) copy-start(f32[8,8,128]{2,1,0:T(8,128)} %param.14) | copy-start | bytes 98308
  18.7 11.4 %all-to-all-start = ((f32[32,1,128]{2,1,0:T(1,128)}), f32[32,1,128]{2,1,0:T(1,128)S(1)}, u32[]{:S(2)}, u32[]{:S(2)}) async-start(f32[32,1,128]{2,1,0:T(1,128)} %bitcast.9), calls=%async_computation | async-start | bytes 32768 | tf_op jit(solution)/shard_map/all_to_all | solution.py:579
  22.2 7.9 %collective-permute-start.10 = (f32[5,8,128]{2,1,0:T(8,128)S(1)}, f32[5,8,128]{2,1,0:T(8,128)S(1)}, u32[]{:S(2)}, u32[]{:S(2)}) collective-permute-start(f32[5,8,128]{2,1,0:T(8,128)S(1)} %get-tuple-element.43), channel_id=1, source_target_pairs={{0,2},{1,3},{2,0},{3,1},{4,6},{5,7},{6,4},{7,5},{8,10},{9,11},{10,... | collective-permute-start | bytes 61448 | tf_op jit(solution)/shard_map/ppermute | solution.py:517
  22.5 7.6 %collective-permute-start.12 = (f32[5,8,128]{2,1,0:T(8,128)S(1)}, f32[5,8,128]{2,1,0:T(8,128)S(1)}, u32[]{:S(2)}, u32[]{:S(2)}) collective-permute-start(f32[5,8,128]{2,1,0:T(8,128)S(1)} %get-tuple-element.45), channel_id=1, source_target_pairs={{0,2},{1,3},{2,0},{3,1},{4,6},{5,7},{6,4},{7,5},{8,16},{9,17},{10,... | collective-permute-start | bytes 61448 | tf_op jit(solution)/shard_map/ppermute | solution.py:517
  22.7 7.4 %collective-permute-start.13 = (f32[5,8,128]{2,1,0:T(8,128)S(1)}, f32[5,8,128]{2,1,0:T(8,128)S(1)}, u32[]{:S(2)}, u32[]{:S(2)}) collective-permute-start(f32[5,8,128]{2,1,0:T(8,128)S(1)} %get-tuple-element.46), channel_id=1, source_target_pairs={{0,8},{1,9},{2,10},{3,11},{4,12},{5,13},{6,14},{7,15},{8,0},{9,1},... | collective-permute-start | bytes 61448 | tf_op jit(solution)/shard_map/ppermute | solution.py:517
  25.6 4.5 %collective-permute-start.14 = (f32[5,8,128]{2,1,0:T(8,128)S(1)}, f32[5,8,128]{2,1,0:T(8,128)S(1)}, u32[]{:S(2)}, u32[]{:S(2)}) collective-permute-start(f32[5,8,128]{2,1,0:T(8,128)S(1)} %get-tuple-element.47), channel_id=1, source_target_pairs={{0,6},{1,7},{2,4},{3,5},{4,2},{5,3},{6,0},{7,1},{8,14},{9,15},{10,... | collective-permute-start | bytes 61448 | tf_op jit(solution)/shard_map/ppermute | solution.py:517
  26.5 3.6 %collective-permute-start.11 = (f32[8,128]{1,0:T(8,128)S(1)}, f32[8,128]{1,0:T(8,128)S(1)}, u32[]{:S(2)}, u32[]{:S(2)}) collective-permute-start(f32[8,128]{1,0:T(8,128)S(1)} %get-tuple-element.44), channel_id=1, source_target_pairs={{0,1},{1,0},{2,3},{3,2},{4,5},{5,4},{6,7},{7,6},{8,9},{9,8},{10,11... | collective-permute-start | bytes 12296 | tf_op jit(solution)/shard_map/ppermute | solution.py:517

commit v6 on v5

--- a/solution.py
+++ b/solution.py
@@ -19,6 +19,9 @@
 step_length = 0.14
 third = 1.0 / 3.0
 two_thirds = 2.0 / 3.0
+
+BASE = 5 * BOXES
+SHARE = CY // 2
 
 TILE = (CY, CZ)
 FLAT = (ROWS, CZ)
@@ -79,13 +82,21 @@
 
 
 def pack_lanes(fields):
-    lanes = lax.broadcasted_iota(jnp.int32, TILE, 1) // 2
-    packed = jnp.zeros(TILE, jnp.float32)
+    lanes = (lax.broadcasted_iota(jnp.int32, TILE, 1) + (CZ - BASE)) % CZ // 2
+    tiles = []
     for index, field in enumerate(fields):
         for x in range(CX):
             k = index * CX + x
-            packed = jnp.where(lanes == k, pltpu.roll(field[x], (2 * k + 1) % CZ, 1), packed)
-    return packed
+            tiles.append(pltpu.roll(field[x], (BASE + 2 * k + 1) % CZ, 1))
+    bit = 1
+    while len(tiles) > 1:
+        upper = (lanes & bit) != 0
+        pairs = [
+            jnp.where(upper, tiles[at + 1], tiles[at]) if at + 1 < len(tiles) else tiles[at]
+            for at in range(0, len(tiles), 2)
+        ]
+        tiles, bit = pairs, 2 * bit
+    return tiles[0]
 
 
 def put_pair(low, high, position, outs):
@@ -96,25 +107,28 @@
             outs[1][index] = jnp.where(even, below, above)
 
 
-def put_messages(state, scaled, source, outs):
-    here = positions()
+def outer_faces(state, scaled):
     x_low = faces_at(state, scaled, tile_at(0), 0)
     x_high = faces_at(state, scaled, tile_at(CX - 1), 0)
     y_low = faces_at(state, scaled, row_at(0), 1)
     y_high = faces_at(state, scaled, row_at(CY - 1), 1)
     z_tiles = [faces_at(state, scaled, tile_at(x), 2) for x in range(CX)]
     z_fields = [[z_tiles[x][component] for x in range(CX)] for component in range(5)]
-    if source is None:
-        extra = [[]] * 4
-    else:
-        rows = (tile_at(0), tile_at(CX - 1), row_at(0), row_at(CY - 1))
-        extra = [[source[row, :]] for row in rows]
+    return x_low, x_high, y_low, y_high, z_fields
+
+
+def put_messages(state, scaled, source, outs):
+    here = positions()
+    x_low, x_high, y_low, y_high, z_fields = outer_faces(state, scaled)
+    if source is not None:
+        x_low.append(source[tile_at(0), :])
+        x_high.append(source[tile_at(CX - 1), :])
+        y_low.append(source[row_at(0), :])
+        y_high.append(source[row_at(CY - 1), :])
         z_fields.append([source[tile_at(x), :] for x in range(CX)])
-    put_pair(x_low + extra[0], x_high + extra[1], here[0], outs[0])
-    put_pair(y_low + extra[2], y_high + extra[3], here[1], outs[1])
-    packed = pack_lanes(z_fields)
-    outs[2][0][...] = packed
-    return x_low, x_high, y_low, y_high, packed
+    outs[2][0][...] = pack_lanes(z_fields)
+    put_pair(x_low, x_high, here[0], outs[0])
+    put_pair(y_low, y_high, here[1], outs[1])
 
 
 def sort_pair(first, second, position, size):
@@ -137,21 +151,23 @@
     return sort_pair(first[...], None if second is None else second[...], position, size)
 
 
-def add_halo(base, received, weight, sizes, out, finish=None):
+def add_halo(base, received, weight, sizes, out, finish=None, z_halo=None):
     here = positions()
     lanes = lax.broadcasted_iota(jnp.int32, TILE, 1)
     edges = (lanes == 0) | (lanes == CZ - 1)
-    z_below, z_above = sorted_lanes(received[2], here[2], sizes[2])
-    z_halo = weight * jnp.where(
-        lanes % 2 == 0, pltpu.roll(z_above, CZ - 1, 1), -pltpu.roll(z_below, 1, 1)
-    )
+    if z_halo is None:
+        z_below, z_above = sorted_lanes(received[2], here[2], sizes[2])
+        z_halo = jnp.where(
+            lanes % 2 == 0, pltpu.roll(z_above, CZ - 1, 1), -pltpu.roll(z_below, 1, 1)
+        )
+    z_halo = weight * z_halo
     for component in range(5):
         x_below, x_above = sorted_field(received[0], component, here[0], sizes[0])
         y_below, y_above = sorted_field(received[1], component, here[1], sizes[1])
         for x in range(CX):
             k = component * CX + x
             value = base[component, tile_at(x), :]
-            value = value + jnp.where(edges, pltpu.roll(z_halo, (CZ - 1 - 2 * k) % CZ, 1), 0.0)
+            value = value + jnp.where(edges, pltpu.roll(z_halo, (CZ - 1 - BASE - 2 * k) % CZ, 1), 0.0)
             if x == 0:
                 value = value - weight * x_below
             if x == CX - 1:
@@ -166,14 +182,15 @@
 ORDER = ((1, 0), (2, 0), (0, 1), (0, 0), (1, 1), (2, 1))
 
 
-def message_keys(sizes, sent):
+def message_keys(sizes, sent, with_z=True):
     keys = [key for key in ORDER if key[1] == 0 or sizes[key[0]] > 2]
+    keys = [key for key in keys if with_z or key[0] != 2]
     return [key for key in keys if not (sent and key == (2, 1))]
 
 
-def split(refs, sizes, sent=False):
+def split(refs, sizes, sent=False, with_z=True):
     refs, out = list(refs), [[None, None] for axis in range(3)]
-    for axis, which in message_keys(sizes, sent):
+    for axis, which in message_keys(sizes, sent, with_z):
         out[axis][which] = refs.pop(0)
     return out, refs
 
@@ -279,7 +296,7 @@
     aligned_above = jnp.zeros(TILE, jnp.float32)
     aligned_below = jnp.zeros(TILE, jnp.float32)
     for component in range(5):
-        group = lanes // (2 * CX) == component
+        group = (lanes >= BASE) & ((lanes - BASE) // (2 * CX) == component)
         shift = 2 * CX * (component - 5)
         aligned_above = jnp.where(
             group & (lanes % 2 == 0), pltpu.roll(z_above, (shift - 1) % CZ, 1), aligned_above
@@ -312,23 +329,47 @@
     return tile
 
 
-def group_totals(tile):
-    for shift in (1, 2, 4, 8):
-        tile = tile + pltpu.roll(tile, CZ - shift, 1)
-    return tile
-
-
-def target_kernel(sizes, patches, owners, out):
+def three_parts(value):
+    parts = []
+    for _ in range(3):
+        part = value.astype(jnp.bfloat16)
+        parts.append(part)
+        value = value - part.astype(jnp.float32)
+    return parts
+
+
+def product(value, matrix):
+    count = value.shape[0]
+    stacked = jnp.concatenate(three_parts(value), axis=0)
+    result = jnp.dot(stacked, matrix, preferred_element_type=jnp.float32)
+    return result[:count] + result[count : 2 * count] + result[2 * count :]
+
+
+def target_kernel(sizes, patches, owners, routes, gather):
     here = positions()
-    sublanes = lax.broadcasted_iota(jnp.int32, TILE, 0)
-    result = jnp.zeros(TILE, jnp.int32)
+    shape = routes.shape
+    rows = lax.broadcasted_iota(jnp.int32, shape, 0)
+    lanes = lax.broadcasted_iota(jnp.int32, shape, 1) % (CY * CY)
+    chosen = jnp.zeros(shape, jnp.bool_)
     for index, offset in enumerate(OFFSETS):
         place = [
             jnp.clip(here[axis] + offset[axis], 0, sizes[axis] - 1) for axis in range(3)
         ]
         target = owners[patches[place[0], place[2], place[1]]]
-        result = jnp.where(sublanes == index, target, result)
-    out[...] = result
+        chosen = chosen | ((lanes // CY == index) & (rows == target))
+    routes[...] = jnp.where(chosen, 1.0, 0.0).astype(jnp.bfloat16)
+    rows = lax.broadcasted_iota(jnp.int32, (CZ, CZ), 0)
+    lanes = lax.broadcasted_iota(jnp.int32, (CZ, CZ), 1)
+    for component in range(5):
+        ones = lanes == BOXES * component + rows // BZ
+        gather[component * CZ : (component + 1) * CZ, :] = jnp.where(ones, 1.0, 0.0).astype(
+            jnp.bfloat16
+        )
+    for index, box in enumerate((0, BOXES - 1)):
+        ones = (lanes == BOXES * ((rows - BASE) // (2 * CX)) + box) & (rows >= BASE)
+        ones = ones & (rows < BASE + 5 * 2 * CX)
+        start = (5 + index) * CZ
+        gather[start : start + CZ, :] = jnp.where(ones, 1.0, 0.0).astype(jnp.bfloat16)
 
 
 OFFSETS = (
@@ -342,11 +383,12 @@
 )
 
 
-def gradient_kernel(sizes, weight, base, scaled, shapes, sums, faces, targets, *refs):
+def gradient_kernel(sizes, weight, base, scaled, shapes, sums, faces, routes, gather, *refs):
     received, (section, table, *rest) = split(refs, sizes)
-    outs, (tiles, blocks) = split(rest, sizes, True)
+    outs, (rows_out, sent) = split(rest, sizes, True, False)
     add_halo(base, received, weight, sizes, section)
-    x_low, x_high, y_low, y_high, packed = put_messages(section, scaled, None, outs)
+    x_low, x_high, y_low, y_high, z_fields = outer_faces(section, scaled)
+    packed = pack_lanes(z_fields)
     main = [sums[component] for component in range(5)]
     before = [None] * 5
     after = [None] * 5
@@ -374,76 +416,75 @@
         accumulate(main, 4, along_x * drawn[0] + along_y * drawn[1])
         accumulate(before, 4, shape_before * drawn[2])
         accumulate(after, 4, shape_after * drawn[2])
-    lanes = lax.broadcasted_iota(jnp.int32, TILE, 1)
+    columns = []
     for f in range(5):
         own = main[f] + pltpu.roll(before[f], CZ - 1, 1) - pltpu.roll(after[f], 1, 1)
-        for index, tile in enumerate(
-            (own, faces[0] * x_high[f], faces[1] * x_low[f], faces[2] * y_high[f], faces[3] * y_low[f])
-        ):
-            tiles[index, f * CY : (f + 1) * CY, :] = tile
+        columns.append(
+            jnp.concatenate(
+                [own, faces[0] * x_high[f], faces[1] * x_low[f], faces[2] * y_high[f], faces[3] * y_low[f]],
+                axis=0,
+            )
+        )
+    blocks = product(jnp.concatenate(columns, axis=1), gather[: 5 * CZ, :])
+    above = product(faces[4] * packed, gather[5 * CZ : 6 * CZ, :])
+    below = product(faces[5] * packed, gather[6 * CZ :, :])
+    blocks = jnp.concatenate([blocks, above, below, jnp.zeros(TILE, jnp.float32)], axis=0)
+    devices = routes.shape[0]
+    rows_out[pl.ds(0, devices, stride=SHARE), :] = jnp.dot(
+        routes[...],
+        jnp.concatenate(three_parts(blocks), axis=0),
+        preferred_element_type=jnp.float32,
+    )
+    lanes = lax.broadcasted_iota(jnp.int32, TILE, 1)
+    here = positions()
+    own_place = (here[0] * sizes[1] + here[1]) * sizes[2] + here[2]
+    paired = pltpu.roll(packed, CY - SHARE, 0)
+    up = jnp.where(lanes % 2 == 0, packed, pltpu.roll(paired, 1, 1))[:SHARE]
+    down = jnp.where(lanes % 2 == 1, packed, pltpu.roll(paired, CZ - 1, 1))[:SHARE]
+    lanes = lax.broadcasted_iota(jnp.int32, (SHARE, CZ), 1)
+    for step, message in ((1, up), (-1, down)):
+        position = here[2] + step
+
+        @pl.when((position >= 0) & (position < sizes[2]))
+        def _():
+            at = pl.ds(pl.multiple_of((own_place + step) * SHARE, SHARE), SHARE)
+            rows_out[at, :] = jnp.where(lanes < BASE, rows_out[at, :], message)
+
+    copy = pltpu.make_async_copy(rows_out, table, sent)
+    copy.start()
+    put_pair(x_low, x_high, here[0], outs[0])
+    put_pair(y_low, y_high, here[1], outs[1])
+    copy.wait()
+
+
+def last_kernel(sizes, base, table, *refs):
+    received, (out, gradient, done, block, sent) = split(refs, sizes, False, False)
+    devices = table.shape[0] // SHARE
+    here = positions()
+    own_place = (here[0] * sizes[1] + here[1]) * sizes[2] + here[2]
     sublanes = lax.broadcasted_iota(jnp.int32, TILE, 0)
-    for index in range(5):
-        total = tiles[index, pl.ds(0, 5, stride=CY), :]
-        for row in range(1, CY):
-            total = total + tiles[index, pl.ds(row, 5, stride=CY), :]
-        total = jnp.concatenate([total, jnp.zeros((CY - 5, CZ), jnp.float32)], axis=0)
-        total = jnp.where(lanes % BZ == 0, group_totals(total), 0.0)
-        total = pltpu.roll(total, 0, 1, stride=1, stride_axis=0)
-        blocks[index] = total
-    for index, (face, first) in enumerate(((faces[4], 0), (faces[5], CZ - BZ))):
-        total = group_totals(sublane_total(face * packed))
-        placed = jnp.zeros(TILE, jnp.float32)
-        for f in range(5):
-            moved = pltpu.roll(total, (first + f - 2 * CX * f) % CZ, 1)
-            placed = jnp.where(lanes == first + f, moved, placed)
-        blocks[5 + index] = jnp.where(sublanes == 0, placed, 0.0)
-    sums_over = []
-    for index in range(7):
-        total = blocks[index, 0:1, :]
-        for row in range(1, 5 if index < 5 else 1):
-            total = total + blocks[index, row : row + 1, :]
-        sums_over.append(jnp.broadcast_to(total, TILE))
-    aims = [jnp.broadcast_to(targets[j : j + 1, :], TILE) for j in range(len(OFFSETS))]
-
-    def fill(start):
-        total = None
-        for block, aim in zip(sums_over, aims):
-            part = jnp.where(aim == sublanes + start, block, 0.0)
-            total = part if total is None else total + part
-        table[pl.ds(start, CY), :] = total
-
-    devices = table.shape[0]
-    if devices <= 64:
-        for start in range(0, devices, CY):
-            fill(start)
-    else:
-        lax.fori_loop(
-            0, devices // CY, lambda step, carry: (fill(pl.multiple_of(step * CY, CY)), carry)[1], 0
-        )
-
-
-def last_kernel(sizes, base, table, *refs):
-    received, (out, gradient, done, block, sent) = split(refs, sizes)
-    devices = table.shape[0]
-    total = table[0:CY, :]
-    if devices <= 64:
-        for start in range(CY, devices, CY):
-            total = total + table[start : start + CY, :]
-    else:
-        total = lax.fori_loop(
-            1,
-            devices // CY,
-            lambda step, old: old + table[pl.ds(pl.multiple_of(step * CY, CY), CY), :],
-            total,
-        )
-    total = sublane_total(total)
     lanes = lax.broadcasted_iota(jnp.int32, TILE, 1)
-    result = jnp.zeros(TILE, jnp.float32)
-    for component in range(5):
-        for box in range(BOXES):
-            want, have = component * BOXES + box, box * BZ + component
-            result = jnp.where(lanes == want, pltpu.roll(total, (want - have) % CZ, 1), result)
-    block[...] = result[0:1, : 5 * BOXES]
+
+    def z_rows(step):
+        inside = (here[2] + step >= 0) & (here[2] + step < sizes[2])
+        place = jnp.where(inside, own_place + step, own_place)
+        rows = table[pl.ds(pl.multiple_of(place * SHARE, SHARE), SHARE), :]
+        return jnp.where(inside, jnp.concatenate([rows, rows], axis=0), 0.0)
+
+    z_above, z_below = z_rows(1), z_rows(-1)
+    first_half = sublanes < SHARE
+    z_halo = jnp.where(
+        lanes % 2 == 0,
+        jnp.where(first_half, pltpu.roll(z_above, CZ - 1, 1), z_above),
+        -jnp.where(first_half, pltpu.roll(z_below, 1, 1), z_below),
+    )
+    totals = [None] * 4
+    for device in range(devices):
+        part = table[device * SHARE : device * SHARE + 1, :]
+        old = totals[device % 4]
+        totals[device % 4] = part if old is None else old + part
+    total = (totals[0] + totals[1]) + (totals[2] + totals[3])
+    block[...] = total[:, : 5 * BOXES]
     copies = [pltpu.make_async_copy(block, gradient, sent.at[5])]
     copies[0].start()
 
@@ -452,7 +493,7 @@
         copy.start()
         copies.append(copy)
 
-    add_halo(base, received, two_thirds * step_length, sizes, done, send)
+    add_halo(base, received, two_thirds * step_length, sizes, done, send, z_halo)
     for copy in copies:
         copy.wait()
 
@@ -462,16 +503,17 @@
 HBM = pl.BlockSpec(memory_space=pltpu.HBM)
 
 
-def call(kernel, in_specs, operands, out_shapes, scratch=(), dtype=jnp.float32, space=pltpu.VMEM):
+def call(kernel, in_specs, operands, out_shapes, scratch=(), spaces=None, dtype=jnp.float32):
+    spaces = spaces or [pltpu.VMEM] * len(out_shapes)
     operands = [
         pltpu.with_memory_space_constraint(operand, pltpu.HBM) if spec is HBM else operand
         for spec, operand in zip(in_specs, operands)
     ]
     return pl.pallas_call(
         kernel,
-        out_shape=[space(shape, dtype) for shape in out_shapes],
+        out_shape=[space(shape, dtype) for space, shape in zip(spaces, out_shapes)],
         in_specs=in_specs,
-        out_specs=[pl.BlockSpec(memory_space=space)] * len(out_shapes),
+        out_specs=[pl.BlockSpec(memory_space=space) for space in spaces],
         scratch_shapes=list(scratch),
         compiler_params=pltpu.CompilerParams(vmem_limit_bytes=16 * 1024 * 1024),
         cost_estimate=pl.CostEstimate(flops=2000000, bytes_accessed=1000000, transcendentals=0),
@@ -505,17 +547,18 @@
     level = jnp.transpose(brick_level, (0, 2, 1))
     patches = jnp.transpose(brick_patch, (0, 2, 1))
 
-    def message_shapes(fields):
+    def message_shapes(fields, with_z=True):
         return [
-            TILE if key[0] == 2 else (fields,) + TILE for key in message_keys(sizes, True)
+            TILE if key[0] == 2 else (fields,) + TILE
+            for key in message_keys(sizes, True, with_z)
         ]
 
-    def exchange(messages):
-        sends = dict(zip(message_keys(sizes, True), messages))
-        sends[2, 1] = sends[2, 0]
+    def exchange(messages, with_z=True):
+        sends = dict(zip(message_keys(sizes, True, with_z), messages))
+        sends[2, 1] = sends.get((2, 0))
         return [
             lax.ppermute(sends[key], AXES, permutations[key[0]][key[1]])
-            for key in message_keys(sizes, False)
+            for key in message_keys(sizes, False, with_z)
         ]
 
     scaled, *sent = call(
@@ -534,12 +577,12 @@
         ],
     )
     received_one = exchange(sent)
-    (targets,) = call(
+    routes, gather = call(
         functools.partial(target_kernel, sizes),
         [SMEM] * 2,
         (patches, patch_owner),
-        [TILE],
-        dtype=jnp.int32,
+        [(devices, 3 * CY * CY), (7 * CZ, CZ)],
+        dtype=jnp.bfloat16,
     )
     (base,) = call(
         functools.partial(own_kernel, (0.0, 1.0)), [VMEM] * 3, (scaled, sponge, start), [STATE]
@@ -565,26 +608,24 @@
         operands,
         [(7,) + FLAT, (5,) + TILE, (6,) + TILE],
     )
-    operands = (base, scaled, shapes, sums, faces, targets, *received)
+    operands = (base, scaled, shapes, sums, faces, routes, gather, *received)
     section, table, *sent = call(
         functools.partial(gradient_kernel, sizes, 0.25 * step_length),
         [VMEM] * len(operands),
         operands,
-        [STATE, (devices, CZ)] + message_shapes(5),
-        scratch=[
-            pltpu.VMEM((5, 5 * CY, CZ), jnp.float32),
-            pltpu.VMEM((7,) + TILE, jnp.float32),
-        ],
-    )
-    table = lax.all_to_all(table.reshape(devices, 1, CZ), AXES, 0, 0, tiled=True)
-    received = exchange(sent)
+        [STATE, (devices * SHARE, CZ)] + message_shapes(5, False),
+        scratch=[pltpu.VMEM((devices * SHARE, CZ), jnp.float32), pltpu.SemaphoreType.DMA],
+        spaces=[pltpu.VMEM, pltpu.HBM] + [pltpu.VMEM] * len(message_shapes(5, False)),
+    )
+    table = lax.all_to_all(table.reshape(devices, SHARE, CZ), AXES, 0, 0, tiled=True)
+    received = exchange(sent, False)
     (base,) = call(
         functools.partial(own_kernel, (third, two_thirds)),
         [VMEM] * 4,
         (scaled, sponge, start, section),
         [STATE],
     )
-    operands = (base, table.reshape(devices, CZ), *received)
+    operands = (base, table.reshape(devices * SHARE, CZ), *received)
     adjoint, gradient = call(
         functools.partial(last_kernel, sizes),
         [VMEM] * len(operands),
@@ -595,7 +636,7 @@
             pltpu.VMEM((1, 5 * BOXES), jnp.float32),
             pltpu.SemaphoreType.DMA((6,)),
         ],
-        space=pltpu.HBM,
+        spaces=[pltpu.HBM] * 2,
     )
     return adjoint.reshape(state_shape), gradient
 

time: 31.3 us -> 31.1 us (level)
  starting transfers between devices: 20.2 us -> 18.7 us
  waiting for transfers between devices: 4.45 us -> 5.78 us
    ppermute x15 -> x14, starting transfers between devices: 16.7 us -> 15.2 us  [exchange(): lax.ppermute(sends[key], AXES, permutations[key[0]][key[1]])]
    all_to_all x1, waiting for transfers between devices: 0.01 us -> 0.95 us  [body(): lax.all_to_all(table.reshape(devices, SHARE, CZ), AXES, 0, 0, tiled=True)]
    ppermute x15 -> x14, waiting for transfers between devices: 4.45 us -> 4.83 us  [exchange(): lax.ppermute(sends[key], AXES, permutations[key[0]][key[1]])]
  transfers between devices with their start and end apart: 16 -> 15, of which waited for: 3 -> 5; matrix products, arithmetic and copies ran while one was open for 0% -> 0% of each run, Pallas kernels for 4% -> 4%
where the time goes in v6:
time: 31.1 us; the launch traced here: 30.9 us
  starting transfers between devices  18.7 us (60%)
  waiting for transfers between devices  5.78 us (19%)
  Pallas kernels  5.03 us (16%)
  between operations  0.78 us (3%)
  local copies, waits for them, and re-layouts  0.58 us (2%)
    ppermute x14, starting transfers between devices, exchange(): lax.ppermute(sends[key], AXES, permutations[key[0]][key[1]])  15.2 us
    pallas_call x9, Pallas kernels, call(): pl.pallas_call(kernel, out_shape=[space(shape, dtype) for space, shape in...  5.03 us
    ppermute x14, waiting for transfers between devices, exchange(): lax.ppermute(sends[key], AXES, permutations[key[0]][key[1]])  4.83 us
    all_to_all x1, starting transfers between devices, body(): lax.all_to_all(table.reshape(devices, SHARE, CZ), AXES, 0, 0, tiled=True)  3.48 us
    all_to_all x1, waiting for transfers between devices, body(): lax.all_to_all(table.reshape(devices, SHARE, CZ), AXES, 0, 0, tiled=True)  0.95 us
  transfers between devices with their start and end apart: 15, of which 5 were waited for; matrix products, arithmetic and copies ran while one was open for 0% of the time, Pallas kernels for 4%

profile of v6, /device:TPU:0, one launch (start us, length us, event | category | flops | bytes accessed | tf_op | source)
XLA Modules:
  0.0 30.9 jit_solution(5285987711368734883)
XLA Ops:
  0.7 1.2 %shard_map.104 = (f32[6,64,128]{2,1,0:T(8,128)S(1)}, f32[6,8,128]{2,1,0:T(8,128)S(1)}, f32[8,128]{1,0:T(8,128)S(1)}, f32[6,8,128]{2,1,0:T(8,128)S(1)}, f32[6,8,1...) custom-call(s32[4,2,4]{2,1,0:T(2,128)} %bitcast.28, f32[5,64,128]{2,1,0:T(8,128)} %bitcast.11, f32[64,128]{1,0:T(8,128)} %bitcast.26, ...), custom_call_target="tpu_custom_call" | custom-call | flops 2000000 | bytes 1000000 | tf_op jit(solution)/shard_map/pallas_call | solution.py:512
  1.9 0.5 %collective-permute-start = (f32[6,8,128]{2,1,0:T(8,128)S(1)}, f32[6,8,128]{2,1,0:T(8,128)S(1)}, u32[]{:S(2)}, u32[]{:S(2)}) collective-permute-start(f32[6,8,128]{2,1,0:T(8,128)S(1)} %get-tuple-element.28), channel_id=1, source_target_pairs={{0,2},{1,3},{2,0},{3,1},{4,6},{5,7},{6,4},{7,5},{8,10},{9,11},{10,... | collective-permute-start | bytes 73736 | tf_op jit(solution)/shard_map/ppermute | solution.py:560
  2.5 4.1 %collective-permute-start.3 = (f32[6,8,128]{2,1,0:T(8,128)S(1)}, f32[6,8,128]{2,1,0:T(8,128)S(1)}, u32[]{:S(2)}, u32[]{:S(2)}) collective-permute-start(f32[6,8,128]{2,1,0:T(8,128)S(1)} %get-tuple-element.31), channel_id=1, source_target_pairs={{0,8},{1,9},{2,10},{3,11},{4,12},{5,13},{6,14},{7,15},{8,0},{9,1},... | collective-permute-start | bytes 73736 | tf_op jit(solution)/shard_map/ppermute | solution.py:560
  6.6 1.0 %collective-permute-start.4 = (f32[6,8,128]{2,1,0:T(8,128)S(1)}, f32[6,8,128]{2,1,0:T(8,128)S(1)}, u32[]{:S(2)}, u32[]{:S(2)}) collective-permute-start(f32[6,8,128]{2,1,0:T(8,128)S(1)} %get-tuple-element.32), channel_id=1, source_target_pairs={{0,6},{1,7},{2,4},{3,5},{4,2},{5,3},{6,0},{7,1},{8,14},{9,15},{10,... | collective-permute-start | bytes 73736 | tf_op jit(solution)/shard_map/ppermute | solution.py:560
  7.6 1.5 %collective-permute-start.1 = (f32[8,128]{1,0:T(8,128)S(1)}, f32[8,128]{1,0:T(8,128)S(1)}, u32[]{:S(2)}, u32[]{:S(2)}) collective-permute-start(f32[8,128]{1,0:T(8,128)S(1)} %get-tuple-element.29), channel_id=1, source_target_pairs={{0,1},{1,0},{2,3},{3,2},{4,5},{5,4},{6,7},{7,6},{8,9},{9,8},{10,11... | collective-permute-start | bytes 12296 | tf_op jit(solution)/shard_map/ppermute | solution.py:560
  9.3 1.9 %collective-permute-done.1.refs_1_ = f32[8,128]{1,0:T(8,128)S(1)} collective-permute-done((f32[8,128]{1,0:T(8,128)S(1)}, f32[8,128]{1,0:T(8,128)S(1)}, u32[]{:S(2)}, u32[]{:S(2)}) %collective-permute-start.1) | collective-permute-done | bytes 4128 | tf_op jit(solution)/shard_map/ppermute | solution.py:560
  11.2 0.3 %shard_map.106 = (f32[5,64,128]{2,1,0:T(8,128)S(1)}, f32[5,8,128]{2,1,0:T(8,128)S(1)}, f32[8,128]{1,0:T(8,128)S(1)}, f32[5,8,128]{2,1,0:T(8,128)S(1)}, f32[5,8,1...) custom-call(f32[5,64,128]{2,1,0:T(8,128)S(1)} %shard_map.105.base, f32[6,64,128]{2,1,0:T(8,128)S(1)} %get-tuple-element.27.scaled, ...), custom_call_target="tpu_custom_call" | custom-call | flops 2000000 | bytes 1000000 | tf_op jit(solution)/shard_map/pallas_call | solution.py:512
  11.7 0.5 %collective-permute-start.7 = (f32[5,8,128]{2,1,0:T(8,128)S(1)}, f32[5,8,128]{2,1,0:T(8,128)S(1)}, u32[]{:S(2)}, u32[]{:S(2)}) collective-permute-start(f32[5,8,128]{2,1,0:T(8,128)S(1)} %get-tuple-element.41), channel_id=1, source_target_pairs={{0,2},{1,3},{2,0},{3,1},{4,6},{5,7},{6,4},{7,5},{8,16},{9,17},{10,... | collective-permute-start | bytes 61448 | tf_op jit(solution)/shard_map/ppermute | solution.py:560
  12.2 1.5 %collective-permute-start.8 = (f32[5,8,128]{2,1,0:T(8,128)S(1)}, f32[5,8,128]{2,1,0:T(8,128)S(1)}, u32[]{:S(2)}, u32[]{:S(2)}) collective-permute-start(f32[5,8,128]{2,1,0:T(8,128)S(1)} %get-tuple-element.42), channel_id=1, source_target_pairs={{0,8},{1,9},{2,10},{3,11},{4,12},{5,13},{6,14},{7,15},{8,0},{9,1},... | collective-permute-start | bytes 61448 | tf_op jit(solution)/shard_map/ppermute | solution.py:560
  13.7 1.5 %collective-permute-start.6 = (f32[8,128]{1,0:T(8,128)S(1)}, f32[8,128]{1,0:T(8,128)S(1)}, u32[]{:S(2)}, u32[]{:S(2)}) collective-permute-start(f32[8,128]{1,0:T(8,128)S(1)} %get-tuple-element.40), channel_id=1, source_target_pairs={{0,1},{1,0},{2,3},{3,2},{4,5},{5,4},{6,7},{7,6},{8,9},{9,8},{10,11... | collective-permute-start | bytes 12296 | tf_op jit(solution)/shard_map/ppermute | solution.py:560
  15.3 0.7 %shard_map.109 = (bf16[32,192]{1,0:T(8,128)(2,1)S(1)}, bf16[896,128]{1,0:T(8,128)(2,1)S(1)}) custom-call(s32[4,2,4]{2,1,0:T(2,128)S(1)} %bitcast.23, s32[32]{0:T(128)S(1)} %copy-done.4), custom_call_target="tpu_custom_call" | custom-call | flops 2000000 | bytes 1000000 | tf_op jit(solution)/shard_map/pallas_call | solution.py:512
  16.0 0.2 shard_map.107.base
  16.2 0.6 %copy-done.2 = f32[8,8,128]{2,1,0:T(8,128)S(1)} copy-done((f32[8,8,128]{2,1,0:T(8,128)S(1)}, f32[8,8,128]{2,1,0:T(8,128)}, u32[]{:S(2)}) %copy-start.2) | copy-done | bytes 32792
  16.8 0.5 %collective-permute-done.6.refs_1_ = f32[8,128]{1,0:T(8,128)S(1)} collective-permute-done((f32[8,128]{1,0:T(8,128)S(1)}, f32[8,128]{1,0:T(8,128)S(1)}, u32[]{:S(2)}, u32[]{:S(2)}) %collective-permute-start.6) | collective-permute-done | bytes 4128 | tf_op jit(solution)/shard_map/ppermute | solution.py:560
  17.4 1.3 %shard_map.110 = (f32[5,64,128]{2,1,0:T(8,128)S(1)}, f32[128,128]{1,0:T(8,128)}, f32[5,8,128]{2,1,0:T(8,128)S(1)}, f32[5,8,128]{2,1,0:T(8,128)S(1)}, f32[5,8,128]{2,1,0:T(8,128)S(1)}, /*index=5*/f32[5,8,128]{2,1,0:T(8,128)S(1)}) custom-call(f32[5,64,128]{2,1,0:T(8,128)S(1)} %shard_map.107.base, f32[6,64,128]{2,1,0:T(8,128)S(1)} %get-tuple-element.27.scaled, ...), custom_call_target="tpu_custom_call" | custom-call | flops 2000000 | bytes 1000000 | tf_op jit(solution)/shard_map/pallas_call | solution.py:512
  18.7 3.5 %all-to-all-start = ((f32[32,4,128]{2,1,0:T(4,128)}), f32[32,4,128]{2,1,0:T(4,128)S(1)}, u32[]{:S(2)}, u32[]{:S(2)}) async-start(f32[32,4,128]{2,1,0:T(4,128)} %bitcast.25), calls=%async_computation | async-start | bytes 131072 | tf_op jit(solution)/shard_map/all_to_all | solution.py:620
  22.1 0.3 %collective-permute-start.10 = (f32[5,8,128]{2,1,0:T(8,128)S(1)}, f32[5,8,128]{2,1,0:T(8,128)S(1)}, u32[]{:S(2)}, u32[]{:S(2)}) collective-permute-start(f32[5,8,128]{2,1,0:T(8,128)S(1)} %get-tuple-element.46), channel_id=1, source_target_pairs={{0,2},{1,3},{2,0},{3,1},{4,6},{5,7},{6,4},{7,5},{8,10},{9,11},{10,... | collective-permute-start | bytes 61448 | tf_op jit(solution)/shard_map/ppermute | solution.py:560
  22.5 0.3 collective-permute-start.11
  22.7 2.9 %collective-permute-start.12 = (f32[5,8,128]{2,1,0:T(8,128)S(1)}, f32[5,8,128]{2,1,0:T(8,128)S(1)}, u32[]{:S(2)}, u32[]{:S(2)}) collective-permute-start(f32[5,8,128]{2,1,0:T(8,128)S(1)} %get-tuple-element.48), channel_id=1, source_target_pairs={{0,8},{1,9},{2,10},{3,11},{4,12},{5,13},{6,14},{7,15},{8,0},{9,1},... | collective-permute-start | bytes 61448 | tf_op jit(solution)/shard_map/ppermute | solution.py:560
  25.6 0.9 %collective-permute-start.13 = (f32[5,8,128]{2,1,0:T(8,128)S(1)}, f32[5,8,128]{2,1,0:T(8,128)S(1)}, u32[]{:S(2)}, u32[]{:S(2)}) collective-permute-start(f32[5,8,128]{2,1,0:T(8,128)S(1)} %get-tuple-element.49), channel_id=1, source_target_pairs={{0,6},{1,7},{2,4},{3,5},{4,2},{5,3},{6,0},{7,1},{8,14},{9,15},{10,... | collective-permute-start | bytes 61448 | tf_op jit(solution)/shard_map/ppermute | solution.py:560
  26.7 0.9 %collective-permute-done.12.refs_2_ = f32[5,8,128]{2,1,0:T(8,128)S(1)} collective-permute-done((f32[5,8,128]{2,1,0:T(8,128)S(1)}, f32[5,8,128]{2,1,0:T(8,128)S(1)}, u32[]{:S(2)}, u32[]{:S(2)}) %collective-permute-start.12) | collective-permute-done | bytes 20512 | tf_op jit(solution)/shard_map/ppermute | solution.py:560
  27.5 1.5 %collective-permute-done.13.refs_3_ = f32[5,8,128]{2,1,0:T(8,128)S(1)} collective-permute-done((f32[5,8,128]{2,1,0:T(8,128)S(1)}, f32[5,8,128]{2,1,0:T(8,128)S(1)}, u32[]{:S(2)}, u32[]{:S(2)}) %collective-permute-start.13) | collective-permute-done | bytes 20512 | tf_op jit(solution)/shard_map/ppermute | solution.py:560
  29.0 0.9 %all-to-all-done = f32[32,4,128]{2,1,0:T(4,128)S(1)} async-done(((f32[32,4,128]{2,1,0:T(4,128)}), f32[32,4,128]{2,1,0:T(4,128)S(1)}, u32[]{:S(2)}, u32[]{:S(2)}) %all-to-all-start) | async-done | bytes 65568 | tf_op jit(solution)/shard_map/all_to_all | solution.py:620
  30.0 0.9 %shard_map.112 = (f32[5,64,128]{2,1,0:T(8,128)}, f32[1,40]{1,0:T(1,128)}) custom-call(f32[5,64,128]{2,1,0:T(8,128)S(1)} %shard_map.111.base, f32[128,128]{1,0:T(8,128)S(1)} %bitcast.20, f32[5,8,128]{2,1,0:T(8,128)S(1)} %collective-permute-done.10.refs_0_, f32[5,8,128]{2,1,0:T(8,128)S(1)} %collective-permute-done.11.refs_1_, ...), custom_call_target="tpu_custom_call" | custom-call | flops 2000000 | bytes 1000000 | tf_op jit(solution)/shard_map/pallas_call | solution.py:512
  (25 shorter events, 0.7 us)
Async XLA Ops:
  0.6 8.5 %copy-start = (f32[5,8,8,128]{3,2,1,0:T(8,128)S(1)}, f32[5,8,8,128]{3,2,1,0:T(8,128)}, u32[]{:S(2)}) copy-start(f32[5,8,8,128]{3,2,1,0:T(8,128)} %param.9) | copy-start | bytes 491524
  0.6 8.5 %copy-start.1 = (f32[8,8,128]{2,1,0:T(8,128)S(1)}, f32[8,8,128]{2,1,0:T(8,128)}, u32[]{:S(2)}) copy-start(f32[8,8,128]{2,1,0:T(8,128)} %param.13) | copy-start | bytes 98308
  1.9 9.3 %collective-permute-start = (f32[6,8,128]{2,1,0:T(8,128)S(1)}, f32[6,8,128]{2,1,0:T(8,128)S(1)}, u32[]{:S(2)}, u32[]{:S(2)}) collective-permute-start(f32[6,8,128]{2,1,0:T(8,128)S(1)} %get-tuple-element.28), channel_id=1, source_target_pairs={{0,2},{1,3},{2,0},{3,1},{4,6},{5,7},{6,4},{7,5},{8,10},{9,11},{10,... | collective-permute-start | bytes 73736 | tf_op jit(solution)/shard_map/ppermute | solution.py:560
  2.4 8.8 %collective-permute-start.2 = (f32[6,8,128]{2,1,0:T(8,128)S(1)}, f32[6,8,128]{2,1,0:T(8,128)S(1)}, u32[]{:S(2)}, u32[]{:S(2)}) collective-permute-start(f32[6,8,128]{2,1,0:T(8,128)S(1)} %get-tuple-element.30), channel_id=1, source_target_pairs={{0,2},{1,3},{2,0},{3,1},{4,6},{5,7},{6,4},{7,5},{8,16},{9,17},{10,... | collective-permute-start | bytes 73736 | tf_op jit(solution)/shard_map/ppermute | solution.py:560
  2.5 8.7 %collective-permute-start.3 = (f32[6,8,128]{2,1,0:T(8,128)S(1)}, f32[6,8,128]{2,1,0:T(8,128)S(1)}, u32[]{:S(2)}, u32[]{:S(2)}) collective-permute-start(f32[6,8,128]{2,1,0:T(8,128)S(1)} %get-tuple-element.31), channel_id=1, source_target_pairs={{0,8},{1,9},{2,10},{3,11},{4,12},{5,13},{6,14},{7,15},{8,0},{9,1},... | collective-permute-start | bytes 73736 | tf_op jit(solution)/shard_map/ppermute | solution.py:560
  6.6 4.6 %collective-permute-start.4 = (f32[6,8,128]{2,1,0:T(8,128)S(1)}, f32[6,8,128]{2,1,0:T(8,128)S(1)}, u32[]{:S(2)}, u32[]{:S(2)}) collective-permute-start(f32[6,8,128]{2,1,0:T(8,128)S(1)} %get-tuple-element.32), channel_id=1, source_target_pairs={{0,6},{1,7},{2,4},{3,5},{4,2},{5,3},{6,0},{7,1},{8,14},{9,15},{10,... | collective-permute-start | bytes 73736 | tf_op jit(solution)/shard_map/ppermute | solution.py:560
  7.6 3.6 %collective-permute-start.1 = (f32[8,128]{1,0:T(8,128)S(1)}, f32[8,128]{1,0:T(8,128)S(1)}, u32[]{:S(2)}, u32[]{:S(2)}) collective-permute-start(f32[8,128]{1,0:T(8,128)S(1)} %get-tuple-element.29), channel_id=1, source_target_pairs={{0,1},{1,0},{2,3},{3,2},{4,5},{5,4},{6,7},{7,6},{8,9},{9,8},{10,11... | collective-permute-start | bytes 12296 | tf_op jit(solution)/shard_map/ppermute | solution.py:560
  11.6 5.8 %collective-permute-start.5 = (f32[5,8,128]{2,1,0:T(8,128)S(1)}, f32[5,8,128]{2,1,0:T(8,128)S(1)}, u32[]{:S(2)}, u32[]{:S(2)}) collective-permute-start(f32[5,8,128]{2,1,0:T(8,128)S(1)} %get-tuple-element.39), channel_id=1, source_target_pairs={{0,2},{1,3},{2,0},{3,1},{4,6},{5,7},{6,4},{7,5},{8,10},{9,11},{10,... | collective-permute-start | bytes 61448 | tf_op jit(solution)/shard_map/ppermute | solution.py:560
  11.7 3.6 %copy-start.3 = (s32[4,4,2]{1,2,0:T(2,128)S(1)}, s32[4,4,2]{1,2,0:T(2,128)}, u32[]{:S(2)}) copy-start(s32[4,4,2]{1,2,0:T(2,128)} %param.16) | copy-start | bytes 388
  11.7 5.7 %collective-permute-start.7 = (f32[5,8,128]{2,1,0:T(8,128)S(1)}, f32[5,8,128]{2,1,0:T(8,128)S(1)}, u32[]{:S(2)}, u32[]{:S(2)}) collective-permute-start(f32[5,8,128]{2,1,0:T(8,128)S(1)} %get-tuple-element.41), channel_id=1, source_target_pairs={{0,2},{1,3},{2,0},{3,1},{4,6},{5,7},{6,4},{7,5},{8,16},{9,17},{10,... | collective-permute-start | bytes 61448 | tf_op jit(solution)/shard_map/ppermute | solution.py:560
  12.2 5.2 %collective-permute-start.8 = (f32[5,8,128]{2,1,0:T(8,128)S(1)}, f32[5,8,128]{2,1,0:T(8,128)S(1)}, u32[]{:S(2)}, u32[]{:S(2)}) collective-permute-start(f32[5,8,128]{2,1,0:T(8,128)S(1)} %get-tuple-element.42), channel_id=1, source_target_pairs={{0,8},{1,9},{2,10},{3,11},{4,12},{5,13},{6,14},{7,15},{8,0},{9,1},... | collective-permute-start | bytes 61448 | tf_op jit(solution)/shard_map/ppermute | solution.py:560
  13.7 3.7 %collective-permute-start.9 = (f32[5,8,128]{2,1,0:T(8,128)S(1)}, f32[5,8,128]{2,1,0:T(8,128)S(1)}, u32[]{:S(2)}, u32[]{:S(2)}) collective-permute-start(f32[5,8,128]{2,1,0:T(8,128)S(1)} %get-tuple-element.43), channel_id=1, source_target_pairs={{0,6},{1,7},{2,4},{3,5},{4,2},{5,3},{6,0},{7,1},{8,14},{9,15},{10,... | collective-permute-start | bytes 61448 | tf_op jit(solution)/shard_map/ppermute | solution.py:560
  13.7 1.5 %copy-start.4 = (s32[32]{0:T(128)S(1)}, s32[32]{0:T(128)}, u32[]{:S(2)}) copy-start(s32[32]{0:T(128)} %owners.1) | copy-start | bytes 388
  13.7 3.6 %collective-permute-start.6 = (f32[8,128]{1,0:T(8,128)S(1)}, f32[8,128]{1,0:T(8,128)S(1)}, u32[]{:S(2)}, u32[]{:S(2)}) collective-permute-start(f32[8,128]{1,0:T(8,128)S(1)} %get-tuple-element.40), channel_id=1, source_target_pairs={{0,1},{1,0},{2,3},{3,2},{4,5},{5,4},{6,7},{7,6},{8,9},{9,8},{10,11... | collective-permute-start | bytes 12296 | tf_op jit(solution)/shard_map/ppermute | solution.py:560
  16.0 0.8 %copy-start.2 = (f32[8,8,128]{2,1,0:T(8,128)S(1)}, f32[8,8,128]{2,1,0:T(8,128)}, u32[]{:S(2)}) copy-start(f32[8,8,128]{2,1,0:T(8,128)} %param.14) | copy-start | bytes 98308
  18.7 11.3 %all-to-all-start = ((f32[32,4,128]{2,1,0:T(4,128)}), f32[32,4,128]{2,1,0:T(4,128)S(1)}, u32[]{:S(2)}, u32[]{:S(2)}) async-start(f32[32,4,128]{2,1,0:T(4,128)} %bitcast.25), calls=%async_computation | async-start | bytes 131072 | tf_op jit(solution)/shard_map/all_to_all | solution.py:620
  22.1 4.5 %collective-permute-start.10 = (f32[5,8,128]{2,1,0:T(8,128)S(1)}, f32[5,8,128]{2,1,0:T(8,128)S(1)}, u32[]{:S(2)}, u32[]{:S(2)}) collective-permute-start(f32[5,8,128]{2,1,0:T(8,128)S(1)} %get-tuple-element.46), channel_id=1, source_target_pairs={{0,2},{1,3},{2,0},{3,1},{4,6},{5,7},{6,4},{7,5},{8,10},{9,11},{10,... | collective-permute-start | bytes 61448 | tf_op jit(solution)/shard_map/ppermute | solution.py:560
  22.5 4.2 %collective-permute-start.11 = (f32[5,8,128]{2,1,0:T(8,128)S(1)}, f32[5,8,128]{2,1,0:T(8,128)S(1)}, u32[]{:S(2)}, u32[]{:S(2)}) collective-permute-start(f32[5,8,128]{2,1,0:T(8,128)S(1)} %get-tuple-element.47), channel_id=1, source_target_pairs={{0,2},{1,3},{2,0},{3,1},{4,6},{5,7},{6,4},{7,5},{8,16},{9,17},{10,... | collective-permute-start | bytes 61448 | tf_op jit(solution)/shard_map/ppermute | solution.py:560
  22.7 4.8 %collective-permute-start.12 = (f32[5,8,128]{2,1,0:T(8,128)S(1)}, f32[5,8,128]{2,1,0:T(8,128)S(1)}, u32[]{:S(2)}, u32[]{:S(2)}) collective-permute-start(f32[5,8,128]{2,1,0:T(8,128)S(1)} %get-tuple-element.48), channel_id=1, source_target_pairs={{0,8},{1,9},{2,10},{3,11},{4,12},{5,13},{6,14},{7,15},{8,0},{9,1},... | collective-permute-start | bytes 61448 | tf_op jit(solution)/shard_map/ppermute | solution.py:560
  25.6 3.4 %collective-permute-start.13 = (f32[5,8,128]{2,1,0:T(8,128)S(1)}, f32[5,8,128]{2,1,0:T(8,128)S(1)}, u32[]{:S(2)}, u32[]{:S(2)}) collective-permute-start(f32[5,8,128]{2,1,0:T(8,128)S(1)} %get-tuple-element.49), channel_id=1, source_target_pairs={{0,6},{1,7},{2,4},{3,5},{4,2},{5,3},{6,0},{7,1},{8,14},{9,15},{10,... | collective-permute-start | bytes 61448 | tf_op jit(solution)/shard_map/ppermute | solution.py:560

commit v7 on v6

--- a/solution.py
+++ b/solution.py
@@ -126,7 +126,9 @@
         y_low.append(source[row_at(0), :])
         y_high.append(source[row_at(CY - 1), :])
         z_fields.append([source[tile_at(x), :] for x in range(CX)])
-    outs[2][0][...] = pack_lanes(z_fields)
+    outs[2][0][0] = pack_lanes(z_fields)
+    for index in range(1, outs[2][0].shape[0]):
+        outs[2][0][index] = jnp.zeros(TILE, jnp.float32)
     put_pair(x_low, x_high, here[0], outs[0])
     put_pair(y_low, y_high, here[1], outs[1])
 
@@ -147,8 +149,7 @@
 
 
 def sorted_lanes(refs, position, size):
-    first, second = refs
-    return sort_pair(first[...], None if second is None else second[...], position, size)
+    return sorted_field(refs, 0, position, size)
 
 
 def add_halo(base, received, weight, sizes, out, finish=None, z_halo=None):
@@ -179,36 +180,36 @@
             finish(component)
 
 
-ORDER = ((1, 0), (2, 0), (0, 1), (0, 0), (1, 1), (2, 1))
-
-
-def message_keys(sizes, sent, with_z=True):
-    keys = [key for key in ORDER if key[1] == 0 or sizes[key[0]] > 2]
-    keys = [key for key in keys if with_z or key[0] != 2]
+ORDERS = (
+    ((1, 0), (0, 1), (0, 0), (1, 1), (2, 0), (2, 1)),
+    ((1, 0), (0, 1), (0, 0), (1, 1)),
+    ((1, 0), (0, 1), (0, 0), (1, 1)),
+)
+
+
+def message_keys(sizes, sent, stage):
+    keys = [key for key in ORDERS[stage] if key[1] == 0 or sizes[key[0]] > 2]
     return [key for key in keys if not (sent and key == (2, 1))]
 
 
-def split(refs, sizes, sent=False, with_z=True):
+def split(refs, sizes, stage, sent=False):
     refs, out = list(refs), [[None, None] for axis in range(3)]
-    for axis, which in message_keys(sizes, sent, with_z):
+    for axis, which in message_keys(sizes, sent, stage):
         out[axis][which] = refs.pop(0)
     return out, refs
 
 
-def first_kernel(sizes, level, adjoint, density, velocity, stiffness, source, scaled, *refs):
-    outs, scratch = split(refs, sizes, True)
-    level_now, adjoint_now, density_now, velocity_now, stiffness_now, source_now, arrived = scratch
-    pairs = (
-        (level, level_now),
-        (density, density_now),
-        (velocity, velocity_now),
-        (stiffness, stiffness_now),
-        (adjoint, adjoint_now),
-        (source, source_now),
-    )
+def first_kernel(
+    sizes, level, adjoint, density, velocity, stiffness, sponge, source, scaled, base, *refs
+):
+    outs, scratch = split(refs, sizes, 0, True)
+    *targets, arrived = scratch
+    level_now, adjoint_now, density_now, velocity_now, stiffness_now, sponge_now, source_now = targets
     copies = [
         pltpu.make_async_copy(there, here, arrived.at[index])
-        for index, (there, here) in enumerate(pairs)
+        for index, (there, here) in enumerate(
+            zip((level, adjoint, density, velocity, stiffness, sponge, source), targets)
+        )
     ]
     for copy in copies:
         copy.start()
@@ -222,12 +223,37 @@
     scaled[3] = half_inverse * density_now[...]
     scaled[4] = half_inverse * stiffness_now[...]
     scaled[5] = half_inverse / density_now[...]
-    put_messages(adjoint_now, scaled, source_now, outs)
-
-
-def own_kernel(weights, scaled, sponge, *refs):
+    tiles = own_part((0.0, 1.0), scaled, sponge_now, None, adjoint_now, base)
+    x_low = tiles[0][0] + [source_now[tile_at(0), :]]
+    x_high = tiles[CX - 1][0] + [source_now[tile_at(CX - 1), :]]
+    y_low = faces_at(adjoint_now, scaled, row_at(0), 1) + [source_now[row_at(0), :]]
+    y_high = faces_at(adjoint_now, scaled, row_at(CY - 1), 1) + [source_now[row_at(CY - 1), :]]
+    put_pair(x_low, x_high, here[0], outs[0])
+    put_pair(y_low, y_high, here[1], outs[1])
+    along = [
+        [[tiles[x][direction][component] for x in range(CX)] for component in range(5)]
+        for direction in range(3)
+    ]
+    along[2].append([source_now[tile_at(x), :] for x in range(CX)])
+    for index, fields in enumerate(
+        (
+            along[2],
+            [[base[component, tile_at(x), :] for x in range(CX)] for component in range(5)],
+            along[0],
+            along[1],
+            [[scaled[row, tile_at(x), :] for x in range(CX)] for row in range(2, 6)],
+        )
+    ):
+        outs[2][0][index] = pack_lanes(fields)
+    outs[2][0][5] = jnp.zeros(TILE, jnp.float32)
+
+
+def own_kernel(weights, scaled, sponge, start, state, out):
+    own_part(weights, scaled, sponge, start, state, out)
+
+
+def own_part(weights, scaled, sponge, start, state, out):
     keep, blend = weights
-    start, state, out = refs if keep else (None,) + refs
     rows = lax.broadcasted_iota(jnp.int32, TILE, 0)
     lanes = lax.broadcasted_iota(jnp.int32, TILE, 1)
     tiles = [
@@ -254,10 +280,11 @@
             if keep:
                 value = value + keep * start[component, tile_at(x), :]
             out[component, tile_at(x), :] = value
+    return tiles
 
 
 def shape_kernel(sizes, source, scaled, sponge, start, *refs):
-    sources, (shapes, sums, faces) = split(refs, sizes)
+    sources, (shapes, sums, faces) = split(refs, sizes, 0)
     rows = lax.broadcasted_iota(jnp.int32, TILE, 0)
     lanes = lax.broadcasted_iota(jnp.int32, TILE, 1)
     outer = step_length * two_thirds
@@ -318,9 +345,65 @@
 
 
 def stage_kernel(sizes, weight, base, scaled, *refs):
-    received, (section, *outs) = split(refs, sizes)
+    received, (section, *outs) = split(refs, sizes, 0)
     add_halo(base, received, weight, sizes, section)
-    put_messages(section, scaled, None, split(outs, sizes, True)[0])
+    outs = split(outs, sizes, 1, True)[0]
+    here = positions()
+    x_low, x_high, y_low, y_high, z_fields = outer_faces(section, scaled)
+    lanes = lax.broadcasted_iota(jnp.int32, TILE, 1)
+    rows = lax.broadcasted_iota(jnp.int32, TILE, 0)
+    place = (lanes + (CZ - BASE)) % CZ // 2 % CX
+    x_below, x_above = sorted_field(received[2], 2, here[2], sizes[2])
+    y_below, y_above = sorted_field(received[2], 3, here[2], sizes[2])
+    far = 2 * (CX - 1)
+    x_high.append(jnp.where(place == 0, both_layers(x_below, x_above, -far), 0.0))
+    x_low.append(jnp.where(place == CX - 1, both_layers(x_below, x_above, far), 0.0))
+    y_layers = both_layers(y_below, y_above, 0)
+    y_high.append(jnp.where(rows == 0, pltpu.roll(y_layers, 1, 0), 0.0))
+    y_low.append(jnp.where(rows == CY - 1, pltpu.roll(y_layers, CY - 1, 0), 0.0))
+    put_pair(x_low, x_high, here[0], outs[0])
+    put_pair(y_low, y_high, here[1], outs[1])
+
+
+def both_layers(below, above, shift):
+    lanes = lax.broadcasted_iota(jnp.int32, TILE, 1)
+    return jnp.where(
+        lanes % 2 == 0,
+        pltpu.roll(above, (shift - 1) % CZ, 1),
+        pltpu.roll(below, (shift + 1) % CZ, 1),
+    )
+
+
+def layer_partials(state, layer):
+    group = 2 * CX
+    return (
+        layer[0] * state
+        + layer[1] * pltpu.roll(state, 3 * group, 1)
+        + layer[2] * pltpu.roll(state, CZ - group, 1)
+        + layer[3] * pltpu.roll(state, group, 1)
+    )
+
+
+def layer_kernel(sizes, own, *refs):
+    received, (layer, known) = split(refs, sizes, 0)
+    here = positions()
+    lanes = lax.broadcasted_iota(jnp.int32, TILE, 1)
+    even = lanes % 2 == 0
+    inside = (lanes >= BASE) & (lanes < BASE + 5 * 2 * CX)
+    group = (lanes - BASE) // (2 * CX)
+    below, above = sorted_field(received[2], 4, here[2], sizes[2])
+    packed = jnp.where(even, 1.0, -1.0) * both_layers(below, above, 0)
+    speed = jnp.zeros(TILE, jnp.float32)
+    for component in range(5):
+        speed = jnp.where(group == component, pltpu.roll(packed, 2 * CX * component, 1), speed)
+    layer[0] = jnp.where(inside, speed, 0.0)
+    layer[1] = jnp.where(inside & (group == 3), pltpu.roll(packed, 2 * CX * 2, 1), 0.0)
+    layer[2] = jnp.where(inside & (group == 3), pltpu.roll(packed, 2 * CX, 1), 0.0)
+    layer[3] = jnp.where(inside & (group == 4), pltpu.roll(packed, 2 * CX, 1), 0.0)
+    below, above = sorted_field(received[2], 1, here[2], sizes[2])
+    state = both_layers(below, above, 0)
+    state = state + step_length * jnp.where(even, -own[0], own[0])
+    known[...] = layer_partials(jnp.where(inside, state, 0.0), layer)
 
 
 def sublane_total(tile):
@@ -383,10 +466,17 @@
 )
 
 
-def gradient_kernel(sizes, weight, base, scaled, shapes, sums, faces, routes, gather, *refs):
-    received, (section, table, *rest) = split(refs, sizes)
-    outs, (rows_out, sent) = split(rest, sizes, True, False)
-    add_halo(base, received, weight, sizes, section)
+def gradient_kernel(
+    sizes, weight, base, scaled, shapes, sums, faces, routes, gather, layer, known, *refs
+):
+    received, (section, table, *rest) = split(refs, sizes, 1)
+    outs, (rows_out, sent) = split(rest, sizes, 2, True)
+    here = positions()
+    x_below, x_above = sorted_field(received[0], 5, here[0], sizes[0])
+    y_below, y_above = sorted_field(received[1], 5, here[1], sizes[1])
+    late = step_length * ((x_above - x_below) + (y_above - y_below))
+    z_halo = known[...] + layer_partials(late, layer)
+    add_halo(base, received, weight, sizes, section, z_halo=z_halo)
     x_low, x_high, y_low, y_high, z_fields = outer_faces(section, scaled)
     packed = pack_lanes(z_fields)
     main = [sums[component] for component in range(5)]
@@ -436,7 +526,6 @@
         preferred_element_type=jnp.float32,
     )
     lanes = lax.broadcasted_iota(jnp.int32, TILE, 1)
-    here = positions()
     own_place = (here[0] * sizes[1] + here[1]) * sizes[2] + here[2]
     paired = pltpu.roll(packed, CY - SHARE, 0)
     up = jnp.where(lanes % 2 == 0, packed, pltpu.roll(paired, 1, 1))[:SHARE]
@@ -458,7 +547,7 @@
 
 
 def last_kernel(sizes, base, table, *refs):
-    received, (out, gradient, done, block, sent) = split(refs, sizes, False, False)
+    received, (out, gradient, done, block, sent) = split(refs, sizes, 2)
     devices = table.shape[0] // SHARE
     here = positions()
     own_place = (here[0] * sizes[1] + here[1]) * sizes[2] + here[2]
@@ -547,36 +636,39 @@
     level = jnp.transpose(brick_level, (0, 2, 1))
     patches = jnp.transpose(brick_patch, (0, 2, 1))
 
-    def message_shapes(fields, with_z=True):
+    def message_shapes(fields, stage):
         return [
-            TILE if key[0] == 2 else (fields,) + TILE
-            for key in message_keys(sizes, True, with_z)
+            (fields,) + TILE for key in message_keys(sizes, True, stage)
         ]
 
-    def exchange(messages, with_z=True):
-        sends = dict(zip(message_keys(sizes, True, with_z), messages))
+    def exchange(messages, stage):
+        sends = dict(zip(message_keys(sizes, True, stage), messages))
         sends[2, 1] = sends.get((2, 0))
         return [
             lax.ppermute(sends[key], AXES, permutations[key[0]][key[1]])
-            for key in message_keys(sizes, False, with_z)
+            for key in message_keys(sizes, False, stage)
         ]
 
-    scaled, *sent = call(
+    flat = pltpu.VMEM(FLAT, jnp.float32)
+    state = pltpu.VMEM(STATE, jnp.float32)
+    scaled, base, *sent = call(
         functools.partial(first_kernel, sizes),
-        [HBM] * 6,
-        (level, start, density, velocity, stiffness, source),
-        [(6,) + FLAT] + message_shapes(6),
+        [HBM] * 7,
+        (level, start, density, velocity, stiffness, sponge, source),
+        [(6,) + FLAT, STATE] + message_shapes(6, 0),
         scratch=[
             pltpu.SMEM(level.shape, jnp.int32),
-            pltpu.VMEM(STATE, jnp.float32),
-            pltpu.VMEM(FLAT, jnp.float32),
+            state,
+            flat,
             pltpu.VMEM((3,) + FLAT, jnp.float32),
-            pltpu.VMEM(FLAT, jnp.float32),
-            pltpu.VMEM(FLAT, jnp.float32),
-            pltpu.SemaphoreType.DMA((6,)),
+            flat,
+            flat,
+            flat,
+            pltpu.SemaphoreType.DMA((7,)),
         ],
     )
-    received_one = exchange(sent)
+    received_one = exchange(sent, 0)
+    own_layers = dict(zip(message_keys(sizes, True, 0), sent))[2, 0]
     routes, gather = call(
         functools.partial(target_kernel, sizes),
         [SMEM] * 2,
@@ -584,17 +676,21 @@
         [(devices, 3 * CY * CY), (7 * CZ, CZ)],
         dtype=jnp.bfloat16,
     )
-    (base,) = call(
-        functools.partial(own_kernel, (0.0, 1.0)), [VMEM] * 3, (scaled, sponge, start), [STATE]
-    )
     operands = (base, scaled, *received_one)
     section, *sent = call(
         functools.partial(stage_kernel, sizes, step_length),
         [VMEM] * len(operands),
         operands,
-        [STATE] + message_shapes(5),
-    )
-    received = exchange(sent)
+        [STATE] + message_shapes(6, 1),
+    )
+    received = exchange(sent, 1)
+    operands = (own_layers, *received_one)
+    layer, known = call(
+        functools.partial(layer_kernel, sizes),
+        [VMEM] * len(operands),
+        operands,
+        [(4,) + TILE, TILE],
+    )
     (base,) = call(
         functools.partial(own_kernel, (0.75, 0.25)),
         [VMEM] * 4,
@@ -608,17 +704,17 @@
         operands,
         [(7,) + FLAT, (5,) + TILE, (6,) + TILE],
     )
-    operands = (base, scaled, shapes, sums, faces, routes, gather, *received)
+    operands = (base, scaled, shapes, sums, faces, routes, gather, layer, known, *received)
     section, table, *sent = call(
         functools.partial(gradient_kernel, sizes, 0.25 * step_length),
         [VMEM] * len(operands),
         operands,
-        [STATE, (devices * SHARE, CZ)] + message_shapes(5, False),
+        [STATE, (devices * SHARE, CZ)] + message_shapes(5, 2),
         scratch=[pltpu.VMEM((devices * SHARE, CZ), jnp.float32), pltpu.SemaphoreType.DMA],
-        spaces=[pltpu.VMEM, pltpu.HBM] + [pltpu.VMEM] * len(message_shapes(5, False)),
+        spaces=[pltpu.VMEM, pltpu.HBM] + [pltpu.VMEM] * len(message_shapes(5, 2)),
     )
     table = lax.all_to_all(table.reshape(devices, SHARE, CZ), AXES, 0, 0, tiled=True)
-    received = exchange(sent, False)
+    received = exchange(sent, 2)
     (base,) = call(
         functools.partial(own_kernel, (third, two_thirds)),
         [VMEM] * 4,

time: 31.1 us -> 30.3 us (0.974)
  starting transfers between devices: 18.7 us -> 16.3 us
  waiting for transfers between devices: 5.78 us -> 6.63 us
  local copies, waits for them, and re-layouts: 0.58 us -> 1.18 us
    ppermute x14 -> x13, starting transfers between devices: 15.2 us -> 13.7 us  [exchange(): lax.ppermute(sends[key], AXES, permutations[key[0]][key[1]])]
    all_to_all x1, starting transfers between devices: 3.48 us -> 2.61 us  [body(): lax.all_to_all(table.reshape(devices, SHARE, CZ), AXES, 0, 0, tiled=True)]
    ppermute x14 -> x13, waiting for transfers between devices: 4.83 us -> 5.68 us  [exchange(): lax.ppermute(sends[key], AXES, permutations[key[0]][key[1]])]
    unnamed x10, local copies, waits for them, and re-layouts: 0.58 us -> 1.18 us
  transfers between devices with their start and end apart: 15 -> 14, of which waited for: 5 -> 6; matrix products, arithmetic and copies ran while one was open for 0% -> 0% of each run, Pallas kernels for 4% -> 4%
where the time goes in v7:
time: 30.3 us; the launch traced here: 30.1 us
  starting transfers between devices  16.3 us (54%)
  waiting for transfers between devices  6.63 us (22%)
  Pallas kernels  5.15 us (17%)
  local copies, waits for them, and re-layouts  1.18 us (4%)
  between operations  0.78 us (3%)
    ppermute x13, starting transfers between devices, exchange(): lax.ppermute(sends[key], AXES, permutations[key[0]][key[1]])  13.7 us
    ppermute x13, waiting for transfers between devices, exchange(): lax.ppermute(sends[key], AXES, permutations[key[0]][key[1]])  5.68 us
    pallas_call x9, Pallas kernels, call(): pl.pallas_call(kernel, out_shape=[space(shape, dtype) for space, shape in...  5.15 us
    all_to_all x1, starting transfers between devices, body(): lax.all_to_all(table.reshape(devices, SHARE, CZ), AXES, 0, 0, tiled=True)  2.61 us
    unnamed x10, local copies, waits for them, and re-layouts  1.18 us
    all_to_all x1, waiting for transfers between devices, body(): lax.all_to_all(table.reshape(devices, SHARE, CZ), AXES, 0, 0, tiled=True)  0.95 us
  transfers between devices with their start and end apart: 14, of which 6 were waited for; matrix products, arithmetic and copies ran while one was open for 0% of the time, Pallas kernels for 4%

profile of v7, /device:TPU:0, one launch (start us, length us, event | category | flops | bytes accessed | tf_op | source)
XLA Modules:
  0.0 30.1 jit_solution(11524902749231644527)
XLA Ops:
  0.6 1.5 %shard_map.104 = (f32[6,64,128]{2,1,0:T(8,128)S(1)}, f32[5,64,128]{2,1,0:T(8,128)S(1)}, f32[6,8,128]{2,1,0:T(8,128)S(1)}, f32[6,8,128]{2,1,0:T(8,128)S(1)}, f32[...) custom-call(s32[4,2,4]{2,1,0:T(2,128)} %bitcast.27, f32[5,64,128]{2,1,0:T(8,128)} %bitcast.11, ...), custom_call_target="tpu_custom_call" | custom-call | flops 2000000 | bytes 1000000 | tf_op jit(solution)/shard_map/pallas_call | solution.py:601
  2.1 0.5 %collective-permute-start = (f32[6,8,128]{2,1,0:T(8,128)S(1)}, f32[6,8,128]{2,1,0:T(8,128)S(1)}, u32[]{:S(2)}, u32[]{:S(2)}) collective-permute-start(f32[6,8,128]{2,1,0:T(8,128)S(1)} %get-tuple-element.31), channel_id=1, source_target_pairs={{0,2},{1,3},{2,0},{3,1},{4,6},{5,7},{6,4},{7,5},{8,10},{9,11},{10,... | collective-permute-start | bytes 73736 | tf_op jit(solution)/shard_map/ppermute | solution.py:648
  2.7 4.1 %collective-permute-start.2 = (f32[6,8,128]{2,1,0:T(8,128)S(1)}, f32[6,8,128]{2,1,0:T(8,128)S(1)}, u32[]{:S(2)}, u32[]{:S(2)}) collective-permute-start(f32[6,8,128]{2,1,0:T(8,128)S(1)} %get-tuple-element.33), channel_id=1, source_target_pairs={{0,8},{1,9},{2,10},{3,11},{4,12},{5,13},{6,14},{7,15},{8,0},{9,1},... | collective-permute-start | bytes 73736 | tf_op jit(solution)/shard_map/ppermute | solution.py:648
  6.8 1.0 %collective-permute-start.3 = (f32[6,8,128]{2,1,0:T(8,128)S(1)}, f32[6,8,128]{2,1,0:T(8,128)S(1)}, u32[]{:S(2)}, u32[]{:S(2)}) collective-permute-start(f32[6,8,128]{2,1,0:T(8,128)S(1)} %get-tuple-element.34), channel_id=1, source_target_pairs={{0,6},{1,7},{2,4},{3,5},{4,2},{5,3},{6,0},{7,1},{8,14},{9,15},{10,... | collective-permute-start | bytes 73736 | tf_op jit(solution)/shard_map/ppermute | solution.py:648
  7.8 1.5 %collective-permute-start.4 = (f32[6,8,128]{2,1,0:T(8,128)S(1)}, f32[6,8,128]{2,1,0:T(8,128)S(1)}, u32[]{:S(2)}, u32[]{:S(2)}) collective-permute-start(f32[6,8,128]{2,1,0:T(8,128)S(1)} %get-tuple-element.35.own), channel_id=1, source_target_pairs={{0,1},{1,0},{2,3},{3,2},{4,5},{5,4},{6,7},{7,6},{8,9},{9,8},{10,11... | collective-permute-start | bytes 73736 | tf_op jit(solution)/shard_map/ppermute | solution.py:648
  9.4 0.9 %collective-permute-done.3.refs_3_ = f32[6,8,128]{2,1,0:T(8,128)S(1)} collective-permute-done((f32[6,8,128]{2,1,0:T(8,128)S(1)}, f32[6,8,128]{2,1,0:T(8,128)S(1)}, u32[]{:S(2)}, u32[]{:S(2)}) %collective-permute-start.3) | collective-permute-done | bytes 24608 | tf_op jit(solution)/shard_map/ppermute | solution.py:648
  10.3 1.4 %collective-permute-done.4.refs_4_ = f32[6,8,128]{2,1,0:T(8,128)S(1)} collective-permute-done((f32[6,8,128]{2,1,0:T(8,128)S(1)}, f32[6,8,128]{2,1,0:T(8,128)S(1)}, u32[]{:S(2)}, u32[]{:S(2)}) %collective-permute-start.4) | collective-permute-done | bytes 24608 | tf_op jit(solution)/shard_map/ppermute | solution.py:648
  11.7 0.2 shard_map.105
  12.0 0.5 %collective-permute-start.6 = (f32[6,8,128]{2,1,0:T(8,128)S(1)}, f32[6,8,128]{2,1,0:T(8,128)S(1)}, u32[]{:S(2)}, u32[]{:S(2)}) collective-permute-start(f32[6,8,128]{2,1,0:T(8,128)S(1)} %get-tuple-element.45), channel_id=1, source_target_pairs={{0,2},{1,3},{2,0},{3,1},{4,6},{5,7},{6,4},{7,5},{8,16},{9,17},{10,... | collective-permute-start | bytes 73736 | tf_op jit(solution)/shard_map/ppermute | solution.py:648
  12.5 1.5 %collective-permute-start.7 = (f32[6,8,128]{2,1,0:T(8,128)S(1)}, f32[6,8,128]{2,1,0:T(8,128)S(1)}, u32[]{:S(2)}, u32[]{:S(2)}) collective-permute-start(f32[6,8,128]{2,1,0:T(8,128)S(1)} %get-tuple-element.46), channel_id=1, source_target_pairs={{0,8},{1,9},{2,10},{3,11},{4,12},{5,13},{6,14},{7,15},{8,0},{9,1},... | collective-permute-start | bytes 73736 | tf_op jit(solution)/shard_map/ppermute | solution.py:648
  14.1 0.6 %copy-done.4 = s32[32]{0:T(128)S(1)} copy-done((s32[32]{0:T(128)S(1)}, s32[32]{0:T(128)}, u32[]{:S(2)}) %copy-start.4) | copy-done | bytes 152
  14.6 0.7 %shard_map.108 = (bf16[32,192]{1,0:T(8,128)(2,1)S(1)}, bf16[896,128]{1,0:T(8,128)(2,1)S(1)}) custom-call(s32[4,2,4]{2,1,0:T(2,128)S(1)} %bitcast.22, s32[32]{0:T(128)S(1)} %copy-done.4), custom_call_target="tpu_custom_call" | custom-call | flops 2000000 | bytes 1000000 | tf_op jit(solution)/shard_map/pallas_call | solution.py:601
  15.7 0.6 %copy-done.2 = f32[8,8,128]{2,1,0:T(8,128)S(1)} copy-done((f32[8,8,128]{2,1,0:T(8,128)S(1)}, f32[8,8,128]{2,1,0:T(8,128)}, u32[]{:S(2)}) %copy-start.2) | copy-done | bytes 32792
  16.4 1.0 %collective-permute-done.8.refs_3_ = f32[6,8,128]{2,1,0:T(8,128)S(1)} collective-permute-done((f32[6,8,128]{2,1,0:T(8,128)S(1)}, f32[6,8,128]{2,1,0:T(8,128)S(1)}, u32[]{:S(2)}, u32[]{:S(2)}) %collective-permute-start.8) | collective-permute-done | bytes 24608 | tf_op jit(solution)/shard_map/ppermute | solution.py:648
  17.4 1.3 %shard_map.110 = (f32[5,64,128]{2,1,0:T(8,128)S(1)}, f32[128,128]{1,0:T(8,128)}, f32[5,8,128]{2,1,0:T(8,128)S(1)}, f32[5,8,128]{2,1,0:T(8,128)S(1)}, f32[5,8,128]{2,1,0:T(8,128)S(1)}, /*index=5*/f32[5,8,128]{2,1,0:T(8,128)S(1)}) custom-call(f32[5,64,128]{2,1,0:T(8,128)S(1)} %shard_map.106.base, f32[6,64,128]{2,1,0:T(8,128)S(1)} %get-tuple-element.29.scaled, ...), custom_call_target="tpu_custom_call" | custom-call | flops 2000000 | bytes 1000000 | tf_op jit(solution)/shard_map/pallas_call | solution.py:601
  18.7 2.6 %all-to-all-start = ((f32[32,4,128]{2,1,0:T(4,128)}), f32[32,4,128]{2,1,0:T(4,128)S(1)}, u32[]{:S(2)}, u32[]{:S(2)}) async-start(f32[32,4,128]{2,1,0:T(4,128)} %bitcast.24), calls=%async_computation | async-start | bytes 131072 | tf_op jit(solution)/shard_map/all_to_all | solution.py:716
  21.3 0.3 %collective-permute-start.9 = (f32[5,8,128]{2,1,0:T(8,128)S(1)}, f32[5,8,128]{2,1,0:T(8,128)S(1)}, u32[]{:S(2)}, u32[]{:S(2)}) collective-permute-start(f32[5,8,128]{2,1,0:T(8,128)S(1)} %get-tuple-element.50), channel_id=1, source_target_pairs={{0,2},{1,3},{2,0},{3,1},{4,6},{5,7},{6,4},{7,5},{8,10},{9,11},{10,... | collective-permute-start | bytes 61448 | tf_op jit(solution)/shard_map/ppermute | solution.py:648
  21.6 0.3 collective-permute-start.10
  21.9 2.9 %collective-permute-start.11 = (f32[5,8,128]{2,1,0:T(8,128)S(1)}, f32[5,8,128]{2,1,0:T(8,128)S(1)}, u32[]{:S(2)}, u32[]{:S(2)}) collective-permute-start(f32[5,8,128]{2,1,0:T(8,128)S(1)} %get-tuple-element.52), channel_id=1, source_target_pairs={{0,8},{1,9},{2,10},{3,11},{4,12},{5,13},{6,14},{7,15},{8,0},{9,1},... | collective-permute-start | bytes 61448 | tf_op jit(solution)/shard_map/ppermute | solution.py:648
  24.8 0.9 %collective-permute-start.12 = (f32[5,8,128]{2,1,0:T(8,128)S(1)}, f32[5,8,128]{2,1,0:T(8,128)S(1)}, u32[]{:S(2)}, u32[]{:S(2)}) collective-permute-start(f32[5,8,128]{2,1,0:T(8,128)S(1)} %get-tuple-element.53), channel_id=1, source_target_pairs={{0,6},{1,7},{2,4},{3,5},{4,2},{5,3},{6,0},{7,1},{8,14},{9,15},{10,... | collective-permute-start | bytes 61448 | tf_op jit(solution)/shard_map/ppermute | solution.py:648
  25.8 0.9 %collective-permute-done.11.refs_2_ = f32[5,8,128]{2,1,0:T(8,128)S(1)} collective-permute-done((f32[5,8,128]{2,1,0:T(8,128)S(1)}, f32[5,8,128]{2,1,0:T(8,128)S(1)}, u32[]{:S(2)}, u32[]{:S(2)}) %collective-permute-start.11) | collective-permute-done | bytes 20512 | tf_op jit(solution)/shard_map/ppermute | solution.py:648
  26.7 1.5 %collective-permute-done.12.refs_3_ = f32[5,8,128]{2,1,0:T(8,128)S(1)} collective-permute-done((f32[5,8,128]{2,1,0:T(8,128)S(1)}, f32[5,8,128]{2,1,0:T(8,128)S(1)}, u32[]{:S(2)}, u32[]{:S(2)}) %collective-permute-start.12) | collective-permute-done | bytes 20512 | tf_op jit(solution)/shard_map/ppermute | solution.py:648
  28.2 0.9 %all-to-all-done = f32[32,4,128]{2,1,0:T(4,128)S(1)} async-done(((f32[32,4,128]{2,1,0:T(4,128)}), f32[32,4,128]{2,1,0:T(4,128)S(1)}, u32[]{:S(2)}, u32[]{:S(2)}) %all-to-all-start) | async-done | bytes 65568 | tf_op jit(solution)/shard_map/all_to_all | solution.py:716
  29.2 0.9 %shard_map.112 = (f32[5,64,128]{2,1,0:T(8,128)}, f32[1,40]{1,0:T(1,128)}) custom-call(f32[5,64,128]{2,1,0:T(8,128)S(1)} %shard_map.111.base, f32[128,128]{1,0:T(8,128)S(1)} %bitcast.19, f32[5,8,128]{2,1,0:T(8,128)S(1)} %collective-permute-done.9.refs_0_, f32[5,8,128]{2,1,0:T(8,128)S(1)} %collective-permute-done.10.refs_1_, ...), custom_call_target="tpu_custom_call" | custom-call | flops 2000000 | bytes 1000000 | tf_op jit(solution)/shard_map/pallas_call | solution.py:601
  (23 shorter events, 0.9 us)
Async XLA Ops:
  2.1 7.2 %collective-permute-start = (f32[6,8,128]{2,1,0:T(8,128)S(1)}, f32[6,8,128]{2,1,0:T(8,128)S(1)}, u32[]{:S(2)}, u32[]{:S(2)}) collective-permute-start(f32[6,8,128]{2,1,0:T(8,128)S(1)} %get-tuple-element.31), channel_id=1, source_target_pairs={{0,2},{1,3},{2,0},{3,1},{4,6},{5,7},{6,4},{7,5},{8,10},{9,11},{10,... | collective-permute-start | bytes 73736 | tf_op jit(solution)/shard_map/ppermute | solution.py:648
  2.6 6.7 %collective-permute-start.1 = (f32[6,8,128]{2,1,0:T(8,128)S(1)}, f32[6,8,128]{2,1,0:T(8,128)S(1)}, u32[]{:S(2)}, u32[]{:S(2)}) collective-permute-start(f32[6,8,128]{2,1,0:T(8,128)S(1)} %get-tuple-element.32), channel_id=1, source_target_pairs={{0,2},{1,3},{2,0},{3,1},{4,6},{5,7},{6,4},{7,5},{8,16},{9,17},{10,... | collective-permute-start | bytes 73736 | tf_op jit(solution)/shard_map/ppermute | solution.py:648
  2.7 6.7 %collective-permute-start.2 = (f32[6,8,128]{2,1,0:T(8,128)S(1)}, f32[6,8,128]{2,1,0:T(8,128)S(1)}, u32[]{:S(2)}, u32[]{:S(2)}) collective-permute-start(f32[6,8,128]{2,1,0:T(8,128)S(1)} %get-tuple-element.33), channel_id=1, source_target_pairs={{0,8},{1,9},{2,10},{3,11},{4,12},{5,13},{6,14},{7,15},{8,0},{9,1},... | collective-permute-start | bytes 73736 | tf_op jit(solution)/shard_map/ppermute | solution.py:648
  6.8 3.4 %collective-permute-start.3 = (f32[6,8,128]{2,1,0:T(8,128)S(1)}, f32[6,8,128]{2,1,0:T(8,128)S(1)}, u32[]{:S(2)}, u32[]{:S(2)}) collective-permute-start(f32[6,8,128]{2,1,0:T(8,128)S(1)} %get-tuple-element.34), channel_id=1, source_target_pairs={{0,6},{1,7},{2,4},{3,5},{4,2},{5,3},{6,0},{7,1},{8,14},{9,15},{10,... | collective-permute-start | bytes 73736 | tf_op jit(solution)/shard_map/ppermute | solution.py:648
  7.8 3.8 %collective-permute-start.4 = (f32[6,8,128]{2,1,0:T(8,128)S(1)}, f32[6,8,128]{2,1,0:T(8,128)S(1)}, u32[]{:S(2)}, u32[]{:S(2)}) collective-permute-start(f32[6,8,128]{2,1,0:T(8,128)S(1)} %get-tuple-element.35.own), channel_id=1, source_target_pairs={{0,1},{1,0},{2,3},{3,2},{4,5},{5,4},{6,7},{7,6},{8,9},{9,8},{10,11... | collective-permute-start | bytes 73736 | tf_op jit(solution)/shard_map/ppermute | solution.py:648
  11.6 3.7 %copy-start = (f32[5,8,8,128]{3,2,1,0:T(8,128)S(1)}, f32[5,8,8,128]{3,2,1,0:T(8,128)}, u32[]{:S(2)}) copy-start(f32[5,8,8,128]{3,2,1,0:T(8,128)} %param.9) | copy-start | bytes 491524
  11.6 3.7 %copy-start.1 = (f32[8,8,128]{2,1,0:T(8,128)S(1)}, f32[8,8,128]{2,1,0:T(8,128)}, u32[]{:S(2)}) copy-start(f32[8,8,128]{2,1,0:T(8,128)} %param.13) | copy-start | bytes 98308
  11.9 2.2 %copy-start.3 = (s32[4,4,2]{1,2,0:T(2,128)S(1)}, s32[4,4,2]{1,2,0:T(2,128)}, u32[]{:S(2)}) copy-start(s32[4,4,2]{1,2,0:T(2,128)} %param.16) | copy-start | bytes 388
  11.9 4.5 %collective-permute-start.5 = (f32[6,8,128]{2,1,0:T(8,128)S(1)}, f32[6,8,128]{2,1,0:T(8,128)S(1)}, u32[]{:S(2)}, u32[]{:S(2)}) collective-permute-start(f32[6,8,128]{2,1,0:T(8,128)S(1)} %get-tuple-element.44), channel_id=1, source_target_pairs={{0,2},{1,3},{2,0},{3,1},{4,6},{5,7},{6,4},{7,5},{8,10},{9,11},{10,... | collective-permute-start | bytes 73736 | tf_op jit(solution)/shard_map/ppermute | solution.py:648
  12.0 4.4 %collective-permute-start.6 = (f32[6,8,128]{2,1,0:T(8,128)S(1)}, f32[6,8,128]{2,1,0:T(8,128)S(1)}, u32[]{:S(2)}, u32[]{:S(2)}) collective-permute-start(f32[6,8,128]{2,1,0:T(8,128)S(1)} %get-tuple-element.45), channel_id=1, source_target_pairs={{0,2},{1,3},{2,0},{3,1},{4,6},{5,7},{6,4},{7,5},{8,16},{9,17},{10,... | collective-permute-start | bytes 73736 | tf_op jit(solution)/shard_map/ppermute | solution.py:648
  12.5 4.0 %collective-permute-start.7 = (f32[6,8,128]{2,1,0:T(8,128)S(1)}, f32[6,8,128]{2,1,0:T(8,128)S(1)}, u32[]{:S(2)}, u32[]{:S(2)}) collective-permute-start(f32[6,8,128]{2,1,0:T(8,128)S(1)} %get-tuple-element.46), channel_id=1, source_target_pairs={{0,8},{1,9},{2,10},{3,11},{4,12},{5,13},{6,14},{7,15},{8,0},{9,1},... | collective-permute-start | bytes 73736 | tf_op jit(solution)/shard_map/ppermute | solution.py:648
  14.0 0.7 %copy-start.4 = (s32[32]{0:T(128)S(1)}, s32[32]{0:T(128)}, u32[]{:S(2)}) copy-start(s32[32]{0:T(128)} %owners.1) | copy-start | bytes 388
  14.0 3.4 %collective-permute-start.8 = (f32[6,8,128]{2,1,0:T(8,128)S(1)}, f32[6,8,128]{2,1,0:T(8,128)S(1)}, u32[]{:S(2)}, u32[]{:S(2)}) collective-permute-start(f32[6,8,128]{2,1,0:T(8,128)S(1)} %get-tuple-element.47), channel_id=1, source_target_pairs={{0,6},{1,7},{2,4},{3,5},{4,2},{5,3},{6,0},{7,1},{8,14},{9,15},{10,... | collective-permute-start | bytes 73736 | tf_op jit(solution)/shard_map/ppermute | solution.py:648
  15.5 0.8 %copy-start.2 = (f32[8,8,128]{2,1,0:T(8,128)S(1)}, f32[8,8,128]{2,1,0:T(8,128)}, u32[]{:S(2)}) copy-start(f32[8,8,128]{2,1,0:T(8,128)} %param.14) | copy-start | bytes 98308
  18.7 10.5 %all-to-all-start = ((f32[32,4,128]{2,1,0:T(4,128)}), f32[32,4,128]{2,1,0:T(4,128)S(1)}, u32[]{:S(2)}, u32[]{:S(2)}) async-start(f32[32,4,128]{2,1,0:T(4,128)} %bitcast.24), calls=%async_computation | async-start | bytes 131072 | tf_op jit(solution)/shard_map/all_to_all | solution.py:716
  21.3 4.5 %collective-permute-start.9 = (f32[5,8,128]{2,1,0:T(8,128)S(1)}, f32[5,8,128]{2,1,0:T(8,128)S(1)}, u32[]{:S(2)}, u32[]{:S(2)}) collective-permute-start(f32[5,8,128]{2,1,0:T(8,128)S(1)} %get-tuple-element.50), channel_id=1, source_target_pairs={{0,2},{1,3},{2,0},{3,1},{4,6},{5,7},{6,4},{7,5},{8,10},{9,11},{10,... | collective-permute-start | bytes 61448 | tf_op jit(solution)/shard_map/ppermute | solution.py:648
  21.6 4.2 %collective-permute-start.10 = (f32[5,8,128]{2,1,0:T(8,128)S(1)}, f32[5,8,128]{2,1,0:T(8,128)S(1)}, u32[]{:S(2)}, u32[]{:S(2)}) collective-permute-start(f32[5,8,128]{2,1,0:T(8,128)S(1)} %get-tuple-element.51), channel_id=1, source_target_pairs={{0,2},{1,3},{2,0},{3,1},{4,6},{5,7},{6,4},{7,5},{8,16},{9,17},{10,... | collective-permute-start | bytes 61448 | tf_op jit(solution)/shard_map/ppermute | solution.py:648
  21.9 4.8 %collective-permute-start.11 = (f32[5,8,128]{2,1,0:T(8,128)S(1)}, f32[5,8,128]{2,1,0:T(8,128)S(1)}, u32[]{:S(2)}, u32[]{:S(2)}) collective-permute-start(f32[5,8,128]{2,1,0:T(8,128)S(1)} %get-tuple-element.52), channel_id=1, source_target_pairs={{0,8},{1,9},{2,10},{3,11},{4,12},{5,13},{6,14},{7,15},{8,0},{9,1},... | collective-permute-start | bytes 61448 | tf_op jit(solution)/shard_map/ppermute | solution.py:648
  24.8 3.4 %collective-permute-start.12 = (f32[5,8,128]{2,1,0:T(8,128)S(1)}, f32[5,8,128]{2,1,0:T(8,128)S(1)}, u32[]{:S(2)}, u32[]{:S(2)}) collective-permute-start(f32[5,8,128]{2,1,0:T(8,128)S(1)} %get-tuple-element.53), channel_id=1, source_target_pairs={{0,6},{1,7},{2,4},{3,5},{4,2},{5,3},{6,0},{7,1},{8,14},{9,15},{10,... | collective-permute-start | bytes 61448 | tf_op jit(solution)/shard_map/ppermute | solution.py:648

commit v8 on v7

--- a/solution.py
+++ b/solution.py
@@ -21,7 +21,6 @@
 two_thirds = 2.0 / 3.0
 
 BASE = 5 * BOXES
-SHARE = CY // 2
 
 TILE = (CY, CZ)
 FLAT = (ROWS, CZ)
@@ -183,7 +182,7 @@
 ORDERS = (
     ((1, 0), (0, 1), (0, 0), (1, 1), (2, 0), (2, 1)),
     ((1, 0), (0, 1), (0, 0), (1, 1)),
-    ((1, 0), (0, 1), (0, 0), (1, 1)),
+    ((0, 0), (1, 1), (2, 0), (2, 1), (1, 0), (0, 1)),
 )
 
 
@@ -519,57 +518,26 @@
     above = product(faces[4] * packed, gather[5 * CZ : 6 * CZ, :])
     below = product(faces[5] * packed, gather[6 * CZ :, :])
     blocks = jnp.concatenate([blocks, above, below, jnp.zeros(TILE, jnp.float32)], axis=0)
-    devices = routes.shape[0]
-    rows_out[pl.ds(0, devices, stride=SHARE), :] = jnp.dot(
+    rows_out[...] = jnp.dot(
         routes[...],
         jnp.concatenate(three_parts(blocks), axis=0),
         preferred_element_type=jnp.float32,
     )
-    lanes = lax.broadcasted_iota(jnp.int32, TILE, 1)
-    own_place = (here[0] * sizes[1] + here[1]) * sizes[2] + here[2]
-    paired = pltpu.roll(packed, CY - SHARE, 0)
-    up = jnp.where(lanes % 2 == 0, packed, pltpu.roll(paired, 1, 1))[:SHARE]
-    down = jnp.where(lanes % 2 == 1, packed, pltpu.roll(paired, CZ - 1, 1))[:SHARE]
-    lanes = lax.broadcasted_iota(jnp.int32, (SHARE, CZ), 1)
-    for step, message in ((1, up), (-1, down)):
-        position = here[2] + step
-
-        @pl.when((position >= 0) & (position < sizes[2]))
-        def _():
-            at = pl.ds(pl.multiple_of((own_place + step) * SHARE, SHARE), SHARE)
-            rows_out[at, :] = jnp.where(lanes < BASE, rows_out[at, :], message)
-
     copy = pltpu.make_async_copy(rows_out, table, sent)
     copy.start()
     put_pair(x_low, x_high, here[0], outs[0])
     put_pair(y_low, y_high, here[1], outs[1])
+    outs[2][0][0] = packed
+    for index in range(1, 5):
+        outs[2][0][index] = jnp.zeros(TILE, jnp.float32)
     copy.wait()
 
 
 def last_kernel(sizes, base, table, *refs):
     received, (out, gradient, done, block, sent) = split(refs, sizes, 2)
-    devices = table.shape[0] // SHARE
-    here = positions()
-    own_place = (here[0] * sizes[1] + here[1]) * sizes[2] + here[2]
-    sublanes = lax.broadcasted_iota(jnp.int32, TILE, 0)
-    lanes = lax.broadcasted_iota(jnp.int32, TILE, 1)
-
-    def z_rows(step):
-        inside = (here[2] + step >= 0) & (here[2] + step < sizes[2])
-        place = jnp.where(inside, own_place + step, own_place)
-        rows = table[pl.ds(pl.multiple_of(place * SHARE, SHARE), SHARE), :]
-        return jnp.where(inside, jnp.concatenate([rows, rows], axis=0), 0.0)
-
-    z_above, z_below = z_rows(1), z_rows(-1)
-    first_half = sublanes < SHARE
-    z_halo = jnp.where(
-        lanes % 2 == 0,
-        jnp.where(first_half, pltpu.roll(z_above, CZ - 1, 1), z_above),
-        -jnp.where(first_half, pltpu.roll(z_below, 1, 1), z_below),
-    )
     totals = [None] * 4
-    for device in range(devices):
-        part = table[device * SHARE : device * SHARE + 1, :]
+    for device in range(table.shape[0]):
+        part = table[device : device + 1, :]
         old = totals[device % 4]
         totals[device % 4] = part if old is None else old + part
     total = (totals[0] + totals[1]) + (totals[2] + totals[3])
@@ -582,7 +550,7 @@
         copy.start()
         copies.append(copy)
 
-    add_halo(base, received, two_thirds * step_length, sizes, done, send, z_halo)
+    add_halo(base, received, two_thirds * step_length, sizes, done, send)
     for copy in copies:
         copy.wait()
 
@@ -709,11 +677,11 @@
         functools.partial(gradient_kernel, sizes, 0.25 * step_length),
         [VMEM] * len(operands),
         operands,
-        [STATE, (devices * SHARE, CZ)] + message_shapes(5, 2),
-        scratch=[pltpu.VMEM((devices * SHARE, CZ), jnp.float32), pltpu.SemaphoreType.DMA],
+        [STATE, (devices, CZ)] + message_shapes(5, 2),
+        scratch=[pltpu.VMEM((devices, CZ), jnp.float32), pltpu.SemaphoreType.DMA],
         spaces=[pltpu.VMEM, pltpu.HBM] + [pltpu.VMEM] * len(message_shapes(5, 2)),
     )
-    table = lax.all_to_all(table.reshape(devices, SHARE, CZ), AXES, 0, 0, tiled=True)
+    table = lax.all_to_all(table.reshape(devices, 1, CZ), AXES, 0, 0, tiled=True)
     received = exchange(sent, 2)
     (base,) = call(
         functools.partial(own_kernel, (third, two_thirds)),
@@ -721,17 +689,13 @@
         (scaled, sponge, start, section),
         [STATE],
     )
-    operands = (base, table.reshape(devices * SHARE, CZ), *received)
+    operands = (base, table.reshape(devices, CZ), *received)
     adjoint, gradient = call(
         functools.partial(last_kernel, sizes),
         [VMEM] * len(operands),
         operands,
         [STATE, (1, 5 * BOXES)],
-        scratch=[
-            pltpu.VMEM(STATE, jnp.float32),
-            pltpu.VMEM((1, 5 * BOXES), jnp.float32),
-            pltpu.SemaphoreType.DMA((6,)),
-        ],
+        scratch=[state, pltpu.VMEM((1, 5 * BOXES), jnp.float32), pltpu.SemaphoreType.DMA((6,))],
         spaces=[pltpu.HBM] * 2,
     )
     return adjoint.reshape(state_shape), gradient

time: 30.3 us -> 29.5 us (0.974)
  waiting for transfers between devices: 6.63 us -> 5.48 us
  starting transfers between devices: 16.3 us -> 16.7 us
    ppermute x13 -> x14, waiting for transfers between devices: 5.68 us -> 4.93 us  [exchange(): lax.ppermute(sends[key], AXES, permutations[key[0]][key[1]])]
    ppermute x13 -> x14, starting transfers between devices: 13.7 us -> 14.1 us  [exchange(): lax.ppermute(sends[key], AXES, permutations[key[0]][key[1]])]
    all_to_all x1, waiting for transfers between devices: 0.95 us -> 0.55 us  [body(): lax.all_to_all(table.reshape(devices, 1, CZ), AXES, 0, 0, tiled=True)]
  transfers between devices with their start and end apart: 14 -> 15, of which waited for: 6 -> 6; matrix products, arithmetic and copies ran while one was open for 0% -> 0% of each run, Pallas kernels for 4% -> 4%
where the time goes in v8:
time: 29.5 us; the launch traced here: 29.3 us
  starting transfers between devices  16.7 us (57%)
  waiting for transfers between devices  5.48 us (19%)
  Pallas kernels  5.12 us (17%)
  local copies, waits for them, and re-layouts  1.18 us (4%)
  between operations  0.77 us (3%)
    ppermute x14, starting transfers between devices, exchange(): lax.ppermute(sends[key], AXES, permutations[key[0]][key[1]])  14.1 us
    pallas_call x9, Pallas kernels, call(): pl.pallas_call(kernel, out_shape=[space(shape, dtype) for space, shape in...  5.12 us
    ppermute x14, waiting for transfers between devices, exchange(): lax.ppermute(sends[key], AXES, permutations[key[0]][key[1]])  4.93 us
    all_to_all x1, starting transfers between devices, body(): lax.all_to_all(table.reshape(devices, 1, CZ), AXES, 0, 0, tiled=True)  2.61 us
    unnamed x10, local copies, waits for them, and re-layouts  1.18 us
  transfers between devices with their start and end apart: 15, of which 6 were waited for; matrix products, arithmetic and copies ran while one was open for 0% of the time, Pallas kernels for 4%

profile of v8, /device:TPU:0, one launch (start us, length us, event | category | flops | bytes accessed | tf_op | source)
XLA Modules:
  0.0 29.3 jit_solution(3038283412105005354)
XLA Ops:
  0.6 1.5 %shard_map.104 = (f32[6,64,128]{2,1,0:T(8,128)S(1)}, f32[5,64,128]{2,1,0:T(8,128)S(1)}, f32[6,8,128]{2,1,0:T(8,128)S(1)}, f32[6,8,128]{2,1,0:T(8,128)S(1)}, f32[...) custom-call(s32[4,2,4]{2,1,0:T(2,128)} %bitcast.29, f32[5,64,128]{2,1,0:T(8,128)} %bitcast.13, ...), custom_call_target="tpu_custom_call" | custom-call | flops 2000000 | bytes 1000000 | tf_op jit(solution)/shard_map/pallas_call | solution.py:569
  2.1 0.5 %collective-permute-start = (f32[6,8,128]{2,1,0:T(8,128)S(1)}, f32[6,8,128]{2,1,0:T(8,128)S(1)}, u32[]{:S(2)}, u32[]{:S(2)}) collective-permute-start(f32[6,8,128]{2,1,0:T(8,128)S(1)} %get-tuple-element.32), channel_id=1, source_target_pairs={{0,2},{1,3},{2,0},{3,1},{4,6},{5,7},{6,4},{7,5},{8,10},{9,11},{10,... | collective-permute-start | bytes 73736 | tf_op jit(solution)/shard_map/ppermute | solution.py:616
  2.7 4.1 %collective-permute-start.2 = (f32[6,8,128]{2,1,0:T(8,128)S(1)}, f32[6,8,128]{2,1,0:T(8,128)S(1)}, u32[]{:S(2)}, u32[]{:S(2)}) collective-permute-start(f32[6,8,128]{2,1,0:T(8,128)S(1)} %get-tuple-element.34), channel_id=1, source_target_pairs={{0,8},{1,9},{2,10},{3,11},{4,12},{5,13},{6,14},{7,15},{8,0},{9,1},... | collective-permute-start | bytes 73736 | tf_op jit(solution)/shard_map/ppermute | solution.py:616
  6.8 1.0 %collective-permute-start.3 = (f32[6,8,128]{2,1,0:T(8,128)S(1)}, f32[6,8,128]{2,1,0:T(8,128)S(1)}, u32[]{:S(2)}, u32[]{:S(2)}) collective-permute-start(f32[6,8,128]{2,1,0:T(8,128)S(1)} %get-tuple-element.35), channel_id=1, source_target_pairs={{0,6},{1,7},{2,4},{3,5},{4,2},{5,3},{6,0},{7,1},{8,14},{9,15},{10,... | collective-permute-start | bytes 73736 | tf_op jit(solution)/shard_map/ppermute | solution.py:616
  7.8 1.5 %collective-permute-start.4 = (f32[6,8,128]{2,1,0:T(8,128)S(1)}, f32[6,8,128]{2,1,0:T(8,128)S(1)}, u32[]{:S(2)}, u32[]{:S(2)}) collective-permute-start(f32[6,8,128]{2,1,0:T(8,128)S(1)} %get-tuple-element.36.own), channel_id=1, source_target_pairs={{0,1},{1,0},{2,3},{3,2},{4,5},{5,4},{6,7},{7,6},{8,9},{9,8},{10,11... | collective-permute-start | bytes 73736 | tf_op jit(solution)/shard_map/ppermute | solution.py:616
  9.4 0.9 %collective-permute-done.3.refs_3_ = f32[6,8,128]{2,1,0:T(8,128)S(1)} collective-permute-done((f32[6,8,128]{2,1,0:T(8,128)S(1)}, f32[6,8,128]{2,1,0:T(8,128)S(1)}, u32[]{:S(2)}, u32[]{:S(2)}) %collective-permute-start.3) | collective-permute-done | bytes 24608 | tf_op jit(solution)/shard_map/ppermute | solution.py:616
  10.3 1.4 %collective-permute-done.4.refs_4_ = f32[6,8,128]{2,1,0:T(8,128)S(1)} collective-permute-done((f32[6,8,128]{2,1,0:T(8,128)S(1)}, f32[6,8,128]{2,1,0:T(8,128)S(1)}, u32[]{:S(2)}, u32[]{:S(2)}) %collective-permute-start.4) | collective-permute-done | bytes 24608 | tf_op jit(solution)/shard_map/ppermute | solution.py:616
  11.7 0.2 shard_map.105
  12.0 0.5 %collective-permute-start.6 = (f32[6,8,128]{2,1,0:T(8,128)S(1)}, f32[6,8,128]{2,1,0:T(8,128)S(1)}, u32[]{:S(2)}, u32[]{:S(2)}) collective-permute-start(f32[6,8,128]{2,1,0:T(8,128)S(1)} %get-tuple-element.46), channel_id=1, source_target_pairs={{0,2},{1,3},{2,0},{3,1},{4,6},{5,7},{6,4},{7,5},{8,16},{9,17},{10,... | collective-permute-start | bytes 73736 | tf_op jit(solution)/shard_map/ppermute | solution.py:616
  12.5 1.5 %collective-permute-start.7 = (f32[6,8,128]{2,1,0:T(8,128)S(1)}, f32[6,8,128]{2,1,0:T(8,128)S(1)}, u32[]{:S(2)}, u32[]{:S(2)}) collective-permute-start(f32[6,8,128]{2,1,0:T(8,128)S(1)} %get-tuple-element.47), channel_id=1, source_target_pairs={{0,8},{1,9},{2,10},{3,11},{4,12},{5,13},{6,14},{7,15},{8,0},{9,1},... | collective-permute-start | bytes 73736 | tf_op jit(solution)/shard_map/ppermute | solution.py:616
  14.1 0.6 %copy-done.4 = s32[32]{0:T(128)S(1)} copy-done((s32[32]{0:T(128)S(1)}, s32[32]{0:T(128)}, u32[]{:S(2)}) %copy-start.4) | copy-done | bytes 152
  14.6 0.7 %shard_map.108 = (bf16[32,192]{1,0:T(8,128)(2,1)S(1)}, bf16[896,128]{1,0:T(8,128)(2,1)S(1)}) custom-call(s32[4,2,4]{2,1,0:T(2,128)S(1)} %bitcast.24, s32[32]{0:T(128)S(1)} %copy-done.4), custom_call_target="tpu_custom_call" | custom-call | flops 2000000 | bytes 1000000 | tf_op jit(solution)/shard_map/pallas_call | solution.py:569
  15.7 0.6 %copy-done.2 = f32[8,8,128]{2,1,0:T(8,128)S(1)} copy-done((f32[8,8,128]{2,1,0:T(8,128)S(1)}, f32[8,8,128]{2,1,0:T(8,128)}, u32[]{:S(2)}) %copy-start.2) | copy-done | bytes 32792
  16.4 1.0 %collective-permute-done.8.refs_3_ = f32[6,8,128]{2,1,0:T(8,128)S(1)} collective-permute-done((f32[6,8,128]{2,1,0:T(8,128)S(1)}, f32[6,8,128]{2,1,0:T(8,128)S(1)}, u32[]{:S(2)}, u32[]{:S(2)}) %collective-permute-start.8) | collective-permute-done | bytes 24608 | tf_op jit(solution)/shard_map/ppermute | solution.py:616
  17.4 1.2 %shard_map.110 = (f32[5,64,128]{2,1,0:T(8,128)S(1)}, f32[32,128]{1,0:T(8,128)}, f32[5,8,128]{2,1,0:T(8,128)S(1)}, f32[5,8,128]{2,1,0:T(8,128)S(1)}, f32[5,8,128]...) custom-call(f32[5,64,128]{2,1,0:T(8,128)S(1)} %shard_map.106.base, ...), custom_call_target="tpu_custom_call" | custom-call | flops 2000000 | bytes 1000000 | tf_op jit(solution)/shard_map/pallas_call | solution.py:569
  18.7 2.6 %all-to-all-start = ((f32[32,1,128]{2,1,0:T(1,128)}), f32[32,1,128]{2,1,0:T(1,128)S(1)}, u32[]{:S(2)}, u32[]{:S(2)}) async-start(f32[32,1,128]{2,1,0:T(1,128)} %bitcast.28), calls=%async_computation | async-start | bytes 32768 | tf_op jit(solution)/shard_map/all_to_all | solution.py:684
  21.3 1.8 %collective-permute-start.9 = (f32[5,8,128]{2,1,0:T(8,128)S(1)}, f32[5,8,128]{2,1,0:T(8,128)S(1)}, u32[]{:S(2)}, u32[]{:S(2)}) collective-permute-start(f32[5,8,128]{2,1,0:T(8,128)S(1)} %get-tuple-element.51), channel_id=1, source_target_pairs={{0,8},{1,9},{2,10},{3,11},{4,12},{5,13},{6,14},{7,15},{8,0},{9,1},... | collective-permute-start | bytes 61448 | tf_op jit(solution)/shard_map/ppermute | solution.py:616
  23.1 0.9 %collective-permute-start.10 = (f32[5,8,128]{2,1,0:T(8,128)S(1)}, f32[5,8,128]{2,1,0:T(8,128)S(1)}, u32[]{:S(2)}, u32[]{:S(2)}) collective-permute-start(f32[5,8,128]{2,1,0:T(8,128)S(1)} %get-tuple-element.52), channel_id=1, source_target_pairs={{0,6},{1,7},{2,4},{3,5},{4,2},{5,3},{6,0},{7,1},{8,14},{9,15},{10,... | collective-permute-start | bytes 61448 | tf_op jit(solution)/shard_map/ppermute | solution.py:616
  24.1 1.5 %collective-permute-start.11 = (f32[5,8,128]{2,1,0:T(8,128)S(1)}, f32[5,8,128]{2,1,0:T(8,128)S(1)}, u32[]{:S(2)}, u32[]{:S(2)}) collective-permute-start(f32[5,8,128]{2,1,0:T(8,128)S(1)} %get-tuple-element.53), channel_id=1, source_target_pairs={{0,1},{1,0},{2,3},{3,2},{4,5},{5,4},{6,7},{7,6},{8,9},{9,8},{10,11... | collective-permute-start | bytes 61448 | tf_op jit(solution)/shard_map/ppermute | solution.py:616
  25.5 0.4 %collective-permute-start.12 = (f32[5,8,128]{2,1,0:T(8,128)S(1)}, f32[5,8,128]{2,1,0:T(8,128)S(1)}, u32[]{:S(2)}, u32[]{:S(2)}) collective-permute-start(f32[5,8,128]{2,1,0:T(8,128)S(1)} %get-tuple-element.54), channel_id=1, source_target_pairs={{0,2},{1,3},{2,0},{3,1},{4,6},{5,7},{6,4},{7,5},{8,10},{9,11},{10,... | collective-permute-start | bytes 61448 | tf_op jit(solution)/shard_map/ppermute | solution.py:616
  26.2 0.3 %collective-permute-done.10.refs_1_ = f32[5,8,128]{2,1,0:T(8,128)S(1)} collective-permute-done((f32[5,8,128]{2,1,0:T(8,128)S(1)}, f32[5,8,128]{2,1,0:T(8,128)S(1)}, u32[]{:S(2)}, u32[]{:S(2)}) %collective-permute-start.10) | collective-permute-done | bytes 20512 | tf_op jit(solution)/shard_map/ppermute | solution.py:616
  26.5 1.3 %collective-permute-done.11.refs_2_ = f32[5,8,128]{2,1,0:T(8,128)S(1)} collective-permute-done((f32[5,8,128]{2,1,0:T(8,128)S(1)}, f32[5,8,128]{2,1,0:T(8,128)S(1)}, u32[]{:S(2)}, u32[]{:S(2)}) %collective-permute-start.11) | collective-permute-done | bytes 20512 | tf_op jit(solution)/shard_map/ppermute | solution.py:616
  27.9 0.6 %all-to-all-done = f32[32,1,128]{2,1,0:T(1,128)S(1)} async-done(((f32[32,1,128]{2,1,0:T(1,128)}), f32[32,1,128]{2,1,0:T(1,128)S(1)}, u32[]{:S(2)}, u32[]{:S(2)}) %all-to-all-start) | async-done | bytes 16416 | tf_op jit(solution)/shard_map/all_to_all | solution.py:684
  28.4 0.9 %shard_map.112 = (f32[5,64,128]{2,1,0:T(8,128)}, f32[1,40]{1,0:T(1,128)}) custom-call(f32[5,64,128]{2,1,0:T(8,128)S(1)} %shard_map.111.base, f32[32,128]{1,0:T(8,128)S(1)} %bitcast.23, f32[5,8,128]{2,1,0:T(8,128)S(1)} %collective-permute-done.9.refs_0_, f32[5,8,128]{2,1,0:T(8,128)S(1)} %collective-permute-done.10.refs_1_, ...), custom_call_target="tpu_custom_call" | custom-call | flops 2000000 | bytes 1000000 | tf_op jit(solution)/shard_map/pallas_call | solution.py:569
  (25 shorter events, 1.0 us)
Async XLA Ops:
  2.1 7.2 %collective-permute-start = (f32[6,8,128]{2,1,0:T(8,128)S(1)}, f32[6,8,128]{2,1,0:T(8,128)S(1)}, u32[]{:S(2)}, u32[]{:S(2)}) collective-permute-start(f32[6,8,128]{2,1,0:T(8,128)S(1)} %get-tuple-element.32), channel_id=1, source_target_pairs={{0,2},{1,3},{2,0},{3,1},{4,6},{5,7},{6,4},{7,5},{8,10},{9,11},{10,... | collective-permute-start | bytes 73736 | tf_op jit(solution)/shard_map/ppermute | solution.py:616
  2.6 6.7 %collective-permute-start.1 = (f32[6,8,128]{2,1,0:T(8,128)S(1)}, f32[6,8,128]{2,1,0:T(8,128)S(1)}, u32[]{:S(2)}, u32[]{:S(2)}) collective-permute-start(f32[6,8,128]{2,1,0:T(8,128)S(1)} %get-tuple-element.33), channel_id=1, source_target_pairs={{0,2},{1,3},{2,0},{3,1},{4,6},{5,7},{6,4},{7,5},{8,16},{9,17},{10,... | collective-permute-start | bytes 73736 | tf_op jit(solution)/shard_map/ppermute | solution.py:616
  2.7 6.7 %collective-permute-start.2 = (f32[6,8,128]{2,1,0:T(8,128)S(1)}, f32[6,8,128]{2,1,0:T(8,128)S(1)}, u32[]{:S(2)}, u32[]{:S(2)}) collective-permute-start(f32[6,8,128]{2,1,0:T(8,128)S(1)} %get-tuple-element.34), channel_id=1, source_target_pairs={{0,8},{1,9},{2,10},{3,11},{4,12},{5,13},{6,14},{7,15},{8,0},{9,1},... | collective-permute-start | bytes 73736 | tf_op jit(solution)/shard_map/ppermute | solution.py:616
  6.8 3.4 %collective-permute-start.3 = (f32[6,8,128]{2,1,0:T(8,128)S(1)}, f32[6,8,128]{2,1,0:T(8,128)S(1)}, u32[]{:S(2)}, u32[]{:S(2)}) collective-permute-start(f32[6,8,128]{2,1,0:T(8,128)S(1)} %get-tuple-element.35), channel_id=1, source_target_pairs={{0,6},{1,7},{2,4},{3,5},{4,2},{5,3},{6,0},{7,1},{8,14},{9,15},{10,... | collective-permute-start | bytes 73736 | tf_op jit(solution)/shard_map/ppermute | solution.py:616
  7.8 3.8 %collective-permute-start.4 = (f32[6,8,128]{2,1,0:T(8,128)S(1)}, f32[6,8,128]{2,1,0:T(8,128)S(1)}, u32[]{:S(2)}, u32[]{:S(2)}) collective-permute-start(f32[6,8,128]{2,1,0:T(8,128)S(1)} %get-tuple-element.36.own), channel_id=1, source_target_pairs={{0,1},{1,0},{2,3},{3,2},{4,5},{5,4},{6,7},{7,6},{8,9},{9,8},{10,11... | collective-permute-start | bytes 73736 | tf_op jit(solution)/shard_map/ppermute | solution.py:616
  11.6 3.7 %copy-start = (f32[5,8,8,128]{3,2,1,0:T(8,128)S(1)}, f32[5,8,8,128]{3,2,1,0:T(8,128)}, u32[]{:S(2)}) copy-start(f32[5,8,8,128]{3,2,1,0:T(8,128)} %param.9) | copy-start | bytes 491524
  11.6 3.7 %copy-start.1 = (f32[8,8,128]{2,1,0:T(8,128)S(1)}, f32[8,8,128]{2,1,0:T(8,128)}, u32[]{:S(2)}) copy-start(f32[8,8,128]{2,1,0:T(8,128)} %param.13) | copy-start | bytes 98308
  11.9 2.2 %copy-start.3 = (s32[4,4,2]{1,2,0:T(2,128)S(1)}, s32[4,4,2]{1,2,0:T(2,128)}, u32[]{:S(2)}) copy-start(s32[4,4,2]{1,2,0:T(2,128)} %param.16) | copy-start | bytes 388
  11.9 4.5 %collective-permute-start.5 = (f32[6,8,128]{2,1,0:T(8,128)S(1)}, f32[6,8,128]{2,1,0:T(8,128)S(1)}, u32[]{:S(2)}, u32[]{:S(2)}) collective-permute-start(f32[6,8,128]{2,1,0:T(8,128)S(1)} %get-tuple-element.45), channel_id=1, source_target_pairs={{0,2},{1,3},{2,0},{3,1},{4,6},{5,7},{6,4},{7,5},{8,10},{9,11},{10,... | collective-permute-start | bytes 73736 | tf_op jit(solution)/shard_map/ppermute | solution.py:616
  12.0 4.4 %collective-permute-start.6 = (f32[6,8,128]{2,1,0:T(8,128)S(1)}, f32[6,8,128]{2,1,0:T(8,128)S(1)}, u32[]{:S(2)}, u32[]{:S(2)}) collective-permute-start(f32[6,8,128]{2,1,0:T(8,128)S(1)} %get-tuple-element.46), channel_id=1, source_target_pairs={{0,2},{1,3},{2,0},{3,1},{4,6},{5,7},{6,4},{7,5},{8,16},{9,17},{10,... | collective-permute-start | bytes 73736 | tf_op jit(solution)/shard_map/ppermute | solution.py:616
  12.5 3.9 %collective-permute-start.7 = (f32[6,8,128]{2,1,0:T(8,128)S(1)}, f32[6,8,128]{2,1,0:T(8,128)S(1)}, u32[]{:S(2)}, u32[]{:S(2)}) collective-permute-start(f32[6,8,128]{2,1,0:T(8,128)S(1)} %get-tuple-element.47), channel_id=1, source_target_pairs={{0,8},{1,9},{2,10},{3,11},{4,12},{5,13},{6,14},{7,15},{8,0},{9,1},... | collective-permute-start | bytes 73736 | tf_op jit(solution)/shard_map/ppermute | solution.py:616
  14.0 0.7 %copy-start.4 = (s32[32]{0:T(128)S(1)}, s32[32]{0:T(128)}, u32[]{:S(2)}) copy-start(s32[32]{0:T(128)} %owners.1) | copy-start | bytes 388
  14.0 3.4 %collective-permute-start.8 = (f32[6,8,128]{2,1,0:T(8,128)S(1)}, f32[6,8,128]{2,1,0:T(8,128)S(1)}, u32[]{:S(2)}, u32[]{:S(2)}) collective-permute-start(f32[6,8,128]{2,1,0:T(8,128)S(1)} %get-tuple-element.48), channel_id=1, source_target_pairs={{0,6},{1,7},{2,4},{3,5},{4,2},{5,3},{6,0},{7,1},{8,14},{9,15},{10,... | collective-permute-start | bytes 73736 | tf_op jit(solution)/shard_map/ppermute | solution.py:616
  15.5 0.8 %copy-start.2 = (f32[8,8,128]{2,1,0:T(8,128)S(1)}, f32[8,8,128]{2,1,0:T(8,128)}, u32[]{:S(2)}) copy-start(f32[8,8,128]{2,1,0:T(8,128)} %param.14) | copy-start | bytes 98308
  18.7 9.7 %all-to-all-start = ((f32[32,1,128]{2,1,0:T(1,128)}), f32[32,1,128]{2,1,0:T(1,128)S(1)}, u32[]{:S(2)}, u32[]{:S(2)}) async-start(f32[32,1,128]{2,1,0:T(1,128)} %bitcast.28), calls=%async_computation | async-start | bytes 32768 | tf_op jit(solution)/shard_map/all_to_all | solution.py:684
  21.3 4.9 %collective-permute-start.9 = (f32[5,8,128]{2,1,0:T(8,128)S(1)}, f32[5,8,128]{2,1,0:T(8,128)S(1)}, u32[]{:S(2)}, u32[]{:S(2)}) collective-permute-start(f32[5,8,128]{2,1,0:T(8,128)S(1)} %get-tuple-element.51), channel_id=1, source_target_pairs={{0,8},{1,9},{2,10},{3,11},{4,12},{5,13},{6,14},{7,15},{8,0},{9,1},... | collective-permute-start | bytes 61448 | tf_op jit(solution)/shard_map/ppermute | solution.py:616
  23.1 3.4 %collective-permute-start.10 = (f32[5,8,128]{2,1,0:T(8,128)S(1)}, f32[5,8,128]{2,1,0:T(8,128)S(1)}, u32[]{:S(2)}, u32[]{:S(2)}) collective-permute-start(f32[5,8,128]{2,1,0:T(8,128)S(1)} %get-tuple-element.52), channel_id=1, source_target_pairs={{0,6},{1,7},{2,4},{3,5},{4,2},{5,3},{6,0},{7,1},{8,14},{9,15},{10,... | collective-permute-start | bytes 61448 | tf_op jit(solution)/shard_map/ppermute | solution.py:616
  24.1 3.8 %collective-permute-start.11 = (f32[5,8,128]{2,1,0:T(8,128)S(1)}, f32[5,8,128]{2,1,0:T(8,128)S(1)}, u32[]{:S(2)}, u32[]{:S(2)}) collective-permute-start(f32[5,8,128]{2,1,0:T(8,128)S(1)} %get-tuple-element.53), channel_id=1, source_target_pairs={{0,1},{1,0},{2,3},{3,2},{4,5},{5,4},{6,7},{7,6},{8,9},{9,8},{10,11... | collective-permute-start | bytes 61448 | tf_op jit(solution)/shard_map/ppermute | solution.py:616
  25.5 2.3 %collective-permute-start.12 = (f32[5,8,128]{2,1,0:T(8,128)S(1)}, f32[5,8,128]{2,1,0:T(8,128)S(1)}, u32[]{:S(2)}, u32[]{:S(2)}) collective-permute-start(f32[5,8,128]{2,1,0:T(8,128)S(1)} %get-tuple-element.54), channel_id=1, source_target_pairs={{0,2},{1,3},{2,0},{3,1},{4,6},{5,7},{6,4},{7,5},{8,10},{9,11},{10,... | collective-permute-start | bytes 61448 | tf_op jit(solution)/shard_map/ppermute | solution.py:616
  25.9 2.0 %collective-permute-start.13 = (f32[5,8,128]{2,1,0:T(8,128)S(1)}, f32[5,8,128]{2,1,0:T(8,128)S(1)}, u32[]{:S(2)}, u32[]{:S(2)}) collective-permute-start(f32[5,8,128]{2,1,0:T(8,128)S(1)} %get-tuple-element.55), channel_id=1, source_target_pairs={{0,2},{1,3},{2,0},{3,1},{4,6},{5,7},{6,4},{7,5},{8,16},{9,17},{10,... | collective-permute-start | bytes 61448 | tf_op jit(solution)/shard_map/ppermute | solution.py:616

commit v9 on v8

--- a/solution.py
+++ b/solution.py
@@ -48,6 +48,29 @@
     return first, second if size > 2 else None
 
 
+def first_round(sizes):
+    x, y, z = pairings(sizes, 0, 1), pairings(sizes, 1, 1), pairings(sizes, 2, 1)
+    if sizes[0] > 2:
+        plane = sizes[1] * sizes[2]
+        first, second = dict(z[0]), dict(x[1])
+        for index in range(plane):
+            first[index], second[index] = second[index], first[index]
+        x, z = (x[0], sorted(second.items())), (sorted(first.items()), z[1])
+    return x, y, z
+
+
+def at_start():
+    return lax.axis_index(AXES[0]) == 0
+
+
+class ZFields:
+    def __init__(self, x_second, z_first):
+        self.x_second, self.z_first = x_second, z_first
+
+    def __getitem__(self, index):
+        return jnp.where(at_start(), self.x_second[index], self.z_first[index])
+
+
 def positions():
     return [lax.axis_index(axis) for axis in AXES]
 
@@ -181,7 +204,7 @@
 
 ORDERS = (
     ((1, 0), (0, 1), (0, 0), (1, 1), (2, 0), (2, 1)),
-    ((1, 0), (0, 1), (0, 0), (1, 1)),
+    ((1, 0), (0, 0), (0, 1), (1, 1)),
     ((0, 0), (1, 1), (2, 0), (2, 1), (1, 0), (0, 1)),
 )
 
@@ -195,33 +218,41 @@
     refs, out = list(refs), [[None, None] for axis in range(3)]
     for axis, which in message_keys(sizes, sent, stage):
         out[axis][which] = refs.pop(0)
+    if stage == 0 and not sent and sizes[0] > 2:
+        out[2][0] = ZFields(out[0][1], out[2][0])
     return out, refs
 
 
-def first_kernel(
-    sizes, level, adjoint, density, velocity, stiffness, sponge, source, scaled, base, *refs
-):
+def first_kernel(sizes, level, adjoint, density, velocity, stiffness, sponge, source, *refs):
+    adjoint_now, sponge_now, source_now, scaled, base, *refs = refs
     outs, scratch = split(refs, sizes, 0, True)
-    *targets, arrived = scratch
-    level_now, adjoint_now, density_now, velocity_now, stiffness_now, sponge_now, source_now = targets
+    level_now, density_now, velocity_now, stiffness_now, arrived = scratch
+    targets = (
+        level_now, density_now, velocity_now, stiffness_now, adjoint_now, sponge_now, source_now
+    )
     copies = [
         pltpu.make_async_copy(there, here, arrived.at[index])
         for index, (there, here) in enumerate(
-            zip((level, adjoint, density, velocity, stiffness, sponge, source), targets)
+            zip((level, density, velocity, stiffness, adjoint, sponge, source), targets)
         )
     ]
     for copy in copies:
         copy.start()
-    for copy in copies:
-        copy.wait()
+    level_copy, density_copy, velocity_copy, stiffness_copy, *other_copies = copies
+    level_copy.wait()
     here = positions()
     own_level = level_now[here[0], here[2], here[1]]
     half_inverse = 0.5 * lax.shift_left(jnp.int32(1), own_level).astype(jnp.float32)
+    density_copy.wait()
+    scaled[3] = half_inverse * density_now[...]
+    scaled[5] = half_inverse / density_now[...]
+    velocity_copy.wait()
     for direction in range(3):
         scaled[direction] = half_inverse * velocity_now[direction]
-    scaled[3] = half_inverse * density_now[...]
+    stiffness_copy.wait()
     scaled[4] = half_inverse * stiffness_now[...]
-    scaled[5] = half_inverse / density_now[...]
+    for copy in other_copies:
+        copy.wait()
     tiles = own_part((0.0, 1.0), scaled, sponge_now, None, adjoint_now, base)
     x_low = tiles[0][0] + [source_now[tile_at(0), :]]
     x_high = tiles[CX - 1][0] + [source_now[tile_at(CX - 1), :]]
@@ -245,6 +276,12 @@
     ):
         outs[2][0][index] = pack_lanes(fields)
     outs[2][0][5] = jnp.zeros(TILE, jnp.float32)
+    if sizes[0] > 2:
+
+        @pl.when(at_start())
+        def _():
+            for index in range(5):
+                outs[0][1][index] = outs[2][0][index]
 
 
 def own_kernel(weights, scaled, sponge, start, state, out):
@@ -343,7 +380,7 @@
         faces[index] = sign * face
 
 
-def stage_kernel(sizes, weight, base, scaled, *refs):
+def stage_kernel(sizes, weight, base, scaled, routes, *refs):
     received, (section, *outs) = split(refs, sizes, 0)
     add_halo(base, received, weight, sizes, section)
     outs = split(outs, sizes, 1, True)[0]
@@ -528,8 +565,6 @@
     put_pair(x_low, x_high, here[0], outs[0])
     put_pair(y_low, y_high, here[1], outs[1])
     outs[2][0][0] = packed
-    for index in range(1, 5):
-        outs[2][0][index] = jnp.zeros(TILE, jnp.float32)
     copy.wait()
 
 
@@ -589,11 +624,8 @@
     patch_owner,
 ):
     sizes = tuple(lax.axis_size(axis) for axis in AXES)
-    permutations = (
-        pairings(sizes, 0, 1),
-        pairings(sizes, 1, 1),
-        pairings(sizes, 2, 1),
-    )
+    later = (pairings(sizes, 0, 1), pairings(sizes, 1, 1), pairings(sizes, 2, 1))
+    permutations = (first_round(sizes), later, later)
     devices = patch_owner.shape[0]
     state_shape = terminal_adjoint.shape
     start = terminal_adjoint.reshape(STATE)
@@ -606,31 +638,29 @@
 
     def message_shapes(fields, stage):
         return [
-            (fields,) + TILE for key in message_keys(sizes, True, stage)
+            (1 if stage == 2 and key[0] == 2 else fields,) + TILE
+            for key in message_keys(sizes, True, stage)
         ]
 
     def exchange(messages, stage):
         sends = dict(zip(message_keys(sizes, True, stage), messages))
         sends[2, 1] = sends.get((2, 0))
         return [
-            lax.ppermute(sends[key], AXES, permutations[key[0]][key[1]])
+            lax.ppermute(sends[key], AXES, permutations[stage][key[0]][key[1]])
             for key in message_keys(sizes, False, stage)
         ]
 
     flat = pltpu.VMEM(FLAT, jnp.float32)
     state = pltpu.VMEM(STATE, jnp.float32)
-    scaled, base, *sent = call(
+    start, sponge, source, scaled, base, *sent = call(
         functools.partial(first_kernel, sizes),
         [HBM] * 7,
         (level, start, density, velocity, stiffness, sponge, source),
-        [(6,) + FLAT, STATE] + message_shapes(6, 0),
+        [STATE, FLAT, FLAT, (6,) + FLAT, STATE] + message_shapes(6, 0),
         scratch=[
             pltpu.SMEM(level.shape, jnp.int32),
-            state,
             flat,
             pltpu.VMEM((3,) + FLAT, jnp.float32),
-            flat,
-            flat,
             flat,
             pltpu.SemaphoreType.DMA((7,)),
         ],
@@ -644,7 +674,7 @@
         [(devices, 3 * CY * CY), (7 * CZ, CZ)],
         dtype=jnp.bfloat16,
     )
-    operands = (base, scaled, *received_one)
+    operands = (base, scaled, routes, *received_one)
     section, *sent = call(
         functools.partial(stage_kernel, sizes, step_length),
         [VMEM] * len(operands),

time: 29.5 us -> 29.5 us (level)
  starting transfers between devices: 16.7 us -> 17.9 us
  local copies, waits for them, and re-layouts: 1.18 us -> 0.02 us
    all_to_all x1, starting transfers between devices: 2.61 us -> 4.15 us  [body(): lax.all_to_all(table.reshape(devices, 1, CZ), AXES, 0, 0, tiled=True)]
    unnamed x10 -> x4, local copies, waits for them, and re-layouts: 1.18 us -> 0.02 us
    all_to_all x1, waiting for transfers between devices: 0.55 us -> 0.07 us  [body(): lax.all_to_all(table.reshape(devices, 1, CZ), AXES, 0, 0, tiled=True)]
    ppermute x14, waiting for transfers between devices: 4.93 us -> 5.37 us  [exchange(): lax.ppermute(sends[key], AXES, permutations[stage][key[0]][key[1]])]
    ppermute x14, starting transfers between devices: 14.1 us -> 13.8 us  [exchange(): lax.ppermute(sends[key], AXES, permutations[stage][key[0]][key[1]])]
  transfers between devices with their start and end apart: 15 -> 15, of which waited for: 6 -> 5; matrix products, arithmetic and copies ran while one was open for 0% -> 0% of each run, Pallas kernels for 4% -> 5%
where the time goes in v9:
time: 29.5 us; the launch traced here: 29.3 us
  starting transfers between devices  17.9 us (61%)
  waiting for transfers between devices  5.45 us (18%)
  Pallas kernels  5.14 us (17%)
  between operations  0.75 us (3%)
    ppermute x14, starting transfers between devices, exchange(): lax.ppermute(sends[key], AXES, permutations[stage][key[0]][key[1]])  13.8 us
    ppermute x14, waiting for transfers between devices, exchange(): lax.ppermute(sends[key], AXES, permutations[stage][key[0]][key[1]])  5.37 us
    pallas_call x9, Pallas kernels, call(): pl.pallas_call(kernel, out_shape=[space(shape, dtype) for space, shape in...  5.14 us
    all_to_all x1, starting transfers between devices, body(): lax.all_to_all(table.reshape(devices, 1, CZ), AXES, 0, 0, tiled=True)  4.15 us
  transfers between devices with their start and end apart: 15, of which 5 were waited for; matrix products, arithmetic and copies ran while one was open for 0% of the time, Pallas kernels for 5%

profile of v9, /device:TPU:0, one launch (start us, length us, event | category | flops | bytes accessed | tf_op | source)
XLA Modules:
  0.0 29.3 jit_solution(12449335906618270605)
XLA Ops:
  0.6 1.5 %shard_map.104 = (f32[5,64,128]{2,1,0:T(8,128)S(1)}, f32[64,128]{1,0:T(8,128)S(1)}, f32[64,128]{1,0:T(8,128)S(1)}, f32[6,64,128]{2,1,0:T(8,128)S(1)}, f32[5,64,1...) custom-call(s32[4,2,4]{2,1,0:T(2,128)} %bitcast.22, ...), custom_call_target="tpu_custom_call" | custom-call | flops 2000000 | bytes 1000000 | tf_op jit(solution)/shard_map/pallas_call | solution.py:604
  2.1 0.5 %collective-permute-start = (f32[6,8,128]{2,1,0:T(8,128)S(1)}, f32[6,8,128]{2,1,0:T(8,128)S(1)}, u32[]{:S(2)}, u32[]{:S(2)}) collective-permute-start(f32[6,8,128]{2,1,0:T(8,128)S(1)} %get-tuple-element.38), channel_id=1, source_target_pairs={{0,2},{1,3},{2,0},{3,1},{4,6},{5,7},{6,4},{7,5},{8,10},{9,11},{10,... | collective-permute-start | bytes 73736 | tf_op jit(solution)/shard_map/ppermute | solution.py:649
  2.6 2.6 %collective-permute-start.1 = (f32[6,8,128]{2,1,0:T(8,128)S(1)}, f32[6,8,128]{2,1,0:T(8,128)S(1)}, u32[]{:S(2)}, u32[]{:S(2)}) collective-permute-start(f32[6,8,128]{2,1,0:T(8,128)S(1)} %get-tuple-element.39), channel_id=1, source_target_pairs={{0,1},{1,0},{2,3},{3,2},{4,5},{5,4},{6,7},{7,6},{8,16},{9,17},{10,... | collective-permute-start | bytes 73736 | tf_op jit(solution)/shard_map/ppermute | solution.py:649
  5.2 1.6 %collective-permute-start.2 = (f32[6,8,128]{2,1,0:T(8,128)S(1)}, f32[6,8,128]{2,1,0:T(8,128)S(1)}, u32[]{:S(2)}, u32[]{:S(2)}) collective-permute-start(f32[6,8,128]{2,1,0:T(8,128)S(1)} %get-tuple-element.40), channel_id=1, source_target_pairs={{0,8},{1,9},{2,10},{3,11},{4,12},{5,13},{6,14},{7,15},{8,0},{9,1},... | collective-permute-start | bytes 73736 | tf_op jit(solution)/shard_map/ppermute | solution.py:649
  6.9 1.0 %collective-permute-start.3 = (f32[6,8,128]{2,1,0:T(8,128)S(1)}, f32[6,8,128]{2,1,0:T(8,128)S(1)}, u32[]{:S(2)}, u32[]{:S(2)}) collective-permute-start(f32[6,8,128]{2,1,0:T(8,128)S(1)} %get-tuple-element.41), channel_id=1, source_target_pairs={{0,6},{1,7},{2,4},{3,5},{4,2},{5,3},{6,0},{7,1},{8,14},{9,15},{10,... | collective-permute-start | bytes 73736 | tf_op jit(solution)/shard_map/ppermute | solution.py:649
  7.8 0.6 %collective-permute-start.4 = (f32[6,8,128]{2,1,0:T(8,128)S(1)}, f32[6,8,128]{2,1,0:T(8,128)S(1)}, u32[]{:S(2)}, u32[]{:S(2)}) collective-permute-start(f32[6,8,128]{2,1,0:T(8,128)S(1)} %get-tuple-element.42.own), channel_id=1, source_target_pairs={{0,2},{1,3},{2,0},{3,1},{4,6},{5,7},{6,4},{7,5},{8,9},{9,8},{10,11... | collective-permute-start | bytes 73736 | tf_op jit(solution)/shard_map/ppermute | solution.py:649
  8.5 0.7 %shard_map.105 = (bf16[32,192]{1,0:T(8,128)(2,1)S(1)}, bf16[896,128]{1,0:T(8,128)(2,1)S(1)}) custom-call(s32[4,2,4]{2,1,0:T(2,128)S(1)} %bitcast.14, s32[32]{0:T(128)S(1)} %copy-done.1), custom_call_target="tpu_custom_call" | custom-call | flops 2000000 | bytes 1000000 | tf_op jit(solution)/shard_map/pallas_call | solution.py:604
  9.2 1.1 %collective-permute-done.3.refs_3_ = f32[6,8,128]{2,1,0:T(8,128)S(1)} collective-permute-done((f32[6,8,128]{2,1,0:T(8,128)S(1)}, f32[6,8,128]{2,1,0:T(8,128)S(1)}, u32[]{:S(2)}, u32[]{:S(2)}) %collective-permute-start.3) | collective-permute-done | bytes 24608 | tf_op jit(solution)/shard_map/ppermute | solution.py:649
  10.3 0.2 shard_map.106
  10.5 0.2 collective-permute-start.5
  10.7 1.7 %collective-permute-start.6 = (f32[6,8,128]{2,1,0:T(8,128)S(1)}, f32[6,8,128]{2,1,0:T(8,128)S(1)}, u32[]{:S(2)}, u32[]{:S(2)}) collective-permute-start(f32[6,8,128]{2,1,0:T(8,128)S(1)} %get-tuple-element.52), channel_id=1, source_target_pairs={{0,8},{1,9},{2,10},{3,11},{4,12},{5,13},{6,14},{7,15},{8,0},{9,1},... | collective-permute-start | bytes 73736 | tf_op jit(solution)/shard_map/ppermute | solution.py:649
  12.6 0.5 %collective-permute-start.8 = (f32[6,8,128]{2,1,0:T(8,128)S(1)}, f32[6,8,128]{2,1,0:T(8,128)S(1)}, u32[]{:S(2)}, u32[]{:S(2)}) collective-permute-start(f32[6,8,128]{2,1,0:T(8,128)S(1)} %get-tuple-element.54), channel_id=1, source_target_pairs={{0,6},{1,7},{2,4},{3,5},{4,2},{5,3},{6,0},{7,1},{8,14},{9,15},{10,... | collective-permute-start | bytes 73736 | tf_op jit(solution)/shard_map/ppermute | solution.py:649
  13.1 0.2 shard_map.107.base
  13.6 1.0 %collective-permute-done.6.refs_1_ = f32[6,8,128]{2,1,0:T(8,128)S(1)} collective-permute-done((f32[6,8,128]{2,1,0:T(8,128)S(1)}, f32[6,8,128]{2,1,0:T(8,128)S(1)}, u32[]{:S(2)}, u32[]{:S(2)}) %collective-permute-start.6) | collective-permute-done | bytes 24608 | tf_op jit(solution)/shard_map/ppermute | solution.py:649
  14.6 1.3 %collective-permute-done.8.refs_3_ = f32[6,8,128]{2,1,0:T(8,128)S(1)} collective-permute-done((f32[6,8,128]{2,1,0:T(8,128)S(1)}, f32[6,8,128]{2,1,0:T(8,128)S(1)}, u32[]{:S(2)}, u32[]{:S(2)}) %collective-permute-start.8) | collective-permute-done | bytes 24608 | tf_op jit(solution)/shard_map/ppermute | solution.py:649
  15.8 1.2 %shard_map.110 = (f32[5,64,128]{2,1,0:T(8,128)S(1)}, f32[32,128]{1,0:T(8,128)}, f32[5,8,128]{2,1,0:T(8,128)S(1)}, f32[5,8,128]{2,1,0:T(8,128)S(1)}, f32[1,8,128]...) custom-call(f32[5,64,128]{2,1,0:T(8,128)S(1)} %shard_map.107.base, ...), custom_call_target="tpu_custom_call" | custom-call | flops 2000000 | bytes 1000000 | tf_op jit(solution)/shard_map/pallas_call | solution.py:604
  17.1 4.2 %all-to-all-start = ((f32[32,1,128]{2,1,0:T(1,128)}), f32[32,1,128]{2,1,0:T(1,128)S(1)}, u32[]{:S(2)}, u32[]{:S(2)}) async-start(f32[32,1,128]{2,1,0:T(1,128)} %bitcast.21), calls=%async_computation | async-start | bytes 32768 | tf_op jit(solution)/shard_map/all_to_all | solution.py:714
  21.3 1.8 %collective-permute-start.9 = (f32[5,8,128]{2,1,0:T(8,128)S(1)}, f32[5,8,128]{2,1,0:T(8,128)S(1)}, u32[]{:S(2)}, u32[]{:S(2)}) collective-permute-start(f32[5,8,128]{2,1,0:T(8,128)S(1)} %get-tuple-element.57), channel_id=1, source_target_pairs={{0,8},{1,9},{2,10},{3,11},{4,12},{5,13},{6,14},{7,15},{8,0},{9,1},... | collective-permute-start | bytes 61448 | tf_op jit(solution)/shard_map/ppermute | solution.py:649
  23.1 0.9 %collective-permute-start.10 = (f32[5,8,128]{2,1,0:T(8,128)S(1)}, f32[5,8,128]{2,1,0:T(8,128)S(1)}, u32[]{:S(2)}, u32[]{:S(2)}) collective-permute-start(f32[5,8,128]{2,1,0:T(8,128)S(1)} %get-tuple-element.58), channel_id=1, source_target_pairs={{0,6},{1,7},{2,4},{3,5},{4,2},{5,3},{6,0},{7,1},{8,14},{9,15},{10,... | collective-permute-start | bytes 61448 | tf_op jit(solution)/shard_map/ppermute | solution.py:649
  24.0 0.6 %collective-permute-start.12 = (f32[5,8,128]{2,1,0:T(8,128)S(1)}, f32[5,8,128]{2,1,0:T(8,128)S(1)}, u32[]{:S(2)}, u32[]{:S(2)}) collective-permute-start(f32[5,8,128]{2,1,0:T(8,128)S(1)} %get-tuple-element.60), channel_id=1, source_target_pairs={{0,2},{1,3},{2,0},{3,1},{4,6},{5,7},{6,4},{7,5},{8,10},{9,11},{10,... | collective-permute-start | bytes 61448 | tf_op jit(solution)/shard_map/ppermute | solution.py:649
  24.7 1.5 %collective-permute-start.11 = (f32[1,8,128]{2,1,0:T(8,128)S(1)}, f32[1,8,128]{2,1,0:T(8,128)S(1)}, u32[]{:S(2)}, u32[]{:S(2)}) collective-permute-start(f32[1,8,128]{2,1,0:T(8,128)S(1)} %get-tuple-element.59), channel_id=1, source_target_pairs={{0,1},{1,0},{2,3},{3,2},{4,5},{5,4},{6,7},{7,6},{8,9},{9,8},{10,11... | collective-permute-start | bytes 12296 | tf_op jit(solution)/shard_map/ppermute | solution.py:649
  26.1 0.2 shard_map.111.base
  26.3 2.0 %collective-permute-done.11.refs_2_ = f32[1,8,128]{2,1,0:T(8,128)S(1)} collective-permute-done((f32[1,8,128]{2,1,0:T(8,128)S(1)}, f32[1,8,128]{2,1,0:T(8,128)S(1)}, u32[]{:S(2)}, u32[]{:S(2)}) %collective-permute-start.11) | collective-permute-done | bytes 4128 | tf_op jit(solution)/shard_map/ppermute | solution.py:649
  28.4 0.9 %shard_map.112 = (f32[5,64,128]{2,1,0:T(8,128)}, f32[1,40]{1,0:T(1,128)}) custom-call(f32[5,64,128]{2,1,0:T(8,128)S(1)} %shard_map.111.base, f32[32,128]{1,0:T(8,128)S(1)} %bitcast.13, f32[5,8,128]{2,1,0:T(8,128)S(1)} %collective-permute-done.9.refs_0_, f32[5,8,128]{2,1,0:T(8,128)S(1)} %collective-permute-done.10.refs_1_, ...), custom_call_target="tpu_custom_call" | custom-call | flops 2000000 | bytes 1000000 | tf_op jit(solution)/shard_map/pallas_call | solution.py:604
  (19 shorter events, 0.6 us)
Async XLA Ops:
  2.1 7.1 %collective-permute-start = (f32[6,8,128]{2,1,0:T(8,128)S(1)}, f32[6,8,128]{2,1,0:T(8,128)S(1)}, u32[]{:S(2)}, u32[]{:S(2)}) collective-permute-start(f32[6,8,128]{2,1,0:T(8,128)S(1)} %get-tuple-element.38), channel_id=1, source_target_pairs={{0,2},{1,3},{2,0},{3,1},{4,6},{5,7},{6,4},{7,5},{8,10},{9,11},{10,... | collective-permute-start | bytes 73736 | tf_op jit(solution)/shard_map/ppermute | solution.py:649
  2.6 5.8 %copy-start = (s32[4,4,2]{1,2,0:T(2,128)S(1)}, s32[4,4,2]{1,2,0:T(2,128)}, u32[]{:S(2)}) copy-start(s32[4,4,2]{1,2,0:T(2,128)} %param.16) | copy-start | bytes 388
  2.6 6.6 %collective-permute-start.1 = (f32[6,8,128]{2,1,0:T(8,128)S(1)}, f32[6,8,128]{2,1,0:T(8,128)S(1)}, u32[]{:S(2)}, u32[]{:S(2)}) collective-permute-start(f32[6,8,128]{2,1,0:T(8,128)S(1)} %get-tuple-element.39), channel_id=1, source_target_pairs={{0,1},{1,0},{2,3},{3,2},{4,5},{5,4},{6,7},{7,6},{8,16},{9,17},{10,... | collective-permute-start | bytes 73736 | tf_op jit(solution)/shard_map/ppermute | solution.py:649
  5.2 4.0 %collective-permute-start.2 = (f32[6,8,128]{2,1,0:T(8,128)S(1)}, f32[6,8,128]{2,1,0:T(8,128)S(1)}, u32[]{:S(2)}, u32[]{:S(2)}) collective-permute-start(f32[6,8,128]{2,1,0:T(8,128)S(1)} %get-tuple-element.40), channel_id=1, source_target_pairs={{0,8},{1,9},{2,10},{3,11},{4,12},{5,13},{6,14},{7,15},{8,0},{9,1},... | collective-permute-start | bytes 73736 | tf_op jit(solution)/shard_map/ppermute | solution.py:649
  6.9 3.5 %collective-permute-start.3 = (f32[6,8,128]{2,1,0:T(8,128)S(1)}, f32[6,8,128]{2,1,0:T(8,128)S(1)}, u32[]{:S(2)}, u32[]{:S(2)}) collective-permute-start(f32[6,8,128]{2,1,0:T(8,128)S(1)} %get-tuple-element.41), channel_id=1, source_target_pairs={{0,6},{1,7},{2,4},{3,5},{4,2},{5,3},{6,0},{7,1},{8,14},{9,15},{10,... | collective-permute-start | bytes 73736 | tf_op jit(solution)/shard_map/ppermute | solution.py:649
  7.8 0.7 %copy-start.1 = (s32[32]{0:T(128)S(1)}, s32[32]{0:T(128)}, u32[]{:S(2)}) copy-start(s32[32]{0:T(128)} %owners.1) | copy-start | bytes 388
  7.8 2.5 %collective-permute-start.4 = (f32[6,8,128]{2,1,0:T(8,128)S(1)}, f32[6,8,128]{2,1,0:T(8,128)S(1)}, u32[]{:S(2)}, u32[]{:S(2)}) collective-permute-start(f32[6,8,128]{2,1,0:T(8,128)S(1)} %get-tuple-element.42.own), channel_id=1, source_target_pairs={{0,2},{1,3},{2,0},{3,1},{4,6},{5,7},{6,4},{7,5},{8,9},{9,8},{10,11... | collective-permute-start | bytes 73736 | tf_op jit(solution)/shard_map/ppermute | solution.py:649
  10.5 3.0 %collective-permute-start.5 = (f32[6,8,128]{2,1,0:T(8,128)S(1)}, f32[6,8,128]{2,1,0:T(8,128)S(1)}, u32[]{:S(2)}, u32[]{:S(2)}) collective-permute-start(f32[6,8,128]{2,1,0:T(8,128)S(1)} %get-tuple-element.51), channel_id=1, source_target_pairs={{0,2},{1,3},{2,0},{3,1},{4,6},{5,7},{6,4},{7,5},{8,10},{9,11},{10,... | collective-permute-start | bytes 73736 | tf_op jit(solution)/shard_map/ppermute | solution.py:649
  10.7 3.9 %collective-permute-start.6 = (f32[6,8,128]{2,1,0:T(8,128)S(1)}, f32[6,8,128]{2,1,0:T(8,128)S(1)}, u32[]{:S(2)}, u32[]{:S(2)}) collective-permute-start(f32[6,8,128]{2,1,0:T(8,128)S(1)} %get-tuple-element.52), channel_id=1, source_target_pairs={{0,8},{1,9},{2,10},{3,11},{4,12},{5,13},{6,14},{7,15},{8,0},{9,1},... | collective-permute-start | bytes 73736 | tf_op jit(solution)/shard_map/ppermute | solution.py:649
  12.4 2.2 %collective-permute-start.7 = (f32[6,8,128]{2,1,0:T(8,128)S(1)}, f32[6,8,128]{2,1,0:T(8,128)S(1)}, u32[]{:S(2)}, u32[]{:S(2)}) collective-permute-start(f32[6,8,128]{2,1,0:T(8,128)S(1)} %get-tuple-element.53), channel_id=1, source_target_pairs={{0,2},{1,3},{2,0},{3,1},{4,6},{5,7},{6,4},{7,5},{8,16},{9,17},{10,... | collective-permute-start | bytes 73736 | tf_op jit(solution)/shard_map/ppermute | solution.py:649
  12.6 3.3 %collective-permute-start.8 = (f32[6,8,128]{2,1,0:T(8,128)S(1)}, f32[6,8,128]{2,1,0:T(8,128)S(1)}, u32[]{:S(2)}, u32[]{:S(2)}) collective-permute-start(f32[6,8,128]{2,1,0:T(8,128)S(1)} %get-tuple-element.54), channel_id=1, source_target_pairs={{0,6},{1,7},{2,4},{3,5},{4,2},{5,3},{6,0},{7,1},{8,14},{9,15},{10,... | collective-permute-start | bytes 73736 | tf_op jit(solution)/shard_map/ppermute | solution.py:649
  17.1 11.3 %all-to-all-start = ((f32[32,1,128]{2,1,0:T(1,128)}), f32[32,1,128]{2,1,0:T(1,128)S(1)}, u32[]{:S(2)}, u32[]{:S(2)}) async-start(f32[32,1,128]{2,1,0:T(1,128)} %bitcast.21), calls=%async_computation | async-start | bytes 32768 | tf_op jit(solution)/shard_map/all_to_all | solution.py:714
  21.3 7.0 %collective-permute-start.9 = (f32[5,8,128]{2,1,0:T(8,128)S(1)}, f32[5,8,128]{2,1,0:T(8,128)S(1)}, u32[]{:S(2)}, u32[]{:S(2)}) collective-permute-start(f32[5,8,128]{2,1,0:T(8,128)S(1)} %get-tuple-element.57), channel_id=1, source_target_pairs={{0,8},{1,9},{2,10},{3,11},{4,12},{5,13},{6,14},{7,15},{8,0},{9,1},... | collective-permute-start | bytes 61448 | tf_op jit(solution)/shard_map/ppermute | solution.py:649
  23.1 5.2 %collective-permute-start.10 = (f32[5,8,128]{2,1,0:T(8,128)S(1)}, f32[5,8,128]{2,1,0:T(8,128)S(1)}, u32[]{:S(2)}, u32[]{:S(2)}) collective-permute-start(f32[5,8,128]{2,1,0:T(8,128)S(1)} %get-tuple-element.58), channel_id=1, source_target_pairs={{0,6},{1,7},{2,4},{3,5},{4,2},{5,3},{6,0},{7,1},{8,14},{9,15},{10,... | collective-permute-start | bytes 61448 | tf_op jit(solution)/shard_map/ppermute | solution.py:649
  24.0 4.3 %collective-permute-start.12 = (f32[5,8,128]{2,1,0:T(8,128)S(1)}, f32[5,8,128]{2,1,0:T(8,128)S(1)}, u32[]{:S(2)}, u32[]{:S(2)}) collective-permute-start(f32[5,8,128]{2,1,0:T(8,128)S(1)} %get-tuple-element.60), channel_id=1, source_target_pairs={{0,2},{1,3},{2,0},{3,1},{4,6},{5,7},{6,4},{7,5},{8,10},{9,11},{10,... | collective-permute-start | bytes 61448 | tf_op jit(solution)/shard_map/ppermute | solution.py:649
  24.7 3.6 %collective-permute-start.13 = (f32[5,8,128]{2,1,0:T(8,128)S(1)}, f32[5,8,128]{2,1,0:T(8,128)S(1)}, u32[]{:S(2)}, u32[]{:S(2)}) collective-permute-start(f32[5,8,128]{2,1,0:T(8,128)S(1)} %get-tuple-element.61), channel_id=1, source_target_pairs={{0,2},{1,3},{2,0},{3,1},{4,6},{5,7},{6,4},{7,5},{8,16},{9,17},{10,... | collective-permute-start | bytes 61448 | tf_op jit(solution)/shard_map/ppermute | solution.py:649
  24.7 3.6 %collective-permute-start.11 = (f32[1,8,128]{2,1,0:T(8,128)S(1)}, f32[1,8,128]{2,1,0:T(8,128)S(1)}, u32[]{:S(2)}, u32[]{:S(2)}) collective-permute-start(f32[1,8,128]{2,1,0:T(8,128)S(1)} %get-tuple-element.59), channel_id=1, source_target_pairs={{0,1},{1,0},{2,3},{3,2},{4,5},{5,4},{6,7},{7,6},{8,9},{9,8},{10,11... | collective-permute-start | bytes 12296 | tf_op jit(solution)/shard_map/ppermute | solution.py:649

commit v10 on v9

--- a/solution.py
+++ b/solution.py
@@ -109,14 +109,18 @@
     for index, field in enumerate(fields):
         for x in range(CX):
             k = index * CX + x
-            tiles.append(pltpu.roll(field[x], (BASE + 2 * k + 1) % CZ, 1))
+            tile = field[x]
+            tiles.append(None if tile is None else pltpu.roll(tile, (BASE + 2 * k + 1) % CZ, 1))
     bit = 1
     while len(tiles) > 1:
         upper = (lanes & bit) != 0
-        pairs = [
-            jnp.where(upper, tiles[at + 1], tiles[at]) if at + 1 < len(tiles) else tiles[at]
-            for at in range(0, len(tiles), 2)
-        ]
+        pairs = []
+        for at in range(0, len(tiles), 2):
+            low, high = tiles[at], tiles[at + 1] if at + 1 < len(tiles) else None
+            if low is None or high is None:
+                pairs.append(high if low is None else low)
+            else:
+                pairs.append(jnp.where(upper, high, low))
         tiles, bit = pairs, 2 * bit
     return tiles[0]
 
@@ -269,13 +273,12 @@
         (
             along[2],
             [[base[component, tile_at(x), :] for x in range(CX)] for component in range(5)],
-            along[0],
+            [[tile if x in (0, CX - 1) else None for x, tile in enumerate(f)] for f in along[0]],
             along[1],
             [[scaled[row, tile_at(x), :] for x in range(CX)] for row in range(2, 6)],
         )
     ):
         outs[2][0][index] = pack_lanes(fields)
-    outs[2][0][5] = jnp.zeros(TILE, jnp.float32)
     if sizes[0] > 2:
 
         @pl.when(at_start())
@@ -459,6 +462,7 @@
 
 def product(value, matrix):
     count = value.shape[0]
+    assert count % 16 == 0
     stacked = jnp.concatenate(three_parts(value), axis=0)
     result = jnp.dot(stacked, matrix, preferred_element_type=jnp.float32)
     return result[:count] + result[count : 2 * count] + result[2 * count :]
@@ -471,6 +475,8 @@
     lanes = lax.broadcasted_iota(jnp.int32, shape, 1) % (CY * CY)
     chosen = jnp.zeros(shape, jnp.bool_)
     for index, offset in enumerate(OFFSETS):
+        if offset is None:
+            continue
         place = [
             jnp.clip(here[axis] + offset[axis], 0, sizes[axis] - 1) for axis in range(3)
         ]
@@ -497,6 +503,7 @@
     (-1, 0, 0),
     (0, 1, 0),
     (0, -1, 0),
+    None,
     (0, 0, 1),
     (0, 0, -1),
 )
@@ -543,18 +550,20 @@
         accumulate(before, 4, shape_before * drawn[2])
         accumulate(after, 4, shape_after * drawn[2])
     columns = []
+    zero = jnp.zeros(TILE, jnp.float32)
     for f in range(5):
         own = main[f] + pltpu.roll(before[f], CZ - 1, 1) - pltpu.roll(after[f], 1, 1)
         columns.append(
             jnp.concatenate(
-                [own, faces[0] * x_high[f], faces[1] * x_low[f], faces[2] * y_high[f], faces[3] * y_low[f]],
+                [own, faces[0] * x_high[f], faces[1] * x_low[f], faces[2] * y_high[f], faces[3] * y_low[f], zero],
                 axis=0,
             )
         )
     blocks = product(jnp.concatenate(columns, axis=1), gather[: 5 * CZ, :])
-    above = product(faces[4] * packed, gather[5 * CZ : 6 * CZ, :])
-    below = product(faces[5] * packed, gather[6 * CZ :, :])
-    blocks = jnp.concatenate([blocks, above, below, jnp.zeros(TILE, jnp.float32)], axis=0)
+    above = jnp.concatenate([faces[4] * packed, zero], axis=1)
+    below = jnp.concatenate([zero, faces[5] * packed], axis=1)
+    z_blocks = product(jnp.concatenate([above, below], axis=0), gather[5 * CZ :, :])
+    blocks = jnp.concatenate([blocks, z_blocks], axis=0)
     rows_out[...] = jnp.dot(
         routes[...],
         jnp.concatenate(three_parts(blocks), axis=0),
@@ -638,7 +647,7 @@
 
     def message_shapes(fields, stage):
         return [
-            (1 if stage == 2 and key[0] == 2 else fields,) + TILE
+            ({0: 5, 2: 1}.get(stage) if key[0] == 2 else fields,) + TILE
             for key in message_keys(sizes, True, stage)
         ]
 

time: 29.5 us -> 29.4 us (level)
  transfers between devices with their start and end apart: 15 -> 15, of which waited for: 5 -> 6; matrix products, arithmetic and copies ran while one was open for 0% -> 0% of each run, Pallas kernels for 5% -> 5%
where the time goes in v10:
time: 29.4 us; the launch traced here: 29.2 us
  starting transfers between devices  17.9 us (61%)
  waiting for transfers between devices  5.46 us (19%)
  Pallas kernels  5.11 us (17%)
  between operations  0.73 us (2%)
    ppermute x14, starting transfers between devices, exchange(): lax.ppermute(sends[key], AXES, permutations[stage][key[0]][key[1]])  13.8 us
    ppermute x14, waiting for transfers between devices, exchange(): lax.ppermute(sends[key], AXES, permutations[stage][key[0]][key[1]])  5.39 us
    pallas_call x9, Pallas kernels, call(): pl.pallas_call(kernel, out_shape=[space(shape, dtype) for space, shape in...  5.11 us
    all_to_all x1, starting transfers between devices, body(): lax.all_to_all(table.reshape(devices, 1, CZ), AXES, 0, 0, tiled=True)  4.15 us
  transfers between devices with their start and end apart: 15, of which 6 were waited for; matrix products, arithmetic and copies ran while one was open for 0% of the time, Pallas kernels for 5%

profile of v10, /device:TPU:0, one launch (start us, length us, event | category | flops | bytes accessed | tf_op | source)
XLA Modules:
  0.0 29.2 jit_solution(740762849137074938)
XLA Ops:
  0.6 1.4 %shard_map.104 = (f32[5,64,128]{2,1,0:T(8,128)S(1)}, f32[64,128]{1,0:T(8,128)S(1)}, f32[64,128]{1,0:T(8,128)S(1)}, f32[6,64,128]{2,1,0:T(8,128)S(1)}, f32[5,64,1...) custom-call(s32[4,2,4]{2,1,0:T(2,128)} %bitcast.22, ...), custom_call_target="tpu_custom_call" | custom-call | flops 2000000 | bytes 1000000 | tf_op jit(solution)/shard_map/pallas_call | solution.py:613
  2.1 0.5 %collective-permute-start = (f32[6,8,128]{2,1,0:T(8,128)S(1)}, f32[6,8,128]{2,1,0:T(8,128)S(1)}, u32[]{:S(2)}, u32[]{:S(2)}) collective-permute-start(f32[6,8,128]{2,1,0:T(8,128)S(1)} %get-tuple-element.38), channel_id=1, source_target_pairs={{0,2},{1,3},{2,0},{3,1},{4,6},{5,7},{6,4},{7,5},{8,10},{9,11},{10,... | collective-permute-start | bytes 73736 | tf_op jit(solution)/shard_map/ppermute | solution.py:658
  2.6 2.6 %collective-permute-start.1 = (f32[6,8,128]{2,1,0:T(8,128)S(1)}, f32[6,8,128]{2,1,0:T(8,128)S(1)}, u32[]{:S(2)}, u32[]{:S(2)}) collective-permute-start(f32[6,8,128]{2,1,0:T(8,128)S(1)} %get-tuple-element.39), channel_id=1, source_target_pairs={{0,1},{1,0},{2,3},{3,2},{4,5},{5,4},{6,7},{7,6},{8,16},{9,17},{10,... | collective-permute-start | bytes 73736 | tf_op jit(solution)/shard_map/ppermute | solution.py:658
  5.2 1.6 %collective-permute-start.2 = (f32[6,8,128]{2,1,0:T(8,128)S(1)}, f32[6,8,128]{2,1,0:T(8,128)S(1)}, u32[]{:S(2)}, u32[]{:S(2)}) collective-permute-start(f32[6,8,128]{2,1,0:T(8,128)S(1)} %get-tuple-element.40), channel_id=1, source_target_pairs={{0,8},{1,9},{2,10},{3,11},{4,12},{5,13},{6,14},{7,15},{8,0},{9,1},... | collective-permute-start | bytes 73736 | tf_op jit(solution)/shard_map/ppermute | solution.py:658
  6.8 1.0 %collective-permute-start.3 = (f32[6,8,128]{2,1,0:T(8,128)S(1)}, f32[6,8,128]{2,1,0:T(8,128)S(1)}, u32[]{:S(2)}, u32[]{:S(2)}) collective-permute-start(f32[6,8,128]{2,1,0:T(8,128)S(1)} %get-tuple-element.41), channel_id=1, source_target_pairs={{0,6},{1,7},{2,4},{3,5},{4,2},{5,3},{6,0},{7,1},{8,14},{9,15},{10,... | collective-permute-start | bytes 73736 | tf_op jit(solution)/shard_map/ppermute | solution.py:658
  7.8 0.6 %collective-permute-start.4 = (f32[5,8,128]{2,1,0:T(8,128)S(1)}, f32[5,8,128]{2,1,0:T(8,128)S(1)}, u32[]{:S(2)}, u32[]{:S(2)}) collective-permute-start(f32[5,8,128]{2,1,0:T(8,128)S(1)} %get-tuple-element.42.own), channel_id=1, source_target_pairs={{0,2},{1,3},{2,0},{3,1},{4,6},{5,7},{6,4},{7,5},{8,9},{9,8},{10,11... | collective-permute-start | bytes 61448 | tf_op jit(solution)/shard_map/ppermute | solution.py:658
  8.5 0.7 %shard_map.105 = (bf16[32,192]{1,0:T(8,128)(2,1)S(1)}, bf16[896,128]{1,0:T(8,128)(2,1)S(1)}) custom-call(s32[4,2,4]{2,1,0:T(2,128)S(1)} %bitcast.14, s32[32]{0:T(128)S(1)} %copy-done.1), custom_call_target="tpu_custom_call" | custom-call | flops 2000000 | bytes 1000000 | tf_op jit(solution)/shard_map/pallas_call | solution.py:613
  9.3 1.0 %collective-permute-done.3.refs_3_ = f32[6,8,128]{2,1,0:T(8,128)S(1)} collective-permute-done((f32[6,8,128]{2,1,0:T(8,128)S(1)}, f32[6,8,128]{2,1,0:T(8,128)S(1)}, u32[]{:S(2)}, u32[]{:S(2)}) %collective-permute-start.3) | collective-permute-done | bytes 24608 | tf_op jit(solution)/shard_map/ppermute | solution.py:658
  10.3 0.2 shard_map.106
  10.5 0.2 collective-permute-start.5
  10.7 1.7 %collective-permute-start.6 = (f32[6,8,128]{2,1,0:T(8,128)S(1)}, f32[6,8,128]{2,1,0:T(8,128)S(1)}, u32[]{:S(2)}, u32[]{:S(2)}) collective-permute-start(f32[6,8,128]{2,1,0:T(8,128)S(1)} %get-tuple-element.52), channel_id=1, source_target_pairs={{0,8},{1,9},{2,10},{3,11},{4,12},{5,13},{6,14},{7,15},{8,0},{9,1},... | collective-permute-start | bytes 73736 | tf_op jit(solution)/shard_map/ppermute | solution.py:658
  12.6 0.5 %collective-permute-start.8 = (f32[6,8,128]{2,1,0:T(8,128)S(1)}, f32[6,8,128]{2,1,0:T(8,128)S(1)}, u32[]{:S(2)}, u32[]{:S(2)}) collective-permute-start(f32[6,8,128]{2,1,0:T(8,128)S(1)} %get-tuple-element.54), channel_id=1, source_target_pairs={{0,6},{1,7},{2,4},{3,5},{4,2},{5,3},{6,0},{7,1},{8,14},{9,15},{10,... | collective-permute-start | bytes 73736 | tf_op jit(solution)/shard_map/ppermute | solution.py:658
  13.0 0.2 shard_map.107.base
  13.5 1.0 %collective-permute-done.6.refs_1_ = f32[6,8,128]{2,1,0:T(8,128)S(1)} collective-permute-done((f32[6,8,128]{2,1,0:T(8,128)S(1)}, f32[6,8,128]{2,1,0:T(8,128)S(1)}, u32[]{:S(2)}, u32[]{:S(2)}) %collective-permute-start.6) | collective-permute-done | bytes 24608 | tf_op jit(solution)/shard_map/ppermute | solution.py:658
  14.6 1.3 %collective-permute-done.8.refs_3_ = f32[6,8,128]{2,1,0:T(8,128)S(1)} collective-permute-done((f32[6,8,128]{2,1,0:T(8,128)S(1)}, f32[6,8,128]{2,1,0:T(8,128)S(1)}, u32[]{:S(2)}, u32[]{:S(2)}) %collective-permute-start.8) | collective-permute-done | bytes 24608 | tf_op jit(solution)/shard_map/ppermute | solution.py:658
  15.8 1.3 %shard_map.110 = (f32[5,64,128]{2,1,0:T(8,128)S(1)}, f32[32,128]{1,0:T(8,128)}, f32[5,8,128]{2,1,0:T(8,128)S(1)}, f32[5,8,128]{2,1,0:T(8,128)S(1)}, f32[1,8,128]...) custom-call(f32[5,64,128]{2,1,0:T(8,128)S(1)} %shard_map.107.base, ...), custom_call_target="tpu_custom_call" | custom-call | flops 2000000 | bytes 1000000 | tf_op jit(solution)/shard_map/pallas_call | solution.py:613
  17.1 4.2 %all-to-all-start = ((f32[32,1,128]{2,1,0:T(1,128)}), f32[32,1,128]{2,1,0:T(1,128)S(1)}, u32[]{:S(2)}, u32[]{:S(2)}) async-start(f32[32,1,128]{2,1,0:T(1,128)} %bitcast.21), calls=%async_computation | async-start | bytes 32768 | tf_op jit(solution)/shard_map/all_to_all | solution.py:723
  21.2 1.8 %collective-permute-start.9 = (f32[5,8,128]{2,1,0:T(8,128)S(1)}, f32[5,8,128]{2,1,0:T(8,128)S(1)}, u32[]{:S(2)}, u32[]{:S(2)}) collective-permute-start(f32[5,8,128]{2,1,0:T(8,128)S(1)} %get-tuple-element.57), channel_id=1, source_target_pairs={{0,8},{1,9},{2,10},{3,11},{4,12},{5,13},{6,14},{7,15},{8,0},{9,1},... | collective-permute-start | bytes 61448 | tf_op jit(solution)/shard_map/ppermute | solution.py:658
  23.1 0.9 %collective-permute-start.10 = (f32[5,8,128]{2,1,0:T(8,128)S(1)}, f32[5,8,128]{2,1,0:T(8,128)S(1)}, u32[]{:S(2)}, u32[]{:S(2)}) collective-permute-start(f32[5,8,128]{2,1,0:T(8,128)S(1)} %get-tuple-element.58), channel_id=1, source_target_pairs={{0,6},{1,7},{2,4},{3,5},{4,2},{5,3},{6,0},{7,1},{8,14},{9,15},{10,... | collective-permute-start | bytes 61448 | tf_op jit(solution)/shard_map/ppermute | solution.py:658
  24.0 0.6 %collective-permute-start.12 = (f32[5,8,128]{2,1,0:T(8,128)S(1)}, f32[5,8,128]{2,1,0:T(8,128)S(1)}, u32[]{:S(2)}, u32[]{:S(2)}) collective-permute-start(f32[5,8,128]{2,1,0:T(8,128)S(1)} %get-tuple-element.60), channel_id=1, source_target_pairs={{0,2},{1,3},{2,0},{3,1},{4,6},{5,7},{6,4},{7,5},{8,10},{9,11},{10,... | collective-permute-start | bytes 61448 | tf_op jit(solution)/shard_map/ppermute | solution.py:658
  24.7 1.5 %collective-permute-start.11 = (f32[1,8,128]{2,1,0:T(8,128)S(1)}, f32[1,8,128]{2,1,0:T(8,128)S(1)}, u32[]{:S(2)}, u32[]{:S(2)}) collective-permute-start(f32[1,8,128]{2,1,0:T(8,128)S(1)} %get-tuple-element.59), channel_id=1, source_target_pairs={{0,1},{1,0},{2,3},{3,2},{4,5},{5,4},{6,7},{7,6},{8,9},{9,8},{10,11... | collective-permute-start | bytes 12296 | tf_op jit(solution)/shard_map/ppermute | solution.py:658
  26.1 0.2 shard_map.111.base
  26.3 2.0 %collective-permute-done.11.refs_2_ = f32[1,8,128]{2,1,0:T(8,128)S(1)} collective-permute-done((f32[1,8,128]{2,1,0:T(8,128)S(1)}, f32[1,8,128]{2,1,0:T(8,128)S(1)}, u32[]{:S(2)}, u32[]{:S(2)}) %collective-permute-start.11) | collective-permute-done | bytes 4128 | tf_op jit(solution)/shard_map/ppermute | solution.py:658
  28.4 0.9 %shard_map.112 = (f32[5,64,128]{2,1,0:T(8,128)}, f32[1,40]{1,0:T(1,128)}) custom-call(f32[5,64,128]{2,1,0:T(8,128)S(1)} %shard_map.111.base, f32[32,128]{1,0:T(8,128)S(1)} %bitcast.13, f32[5,8,128]{2,1,0:T(8,128)S(1)} %collective-permute-done.9.refs_0_, f32[5,8,128]{2,1,0:T(8,128)S(1)} %collective-permute-done.10.refs_1_, ...), custom_call_target="tpu_custom_call" | custom-call | flops 2000000 | bytes 1000000 | tf_op jit(solution)/shard_map/pallas_call | solution.py:613
  (19 shorter events, 0.7 us)
Async XLA Ops:
  2.1 7.2 %collective-permute-start = (f32[6,8,128]{2,1,0:T(8,128)S(1)}, f32[6,8,128]{2,1,0:T(8,128)S(1)}, u32[]{:S(2)}, u32[]{:S(2)}) collective-permute-start(f32[6,8,128]{2,1,0:T(8,128)S(1)} %get-tuple-element.38), channel_id=1, source_target_pairs={{0,2},{1,3},{2,0},{3,1},{4,6},{5,7},{6,4},{7,5},{8,10},{9,11},{10,... | collective-permute-start | bytes 73736 | tf_op jit(solution)/shard_map/ppermute | solution.py:658
  2.6 5.8 %copy-start = (s32[4,4,2]{1,2,0:T(2,128)S(1)}, s32[4,4,2]{1,2,0:T(2,128)}, u32[]{:S(2)}) copy-start(s32[4,4,2]{1,2,0:T(2,128)} %param.16) | copy-start | bytes 388
  2.6 6.7 %collective-permute-start.1 = (f32[6,8,128]{2,1,0:T(8,128)S(1)}, f32[6,8,128]{2,1,0:T(8,128)S(1)}, u32[]{:S(2)}, u32[]{:S(2)}) collective-permute-start(f32[6,8,128]{2,1,0:T(8,128)S(1)} %get-tuple-element.39), channel_id=1, source_target_pairs={{0,1},{1,0},{2,3},{3,2},{4,5},{5,4},{6,7},{7,6},{8,16},{9,17},{10,... | collective-permute-start | bytes 73736 | tf_op jit(solution)/shard_map/ppermute | solution.py:658
  5.2 4.1 %collective-permute-start.2 = (f32[6,8,128]{2,1,0:T(8,128)S(1)}, f32[6,8,128]{2,1,0:T(8,128)S(1)}, u32[]{:S(2)}, u32[]{:S(2)}) collective-permute-start(f32[6,8,128]{2,1,0:T(8,128)S(1)} %get-tuple-element.40), channel_id=1, source_target_pairs={{0,8},{1,9},{2,10},{3,11},{4,12},{5,13},{6,14},{7,15},{8,0},{9,1},... | collective-permute-start | bytes 73736 | tf_op jit(solution)/shard_map/ppermute | solution.py:658
  6.8 3.5 %collective-permute-start.3 = (f32[6,8,128]{2,1,0:T(8,128)S(1)}, f32[6,8,128]{2,1,0:T(8,128)S(1)}, u32[]{:S(2)}, u32[]{:S(2)}) collective-permute-start(f32[6,8,128]{2,1,0:T(8,128)S(1)} %get-tuple-element.41), channel_id=1, source_target_pairs={{0,6},{1,7},{2,4},{3,5},{4,2},{5,3},{6,0},{7,1},{8,14},{9,15},{10,... | collective-permute-start | bytes 73736 | tf_op jit(solution)/shard_map/ppermute | solution.py:658
  7.8 0.7 %copy-start.1 = (s32[32]{0:T(128)S(1)}, s32[32]{0:T(128)}, u32[]{:S(2)}) copy-start(s32[32]{0:T(128)} %owners.1) | copy-start | bytes 388
  7.8 1.5 %collective-permute-start.4 = (f32[5,8,128]{2,1,0:T(8,128)S(1)}, f32[5,8,128]{2,1,0:T(8,128)S(1)}, u32[]{:S(2)}, u32[]{:S(2)}) collective-permute-start(f32[5,8,128]{2,1,0:T(8,128)S(1)} %get-tuple-element.42.own), channel_id=1, source_target_pairs={{0,2},{1,3},{2,0},{3,1},{4,6},{5,7},{6,4},{7,5},{8,9},{9,8},{10,11... | collective-permute-start | bytes 61448 | tf_op jit(solution)/shard_map/ppermute | solution.py:658
  10.5 3.0 %collective-permute-start.5 = (f32[6,8,128]{2,1,0:T(8,128)S(1)}, f32[6,8,128]{2,1,0:T(8,128)S(1)}, u32[]{:S(2)}, u32[]{:S(2)}) collective-permute-start(f32[6,8,128]{2,1,0:T(8,128)S(1)} %get-tuple-element.51), channel_id=1, source_target_pairs={{0,2},{1,3},{2,0},{3,1},{4,6},{5,7},{6,4},{7,5},{8,10},{9,11},{10,... | collective-permute-start | bytes 73736 | tf_op jit(solution)/shard_map/ppermute | solution.py:658
  10.7 3.9 %collective-permute-start.6 = (f32[6,8,128]{2,1,0:T(8,128)S(1)}, f32[6,8,128]{2,1,0:T(8,128)S(1)}, u32[]{:S(2)}, u32[]{:S(2)}) collective-permute-start(f32[6,8,128]{2,1,0:T(8,128)S(1)} %get-tuple-element.52), channel_id=1, source_target_pairs={{0,8},{1,9},{2,10},{3,11},{4,12},{5,13},{6,14},{7,15},{8,0},{9,1},... | collective-permute-start | bytes 73736 | tf_op jit(solution)/shard_map/ppermute | solution.py:658
  12.4 2.2 %collective-permute-start.7 = (f32[6,8,128]{2,1,0:T(8,128)S(1)}, f32[6,8,128]{2,1,0:T(8,128)S(1)}, u32[]{:S(2)}, u32[]{:S(2)}) collective-permute-start(f32[6,8,128]{2,1,0:T(8,128)S(1)} %get-tuple-element.53), channel_id=1, source_target_pairs={{0,2},{1,3},{2,0},{3,1},{4,6},{5,7},{6,4},{7,5},{8,16},{9,17},{10,... | collective-permute-start | bytes 73736 | tf_op jit(solution)/shard_map/ppermute | solution.py:658
  12.6 3.3 %collective-permute-start.8 = (f32[6,8,128]{2,1,0:T(8,128)S(1)}, f32[6,8,128]{2,1,0:T(8,128)S(1)}, u32[]{:S(2)}, u32[]{:S(2)}) collective-permute-start(f32[6,8,128]{2,1,0:T(8,128)S(1)} %get-tuple-element.54), channel_id=1, source_target_pairs={{0,6},{1,7},{2,4},{3,5},{4,2},{5,3},{6,0},{7,1},{8,14},{9,15},{10,... | collective-permute-start | bytes 73736 | tf_op jit(solution)/shard_map/ppermute | solution.py:658
  17.1 11.3 %all-to-all-start = ((f32[32,1,128]{2,1,0:T(1,128)}), f32[32,1,128]{2,1,0:T(1,128)S(1)}, u32[]{:S(2)}, u32[]{:S(2)}) async-start(f32[32,1,128]{2,1,0:T(1,128)} %bitcast.21), calls=%async_computation | async-start | bytes 32768 | tf_op jit(solution)/shard_map/all_to_all | solution.py:723
  21.2 7.0 %collective-permute-start.9 = (f32[5,8,128]{2,1,0:T(8,128)S(1)}, f32[5,8,128]{2,1,0:T(8,128)S(1)}, u32[]{:S(2)}, u32[]{:S(2)}) collective-permute-start(f32[5,8,128]{2,1,0:T(8,128)S(1)} %get-tuple-element.57), channel_id=1, source_target_pairs={{0,8},{1,9},{2,10},{3,11},{4,12},{5,13},{6,14},{7,15},{8,0},{9,1},... | collective-permute-start | bytes 61448 | tf_op jit(solution)/shard_map/ppermute | solution.py:658
  23.1 5.2 %collective-permute-start.10 = (f32[5,8,128]{2,1,0:T(8,128)S(1)}, f32[5,8,128]{2,1,0:T(8,128)S(1)}, u32[]{:S(2)}, u32[]{:S(2)}) collective-permute-start(f32[5,8,128]{2,1,0:T(8,128)S(1)} %get-tuple-element.58), channel_id=1, source_target_pairs={{0,6},{1,7},{2,4},{3,5},{4,2},{5,3},{6,0},{7,1},{8,14},{9,15},{10,... | collective-permute-start | bytes 61448 | tf_op jit(solution)/shard_map/ppermute | solution.py:658
  24.0 4.3 %collective-permute-start.12 = (f32[5,8,128]{2,1,0:T(8,128)S(1)}, f32[5,8,128]{2,1,0:T(8,128)S(1)}, u32[]{:S(2)}, u32[]{:S(2)}) collective-permute-start(f32[5,8,128]{2,1,0:T(8,128)S(1)} %get-tuple-element.60), channel_id=1, source_target_pairs={{0,2},{1,3},{2,0},{3,1},{4,6},{5,7},{6,4},{7,5},{8,10},{9,11},{10,... | collective-permute-start | bytes 61448 | tf_op jit(solution)/shard_map/ppermute | solution.py:658
  24.6 3.6 %collective-permute-start.13 = (f32[5,8,128]{2,1,0:T(8,128)S(1)}, f32[5,8,128]{2,1,0:T(8,128)S(1)}, u32[]{:S(2)}, u32[]{:S(2)}) collective-permute-start(f32[5,8,128]{2,1,0:T(8,128)S(1)} %get-tuple-element.61), channel_id=1, source_target_pairs={{0,2},{1,3},{2,0},{3,1},{4,6},{5,7},{6,4},{7,5},{8,16},{9,17},{10,... | collective-permute-start | bytes 61448 | tf_op jit(solution)/shard_map/ppermute | solution.py:658
  24.7 3.6 %collective-permute-start.11 = (f32[1,8,128]{2,1,0:T(8,128)S(1)}, f32[1,8,128]{2,1,0:T(8,128)S(1)}, u32[]{:S(2)}, u32[]{:S(2)}) collective-permute-start(f32[1,8,128]{2,1,0:T(8,128)S(1)} %get-tuple-element.59), channel_id=1, source_target_pairs={{0,1},{1,0},{2,3},{3,2},{4,5},{5,4},{6,7},{7,6},{8,9},{9,8},{10,11... | collective-permute-start | bytes 12296 | tf_op jit(solution)/shard_map/ppermute | solution.py:658

commit v11 on v10

--- a/solution.py
+++ b/solution.py
@@ -209,7 +209,7 @@
 ORDERS = (
     ((1, 0), (0, 1), (0, 0), (1, 1), (2, 0), (2, 1)),
     ((1, 0), (0, 0), (0, 1), (1, 1)),
-    ((0, 0), (1, 1), (2, 0), (2, 1), (1, 0), (0, 1)),
+    ((0, 0), (1, 1), (0, 1), (2, 0), (2, 1), (1, 0)),
 )
 
 

time: 29.4 us -> 29.4 us (level)
  no operation moved by 1% of the time
where the time goes in v11:
time: 29.4 us; the launch traced here: 29.2 us
  starting transfers between devices  17.9 us (61%)
  waiting for transfers between devices  5.46 us (19%)
  Pallas kernels  5.11 us (17%)
  between operations  0.73 us (2%)
    ppermute x14, starting transfers between devices, exchange(): lax.ppermute(sends[key], AXES, permutations[stage][key[0]][key[1]])  13.8 us
    ppermute x14, waiting for transfers between devices, exchange(): lax.ppermute(sends[key], AXES, permutations[stage][key[0]][key[1]])  5.39 us
    pallas_call x9, Pallas kernels, call(): pl.pallas_call(kernel, out_shape=[space(shape, dtype) for space, shape in...  5.11 us
    all_to_all x1, starting transfers between devices, body(): lax.all_to_all(table.reshape(devices, 1, CZ), AXES, 0, 0, tiled=True)  4.15 us
  transfers between devices with their start and end apart: 15, of which 6 were waited for; matrix products, arithmetic and copies ran while one was open for 0% of the time, Pallas kernels for 5%

profile of v11, /device:TPU:0, one launch (start us, length us, event | category | flops | bytes accessed | tf_op | source)
XLA Modules:
  0.0 29.2 jit_solution(10131842056151908636)
XLA Ops:
  0.6 1.4 %shard_map.104 = (f32[5,64,128]{2,1,0:T(8,128)S(1)}, f32[64,128]{1,0:T(8,128)S(1)}, f32[64,128]{1,0:T(8,128)S(1)}, f32[6,64,128]{2,1,0:T(8,128)S(1)}, f32[5,64,1...) custom-call(s32[4,2,4]{2,1,0:T(2,128)} %bitcast.22, ...), custom_call_target="tpu_custom_call" | custom-call | flops 2000000 | bytes 1000000 | tf_op jit(solution)/shard_map/pallas_call | solution.py:613
  2.1 0.5 %collective-permute-start = (f32[6,8,128]{2,1,0:T(8,128)S(1)}, f32[6,8,128]{2,1,0:T(8,128)S(1)}, u32[]{:S(2)}, u32[]{:S(2)}) collective-permute-start(f32[6,8,128]{2,1,0:T(8,128)S(1)} %get-tuple-element.38), channel_id=1, source_target_pairs={{0,2},{1,3},{2,0},{3,1},{4,6},{5,7},{6,4},{7,5},{8,10},{9,11},{10,... | collective-permute-start | bytes 73736 | tf_op jit(solution)/shard_map/ppermute | solution.py:658
  2.6 2.6 %collective-permute-start.1 = (f32[6,8,128]{2,1,0:T(8,128)S(1)}, f32[6,8,128]{2,1,0:T(8,128)S(1)}, u32[]{:S(2)}, u32[]{:S(2)}) collective-permute-start(f32[6,8,128]{2,1,0:T(8,128)S(1)} %get-tuple-element.39), channel_id=1, source_target_pairs={{0,1},{1,0},{2,3},{3,2},{4,5},{5,4},{6,7},{7,6},{8,16},{9,17},{10,... | collective-permute-start | bytes 73736 | tf_op jit(solution)/shard_map/ppermute | solution.py:658
  5.2 1.6 %collective-permute-start.2 = (f32[6,8,128]{2,1,0:T(8,128)S(1)}, f32[6,8,128]{2,1,0:T(8,128)S(1)}, u32[]{:S(2)}, u32[]{:S(2)}) collective-permute-start(f32[6,8,128]{2,1,0:T(8,128)S(1)} %get-tuple-element.40), channel_id=1, source_target_pairs={{0,8},{1,9},{2,10},{3,11},{4,12},{5,13},{6,14},{7,15},{8,0},{9,1},... | collective-permute-start | bytes 73736 | tf_op jit(solution)/shard_map/ppermute | solution.py:658
  6.8 1.0 %collective-permute-start.3 = (f32[6,8,128]{2,1,0:T(8,128)S(1)}, f32[6,8,128]{2,1,0:T(8,128)S(1)}, u32[]{:S(2)}, u32[]{:S(2)}) collective-permute-start(f32[6,8,128]{2,1,0:T(8,128)S(1)} %get-tuple-element.41), channel_id=1, source_target_pairs={{0,6},{1,7},{2,4},{3,5},{4,2},{5,3},{6,0},{7,1},{8,14},{9,15},{10,... | collective-permute-start | bytes 73736 | tf_op jit(solution)/shard_map/ppermute | solution.py:658
  7.8 0.6 %collective-permute-start.4 = (f32[5,8,128]{2,1,0:T(8,128)S(1)}, f32[5,8,128]{2,1,0:T(8,128)S(1)}, u32[]{:S(2)}, u32[]{:S(2)}) collective-permute-start(f32[5,8,128]{2,1,0:T(8,128)S(1)} %get-tuple-element.42.own), channel_id=1, source_target_pairs={{0,2},{1,3},{2,0},{3,1},{4,6},{5,7},{6,4},{7,5},{8,9},{9,8},{10,11... | collective-permute-start | bytes 61448 | tf_op jit(solution)/shard_map/ppermute | solution.py:658
  8.5 0.7 %shard_map.105 = (bf16[32,192]{1,0:T(8,128)(2,1)S(1)}, bf16[896,128]{1,0:T(8,128)(2,1)S(1)}) custom-call(s32[4,2,4]{2,1,0:T(2,128)S(1)} %bitcast.14, s32[32]{0:T(128)S(1)} %copy-done.1), custom_call_target="tpu_custom_call" | custom-call | flops 2000000 | bytes 1000000 | tf_op jit(solution)/shard_map/pallas_call | solution.py:613
  9.3 1.0 %collective-permute-done.3.refs_3_ = f32[6,8,128]{2,1,0:T(8,128)S(1)} collective-permute-done((f32[6,8,128]{2,1,0:T(8,128)S(1)}, f32[6,8,128]{2,1,0:T(8,128)S(1)}, u32[]{:S(2)}, u32[]{:S(2)}) %collective-permute-start.3) | collective-permute-done | bytes 24608 | tf_op jit(solution)/shard_map/ppermute | solution.py:658
  10.3 0.2 shard_map.106
  10.5 0.2 collective-permute-start.5
  10.7 1.7 %collective-permute-start.6 = (f32[6,8,128]{2,1,0:T(8,128)S(1)}, f32[6,8,128]{2,1,0:T(8,128)S(1)}, u32[]{:S(2)}, u32[]{:S(2)}) collective-permute-start(f32[6,8,128]{2,1,0:T(8,128)S(1)} %get-tuple-element.52), channel_id=1, source_target_pairs={{0,8},{1,9},{2,10},{3,11},{4,12},{5,13},{6,14},{7,15},{8,0},{9,1},... | collective-permute-start | bytes 73736 | tf_op jit(solution)/shard_map/ppermute | solution.py:658
  12.6 0.5 %collective-permute-start.8 = (f32[6,8,128]{2,1,0:T(8,128)S(1)}, f32[6,8,128]{2,1,0:T(8,128)S(1)}, u32[]{:S(2)}, u32[]{:S(2)}) collective-permute-start(f32[6,8,128]{2,1,0:T(8,128)S(1)} %get-tuple-element.54), channel_id=1, source_target_pairs={{0,6},{1,7},{2,4},{3,5},{4,2},{5,3},{6,0},{7,1},{8,14},{9,15},{10,... | collective-permute-start | bytes 73736 | tf_op jit(solution)/shard_map/ppermute | solution.py:658
  13.0 0.2 shard_map.107.base
  13.5 1.0 %collective-permute-done.6.refs_1_ = f32[6,8,128]{2,1,0:T(8,128)S(1)} collective-permute-done((f32[6,8,128]{2,1,0:T(8,128)S(1)}, f32[6,8,128]{2,1,0:T(8,128)S(1)}, u32[]{:S(2)}, u32[]{:S(2)}) %collective-permute-start.6) | collective-permute-done | bytes 24608 | tf_op jit(solution)/shard_map/ppermute | solution.py:658
  14.6 1.3 %collective-permute-done.8.refs_3_ = f32[6,8,128]{2,1,0:T(8,128)S(1)} collective-permute-done((f32[6,8,128]{2,1,0:T(8,128)S(1)}, f32[6,8,128]{2,1,0:T(8,128)S(1)}, u32[]{:S(2)}, u32[]{:S(2)}) %collective-permute-start.8) | collective-permute-done | bytes 24608 | tf_op jit(solution)/shard_map/ppermute | solution.py:658
  15.8 1.3 %shard_map.110 = (f32[5,64,128]{2,1,0:T(8,128)S(1)}, f32[32,128]{1,0:T(8,128)}, f32[5,8,128]{2,1,0:T(8,128)S(1)}, f32[5,8,128]{2,1,0:T(8,128)S(1)}, f32[5,8,128]...) custom-call(f32[5,64,128]{2,1,0:T(8,128)S(1)} %shard_map.107.base, ...), custom_call_target="tpu_custom_call" | custom-call | flops 2000000 | bytes 1000000 | tf_op jit(solution)/shard_map/pallas_call | solution.py:613
  17.1 4.2 %all-to-all-start = ((f32[32,1,128]{2,1,0:T(1,128)}), f32[32,1,128]{2,1,0:T(1,128)S(1)}, u32[]{:S(2)}, u32[]{:S(2)}) async-start(f32[32,1,128]{2,1,0:T(1,128)} %bitcast.21), calls=%async_computation | async-start | bytes 32768 | tf_op jit(solution)/shard_map/all_to_all | solution.py:723
  21.2 1.8 %collective-permute-start.9 = (f32[5,8,128]{2,1,0:T(8,128)S(1)}, f32[5,8,128]{2,1,0:T(8,128)S(1)}, u32[]{:S(2)}, u32[]{:S(2)}) collective-permute-start(f32[5,8,128]{2,1,0:T(8,128)S(1)} %get-tuple-element.57), channel_id=1, source_target_pairs={{0,8},{1,9},{2,10},{3,11},{4,12},{5,13},{6,14},{7,15},{8,0},{9,1},... | collective-permute-start | bytes 61448 | tf_op jit(solution)/shard_map/ppermute | solution.py:658
  23.1 0.9 %collective-permute-start.10 = (f32[5,8,128]{2,1,0:T(8,128)S(1)}, f32[5,8,128]{2,1,0:T(8,128)S(1)}, u32[]{:S(2)}, u32[]{:S(2)}) collective-permute-start(f32[5,8,128]{2,1,0:T(8,128)S(1)} %get-tuple-element.58), channel_id=1, source_target_pairs={{0,6},{1,7},{2,4},{3,5},{4,2},{5,3},{6,0},{7,1},{8,14},{9,15},{10,... | collective-permute-start | bytes 61448 | tf_op jit(solution)/shard_map/ppermute | solution.py:658
  24.0 0.6 %collective-permute-start.11 = (f32[5,8,128]{2,1,0:T(8,128)S(1)}, f32[5,8,128]{2,1,0:T(8,128)S(1)}, u32[]{:S(2)}, u32[]{:S(2)}) collective-permute-start(f32[5,8,128]{2,1,0:T(8,128)S(1)} %get-tuple-element.59), channel_id=1, source_target_pairs={{0,2},{1,3},{2,0},{3,1},{4,6},{5,7},{6,4},{7,5},{8,16},{9,17},{10,... | collective-permute-start | bytes 61448 | tf_op jit(solution)/shard_map/ppermute | solution.py:658
  24.7 1.5 %collective-permute-start.12 = (f32[1,8,128]{2,1,0:T(8,128)S(1)}, f32[1,8,128]{2,1,0:T(8,128)S(1)}, u32[]{:S(2)}, u32[]{:S(2)}) collective-permute-start(f32[1,8,128]{2,1,0:T(8,128)S(1)} %get-tuple-element.60), channel_id=1, source_target_pairs={{0,1},{1,0},{2,3},{3,2},{4,5},{5,4},{6,7},{7,6},{8,9},{9,8},{10,11... | collective-permute-start | bytes 12296 | tf_op jit(solution)/shard_map/ppermute | solution.py:658
  26.1 0.2 shard_map.111.base
  26.3 2.0 %collective-permute-done.12.refs_3_ = f32[1,8,128]{2,1,0:T(8,128)S(1)} collective-permute-done((f32[1,8,128]{2,1,0:T(8,128)S(1)}, f32[1,8,128]{2,1,0:T(8,128)S(1)}, u32[]{:S(2)}, u32[]{:S(2)}) %collective-permute-start.12) | collective-permute-done | bytes 4128 | tf_op jit(solution)/shard_map/ppermute | solution.py:658
  28.4 0.9 %shard_map.112 = (f32[5,64,128]{2,1,0:T(8,128)}, f32[1,40]{1,0:T(1,128)}) custom-call(f32[5,64,128]{2,1,0:T(8,128)S(1)} %shard_map.111.base, f32[32,128]{1,0:T(8,128)S(1)} %bitcast.13, f32[5,8,128]{2,1,0:T(8,128)S(1)} %collective-permute-done.9.refs_0_, f32[5,8,128]{2,1,0:T(8,128)S(1)} %collective-permute-done.10.refs_1_, ...), custom_call_target="tpu_custom_call" | custom-call | flops 2000000 | bytes 1000000 | tf_op jit(solution)/shard_map/pallas_call | solution.py:613
  (19 shorter events, 0.7 us)
Async XLA Ops:
  2.1 7.2 %collective-permute-start = (f32[6,8,128]{2,1,0:T(8,128)S(1)}, f32[6,8,128]{2,1,0:T(8,128)S(1)}, u32[]{:S(2)}, u32[]{:S(2)}) collective-permute-start(f32[6,8,128]{2,1,0:T(8,128)S(1)} %get-tuple-element.38), channel_id=1, source_target_pairs={{0,2},{1,3},{2,0},{3,1},{4,6},{5,7},{6,4},{7,5},{8,10},{9,11},{10,... | collective-permute-start | bytes 73736 | tf_op jit(solution)/shard_map/ppermute | solution.py:658
  2.6 5.8 %copy-start = (s32[4,4,2]{1,2,0:T(2,128)S(1)}, s32[4,4,2]{1,2,0:T(2,128)}, u32[]{:S(2)}) copy-start(s32[4,4,2]{1,2,0:T(2,128)} %param.16) | copy-start | bytes 388
  2.6 6.7 %collective-permute-start.1 = (f32[6,8,128]{2,1,0:T(8,128)S(1)}, f32[6,8,128]{2,1,0:T(8,128)S(1)}, u32[]{:S(2)}, u32[]{:S(2)}) collective-permute-start(f32[6,8,128]{2,1,0:T(8,128)S(1)} %get-tuple-element.39), channel_id=1, source_target_pairs={{0,1},{1,0},{2,3},{3,2},{4,5},{5,4},{6,7},{7,6},{8,16},{9,17},{10,... | collective-permute-start | bytes 73736 | tf_op jit(solution)/shard_map/ppermute | solution.py:658
  5.2 4.1 %collective-permute-start.2 = (f32[6,8,128]{2,1,0:T(8,128)S(1)}, f32[6,8,128]{2,1,0:T(8,128)S(1)}, u32[]{:S(2)}, u32[]{:S(2)}) collective-permute-start(f32[6,8,128]{2,1,0:T(8,128)S(1)} %get-tuple-element.40), channel_id=1, source_target_pairs={{0,8},{1,9},{2,10},{3,11},{4,12},{5,13},{6,14},{7,15},{8,0},{9,1},... | collective-permute-start | bytes 73736 | tf_op jit(solution)/shard_map/ppermute | solution.py:658
  6.8 3.5 %collective-permute-start.3 = (f32[6,8,128]{2,1,0:T(8,128)S(1)}, f32[6,8,128]{2,1,0:T(8,128)S(1)}, u32[]{:S(2)}, u32[]{:S(2)}) collective-permute-start(f32[6,8,128]{2,1,0:T(8,128)S(1)} %get-tuple-element.41), channel_id=1, source_target_pairs={{0,6},{1,7},{2,4},{3,5},{4,2},{5,3},{6,0},{7,1},{8,14},{9,15},{10,... | collective-permute-start | bytes 73736 | tf_op jit(solution)/shard_map/ppermute | solution.py:658
  7.8 0.7 %copy-start.1 = (s32[32]{0:T(128)S(1)}, s32[32]{0:T(128)}, u32[]{:S(2)}) copy-start(s32[32]{0:T(128)} %owners.1) | copy-start | bytes 388
  7.8 1.5 %collective-permute-start.4 = (f32[5,8,128]{2,1,0:T(8,128)S(1)}, f32[5,8,128]{2,1,0:T(8,128)S(1)}, u32[]{:S(2)}, u32[]{:S(2)}) collective-permute-start(f32[5,8,128]{2,1,0:T(8,128)S(1)} %get-tuple-element.42.own), channel_id=1, source_target_pairs={{0,2},{1,3},{2,0},{3,1},{4,6},{5,7},{6,4},{7,5},{8,9},{9,8},{10,11... | collective-permute-start | bytes 61448 | tf_op jit(solution)/shard_map/ppermute | solution.py:658
  10.5 3.0 %collective-permute-start.5 = (f32[6,8,128]{2,1,0:T(8,128)S(1)}, f32[6,8,128]{2,1,0:T(8,128)S(1)}, u32[]{:S(2)}, u32[]{:S(2)}) collective-permute-start(f32[6,8,128]{2,1,0:T(8,128)S(1)} %get-tuple-element.51), channel_id=1, source_target_pairs={{0,2},{1,3},{2,0},{3,1},{4,6},{5,7},{6,4},{7,5},{8,10},{9,11},{10,... | collective-permute-start | bytes 73736 | tf_op jit(solution)/shard_map/ppermute | solution.py:658
  10.7 3.9 %collective-permute-start.6 = (f32[6,8,128]{2,1,0:T(8,128)S(1)}, f32[6,8,128]{2,1,0:T(8,128)S(1)}, u32[]{:S(2)}, u32[]{:S(2)}) collective-permute-start(f32[6,8,128]{2,1,0:T(8,128)S(1)} %get-tuple-element.52), channel_id=1, source_target_pairs={{0,8},{1,9},{2,10},{3,11},{4,12},{5,13},{6,14},{7,15},{8,0},{9,1},... | collective-permute-start | bytes 73736 | tf_op jit(solution)/shard_map/ppermute | solution.py:658
  12.4 2.2 %collective-permute-start.7 = (f32[6,8,128]{2,1,0:T(8,128)S(1)}, f32[6,8,128]{2,1,0:T(8,128)S(1)}, u32[]{:S(2)}, u32[]{:S(2)}) collective-permute-start(f32[6,8,128]{2,1,0:T(8,128)S(1)} %get-tuple-element.53), channel_id=1, source_target_pairs={{0,2},{1,3},{2,0},{3,1},{4,6},{5,7},{6,4},{7,5},{8,16},{9,17},{10,... | collective-permute-start | bytes 73736 | tf_op jit(solution)/shard_map/ppermute | solution.py:658
  12.6 3.3 %collective-permute-start.8 = (f32[6,8,128]{2,1,0:T(8,128)S(1)}, f32[6,8,128]{2,1,0:T(8,128)S(1)}, u32[]{:S(2)}, u32[]{:S(2)}) collective-permute-start(f32[6,8,128]{2,1,0:T(8,128)S(1)} %get-tuple-element.54), channel_id=1, source_target_pairs={{0,6},{1,7},{2,4},{3,5},{4,2},{5,3},{6,0},{7,1},{8,14},{9,15},{10,... | collective-permute-start | bytes 73736 | tf_op jit(solution)/shard_map/ppermute | solution.py:658
  17.1 11.3 %all-to-all-start = ((f32[32,1,128]{2,1,0:T(1,128)}), f32[32,1,128]{2,1,0:T(1,128)S(1)}, u32[]{:S(2)}, u32[]{:S(2)}) async-start(f32[32,1,128]{2,1,0:T(1,128)} %bitcast.21), calls=%async_computation | async-start | bytes 32768 | tf_op jit(solution)/shard_map/all_to_all | solution.py:723
  21.2 7.0 %collective-permute-start.9 = (f32[5,8,128]{2,1,0:T(8,128)S(1)}, f32[5,8,128]{2,1,0:T(8,128)S(1)}, u32[]{:S(2)}, u32[]{:S(2)}) collective-permute-start(f32[5,8,128]{2,1,0:T(8,128)S(1)} %get-tuple-element.57), channel_id=1, source_target_pairs={{0,8},{1,9},{2,10},{3,11},{4,12},{5,13},{6,14},{7,15},{8,0},{9,1},... | collective-permute-start | bytes 61448 | tf_op jit(solution)/shard_map/ppermute | solution.py:658
  23.1 5.2 %collective-permute-start.10 = (f32[5,8,128]{2,1,0:T(8,128)S(1)}, f32[5,8,128]{2,1,0:T(8,128)S(1)}, u32[]{:S(2)}, u32[]{:S(2)}) collective-permute-start(f32[5,8,128]{2,1,0:T(8,128)S(1)} %get-tuple-element.58), channel_id=1, source_target_pairs={{0,6},{1,7},{2,4},{3,5},{4,2},{5,3},{6,0},{7,1},{8,14},{9,15},{10,... | collective-permute-start | bytes 61448 | tf_op jit(solution)/shard_map/ppermute | solution.py:658
  24.0 4.3 %collective-permute-start.11 = (f32[5,8,128]{2,1,0:T(8,128)S(1)}, f32[5,8,128]{2,1,0:T(8,128)S(1)}, u32[]{:S(2)}, u32[]{:S(2)}) collective-permute-start(f32[5,8,128]{2,1,0:T(8,128)S(1)} %get-tuple-element.59), channel_id=1, source_target_pairs={{0,2},{1,3},{2,0},{3,1},{4,6},{5,7},{6,4},{7,5},{8,16},{9,17},{10,... | collective-permute-start | bytes 61448 | tf_op jit(solution)/shard_map/ppermute | solution.py:658
  24.6 3.6 %collective-permute-start.13 = (f32[5,8,128]{2,1,0:T(8,128)S(1)}, f32[5,8,128]{2,1,0:T(8,128)S(1)}, u32[]{:S(2)}, u32[]{:S(2)}) collective-permute-start(f32[5,8,128]{2,1,0:T(8,128)S(1)} %get-tuple-element.61), channel_id=1, source_target_pairs={{0,2},{1,3},{2,0},{3,1},{4,6},{5,7},{6,4},{7,5},{8,10},{9,11},{10,... | collective-permute-start | bytes 61448 | tf_op jit(solution)/shard_map/ppermute | solution.py:658
  24.7 3.6 %collective-permute-start.12 = (f32[1,8,128]{2,1,0:T(8,128)S(1)}, f32[1,8,128]{2,1,0:T(8,128)S(1)}, u32[]{:S(2)}, u32[]{:S(2)}) collective-permute-start(f32[1,8,128]{2,1,0:T(8,128)S(1)} %get-tuple-element.60), channel_id=1, source_target_pairs={{0,1},{1,0},{2,3},{3,2},{4,5},{5,4},{6,7},{7,6},{8,9},{9,8},{10,11... | collective-permute-start | bytes 12296 | tf_op jit(solution)/shard_map/ppermute | solution.py:658

commit v12 on v11

--- a/solution.py
+++ b/solution.py
@@ -207,7 +207,7 @@
 
 
 ORDERS = (
-    ((1, 0), (0, 1), (0, 0), (1, 1), (2, 0), (2, 1)),
+    ((1, 0), (0, 1), (0, 0), (2, 0), (2, 1), (1, 1)),
     ((1, 0), (0, 0), (0, 1), (1, 1)),
     ((0, 0), (1, 1), (0, 1), (2, 0), (2, 1), (1, 0)),
 )

time: 29.4 us -> 29.4 us (level)
  no operation moved by 1% of the time
where the time goes in v12:
time: 29.4 us; the launch traced here: 29.2 us
  starting transfers between devices  17.9 us (61%)
  waiting for transfers between devices  5.46 us (19%)
  Pallas kernels  5.11 us (17%)
  between operations  0.73 us (2%)
    ppermute x14, starting transfers between devices, exchange(): lax.ppermute(sends[key], AXES, permutations[stage][key[0]][key[1]])  13.8 us
    ppermute x14, waiting for transfers between devices, exchange(): lax.ppermute(sends[key], AXES, permutations[stage][key[0]][key[1]])  5.39 us
    pallas_call x9, Pallas kernels, call(): pl.pallas_call(kernel, out_shape=[space(shape, dtype) for space, shape in...  5.11 us
    all_to_all x1, starting transfers between devices, body(): lax.all_to_all(table.reshape(devices, 1, CZ), AXES, 0, 0, tiled=True)  4.15 us
  transfers between devices with their start and end apart: 15, of which 6 were waited for; matrix products, arithmetic and copies ran while one was open for 0% of the time, Pallas kernels for 5%

profile of v12, /device:TPU:0, one launch (start us, length us, event | category | flops | bytes accessed | tf_op | source)
XLA Modules:
  0.0 29.2 jit_solution(10705615406056158766)
XLA Ops:
  0.6 1.4 %shard_map.104 = (f32[5,64,128]{2,1,0:T(8,128)S(1)}, f32[64,128]{1,0:T(8,128)S(1)}, f32[64,128]{1,0:T(8,128)S(1)}, f32[6,64,128]{2,1,0:T(8,128)S(1)}, f32[5,64,1...) custom-call(s32[4,2,4]{2,1,0:T(2,128)} %bitcast.22, ...), custom_call_target="tpu_custom_call" | custom-call | flops 2000000 | bytes 1000000 | tf_op jit(solution)/shard_map/pallas_call | solution.py:613
  2.1 0.5 %collective-permute-start = (f32[6,8,128]{2,1,0:T(8,128)S(1)}, f32[6,8,128]{2,1,0:T(8,128)S(1)}, u32[]{:S(2)}, u32[]{:S(2)}) collective-permute-start(f32[6,8,128]{2,1,0:T(8,128)S(1)} %get-tuple-element.38), channel_id=1, source_target_pairs={{0,2},{1,3},{2,0},{3,1},{4,6},{5,7},{6,4},{7,5},{8,10},{9,11},{10,... | collective-permute-start | bytes 73736 | tf_op jit(solution)/shard_map/ppermute | solution.py:658
  2.6 2.6 %collective-permute-start.1 = (f32[6,8,128]{2,1,0:T(8,128)S(1)}, f32[6,8,128]{2,1,0:T(8,128)S(1)}, u32[]{:S(2)}, u32[]{:S(2)}) collective-permute-start(f32[6,8,128]{2,1,0:T(8,128)S(1)} %get-tuple-element.39), channel_id=1, source_target_pairs={{0,1},{1,0},{2,3},{3,2},{4,5},{5,4},{6,7},{7,6},{8,16},{9,17},{10,... | collective-permute-start | bytes 73736 | tf_op jit(solution)/shard_map/ppermute | solution.py:658
  5.2 1.6 %collective-permute-start.2 = (f32[6,8,128]{2,1,0:T(8,128)S(1)}, f32[6,8,128]{2,1,0:T(8,128)S(1)}, u32[]{:S(2)}, u32[]{:S(2)}) collective-permute-start(f32[6,8,128]{2,1,0:T(8,128)S(1)} %get-tuple-element.40), channel_id=1, source_target_pairs={{0,8},{1,9},{2,10},{3,11},{4,12},{5,13},{6,14},{7,15},{8,0},{9,1},... | collective-permute-start | bytes 73736 | tf_op jit(solution)/shard_map/ppermute | solution.py:658
  6.8 1.0 %collective-permute-start.4 = (f32[6,8,128]{2,1,0:T(8,128)S(1)}, f32[6,8,128]{2,1,0:T(8,128)S(1)}, u32[]{:S(2)}, u32[]{:S(2)}) collective-permute-start(f32[6,8,128]{2,1,0:T(8,128)S(1)} %get-tuple-element.42), channel_id=1, source_target_pairs={{0,6},{1,7},{2,4},{3,5},{4,2},{5,3},{6,0},{7,1},{8,14},{9,15},{10,... | collective-permute-start | bytes 73736 | tf_op jit(solution)/shard_map/ppermute | solution.py:658
  7.8 0.6 %collective-permute-start.3 = (f32[5,8,128]{2,1,0:T(8,128)S(1)}, f32[5,8,128]{2,1,0:T(8,128)S(1)}, u32[]{:S(2)}, u32[]{:S(2)}) collective-permute-start(f32[5,8,128]{2,1,0:T(8,128)S(1)} %get-tuple-element.41.own), channel_id=1, source_target_pairs={{0,2},{1,3},{2,0},{3,1},{4,6},{5,7},{6,4},{7,5},{8,9},{9,8},{10,11... | collective-permute-start | bytes 61448 | tf_op jit(solution)/shard_map/ppermute | solution.py:658
  8.5 0.7 %shard_map.105 = (bf16[32,192]{1,0:T(8,128)(2,1)S(1)}, bf16[896,128]{1,0:T(8,128)(2,1)S(1)}) custom-call(s32[4,2,4]{2,1,0:T(2,128)S(1)} %bitcast.14, s32[32]{0:T(128)S(1)} %copy-done.1), custom_call_target="tpu_custom_call" | custom-call | flops 2000000 | bytes 1000000 | tf_op jit(solution)/shard_map/pallas_call | solution.py:613
  9.3 1.0 %collective-permute-done.4.refs_4_ = f32[6,8,128]{2,1,0:T(8,128)S(1)} collective-permute-done((f32[6,8,128]{2,1,0:T(8,128)S(1)}, f32[6,8,128]{2,1,0:T(8,128)S(1)}, u32[]{:S(2)}, u32[]{:S(2)}) %collective-permute-start.4) | collective-permute-done | bytes 24608 | tf_op jit(solution)/shard_map/ppermute | solution.py:658
  10.3 0.2 shard_map.106
  10.5 0.2 collective-permute-start.5
  10.7 1.7 %collective-permute-start.6 = (f32[6,8,128]{2,1,0:T(8,128)S(1)}, f32[6,8,128]{2,1,0:T(8,128)S(1)}, u32[]{:S(2)}, u32[]{:S(2)}) collective-permute-start(f32[6,8,128]{2,1,0:T(8,128)S(1)} %get-tuple-element.52), channel_id=1, source_target_pairs={{0,8},{1,9},{2,10},{3,11},{4,12},{5,13},{6,14},{7,15},{8,0},{9,1},... | collective-permute-start | bytes 73736 | tf_op jit(solution)/shard_map/ppermute | solution.py:658
  12.6 0.5 %collective-permute-start.8 = (f32[6,8,128]{2,1,0:T(8,128)S(1)}, f32[6,8,128]{2,1,0:T(8,128)S(1)}, u32[]{:S(2)}, u32[]{:S(2)}) collective-permute-start(f32[6,8,128]{2,1,0:T(8,128)S(1)} %get-tuple-element.54), channel_id=1, source_target_pairs={{0,6},{1,7},{2,4},{3,5},{4,2},{5,3},{6,0},{7,1},{8,14},{9,15},{10,... | collective-permute-start | bytes 73736 | tf_op jit(solution)/shard_map/ppermute | solution.py:658
  13.0 0.2 shard_map.107.base
  13.5 1.0 %collective-permute-done.6.refs_1_ = f32[6,8,128]{2,1,0:T(8,128)S(1)} collective-permute-done((f32[6,8,128]{2,1,0:T(8,128)S(1)}, f32[6,8,128]{2,1,0:T(8,128)S(1)}, u32[]{:S(2)}, u32[]{:S(2)}) %collective-permute-start.6) | collective-permute-done | bytes 24608 | tf_op jit(solution)/shard_map/ppermute | solution.py:658
  14.6 1.3 %collective-permute-done.8.refs_3_ = f32[6,8,128]{2,1,0:T(8,128)S(1)} collective-permute-done((f32[6,8,128]{2,1,0:T(8,128)S(1)}, f32[6,8,128]{2,1,0:T(8,128)S(1)}, u32[]{:S(2)}, u32[]{:S(2)}) %collective-permute-start.8) | collective-permute-done | bytes 24608 | tf_op jit(solution)/shard_map/ppermute | solution.py:658
  15.8 1.3 %shard_map.110 = (f32[5,64,128]{2,1,0:T(8,128)S(1)}, f32[32,128]{1,0:T(8,128)}, f32[5,8,128]{2,1,0:T(8,128)S(1)}, f32[5,8,128]{2,1,0:T(8,128)S(1)}, f32[5,8,128]...) custom-call(f32[5,64,128]{2,1,0:T(8,128)S(1)} %shard_map.107.base, ...), custom_call_target="tpu_custom_call" | custom-call | flops 2000000 | bytes 1000000 | tf_op jit(solution)/shard_map/pallas_call | solution.py:613
  17.1 4.2 %all-to-all-start = ((f32[32,1,128]{2,1,0:T(1,128)}), f32[32,1,128]{2,1,0:T(1,128)S(1)}, u32[]{:S(2)}, u32[]{:S(2)}) async-start(f32[32,1,128]{2,1,0:T(1,128)} %bitcast.21), calls=%async_computation | async-start | bytes 32768 | tf_op jit(solution)/shard_map/all_to_all | solution.py:723
  21.2 1.8 %collective-permute-start.9 = (f32[5,8,128]{2,1,0:T(8,128)S(1)}, f32[5,8,128]{2,1,0:T(8,128)S(1)}, u32[]{:S(2)}, u32[]{:S(2)}) collective-permute-start(f32[5,8,128]{2,1,0:T(8,128)S(1)} %get-tuple-element.57), channel_id=1, source_target_pairs={{0,8},{1,9},{2,10},{3,11},{4,12},{5,13},{6,14},{7,15},{8,0},{9,1},... | collective-permute-start | bytes 61448 | tf_op jit(solution)/shard_map/ppermute | solution.py:658
  23.1 0.9 %collective-permute-start.10 = (f32[5,8,128]{2,1,0:T(8,128)S(1)}, f32[5,8,128]{2,1,0:T(8,128)S(1)}, u32[]{:S(2)}, u32[]{:S(2)}) collective-permute-start(f32[5,8,128]{2,1,0:T(8,128)S(1)} %get-tuple-element.58), channel_id=1, source_target_pairs={{0,6},{1,7},{2,4},{3,5},{4,2},{5,3},{6,0},{7,1},{8,14},{9,15},{10,... | collective-permute-start | bytes 61448 | tf_op jit(solution)/shard_map/ppermute | solution.py:658
  24.0 0.6 %collective-permute-start.11 = (f32[5,8,128]{2,1,0:T(8,128)S(1)}, f32[5,8,128]{2,1,0:T(8,128)S(1)}, u32[]{:S(2)}, u32[]{:S(2)}) collective-permute-start(f32[5,8,128]{2,1,0:T(8,128)S(1)} %get-tuple-element.59), channel_id=1, source_target_pairs={{0,2},{1,3},{2,0},{3,1},{4,6},{5,7},{6,4},{7,5},{8,16},{9,17},{10,... | collective-permute-start | bytes 61448 | tf_op jit(solution)/shard_map/ppermute | solution.py:658
  24.7 1.5 %collective-permute-start.12 = (f32[1,8,128]{2,1,0:T(8,128)S(1)}, f32[1,8,128]{2,1,0:T(8,128)S(1)}, u32[]{:S(2)}, u32[]{:S(2)}) collective-permute-start(f32[1,8,128]{2,1,0:T(8,128)S(1)} %get-tuple-element.60), channel_id=1, source_target_pairs={{0,1},{1,0},{2,3},{3,2},{4,5},{5,4},{6,7},{7,6},{8,9},{9,8},{10,11... | collective-permute-start | bytes 12296 | tf_op jit(solution)/shard_map/ppermute | solution.py:658
  26.1 0.2 shard_map.111.base
  26.3 2.0 %collective-permute-done.12.refs_3_ = f32[1,8,128]{2,1,0:T(8,128)S(1)} collective-permute-done((f32[1,8,128]{2,1,0:T(8,128)S(1)}, f32[1,8,128]{2,1,0:T(8,128)S(1)}, u32[]{:S(2)}, u32[]{:S(2)}) %collective-permute-start.12) | collective-permute-done | bytes 4128 | tf_op jit(solution)/shard_map/ppermute | solution.py:658
  28.4 0.9 %shard_map.112 = (f32[5,64,128]{2,1,0:T(8,128)}, f32[1,40]{1,0:T(1,128)}) custom-call(f32[5,64,128]{2,1,0:T(8,128)S(1)} %shard_map.111.base, f32[32,128]{1,0:T(8,128)S(1)} %bitcast.13, f32[5,8,128]{2,1,0:T(8,128)S(1)} %collective-permute-done.9.refs_0_, f32[5,8,128]{2,1,0:T(8,128)S(1)} %collective-permute-done.10.refs_1_, ...), custom_call_target="tpu_custom_call" | custom-call | flops 2000000 | bytes 1000000 | tf_op jit(solution)/shard_map/pallas_call | solution.py:613
  (19 shorter events, 0.7 us)
Async XLA Ops:
  2.1 7.2 %collective-permute-start = (f32[6,8,128]{2,1,0:T(8,128)S(1)}, f32[6,8,128]{2,1,0:T(8,128)S(1)}, u32[]{:S(2)}, u32[]{:S(2)}) collective-permute-start(f32[6,8,128]{2,1,0:T(8,128)S(1)} %get-tuple-element.38), channel_id=1, source_target_pairs={{0,2},{1,3},{2,0},{3,1},{4,6},{5,7},{6,4},{7,5},{8,10},{9,11},{10,... | collective-permute-start | bytes 73736 | tf_op jit(solution)/shard_map/ppermute | solution.py:658
  2.6 5.8 %copy-start = (s32[4,4,2]{1,2,0:T(2,128)S(1)}, s32[4,4,2]{1,2,0:T(2,128)}, u32[]{:S(2)}) copy-start(s32[4,4,2]{1,2,0:T(2,128)} %param.16) | copy-start | bytes 388
  2.6 6.7 %collective-permute-start.1 = (f32[6,8,128]{2,1,0:T(8,128)S(1)}, f32[6,8,128]{2,1,0:T(8,128)S(1)}, u32[]{:S(2)}, u32[]{:S(2)}) collective-permute-start(f32[6,8,128]{2,1,0:T(8,128)S(1)} %get-tuple-element.39), channel_id=1, source_target_pairs={{0,1},{1,0},{2,3},{3,2},{4,5},{5,4},{6,7},{7,6},{8,16},{9,17},{10,... | collective-permute-start | bytes 73736 | tf_op jit(solution)/shard_map/ppermute | solution.py:658
  5.2 4.1 %collective-permute-start.2 = (f32[6,8,128]{2,1,0:T(8,128)S(1)}, f32[6,8,128]{2,1,0:T(8,128)S(1)}, u32[]{:S(2)}, u32[]{:S(2)}) collective-permute-start(f32[6,8,128]{2,1,0:T(8,128)S(1)} %get-tuple-element.40), channel_id=1, source_target_pairs={{0,8},{1,9},{2,10},{3,11},{4,12},{5,13},{6,14},{7,15},{8,0},{9,1},... | collective-permute-start | bytes 73736 | tf_op jit(solution)/shard_map/ppermute | solution.py:658
  6.8 3.5 %collective-permute-start.4 = (f32[6,8,128]{2,1,0:T(8,128)S(1)}, f32[6,8,128]{2,1,0:T(8,128)S(1)}, u32[]{:S(2)}, u32[]{:S(2)}) collective-permute-start(f32[6,8,128]{2,1,0:T(8,128)S(1)} %get-tuple-element.42), channel_id=1, source_target_pairs={{0,6},{1,7},{2,4},{3,5},{4,2},{5,3},{6,0},{7,1},{8,14},{9,15},{10,... | collective-permute-start | bytes 73736 | tf_op jit(solution)/shard_map/ppermute | solution.py:658
  7.8 0.7 %copy-start.1 = (s32[32]{0:T(128)S(1)}, s32[32]{0:T(128)}, u32[]{:S(2)}) copy-start(s32[32]{0:T(128)} %owners.1) | copy-start | bytes 388
  7.8 1.5 %collective-permute-start.3 = (f32[5,8,128]{2,1,0:T(8,128)S(1)}, f32[5,8,128]{2,1,0:T(8,128)S(1)}, u32[]{:S(2)}, u32[]{:S(2)}) collective-permute-start(f32[5,8,128]{2,1,0:T(8,128)S(1)} %get-tuple-element.41.own), channel_id=1, source_target_pairs={{0,2},{1,3},{2,0},{3,1},{4,6},{5,7},{6,4},{7,5},{8,9},{9,8},{10,11... | collective-permute-start | bytes 61448 | tf_op jit(solution)/shard_map/ppermute | solution.py:658
  10.5 3.0 %collective-permute-start.5 = (f32[6,8,128]{2,1,0:T(8,128)S(1)}, f32[6,8,128]{2,1,0:T(8,128)S(1)}, u32[]{:S(2)}, u32[]{:S(2)}) collective-permute-start(f32[6,8,128]{2,1,0:T(8,128)S(1)} %get-tuple-element.51), channel_id=1, source_target_pairs={{0,2},{1,3},{2,0},{3,1},{4,6},{5,7},{6,4},{7,5},{8,10},{9,11},{10,... | collective-permute-start | bytes 73736 | tf_op jit(solution)/shard_map/ppermute | solution.py:658
  10.7 3.9 %collective-permute-start.6 = (f32[6,8,128]{2,1,0:T(8,128)S(1)}, f32[6,8,128]{2,1,0:T(8,128)S(1)}, u32[]{:S(2)}, u32[]{:S(2)}) collective-permute-start(f32[6,8,128]{2,1,0:T(8,128)S(1)} %get-tuple-element.52), channel_id=1, source_target_pairs={{0,8},{1,9},{2,10},{3,11},{4,12},{5,13},{6,14},{7,15},{8,0},{9,1},... | collective-permute-start | bytes 73736 | tf_op jit(solution)/shard_map/ppermute | solution.py:658
  12.4 2.2 %collective-permute-start.7 = (f32[6,8,128]{2,1,0:T(8,128)S(1)}, f32[6,8,128]{2,1,0:T(8,128)S(1)}, u32[]{:S(2)}, u32[]{:S(2)}) collective-permute-start(f32[6,8,128]{2,1,0:T(8,128)S(1)} %get-tuple-element.53), channel_id=1, source_target_pairs={{0,2},{1,3},{2,0},{3,1},{4,6},{5,7},{6,4},{7,5},{8,16},{9,17},{10,... | collective-permute-start | bytes 73736 | tf_op jit(solution)/shard_map/ppermute | solution.py:658
  12.6 3.3 %collective-permute-start.8 = (f32[6,8,128]{2,1,0:T(8,128)S(1)}, f32[6,8,128]{2,1,0:T(8,128)S(1)}, u32[]{:S(2)}, u32[]{:S(2)}) collective-permute-start(f32[6,8,128]{2,1,0:T(8,128)S(1)} %get-tuple-element.54), channel_id=1, source_target_pairs={{0,6},{1,7},{2,4},{3,5},{4,2},{5,3},{6,0},{7,1},{8,14},{9,15},{10,... | collective-permute-start | bytes 73736 | tf_op jit(solution)/shard_map/ppermute | solution.py:658
  17.1 11.3 %all-to-all-start = ((f32[32,1,128]{2,1,0:T(1,128)}), f32[32,1,128]{2,1,0:T(1,128)S(1)}, u32[]{:S(2)}, u32[]{:S(2)}) async-start(f32[32,1,128]{2,1,0:T(1,128)} %bitcast.21), calls=%async_computation | async-start | bytes 32768 | tf_op jit(solution)/shard_map/all_to_all | solution.py:723
  21.2 7.0 %collective-permute-start.9 = (f32[5,8,128]{2,1,0:T(8,128)S(1)}, f32[5,8,128]{2,1,0:T(8,128)S(1)}, u32[]{:S(2)}, u32[]{:S(2)}) collective-permute-start(f32[5,8,128]{2,1,0:T(8,128)S(1)} %get-tuple-element.57), channel_id=1, source_target_pairs={{0,8},{1,9},{2,10},{3,11},{4,12},{5,13},{6,14},{7,15},{8,0},{9,1},... | collective-permute-start | bytes 61448 | tf_op jit(solution)/shard_map/ppermute | solution.py:658
  23.1 5.2 %collective-permute-start.10 = (f32[5,8,128]{2,1,0:T(8,128)S(1)}, f32[5,8,128]{2,1,0:T(8,128)S(1)}, u32[]{:S(2)}, u32[]{:S(2)}) collective-permute-start(f32[5,8,128]{2,1,0:T(8,128)S(1)} %get-tuple-element.58), channel_id=1, source_target_pairs={{0,6},{1,7},{2,4},{3,5},{4,2},{5,3},{6,0},{7,1},{8,14},{9,15},{10,... | collective-permute-start | bytes 61448 | tf_op jit(solution)/shard_map/ppermute | solution.py:658
  24.0 4.3 %collective-permute-start.11 = (f32[5,8,128]{2,1,0:T(8,128)S(1)}, f32[5,8,128]{2,1,0:T(8,128)S(1)}, u32[]{:S(2)}, u32[]{:S(2)}) collective-permute-start(f32[5,8,128]{2,1,0:T(8,128)S(1)} %get-tuple-element.59), channel_id=1, source_target_pairs={{0,2},{1,3},{2,0},{3,1},{4,6},{5,7},{6,4},{7,5},{8,16},{9,17},{10,... | collective-permute-start | bytes 61448 | tf_op jit(solution)/shard_map/ppermute | solution.py:658
  24.6 3.6 %collective-permute-start.13 = (f32[5,8,128]{2,1,0:T(8,128)S(1)}, f32[5,8,128]{2,1,0:T(8,128)S(1)}, u32[]{:S(2)}, u32[]{:S(2)}) collective-permute-start(f32[5,8,128]{2,1,0:T(8,128)S(1)} %get-tuple-element.61), channel_id=1, source_target_pairs={{0,2},{1,3},{2,0},{3,1},{4,6},{5,7},{6,4},{7,5},{8,10},{9,11},{10,... | collective-permute-start | bytes 61448 | tf_op jit(solution)/shard_map/ppermute | solution.py:658
  24.7 3.6 %collective-permute-start.12 = (f32[1,8,128]{2,1,0:T(8,128)S(1)}, f32[1,8,128]{2,1,0:T(8,128)S(1)}, u32[]{:S(2)}, u32[]{:S(2)}) collective-permute-start(f32[1,8,128]{2,1,0:T(8,128)S(1)} %get-tuple-element.60), channel_id=1, source_target_pairs={{0,1},{1,0},{2,3},{3,2},{4,5},{5,4},{6,7},{7,6},{8,9},{9,8},{10,11... | collective-permute-start | bytes 12296 | tf_op jit(solution)/shard_map/ppermute | solution.py:658

commit v13 on v10

--- a/solution.py
+++ b/solution.py
@@ -570,7 +570,7 @@
         preferred_element_type=jnp.float32,
     )
     copy = pltpu.make_async_copy(rows_out, table, sent)
-    copy.start()
+    copy.start(priority=1)
     put_pair(x_low, x_high, here[0], outs[0])
     put_pair(y_low, y_high, here[1], outs[1])
     outs[2][0][0] = packed

time: 29.4 us -> 29.4 us (level)
  no operation moved by 1% of the time
where the time goes in v13:
time: 29.4 us; the launch traced here: 29.2 us
  starting transfers between devices  17.9 us (61%)
  waiting for transfers between devices  5.46 us (19%)
  Pallas kernels  5.11 us (17%)
  between operations  0.73 us (2%)
    ppermute x14, starting transfers between devices, exchange(): lax.ppermute(sends[key], AXES, permutations[stage][key[0]][key[1]])  13.8 us
    ppermute x14, waiting for transfers between devices, exchange(): lax.ppermute(sends[key], AXES, permutations[stage][key[0]][key[1]])  5.39 us
    pallas_call x9, Pallas kernels, call(): pl.pallas_call(kernel, out_shape=[space(shape, dtype) for space, shape in...  5.11 us
    all_to_all x1, starting transfers between devices, body(): lax.all_to_all(table.reshape(devices, 1, CZ), AXES, 0, 0, tiled=True)  4.15 us
  transfers between devices with their start and end apart: 15, of which 6 were waited for; matrix products, arithmetic and copies ran while one was open for 0% of the time, Pallas kernels for 5%

profile of v13, /device:TPU:0, one launch (start us, length us, event | category | flops | bytes accessed | tf_op | source)
XLA Modules:
  0.0 29.2 jit_solution(2397062716323545794)
XLA Ops:
  0.6 1.4 %shard_map.104 = (f32[5,64,128]{2,1,0:T(8,128)S(1)}, f32[64,128]{1,0:T(8,128)S(1)}, f32[64,128]{1,0:T(8,128)S(1)}, f32[6,64,128]{2,1,0:T(8,128)S(1)}, f32[5,64,1...) custom-call(s32[4,2,4]{2,1,0:T(2,128)} %bitcast.22, ...), custom_call_target="tpu_custom_call" | custom-call | flops 2000000 | bytes 1000000 | tf_op jit(solution)/shard_map/pallas_call | solution.py:613
  2.1 0.5 %collective-permute-start = (f32[6,8,128]{2,1,0:T(8,128)S(1)}, f32[6,8,128]{2,1,0:T(8,128)S(1)}, u32[]{:S(2)}, u32[]{:S(2)}) collective-permute-start(f32[6,8,128]{2,1,0:T(8,128)S(1)} %get-tuple-element.38), channel_id=1, source_target_pairs={{0,2},{1,3},{2,0},{3,1},{4,6},{5,7},{6,4},{7,5},{8,10},{9,11},{10,... | collective-permute-start | bytes 73736 | tf_op jit(solution)/shard_map/ppermute | solution.py:658
  2.6 2.6 %collective-permute-start.1 = (f32[6,8,128]{2,1,0:T(8,128)S(1)}, f32[6,8,128]{2,1,0:T(8,128)S(1)}, u32[]{:S(2)}, u32[]{:S(2)}) collective-permute-start(f32[6,8,128]{2,1,0:T(8,128)S(1)} %get-tuple-element.39), channel_id=1, source_target_pairs={{0,1},{1,0},{2,3},{3,2},{4,5},{5,4},{6,7},{7,6},{8,16},{9,17},{10,... | collective-permute-start | bytes 73736 | tf_op jit(solution)/shard_map/ppermute | solution.py:658
  5.2 1.6 %collective-permute-start.2 = (f32[6,8,128]{2,1,0:T(8,128)S(1)}, f32[6,8,128]{2,1,0:T(8,128)S(1)}, u32[]{:S(2)}, u32[]{:S(2)}) collective-permute-start(f32[6,8,128]{2,1,0:T(8,128)S(1)} %get-tuple-element.40), channel_id=1, source_target_pairs={{0,8},{1,9},{2,10},{3,11},{4,12},{5,13},{6,14},{7,15},{8,0},{9,1},... | collective-permute-start | bytes 73736 | tf_op jit(solution)/shard_map/ppermute | solution.py:658
  6.8 1.0 %collective-permute-start.3 = (f32[6,8,128]{2,1,0:T(8,128)S(1)}, f32[6,8,128]{2,1,0:T(8,128)S(1)}, u32[]{:S(2)}, u32[]{:S(2)}) collective-permute-start(f32[6,8,128]{2,1,0:T(8,128)S(1)} %get-tuple-element.41), channel_id=1, source_target_pairs={{0,6},{1,7},{2,4},{3,5},{4,2},{5,3},{6,0},{7,1},{8,14},{9,15},{10,... | collective-permute-start | bytes 73736 | tf_op jit(solution)/shard_map/ppermute | solution.py:658
  7.8 0.6 %collective-permute-start.4 = (f32[5,8,128]{2,1,0:T(8,128)S(1)}, f32[5,8,128]{2,1,0:T(8,128)S(1)}, u32[]{:S(2)}, u32[]{:S(2)}) collective-permute-start(f32[5,8,128]{2,1,0:T(8,128)S(1)} %get-tuple-element.42.own), channel_id=1, source_target_pairs={{0,2},{1,3},{2,0},{3,1},{4,6},{5,7},{6,4},{7,5},{8,9},{9,8},{10,11... | collective-permute-start | bytes 61448 | tf_op jit(solution)/shard_map/ppermute | solution.py:658
  8.5 0.7 %shard_map.105 = (bf16[32,192]{1,0:T(8,128)(2,1)S(1)}, bf16[896,128]{1,0:T(8,128)(2,1)S(1)}) custom-call(s32[4,2,4]{2,1,0:T(2,128)S(1)} %bitcast.14, s32[32]{0:T(128)S(1)} %copy-done.1), custom_call_target="tpu_custom_call" | custom-call | flops 2000000 | bytes 1000000 | tf_op jit(solution)/shard_map/pallas_call | solution.py:613
  9.3 1.0 %collective-permute-done.3.refs_3_ = f32[6,8,128]{2,1,0:T(8,128)S(1)} collective-permute-done((f32[6,8,128]{2,1,0:T(8,128)S(1)}, f32[6,8,128]{2,1,0:T(8,128)S(1)}, u32[]{:S(2)}, u32[]{:S(2)}) %collective-permute-start.3) | collective-permute-done | bytes 24608 | tf_op jit(solution)/shard_map/ppermute | solution.py:658
  10.3 0.2 shard_map.106
  10.5 0.2 collective-permute-start.5
  10.7 1.7 %collective-permute-start.6 = (f32[6,8,128]{2,1,0:T(8,128)S(1)}, f32[6,8,128]{2,1,0:T(8,128)S(1)}, u32[]{:S(2)}, u32[]{:S(2)}) collective-permute-start(f32[6,8,128]{2,1,0:T(8,128)S(1)} %get-tuple-element.52), channel_id=1, source_target_pairs={{0,8},{1,9},{2,10},{3,11},{4,12},{5,13},{6,14},{7,15},{8,0},{9,1},... | collective-permute-start | bytes 73736 | tf_op jit(solution)/shard_map/ppermute | solution.py:658
  12.6 0.5 %collective-permute-start.8 = (f32[6,8,128]{2,1,0:T(8,128)S(1)}, f32[6,8,128]{2,1,0:T(8,128)S(1)}, u32[]{:S(2)}, u32[]{:S(2)}) collective-permute-start(f32[6,8,128]{2,1,0:T(8,128)S(1)} %get-tuple-element.54), channel_id=1, source_target_pairs={{0,6},{1,7},{2,4},{3,5},{4,2},{5,3},{6,0},{7,1},{8,14},{9,15},{10,... | collective-permute-start | bytes 73736 | tf_op jit(solution)/shard_map/ppermute | solution.py:658
  13.0 0.2 shard_map.107.base
  13.5 1.0 %collective-permute-done.6.refs_1_ = f32[6,8,128]{2,1,0:T(8,128)S(1)} collective-permute-done((f32[6,8,128]{2,1,0:T(8,128)S(1)}, f32[6,8,128]{2,1,0:T(8,128)S(1)}, u32[]{:S(2)}, u32[]{:S(2)}) %collective-permute-start.6) | collective-permute-done | bytes 24608 | tf_op jit(solution)/shard_map/ppermute | solution.py:658
  14.6 1.3 %collective-permute-done.8.refs_3_ = f32[6,8,128]{2,1,0:T(8,128)S(1)} collective-permute-done((f32[6,8,128]{2,1,0:T(8,128)S(1)}, f32[6,8,128]{2,1,0:T(8,128)S(1)}, u32[]{:S(2)}, u32[]{:S(2)}) %collective-permute-start.8) | collective-permute-done | bytes 24608 | tf_op jit(solution)/shard_map/ppermute | solution.py:658
  15.8 1.3 %shard_map.110 = (f32[5,64,128]{2,1,0:T(8,128)S(1)}, f32[32,128]{1,0:T(8,128)}, f32[5,8,128]{2,1,0:T(8,128)S(1)}, f32[5,8,128]{2,1,0:T(8,128)S(1)}, f32[1,8,128]...) custom-call(f32[5,64,128]{2,1,0:T(8,128)S(1)} %shard_map.107.base, ...), custom_call_target="tpu_custom_call" | custom-call | flops 2000000 | bytes 1000000 | tf_op jit(solution)/shard_map/pallas_call | solution.py:613
  17.1 4.2 %all-to-all-start = ((f32[32,1,128]{2,1,0:T(1,128)}), f32[32,1,128]{2,1,0:T(1,128)S(1)}, u32[]{:S(2)}, u32[]{:S(2)}) async-start(f32[32,1,128]{2,1,0:T(1,128)} %bitcast.21), calls=%async_computation | async-start | bytes 32768 | tf_op jit(solution)/shard_map/all_to_all | solution.py:723
  21.2 1.8 %collective-permute-start.9 = (f32[5,8,128]{2,1,0:T(8,128)S(1)}, f32[5,8,128]{2,1,0:T(8,128)S(1)}, u32[]{:S(2)}, u32[]{:S(2)}) collective-permute-start(f32[5,8,128]{2,1,0:T(8,128)S(1)} %get-tuple-element.57), channel_id=1, source_target_pairs={{0,8},{1,9},{2,10},{3,11},{4,12},{5,13},{6,14},{7,15},{8,0},{9,1},... | collective-permute-start | bytes 61448 | tf_op jit(solution)/shard_map/ppermute | solution.py:658
  23.1 0.9 %collective-permute-start.10 = (f32[5,8,128]{2,1,0:T(8,128)S(1)}, f32[5,8,128]{2,1,0:T(8,128)S(1)}, u32[]{:S(2)}, u32[]{:S(2)}) collective-permute-start(f32[5,8,128]{2,1,0:T(8,128)S(1)} %get-tuple-element.58), channel_id=1, source_target_pairs={{0,6},{1,7},{2,4},{3,5},{4,2},{5,3},{6,0},{7,1},{8,14},{9,15},{10,... | collective-permute-start | bytes 61448 | tf_op jit(solution)/shard_map/ppermute | solution.py:658
  24.0 0.6 %collective-permute-start.12 = (f32[5,8,128]{2,1,0:T(8,128)S(1)}, f32[5,8,128]{2,1,0:T(8,128)S(1)}, u32[]{:S(2)}, u32[]{:S(2)}) collective-permute-start(f32[5,8,128]{2,1,0:T(8,128)S(1)} %get-tuple-element.60), channel_id=1, source_target_pairs={{0,2},{1,3},{2,0},{3,1},{4,6},{5,7},{6,4},{7,5},{8,10},{9,11},{10,... | collective-permute-start | bytes 61448 | tf_op jit(solution)/shard_map/ppermute | solution.py:658
  24.7 1.5 %collective-permute-start.11 = (f32[1,8,128]{2,1,0:T(8,128)S(1)}, f32[1,8,128]{2,1,0:T(8,128)S(1)}, u32[]{:S(2)}, u32[]{:S(2)}) collective-permute-start(f32[1,8,128]{2,1,0:T(8,128)S(1)} %get-tuple-element.59), channel_id=1, source_target_pairs={{0,1},{1,0},{2,3},{3,2},{4,5},{5,4},{6,7},{7,6},{8,9},{9,8},{10,11... | collective-permute-start | bytes 12296 | tf_op jit(solution)/shard_map/ppermute | solution.py:658
  26.1 0.2 shard_map.111.base
  26.3 2.0 %collective-permute-done.11.refs_2_ = f32[1,8,128]{2,1,0:T(8,128)S(1)} collective-permute-done((f32[1,8,128]{2,1,0:T(8,128)S(1)}, f32[1,8,128]{2,1,0:T(8,128)S(1)}, u32[]{:S(2)}, u32[]{:S(2)}) %collective-permute-start.11) | collective-permute-done | bytes 4128 | tf_op jit(solution)/shard_map/ppermute | solution.py:658
  28.4 0.9 %shard_map.112 = (f32[5,64,128]{2,1,0:T(8,128)}, f32[1,40]{1,0:T(1,128)}) custom-call(f32[5,64,128]{2,1,0:T(8,128)S(1)} %shard_map.111.base, f32[32,128]{1,0:T(8,128)S(1)} %bitcast.13, f32[5,8,128]{2,1,0:T(8,128)S(1)} %collective-permute-done.9.refs_0_, f32[5,8,128]{2,1,0:T(8,128)S(1)} %collective-permute-done.10.refs_1_, ...), custom_call_target="tpu_custom_call" | custom-call | flops 2000000 | bytes 1000000 | tf_op jit(solution)/shard_map/pallas_call | solution.py:613
  (19 shorter events, 0.7 us)
Async XLA Ops:
  2.1 7.2 %collective-permute-start = (f32[6,8,128]{2,1,0:T(8,128)S(1)}, f32[6,8,128]{2,1,0:T(8,128)S(1)}, u32[]{:S(2)}, u32[]{:S(2)}) collective-permute-start(f32[6,8,128]{2,1,0:T(8,128)S(1)} %get-tuple-element.38), channel_id=1, source_target_pairs={{0,2},{1,3},{2,0},{3,1},{4,6},{5,7},{6,4},{7,5},{8,10},{9,11},{10,... | collective-permute-start | bytes 73736 | tf_op jit(solution)/shard_map/ppermute | solution.py:658
  2.6 5.8 %copy-start = (s32[4,4,2]{1,2,0:T(2,128)S(1)}, s32[4,4,2]{1,2,0:T(2,128)}, u32[]{:S(2)}) copy-start(s32[4,4,2]{1,2,0:T(2,128)} %param.16) | copy-start | bytes 388
  2.6 6.7 %collective-permute-start.1 = (f32[6,8,128]{2,1,0:T(8,128)S(1)}, f32[6,8,128]{2,1,0:T(8,128)S(1)}, u32[]{:S(2)}, u32[]{:S(2)}) collective-permute-start(f32[6,8,128]{2,1,0:T(8,128)S(1)} %get-tuple-element.39), channel_id=1, source_target_pairs={{0,1},{1,0},{2,3},{3,2},{4,5},{5,4},{6,7},{7,6},{8,16},{9,17},{10,... | collective-permute-start | bytes 73736 | tf_op jit(solution)/shard_map/ppermute | solution.py:658
  5.2 4.1 %collective-permute-start.2 = (f32[6,8,128]{2,1,0:T(8,128)S(1)}, f32[6,8,128]{2,1,0:T(8,128)S(1)}, u32[]{:S(2)}, u32[]{:S(2)}) collective-permute-start(f32[6,8,128]{2,1,0:T(8,128)S(1)} %get-tuple-element.40), channel_id=1, source_target_pairs={{0,8},{1,9},{2,10},{3,11},{4,12},{5,13},{6,14},{7,15},{8,0},{9,1},... | collective-permute-start | bytes 73736 | tf_op jit(solution)/shard_map/ppermute | solution.py:658
  6.8 3.5 %collective-permute-start.3 = (f32[6,8,128]{2,1,0:T(8,128)S(1)}, f32[6,8,128]{2,1,0:T(8,128)S(1)}, u32[]{:S(2)}, u32[]{:S(2)}) collective-permute-start(f32[6,8,128]{2,1,0:T(8,128)S(1)} %get-tuple-element.41), channel_id=1, source_target_pairs={{0,6},{1,7},{2,4},{3,5},{4,2},{5,3},{6,0},{7,1},{8,14},{9,15},{10,... | collective-permute-start | bytes 73736 | tf_op jit(solution)/shard_map/ppermute | solution.py:658
  7.8 0.7 %copy-start.1 = (s32[32]{0:T(128)S(1)}, s32[32]{0:T(128)}, u32[]{:S(2)}) copy-start(s32[32]{0:T(128)} %owners.1) | copy-start | bytes 388
  7.8 1.5 %collective-permute-start.4 = (f32[5,8,128]{2,1,0:T(8,128)S(1)}, f32[5,8,128]{2,1,0:T(8,128)S(1)}, u32[]{:S(2)}, u32[]{:S(2)}) collective-permute-start(f32[5,8,128]{2,1,0:T(8,128)S(1)} %get-tuple-element.42.own), channel_id=1, source_target_pairs={{0,2},{1,3},{2,0},{3,1},{4,6},{5,7},{6,4},{7,5},{8,9},{9,8},{10,11... | collective-permute-start | bytes 61448 | tf_op jit(solution)/shard_map/ppermute | solution.py:658
  10.5 3.0 %collective-permute-start.5 = (f32[6,8,128]{2,1,0:T(8,128)S(1)}, f32[6,8,128]{2,1,0:T(8,128)S(1)}, u32[]{:S(2)}, u32[]{:S(2)}) collective-permute-start(f32[6,8,128]{2,1,0:T(8,128)S(1)} %get-tuple-element.51), channel_id=1, source_target_pairs={{0,2},{1,3},{2,0},{3,1},{4,6},{5,7},{6,4},{7,5},{8,10},{9,11},{10,... | collective-permute-start | bytes 73736 | tf_op jit(solution)/shard_map/ppermute | solution.py:658
  10.7 3.9 %collective-permute-start.6 = (f32[6,8,128]{2,1,0:T(8,128)S(1)}, f32[6,8,128]{2,1,0:T(8,128)S(1)}, u32[]{:S(2)}, u32[]{:S(2)}) collective-permute-start(f32[6,8,128]{2,1,0:T(8,128)S(1)} %get-tuple-element.52), channel_id=1, source_target_pairs={{0,8},{1,9},{2,10},{3,11},{4,12},{5,13},{6,14},{7,15},{8,0},{9,1},... | collective-permute-start | bytes 73736 | tf_op jit(solution)/shard_map/ppermute | solution.py:658
  12.4 2.2 %collective-permute-start.7 = (f32[6,8,128]{2,1,0:T(8,128)S(1)}, f32[6,8,128]{2,1,0:T(8,128)S(1)}, u32[]{:S(2)}, u32[]{:S(2)}) collective-permute-start(f32[6,8,128]{2,1,0:T(8,128)S(1)} %get-tuple-element.53), channel_id=1, source_target_pairs={{0,2},{1,3},{2,0},{3,1},{4,6},{5,7},{6,4},{7,5},{8,16},{9,17},{10,... | collective-permute-start | bytes 73736 | tf_op jit(solution)/shard_map/ppermute | solution.py:658
  12.6 3.3 %collective-permute-start.8 = (f32[6,8,128]{2,1,0:T(8,128)S(1)}, f32[6,8,128]{2,1,0:T(8,128)S(1)}, u32[]{:S(2)}, u32[]{:S(2)}) collective-permute-start(f32[6,8,128]{2,1,0:T(8,128)S(1)} %get-tuple-element.54), channel_id=1, source_target_pairs={{0,6},{1,7},{2,4},{3,5},{4,2},{5,3},{6,0},{7,1},{8,14},{9,15},{10,... | collective-permute-start | bytes 73736 | tf_op jit(solution)/shard_map/ppermute | solution.py:658
  17.1 11.3 %all-to-all-start = ((f32[32,1,128]{2,1,0:T(1,128)}), f32[32,1,128]{2,1,0:T(1,128)S(1)}, u32[]{:S(2)}, u32[]{:S(2)}) async-start(f32[32,1,128]{2,1,0:T(1,128)} %bitcast.21), calls=%async_computation | async-start | bytes 32768 | tf_op jit(solution)/shard_map/all_to_all | solution.py:723
  21.2 7.0 %collective-permute-start.9 = (f32[5,8,128]{2,1,0:T(8,128)S(1)}, f32[5,8,128]{2,1,0:T(8,128)S(1)}, u32[]{:S(2)}, u32[]{:S(2)}) collective-permute-start(f32[5,8,128]{2,1,0:T(8,128)S(1)} %get-tuple-element.57), channel_id=1, source_target_pairs={{0,8},{1,9},{2,10},{3,11},{4,12},{5,13},{6,14},{7,15},{8,0},{9,1},... | collective-permute-start | bytes 61448 | tf_op jit(solution)/shard_map/ppermute | solution.py:658
  23.1 5.2 %collective-permute-start.10 = (f32[5,8,128]{2,1,0:T(8,128)S(1)}, f32[5,8,128]{2,1,0:T(8,128)S(1)}, u32[]{:S(2)}, u32[]{:S(2)}) collective-permute-start(f32[5,8,128]{2,1,0:T(8,128)S(1)} %get-tuple-element.58), channel_id=1, source_target_pairs={{0,6},{1,7},{2,4},{3,5},{4,2},{5,3},{6,0},{7,1},{8,14},{9,15},{10,... | collective-permute-start | bytes 61448 | tf_op jit(solution)/shard_map/ppermute | solution.py:658
  24.0 4.3 %collective-permute-start.12 = (f32[5,8,128]{2,1,0:T(8,128)S(1)}, f32[5,8,128]{2,1,0:T(8,128)S(1)}, u32[]{:S(2)}, u32[]{:S(2)}) collective-permute-start(f32[5,8,128]{2,1,0:T(8,128)S(1)} %get-tuple-element.60), channel_id=1, source_target_pairs={{0,2},{1,3},{2,0},{3,1},{4,6},{5,7},{6,4},{7,5},{8,10},{9,11},{10,... | collective-permute-start | bytes 61448 | tf_op jit(solution)/shard_map/ppermute | solution.py:658
  24.6 3.6 %collective-permute-start.13 = (f32[5,8,128]{2,1,0:T(8,128)S(1)}, f32[5,8,128]{2,1,0:T(8,128)S(1)}, u32[]{:S(2)}, u32[]{:S(2)}) collective-permute-start(f32[5,8,128]{2,1,0:T(8,128)S(1)} %get-tuple-element.61), channel_id=1, source_target_pairs={{0,2},{1,3},{2,0},{3,1},{4,6},{5,7},{6,4},{7,5},{8,16},{9,17},{10,... | collective-permute-start | bytes 61448 | tf_op jit(solution)/shard_map/ppermute | solution.py:658
  24.7 3.6 %collective-permute-start.11 = (f32[1,8,128]{2,1,0:T(8,128)S(1)}, f32[1,8,128]{2,1,0:T(8,128)S(1)}, u32[]{:S(2)}, u32[]{:S(2)}) collective-permute-start(f32[1,8,128]{2,1,0:T(8,128)S(1)} %get-tuple-element.59), channel_id=1, source_target_pairs={{0,1},{1,0},{2,3},{3,2},{4,5},{5,4},{6,7},{7,6},{8,9},{9,8},{10,11... | collective-permute-start | bytes 12296 | tf_op jit(solution)/shard_map/ppermute | solution.py:658
